TPU v7x, 32 devices: a whole 2x2x4 slice. The times are simulated.
32 devices in a mesh: groups: 2 (over y), dp: 4 (over x, core), mp: 4 (over z).
Axes of the slice: x: 2, y: 2, z: 4, core: 2. Of those that a mesh axis runs over, the one named last changes fastest.
Arguments:
- hidden: bfloat16 [8192, 8192], P(('groups', 'dp'), 'mp'), parts along dimension 0, may hold values from -6 to 6
- w_kv: bfloat16 [8192, 2048], P('mp'), may hold values from -0.0625 to 0.0625
- grad_kv: bfloat16 [8192, 2048], P(('groups', 'dp', 'mp')), parts along dimension 0, may hold values from -6 to 6
- proj_in: bfloat16 [8192, 128], P('mp'), may hold values from -0.0625 to 0.0625
- proj_out: bfloat16 [2, 1024, 64], replicated, may hold values from -0.1875 to 0.1875
- queries: bfloat16 [2048, 8192], P('dp', 'mp'), may hold values from -0.001953125 to 0.001953125
Outputs:
- input_grad: bfloat16 [8192, 8192], P(('groups', 'dp'), 'mp'), parts along dimension 0
- scores: float32 [8, 2048], P(('groups', 'dp'), 'mp'), parts along dimension 0
There are 2 independent parts, one for each index of `groups`. A program takes and returns all parts, laid end to end along the dimension named above; an argument that names none is the same for every part. Nothing has to cross between parts.
All inputs are finite; a program needn't handle non-finite values.
Results may differ from a plain program's by a relative error of at most 0.001.
Values may be sent and summed in bfloat16 or wider, within the bound.
No kernel may reach another device: no remote copies, remote signals or barrier semaphores. Data moves between devices by JAX's collectives and lax.ppermute only.
A program may use at most 128 MiB of HBM per device.

v0:
```python
import jax
import jax.numpy as jnp
from jax import lax
from jax.sharding import PartitionSpec as P

SEQ = 1024


def passed_along(value, axis, steps):
    count = lax.axis_size(axis)
    pairs = [(source, (source + steps) % count) for source in range(count)]
    return lax.ppermute(value, axis, pairs)


def per_sequence(low_rows, grad_rows, seq_index, count):
    rank = low_rows.shape[1] // 2
    onehot = (seq_index[:, None] == jnp.arange(count, dtype=jnp.int32)[None, :]).astype(jnp.float32)
    layers = []
    for layer in range(2):
        part_in = low_rows[:, layer * rank : (layer + 1) * rank]
        part_out = grad_rows[:, layer * rank : (layer + 1) * rank]
        spread = (onehot[:, :, None] * part_in[:, None, :]).reshape(low_rows.shape[0], count * rank)
        outer = lax.dot_general(
            spread,
            part_out,
            (((0,), (0,)), ((), ())),
            precision=lax.Precision.HIGHEST,
            preferred_element_type=jnp.float32,
        )
        layers.append(outer.reshape(count, 1, rank * rank))
    return jnp.concatenate(layers, axis=1).reshape(count, 2 * rank * rank)


def block_scores(features, block):
    return lax.dot_general(
        features,
        block.astype(jnp.float32),
        (((1,), (1,)), ((), ())),
        precision=lax.Precision.HIGHEST,
        preferred_element_type=jnp.float32,
    )


def on_device(hidden, w_kv, grad_kv, proj_in, proj_out, queries):
    rows = hidden.shape[0]
    local_rows = grad_kv.shape[0]
    width_kv = w_kv.shape[1] // 2
    count = rows // SEQ
    model_index = lax.axis_index("mp")
    input_grad = lax.dot_general(
        lax.all_gather(grad_kv, "mp", axis=0, tiled=True),
        w_kv,
        (((1,), (1,)), ((), ())),
        preferred_element_type=jnp.float32,
    ).astype(jnp.bfloat16)
    key_low = jnp.dot(grad_kv[:, :width_kv], proj_out[0], preferred_element_type=jnp.float32)
    value_low = jnp.dot(grad_kv[:, width_kv:], proj_out[1], preferred_element_type=jnp.float32)
    grad_low = jnp.concatenate([key_low, value_low], axis=1)
    block = hidden
    low_mine = lax.psum_scatter(
        jnp.dot(block, proj_in, preferred_element_type=jnp.float32),
        "mp",
        scatter_dimension=0,
        tiled=True,
    )
    seq_index = (model_index * local_rows + jnp.arange(local_rows, dtype=jnp.int32)) // SEQ
    partial_value = per_sequence(low_mine, grad_low, seq_index, count)
    features = lax.psum_scatter(partial_value, "mp", scatter_dimension=1, tiled=True)
    cycle_size = lax.axis_size("dp")
    cycle_index = lax.axis_index("dp")
    block_rows = queries.shape[0]

    def place(totals, block, owner):
        start = owner % cycle_size * block_rows
        return lax.dynamic_update_slice(
            totals, block_scores(features, block), (jnp.int32(0), start)
        )

    totals = jnp.zeros((count, block_rows * cycle_size), jnp.float32)
    totals = place(totals, queries, cycle_index)
    moving = queries
    for step in range(1, cycle_size):
        moving = passed_along(moving, "dp", 1)
        totals = place(totals, moving, cycle_index - step + cycle_size)
    scores = lax.psum_scatter(totals, "mp", scatter_dimension=1, tiled=True)
    return (input_grad, scores)


def solution(mesh):
    in_specs = (
        P(("groups", "dp"), "mp"),
        P("mp", None),
        P(("groups", "dp", "mp"), None),
        P("mp", None),
        P(),
        P("dp", "mp"),
    )
    out_specs = (P(("groups", "dp"), "mp"), P(("groups", "dp"), "mp"))
    return jax.shard_map(
        on_device, mesh=mesh, in_specs=in_specs, out_specs=out_specs, check_vma=False
    )
```

profile of v0, /device:TPU:0, one launch (start us, length us, event | category | flops | bytes accessed | tf_op | source)
XLA Modules:
  0.0 241.5 jit_solution(17335796742255776199)
XLA Ops:
  7.2 0.0 copy-start
  7.2 0.0 copy-start.2
  7.2 0.0 copy-start.3
  7.2 0.0 reduce-scatter.8.cloned.1.call-start
  7.2 1.0 copy-done
  8.2 4.2 %fusion.12 = f32[1024,128]{1,0:T(8,128)} fusion(bf16[1024,2048]{1,0:T(8,128)(2,1)} %param.6, bf16[2048,128]{1,0:T(8,128)(2,1)S(1)} %copy-done), kind=kOutput, calls=%fused_computation.26 | convolution fusion | flops 536870912 | bytes 5242880 | tf_op jit(solution)/shard_map/dot_general | solution.py:61
  12.4 0.0 reduce-scatter.8.cloned.1.call-update
  12.5 0.0 reduce-scatter.10.cloned.1.call-start
  12.5 0.0 copy-done.2
  12.5 0.5 collective-permute-start
  13.0 0.0 copy-done.3
  13.0 1.3 fusion.2
  14.4 1.3 fusion
  15.7 21.0 %reduce-scatter.8.cloned.1.call-done = f32[256,128]{1,0:T(8,128)} async-done(((f32[1024,128]{1,0:T(8,128)}), f32[256,128]{1,0:T(8,128)}) %reduce-scatter.8.cloned.1.call-update) | async-done | bytes 131088 | tf_op jit(solution)/shard_map/reduce_scatter | solution.py:60
  36.8 1.4 fusion.5
  38.1 0.1 reshape.55
  38.2 1.4 fusion.4
  39.6 0.1 reshape.56
  39.8 2.7 %copy.13 = f32[1,8192]{0,1:T(8,128)} copy(f32[1,8192]{1,0:T(1,128)S(1)} %bitcast.47) | data formatting | bytes 65536
  42.5 4.5 %bitcast_bitcast_fusion = f32[8192,1]{1,0:T(8,128)} fusion(f32[1,8192]{0,1:T(8,128)} %copy.13), kind=kLoop, calls=%fused_computation | loop fusion | bytes 65536
  47.0 0.0 reduce-scatter.10.cloned.1.call-update
  47.0 0.0 all-gather.2.cloned.1.call-start
  47.0 0.7 all-gather.2.cloned.1.call-update
  47.7 0.0 reduce-scatter.12.cloned.1.call-start
  47.8 0.0 collective-permute-done
  47.8 0.1 collective-permute-start.1
  47.8 25.8 %collective-permute-done.1 = bf16[512,2048]{1,0:T(8,128)(2,1)} collective-permute-done((bf16[512,2048]{1,0:T(8,128)(2,1)}, bf16[512,2048]{1,0:T(8,128)(2,1)}, u32[]{:S(2)}, u32[]{:S(2)}) %collective-permute-start.1) | collective-permute-done | bytes 2097184 | tf_op jit(solution)/shard_map/ppermute | solution.py:12
  73.6 0.0 collective-permute-start.2
  73.6 48.8 %reduce-scatter.10.cloned.1.call-done = f32[2048,1]{1,0:T(8,128)} async-done(((f32[8192,1]{1,0:T(8,128)}), f32[2048,1]{1,0:T(8,128)}) %reduce-scatter.10.cloned.1.call-update) | async-done | bytes 8208 | tf_op jit(solution)/shard_map/reshape.2
  122.4 0.0 copy-start.1
  122.4 3.1 %convolution_dynamic-update-slice_fusion.3 = f32[1,2048]{1,0:T(1,128)S(1)} fusion(f32[1,2048]{1,0:T(1,128)S(1)} %broadcast_in_dim.2, s32[]{:T(128)S(6)} %select_n.43, f32[2048,1]{1,0:T(8,128)} %reduce-scatter.10.cloned.1.call-done, bf16[512,2048]{1,0:T(8,128)(2,1)S(1)} %copy-done.2), kind=kOutput, calls=%fused_computation.5 | convolution fusion | flops 12582912 | bytes 2107396 | tf_op jit(solution)/shard_map/dot_general | solution.py:35
  125.5 3.7 %convolution_dynamic-update-slice_fusion.2 = f32[1,2048]{1,0:T(1,128)S(1)} fusion(f32[1,2048]{1,0:T(1,128)S(1)} %convolution_dynamic-update-slice_fusion.3, s32[]{:T(128)S(6)} %select_n.45, f32[2048,1]{1,0:T(8,128)} %reduce-scatter.10.cloned.1.call-done, bf16[512,2048]{1,0:T(8,128)(2,1)} %collective-permute-done), kind=kOutput, calls=%fused_computation.4 | convolution fusion | flops 12582912 | bytes 2107396 | tf_op jit(solution)/shard_map/dot_general | solution.py:35
  129.2 0.0 copy-done.1
  129.2 3.4 %convolution_dynamic-update-slice_fusion.1 = f32[1,2048]{1,0:T(1,128)S(1)} fusion(f32[1,2048]{1,0:T(1,128)S(1)} %convolution_dynamic-update-slice_fusion.2, s32[]{:T(128)S(6)} %select_n.47, f32[2048,1]{1,0:T(8,128)S(1)} %copy-done.1, bf16[512,2048]{1,0:T(8,128)(2,1)} %collective-permute-done.1), kind=kOutput, calls=%fused_computation.3 | convolution fusion | flops 12582912 | bytes 3147780 | tf_op jit(solution)/shard_map/dot_general | solution.py:35
  132.6 0.0 collective-permute-done.2
  132.6 3.5 %convolution_dynamic-update-slice_fusion = f32[1,2048]{1,0:T(1,128)S(1)} fusion(f32[1,2048]{1,0:T(1,128)S(1)} %convolution_dynamic-update-slice_fusion.1, s32[]{:T(128)S(6)} %select_n.49, f32[2048,1]{1,0:T(8,128)S(1)} %copy-done.1, bf16[512,2048]{1,0:T(8,128)(2,1)} %collective-permute-done.2), kind=kOutput, calls=%fused_computation.2 | convolution fusion | flops 12582912 | bytes 3147780 | tf_op jit(solution)/shard_map/dot_general | solution.py:35
  136.1 1.4 copy.10
  137.5 0.0 reduce-scatter.12.cloned.1.call-update
  137.5 67.9 %all-gather.2.cloned.1.call-done = bf16[1024,2048]{1,0:T(8,128)(2,1)} async-done(((bf16[256,2048]{1,0:T(8,128)(2,1)}), bf16[1024,2048]{1,0:T(8,128)(2,1)}) %all-gather.2.cloned.1.call-update) | async-done | bytes 4194320 | tf_op jit(solution)/shard_map/all_gather | solution.py:51
  205.4 13.9 %convolution_convert_fusion = bf16[1024,2048]{1,0:T(8,128)(2,1)} fusion(bf16[1024,2048]{1,0:T(8,128)(2,1)} %all-gather.2.cloned.1.call-done, bf16[2048,2048]{1,0:T(8,128)(2,1)} %param.7), kind=kOutput, calls=%fused_computation.1 | convolution fusion | flops 8592031744 | bytes 16777216 | tf_op jit(solution)/shard_map/dot_general | solution.py:50
  219.2 14.1 %reduce-scatter.12.cloned.1.call-done = f32[512,1]{1,0:T(8,128)} async-done(((f32[2048,1]{1,0:T(8,128)}), f32[512,1]{1,0:T(8,128)}) %reduce-scatter.12.cloned.1.call-update) | async-done | bytes 2064
  233.3 1.6 copy.11
  (4 shorter events, 0.1 us)
Async XLA Ops:
  7.2 1.0 copy-start
  7.2 5.3 %copy-start.2 = (bf16[512,2048]{1,0:T(8,128)(2,1)S(1)}, bf16[512,2048]{1,0:T(8,128)(2,1)}, u32[]{:S(2)}) copy-start(bf16[512,2048]{1,0:T(8,128)(2,1)} %param.11) | copy-start | bytes 6291460
  7.2 5.8 %copy-start.3 = (bf16[2,1024,64]{1,2,0:T(8,128)(2,1)S(1)}, bf16[2,1024,64]{1,2,0:T(8,128)(2,1)}, u32[]{:S(2)}) copy-start(bf16[2,1024,64]{1,2,0:T(8,128)(2,1)} %param.10) | copy-start | bytes 786436
  7.2 29.6 %reduce-scatter.8.cloned.1.call-start = ((), (), s32[]{:S(2)}) async-start(), calls=%async_computation.4 | async-start | bytes 655360 | tf_op jit(solution)/shard_map/reduce_scatter | solution.py:60
  12.5 110.0 %reduce-scatter.10.cloned.1.call-start = ((), (), s32[]{:S(2)}) async-start(), calls=%async_computation.5 | async-start | bytes 5242880 | tf_op jit(solution)/shard_map/reshape.2
  12.5 35.3 %collective-permute-start = (bf16[512,2048]{1,0:T(8,128)(2,1)S(1)}, bf16[512,2048]{1,0:T(8,128)(2,1)}, u32[]{:S(2)}, u32[]{:S(2)}) collective-permute-start(bf16[512,2048]{1,0:T(8,128)(2,1)S(1)} %copy-done.2), channel_id=1, source_target_pairs={{0,4},{4,8},{8,12},{12,0},{1,5},{5,9},{9,13},{13,1},{2,6},{6,10},{... | collective-permute-start | bytes 6291464 | tf_op jit(solution)/shard_map/ppermute | solution.py:12
  47.0 158.4 %all-gather.2.cloned.1.call-start = ((), (), s32[]{:S(2)}) async-start(), calls=%async_computation.3 | async-start | bytes 5242880 | tf_op jit(solution)/shard_map/all_gather | solution.py:51
  47.7 185.6 %reduce-scatter.12.cloned.1.call-start = ((), (), s32[]{:S(2)}) async-start(), calls=%async_computation.6 | async-start | bytes 1310720
  47.8 25.8 %collective-permute-start.1 = (bf16[512,2048]{1,0:T(8,128)(2,1)}, bf16[512,2048]{1,0:T(8,128)(2,1)}, u32[]{:S(2)}, u32[]{:S(2)}) collective-permute-start(bf16[512,2048]{1,0:T(8,128)(2,1)} %collective-permute-done), channel_id=1, source_target_pairs={{0,4},{4,8},{8,12},{12,0},{1,5},{5,9},{9,13},{13,1},{2,6},{6,10},{... | collective-permute-start | bytes 6291464 | tf_op jit(solution)/shard_map/ppermute | solution.py:12
  73.6 59.0 %collective-permute-start.2 = (bf16[512,2048]{1,0:T(8,128)(2,1)}, bf16[512,2048]{1,0:T(8,128)(2,1)}, u32[]{:S(2)}, u32[]{:S(2)}) collective-permute-start(bf16[512,2048]{1,0:T(8,128)(2,1)} %collective-permute-done.1), channel_id=1, source_target_pairs={{0,4},{4,8},{8,12},{12,0},{1,5},{5,9},{9,13},{13,1},{2,6},{6,10},{... | collective-permute-start | bytes 6291464 | tf_op jit(solution)/shard_map/ppermute | solution.py:12
  122.4 6.8 %copy-start.1 = (f32[2048,1]{1,0:T(8,128)S(1)}, f32[2048,1]{1,0:T(8,128)}, u32[]{:S(2)}) copy-start(f32[2048,1]{1,0:T(8,128)} %reduce-scatter.10.cloned.1.call-done) | copy-start | bytes 24580
Sparse Core Ops, SparseCore 0:
  12.6 24.1 reduce-scatter.7
  47.1 75.2 reduce-scatter.9
  124.1 81.2 all-gather.1
  207.6 25.6 reduce-scatter.11
where the time goes:
time: 242 us
  waiting for transfers between devices  178 us (74%)
  matrix products  37.2 us (15%)
  between operations  13.9 us (6%)
  local copies, waits for them, and re-layouts  11.4 us (5%)
    all_gather x1, waiting for transfers between devices, on_device(): lax.all_gather(grad_kv, 'mp', axis=0, tiled=True)  67.9 us
    another operation x1, waiting for transfers between devices  48.8 us
    ppermute x3, waiting for transfers between devices, passed_along(): return lax.ppermute(value, axis, pairs)  25.8 us
    reduce_scatter x1, waiting for transfers between devices, on_device(): lax.psum_scatter(jnp.dot(block, proj_in, preferred_element_type=jnp.float...  21 us
    unnamed x5, waiting for transfers between devices  14.8 us
    dot_general x1, matrix products, on_device(): lax.dot_general(lax.all_gather(grad_kv, 'mp', axis=0, tiled=True), w_kv,...  13.9 us
    dot_general x4, matrix products, block_scores(): lax.dot_general(features, block.astype(jnp.float32), (((1,), (1,)), ((),...  13.7 us
    unnamed x13, local copies, waits for them, and re-layouts  11.2 us
  transfers between devices with their start and end apart: 7, of which 5 were waited for; matrix products, arithmetic and copies ran while one was open for 17% of the time, Pallas kernels for 0%

commit v1 on v0

v1 whole, which is shorter than its diff:
```python
import jax
import jax.numpy as jnp
from jax import lax
from jax.sharding import PartitionSpec as P

SEQ = 1024
CHUNKS = 2


def three_terms(value):
    high = lax.reduce_precision(value, 8, 7)
    rest = value - high
    middle = lax.reduce_precision(rest, 8, 7)
    low = rest - middle
    return [term.astype(jnp.bfloat16) for term in (high, middle, low)]


def low_rank_rows(rows, proj_out):
    width = rows.shape[1] // 2
    parts = [
        jnp.dot(rows[:, layer * width : (layer + 1) * width], proj_out[layer], preferred_element_type=jnp.float32)
        for layer in range(2)
    ]
    return jnp.concatenate(parts, axis=1)


def on_device(hidden, w_kv, grad_kv, proj_in, proj_out, queries):
    rows = hidden.shape[0]
    local_rows = grad_kv.shape[0]
    count = rows // SEQ
    rank = proj_out.shape[2]
    n = lax.axis_size("mp")
    me = lax.axis_index("mp")
    half = n // 2
    lower = me < half
    chunk_rows = local_rows // CHUNKS

    own = [grad_kv[c * chunk_rows : (c + 1) * chunk_rows] for c in range(CHUNKS)]
    down = [own]
    up = [own]
    for step in range(1, n):
        down_pairs = [(source, source - 1) for source in range(1, n - step + 1)]
        up_pairs = [(source, source + 1) for source in range(step - 1, n - 1)]
        down_now, up_now = [], []
        for c in range(CHUNKS):
            down_now.append(lax.ppermute(down[-1][c], "mp", down_pairs))
            up_now.append(lax.ppermute(up[-1][c], "mp", up_pairs))
        down.append(down_now)
        up.append(up_now)

    def near(step, c):
        return jnp.where(lower, down[step][c], up[step][c])

    def other(step, c):
        return jnp.where(lower, up[step][c], down[step][c])

    def near_block(step):
        return jnp.where(lower, me + step, me - step + n) % n

    output = jnp.zeros((n * CHUNKS, chunk_rows, w_kv.shape[0]), jnp.bfloat16)
    for step in range(n):
        for c in range(CHUNKS):
            if step == 0:
                chunk = own[c]
            elif step <= half:
                chunk = near(step, c)
            else:
                inside = jnp.where(lower, me + step < n, me - step >= 0)
                chunk = jnp.where(inside, near(step, c), other(n - step, c))
            product = lax.dot_general(
                chunk, w_kv, (((1,), (1,)), ((), ())), preferred_element_type=jnp.float32
            ).astype(jnp.bfloat16)
            place = near_block(step) * CHUNKS + c
            output = lax.dynamic_update_slice(output, product[None], (place, jnp.int32(0), jnp.int32(0)))
    input_grad = output.reshape(rows, w_kv.shape[0])

    partial_in = jnp.dot(hidden, proj_in, preferred_element_type=jnp.float32)
    low_in = partial_in
    for step in range(half - 1):
        pairs = [(step, step + 1), (n - 1 - step, n - 2 - step)]
        low_in = partial_in + lax.ppermute(low_in, "mp", pairs)

    low_out = jnp.zeros((n * CHUNKS, chunk_rows, 2 * rank), jnp.float32)
    for step in range(half + 1):
        for c in range(CHUNKS):
            parts = [(near_block(step), own[c] if step == 0 else near(step, c))]
            if 0 < step < half:
                parts.append((jnp.where(lower, me - step + n, me + step) % n, other(step, c)))
            for block, chunk in parts:
                low_out = lax.dynamic_update_slice(
                    low_out,
                    low_rank_rows(chunk, proj_out)[None],
                    (block * CHUNKS + c, jnp.int32(0), jnp.int32(0)),
                )
    left = low_in.reshape(count, SEQ, 2 * rank)
    right = low_out.reshape(count, SEQ, 2 * rank)
    half_sums = jnp.concatenate(
        [
            lax.dot_general(
                left[:, :, layer * rank : (layer + 1) * rank],
                right[:, :, layer * rank : (layer + 1) * rank],
                (((1,), (1,)), ((0,), (0,))),
                precision=lax.Precision.HIGHEST,
                preferred_element_type=jnp.float32,
            )
            for layer in range(2)
        ],
        axis=1,
    )

    slab = 2 * rank // n

    slabs = lax.optimization_barrier(half_sums.reshape(count, n, slab, rank).transpose(1, 0, 2, 3))

    def slab_of(index):
        return lax.dynamic_index_in_dim(slabs, index, axis=0, keepdims=False)

    first, second = half - 1, half
    mine = jnp.where((me == first) | (me == second), slab_of(me), 0.0)
    for away in range(half):
        if away > 0:
            mine = mine + lax.ppermute(
                slab_of(jnp.where(lower, first - away, second + away)),
                "mp",
                [(first, first - away), (second, second + away)],
            )
        mine = mine + lax.ppermute(
            slab_of(jnp.where(lower, second + away, first - away)),
            "mp",
            [(first, second + away), (second, first - away)],
        )

    shards = lax.axis_size("dp")
    shard = lax.axis_index("dp")
    block_rows = queries.shape[0]
    mine = mine.reshape(count, slab * rank)
    all_features = [mine] + [
        lax.ppermute(mine, "dp", [(source, (source + step) % shards) for source in range(shards)])
        for step in range(1, shards)
    ]
    stacked = jnp.concatenate(all_features, axis=0)
    terms = jnp.concatenate(three_terms(stacked), axis=0)
    products = lax.dot_general(
        terms, queries, (((1,), (1,)), ((), ())), preferred_element_type=jnp.float32
    ).reshape(3, shards, count, block_rows)
    partial_scores = products[0] + (products[1] + products[2])

    total = jnp.zeros((count, shards * block_rows), jnp.float32)
    for step in range(shards):
        back = partial_scores[step]
        if step > 0:
            back = lax.ppermute(back, "dp", [(source, (source - step) % shards) for source in range(shards)])
        total = lax.dynamic_update_slice(
            total, back, (jnp.int32(0), (shard + step) % shards * block_rows)
        )
    out_columns = shards * block_rows // n

    def columns_of(index):
        return lax.dynamic_slice(total, (jnp.int32(0), index * out_columns), (count, out_columns))

    scores = columns_of(me)
    for step in range(1, n):
        scores = scores + lax.ppermute(
            columns_of((me + step) % n), "mp", [(source, (source + step) % n) for source in range(n)]
        )
    return (input_grad, scores)


def solution(mesh):
    in_specs = (
        P(("groups", "dp"), "mp"),
        P("mp", None),
        P(("groups", "dp", "mp"), None),
        P("mp", None),
        P(),
        P("dp", "mp"),
    )
    out_specs = (P(("groups", "dp"), "mp"), P(("groups", "dp"), "mp"))
    return jax.shard_map(
        on_device, mesh=mesh, in_specs=in_specs, out_specs=out_specs, check_vma=False
    )
```

time: 242 us -> 146 us (0.60)
  waiting for transfers between devices: 178 us -> 26.2 us
  starting transfers between devices: 0.72 us -> 42.6 us
  matrix products: 37.2 us -> 59.8 us
  between operations: 13.9 us -> 1.56 us
  other arithmetic: 0.05 us -> 6.59 us
  local copies, waits for them, and re-layouts: 11.4 us -> 7.94 us
    all_gather x1 -> x0, waiting for transfers between devices: 67.9 us -> none  [on_device(): lax.all_gather(grad_kv, 'mp', axis=0, tiled=True)]
    another operation x1 -> x0, waiting for transfers between devices: 48.8 us -> none
    ppermute x3 -> x25, starting transfers between devices: 0.56 us -> 42.6 us  [the longest x6 15.5 us: on_device(): up_now.append(lax.ppermute(up[-1][c], 'mp', up_pairs))]
    dot_general x10 -> x28, matrix products: 37.2 us -> 59.8 us  [the longest x8 45.2 us: on_device(): lax.dot_general(chunk, w_kv, (((1,), (1,)), ((), ())), preferred_element_...]
    reduce_scatter x1 -> x0, waiting for transfers between devices: 21 us -> none  [on_device(): lax.psum_scatter(jnp.dot(block, proj_in, preferred_element_type=jnp.float...]
    unnamed x5 -> x0, waiting for transfers between devices: 14.8 us -> none
    unnamed x13 -> x44, local copies, waits for them, and re-layouts: 11.2 us -> 3.95 us
    select_n x0 -> x4, other arithmetic: none -> 3.7 us  [the longest x2 2.55 us: other(): return jnp.where(lower, up[step][c], down[step][c])]
  transfers between devices with their start and end apart: 7 -> 25, of which waited for: 5 -> 5; matrix products, arithmetic and copies ran while one was open for 17% -> 40% of each run, Pallas kernels for 0% -> 0%
where the time goes in v1:
time: 146 us; the launch traced here: 145 us
  matrix products  59.8 us (41%)
  starting transfers between devices  42.6 us (29%)
  waiting for transfers between devices  26.2 us (18%)
  local copies, waits for them, and re-layouts  7.94 us (5%)
  other arithmetic  6.59 us (5%)
  between operations  1.56 us (1%)
    dot_general x8, matrix products, on_device(): lax.dot_general(chunk, w_kv, (((1,), (1,)), ((), ())), preferred_element_...  45.2 us
    ppermute x6, waiting for transfers between devices, on_device(): down_now.append(lax.ppermute(down[-1][c], 'mp', down_pairs))  23.1 us
    ppermute x6, starting transfers between devices, on_device(): up_now.append(lax.ppermute(up[-1][c], 'mp', up_pairs))  15.5 us
    ppermute x3, starting transfers between devices, on_device(): lax.ppermute(columns_of((me + step) % n), 'mp', [(source, (source + step)...  7.88 us
    ppermute x6, starting transfers between devices, on_device(): down_now.append(lax.ppermute(down[-1][c], 'mp', down_pairs))  7.84 us
    dot_general x16, matrix products, low_rank_rows(): jnp.dot(rows[:, layer * width:(layer + 1) * width], proj_out[layer], pref...  5.26 us
    dot_general x1, matrix products, on_device(): partial_in = jnp.dot(hidden, proj_in, preferred_element_type=jnp.float32)  4.64 us
    dot_general x2, matrix products, on_device(): lax.dot_general(left[:, :, layer * rank:(layer + 1) * rank], right[:, :,...  4.03 us
  transfers between devices with their start and end apart: 25, of which 5 were waited for; matrix products, arithmetic and copies ran while one was open for 40% of the time, Pallas kernels for 0%

profile of v1, /device:TPU:0, one launch (start us, length us, event | category | flops | bytes accessed | tf_op | source)
XLA Modules:
  0.0 144.8 jit_solution(5446709746110770700)
XLA Ops:
  0.7 2.4 %fusion.104 = (bf16[128,2048]{1,0:T(8,128)(2,1)}, bf16[128,2048]{1,0:T(8,128)(2,1)}) fusion(bf16[256,2048]{1,0:T(8,128)(2,1)} %param.8), kind=kLoop, calls=%fused_computation.160 | loop fusion | bytes 2097152 | tf_op jit(solution)/shard_map/slice | solution.py:38
  3.1 1.3 collective-permute-start.2
  4.4 6.4 %collective-permute-start.3 = (bf16[128,2048]{1,0:T(8,128)(2,1)}, bf16[128,2048]{1,0:T(8,128)(2,1)}, u32[]{:S(2)}, u32[]{:S(2)}) collective-permute-start(bf16[128,2048]{1,0:T(8,128)(2,1)} %get-tuple-element.6), channel_id=1, source_target_pairs={{0,1},{1,2},{2,3},{4,5},{5,6},{6,7},{8,9},{9,10},{10,11},{12,13},{... | collective-permute-start | bytes 1572872 | tf_op jit(solution)/shard_map/ppermute | solution.py:47
  10.7 1.3 collective-permute-start
  12.0 5.3 %collective-permute-start.1 = (bf16[128,2048]{1,0:T(8,128)(2,1)}, bf16[128,2048]{1,0:T(8,128)(2,1)}, u32[]{:S(2)}, u32[]{:S(2)}) collective-permute-start(bf16[128,2048]{1,0:T(8,128)(2,1)} %get-tuple-element.7), channel_id=1, source_target_pairs={{0,1},{1,2},{2,3},{4,5},{5,6},{6,7},{8,9},{9,10},{10,11},{12,13},{... | collective-permute-start | bytes 1572872 | tf_op jit(solution)/shard_map/ppermute | solution.py:47
  17.3 4.6 %fusion.106 = f32[1024,128]{0,1:T(8,128)} fusion(bf16[1024,2048]{1,0:T(8,128)(2,1)} %param.6, bf16[2048,128]{1,0:T(8,128)(2,1)} %param.9), kind=kOutput, calls=%fused_computation.162 | convolution fusion | flops 536870912 | bytes 5242880 | tf_op jit(solution)/shard_map/dot_general | solution.py:77
  22.0 3.5 %collective-permute-start.12 = (f32[1024,128]{0,1:T(8,128)}, f32[1024,128]{0,1:T(8,128)}, u32[]{:S(2)}, u32[]{:S(2)}) collective-permute-start(f32[1024,128]{0,1:T(8,128)} %fusion.106), channel_id=1, source_target_pairs={{0,1},{3,2},{4,5},{7,6},{8,9},{11,10},{12,13},{15,14},{16,17},{19,... | collective-permute-start | bytes 1572872 | tf_op jit(solution)/shard_map/ppermute | solution.py:81
  25.5 0.2 fusion.52
  25.7 0.2 fusion.54
  25.9 0.2 fusion.48
  26.1 0.2 fusion.50
  26.8 0.5 broadcast_in_dim.61
  27.3 0.6 copy-done.2
  27.9 6.3 %fusion.1 = bf16[8,128,2048]{2,1,0:T(8,128)(2,1)S(1)} fusion(bf16[8,128,2048]{2,1,0:T(8,128)(2,1)S(1)} %broadcast_in_dim.61, s32[]{:T(128)S(6)} %select_n.249, bf16[2048,2048]{1,0:T(8,128)(2,1)} %param.7, bf16[256,2048]{1,0:T(8,128)(2,1)S(1)} %copy-done.2), kind=kOutput, calls=%fused_computation.9 | convolution fusion | flops 1074003968 | bytes 9437188 | tf_op jit(solution)/shard_map/dot_general | solution.py:70
  34.3 6.3 %fusion.3 = bf16[8,128,2048]{2,1,0:T(8,128)(2,1)S(1)} fusion(bf16[8,128,2048]{2,1,0:T(8,128)(2,1)S(1)} %fusion.1, s32[]{:T(128)S(6)} %select_n.250, bf16[2048,2048]{1,0:T(8,128)(2,1)} %param.7, bf16[256,2048]{1,0:T(8,128)(2,1)S(1)} %copy-done.2), kind=kOutput, calls=%fused_computation.11 | convolution fusion | flops 1074003968 | bytes 9437188 | tf_op jit(solution)/shard_map/dot_general | solution.py:70
  40.6 2.0 %copy-done.3 = bf16[8,128,2048]{2,1,0:T(8,128)(2,1)} copy-done((bf16[8,128,2048]{2,1,0:T(8,128)(2,1)}, bf16[8,128,2048]{2,1,0:T(8,128)(2,1)S(1)}, u32[]{:S(2)}) %copy-start.3) | copy-done | bytes 4194328
  42.6 1.3 broadcast_select_fusion
  43.9 0.2 fusion.32
  44.1 0.2 fusion.34
  44.4 0.2 fusion.36
  44.6 0.2 fusion.38
  44.8 1.3 broadcast_select_fusion.1
  46.1 0.2 fusion.40
  46.3 0.6 copy-done.4
  46.9 0.2 fusion.42
  47.1 0.2 fusion.44
  47.3 0.2 fusion.46
  47.8 1.3 collective-permute-start.6
  49.1 1.5 %collective-permute-start.7 = (bf16[128,2048]{1,0:T(8,128)(2,1)}, bf16[128,2048]{1,0:T(8,128)(2,1)}, u32[]{:S(2)}, u32[]{:S(2)}) collective-permute-start(bf16[128,2048]{1,0:T(8,128)(2,1)} %collective-permute-done.3), channel_id=1, source_target_pairs={{1,2},{2,3},{5,6},{6,7},{9,10},{10,11},{13,14},{14,15},{17,18},{18... | collective-permute-start | bytes 1572872 | tf_op jit(solution)/shard_map/ppermute | solution.py:47
  50.8 1.4 collective-permute-start.4
  52.3 0.7 collective-permute-start.5
  53.0 2.1 %add_bitcast_fusion = f32[1,1024,128]{1,2,0:T(8,128)} fusion(f32[1024,128]{0,1:T(8,128)} %fusion.106, f32[1024,128]{0,1:T(8,128)} %collective-permute-done.12), kind=kLoop, calls=%fused_computation.28 | loop fusion | flops 131072 | bytes 1572864 | tf_op jit(solution)/shard_map/reshape | solution.py:95
  55.1 9.8 %collective-permute-done.6 = bf16[128,2048]{1,0:T(8,128)(2,1)} collective-permute-done((bf16[128,2048]{1,0:T(8,128)(2,1)}, bf16[128,2048]{1,0:T(8,128)(2,1)}, u32[]{:S(2)}, u32[]{:S(2)}) %collective-permute-start.6) | collective-permute-done | bytes 524320 | tf_op jit(solution)/shard_map/ppermute | solution.py:46
  64.9 1.1 broadcast_select_fusion.2
  66.0 1.3 fusion.24
  67.3 1.1 fusion.26
  68.4 5.3 %collective-permute-done.4 = bf16[128,2048]{1,0:T(8,128)(2,1)S(1)} collective-permute-done((bf16[128,2048]{1,0:T(8,128)(2,1)}, bf16[128,2048]{1,0:T(8,128)(2,1)S(1)}, u32[]{:S(2)}, u32[]{:S(2)}) %collective-permute-start.4) | collective-permute-done | bytes 524320 | tf_op jit(solution)/shard_map/ppermute | solution.py:46
  73.8 0.2 fusion.28
  74.0 0.7 copy-done.11
  75.1 2.1 %convolution_bitcast_fusion = f32[1,64,64]{1,2,0:T(8,128)S(1)} fusion(f32[1,1024,128]{2,1,0:T(8,128)S(1)} %bitcast.132, f32[1,1024,128]{1,2,0:T(8,128)} %add_bitcast_fusion), kind=kOutput, calls=%fused_computation.24 | convolution fusion | flops 50331648 | bytes 802816 | tf_op jit(solution)/shard_map/dot_general | solution.py:99
  77.2 1.9 %convolution_bitcast_fusion.1 = f32[1,64,64]{1,2,0:T(8,128)S(1)} fusion(f32[1,1024,128]{2,1,0:T(8,128)S(1)} %bitcast.133, f32[1,1024,128]{1,2,0:T(8,128)} %add_bitcast_fusion), kind=kOutput, calls=%fused_computation.25 | convolution fusion | flops 50331648 | bytes 802816 | tf_op jit(solution)/shard_map/dot_general | solution.py:99
  79.4 0.7 collective-permute-start.13
  80.0 1.3 collective-permute-start.15
  81.4 1.6 %collective-permute-start.14 = (f32[1,32,64]{2,1,0:T(8,128)S(1)}, f32[1,32,64]{2,1,0:T(8,128)S(1)}, u32[]{:S(2)}, u32[]{:S(2)}) collective-permute-start(f32[1,32,64]{2,1,0:T(8,128)S(1)} %get-tuple-element.10), channel_id=1, source_target_pairs={{1,0},{2,3},{5,4},{6,7},{9,8},{10,11},{13,12},{14,15},{17,16},{18,... | collective-permute-start | bytes 24584 | tf_op jit(solution)/shard_map/ppermute | solution.py:122
  83.0 7.3 %fusion.5 = bf16[8,128,2048]{2,1,0:T(8,128)(2,1)} fusion(bf16[8,128,2048]{2,1,0:T(8,128)(2,1)} %copy-done.3, s32[]{:T(128)S(6)} %select_n.255, bf16[128,2048]{1,0:T(8,128)(2,1)} %copy-done.8, bf16[2048,2048]{1,0:T(8,128)(2,1)} %param.7), kind=kOutput, calls=%fused_computation.13 | convolution fusion | flops 1074003968 | bytes 9437188 | tf_op jit(solution)/shard_map/dot_general | solution.py:70
  90.2 0.3 collective-permute-done.14
  90.7 1.6 %collective-permute-start.17 = (f32[1,2048]{1,0:T(1,128)S(1)}, f32[1,2048]{1,0:T(1,128)S(1)}, u32[]{:S(2)}, u32[]{:S(2)}) collective-permute-start(f32[1,2048]{1,0:T(1,128)S(1)} %reshape.69), channel_id=1, source_target_pairs={{0,8},{4,12},{8,0},{12,4},{1,9},{5,13},{9,1},{13,5},{2,10},{6,14},... | collective-permute-start | bytes 24584 | tf_op jit(solution)/shard_map/ppermute | solution.py:138
  92.4 7.2 %fusion.7 = bf16[8,128,2048]{2,1,0:T(8,128)(2,1)} fusion(bf16[8,128,2048]{2,1,0:T(8,128)(2,1)} %fusion.5, s32[]{:T(128)S(6)} %select_n.257, bf16[128,2048]{1,0:T(8,128)(2,1)S(1)} %copy-done.7, bf16[2048,2048]{1,0:T(8,128)(2,1)} %param.7), kind=kOutput, calls=%fused_computation.15 | convolution fusion | flops 1074003968 | bytes 9437188 | tf_op jit(solution)/shard_map/dot_general | solution.py:70
  99.7 0.6 fusion.72
  100.5 1.6 %collective-permute-start.19 = (f32[1,512]{1,0:T(1,128)S(1)}, f32[1,512]{1,0:T(1,128)S(1)}, u32[]{:S(2)}, u32[]{:S(2)}) collective-permute-start(f32[1,512]{1,0:T(1,128)S(1)} %get-tuple-element.19), channel_id=1, source_target_pairs={{0,12},{4,0},{8,4},{12,8},{1,13},{5,1},{9,5},{13,9},{2,14},{6,2},{... | collective-permute-start | bytes 6152 | tf_op jit(solution)/shard_map/ppermute | solution.py:152
  102.1 7.1 %fusion.9 = bf16[8,128,2048]{2,1,0:T(8,128)(2,1)} fusion(bf16[8,128,2048]{2,1,0:T(8,128)(2,1)} %fusion.7, s32[]{:T(128)S(6)} %select_n.260, bf16[128,2048]{1,0:T(8,128)(2,1)S(1)} %copy-done.12, bf16[2048,2048]{1,0:T(8,128)(2,1)} %param.7), kind=kOutput, calls=%fused_computation.17 | convolution fusion | flops 1074003968 | bytes 9437188 | tf_op jit(solution)/shard_map/dot_general | solution.py:70
  109.2 1.3 collective-permute-start.8
  110.5 0.7 collective-permute-start.9
  111.3 0.9 collective-permute-start.20
  112.2 2.7 %collective-permute-done.20 = f32[1,512]{1,0:T(1,128)S(1)} collective-permute-done((f32[1,512]{1,0:T(1,128)S(1)}, f32[1,512]{1,0:T(1,128)S(1)}, u32[]{:S(2)}, u32[]{:S(2)}) %collective-permute-start.20) | collective-permute-done | bytes 2080 | tf_op jit(solution)/shard_map/ppermute | solution.py:152
  115.0 5.8 %collective-permute-start.22 = (f32[1,512]{1,0:T(1,128)S(1)}, f32[1,512]{1,0:T(1,128)S(1)}, u32[]{:S(2)}, u32[]{:S(2)}) collective-permute-start(f32[1,512]{1,0:T(1,128)S(1)} %get-tuple-element.14), channel_id=1, source_target_pairs={{0,1},{1,2},{2,3},{3,0},{4,5},{5,6},{6,7},{7,4},{8,9},{9,10},{10,1... | collective-permute-start | bytes 6152 | tf_op jit(solution)/shard_map/ppermute | solution.py:163
  120.8 2.0 %collective-permute-start.23 = (f32[1,512]{1,0:T(1,128)S(1)}, f32[1,512]{1,0:T(1,128)S(1)}, u32[]{:S(2)}, u32[]{:S(2)}) collective-permute-start(f32[1,512]{1,0:T(1,128)S(1)} %get-tuple-element.16), channel_id=1, source_target_pairs={{0,2},{1,3},{2,0},{3,1},{4,6},{5,7},{6,4},{7,5},{8,10},{9,11},{10,... | collective-permute-start | bytes 6152 | tf_op jit(solution)/shard_map/ppermute | solution.py:163
  122.8 3.7 %fusion.11 = bf16[8,128,2048]{2,1,0:T(8,128)(2,1)} fusion(bf16[8,128,2048]{2,1,0:T(8,128)(2,1)} %fusion.9, s32[]{:T(128)S(6)} %select_n.262, bf16[128,2048]{1,0:T(8,128)(2,1)S(1)} %copy-done.10, bf16[2048,2048]{1,0:T(8,128)(2,1)S(1)} %bitcast.131), kind=kOutput, calls=%fused_computation.19 | convolution fusion | flops 1074003968 | bytes 9437188 | tf_op jit(solution)/shard_map/dot_general | solution.py:70
  126.6 1.3 collective-permute-start.10
  127.9 0.9 collective-permute-start.11
  128.8 0.6 fusion.100
  129.4 3.7 %fusion.13 = bf16[8,128,2048]{2,1,0:T(8,128)(2,1)} fusion(bf16[8,128,2048]{2,1,0:T(8,128)(2,1)} %fusion.11, s32[]{:T(128)S(6)} %select_n.270, bf16[2048,2048]{1,0:T(8,128)(2,1)S(1)} %bitcast.131, bf16[128,2048]{1,0:T(8,128)(2,1)S(1)} %copy-done.5, bf16[128,2048]{1,0:T(8,128)(2,1)S(1)} %collective-permute-done.8, ...), kind=kOutput, calls=%fused_computation.21 | convolution fusion | flops 1074528256 | bytes 10485766 | tf_op jit(solution)/shard_map/dot_general | solution.py:70
  133.1 8.0 %collective-permute-done.10 = bf16[128,2048]{1,0:T(8,128)(2,1)S(1)} collective-permute-done((bf16[128,2048]{1,0:T(8,128)(2,1)}, bf16[128,2048]{1,0:T(8,128)(2,1)S(1)}, u32[]{:S(2)}, u32[]{:S(2)}) %collective-permute-start.10) | collective-permute-done | bytes 524320 | tf_op jit(solution)/shard_map/ppermute | solution.py:46
  141.1 3.7 %fusion.15 = bf16[8,128,2048]{2,1,0:T(8,128)(2,1)} fusion(bf16[8,128,2048]{2,1,0:T(8,128)(2,1)} %fusion.13, s32[]{:T(128)S(6)} %select_n.274, bf16[2048,2048]{1,0:T(8,128)(2,1)S(1)} %bitcast.131, bf16[128,2048]{1,0:T(8,128)(2,1)S(1)} %get-tuple-element.2, bf16[128,2048]{1,0:T(8,128)(2,1)S(1)} %collective-permute-done.10, ...), kind=kOutput, calls=%fused_computation.23 | convolution fusion | flops 1074528256 | bytes 10485766 | tf_op jit(solution)/shard_map/dot_general | solution.py:70
  (105 shorter events, 2.0 us)
Async XLA Ops:
  0.6 99.1 %copy-start = (bf16[512,2048]{1,0:T(8,128)(2,1)S(1)}, bf16[512,2048]{1,0:T(8,128)(2,1)}, u32[]{:S(2)}) copy-start(bf16[512,2048]{1,0:T(8,128)(2,1)} %param.11) | copy-start | bytes 6291460
  0.6 24.9 %copy-start.1 = (bf16[256,2048]{1,0:T(8,128)(2,1)S(1)}, bf16[256,2048]{1,0:T(8,128)(2,1)}, u32[]{:S(2)}) copy-start(bf16[256,2048]{1,0:T(8,128)(2,1)} %param.8) | copy-start | bytes 3145732
  0.7 24.8 %copy-start.17 = (bf16[2,1024,64]{1,2,0:T(8,128)(2,1)S(1)}, bf16[2,1024,64]{1,2,0:T(8,128)(2,1)}, u32[]{:S(2)}) copy-start(bf16[2,1024,64]{1,2,0:T(8,128)(2,1)} %param.10) | copy-start | bytes 786436
  3.1 39.6 %collective-permute-start.2 = (bf16[128,2048]{1,0:T(8,128)(2,1)}, bf16[128,2048]{1,0:T(8,128)(2,1)}, u32[]{:S(2)}, u32[]{:S(2)}) collective-permute-start(bf16[128,2048]{1,0:T(8,128)(2,1)} %get-tuple-element.6), channel_id=1, source_target_pairs={{1,0},{2,1},{3,2},{5,4},{6,5},{7,6},{9,8},{10,9},{11,10},{13,12},{... | collective-permute-start | bytes 1572872 | tf_op jit(solution)/shard_map/ppermute | solution.py:46
  4.4 38.3 %collective-permute-start.3 = (bf16[128,2048]{1,0:T(8,128)(2,1)}, bf16[128,2048]{1,0:T(8,128)(2,1)}, u32[]{:S(2)}, u32[]{:S(2)}) collective-permute-start(bf16[128,2048]{1,0:T(8,128)(2,1)} %get-tuple-element.6), channel_id=1, source_target_pairs={{0,1},{1,2},{2,3},{4,5},{5,6},{6,7},{8,9},{9,10},{10,11},{12,13},{... | collective-permute-start | bytes 1572872 | tf_op jit(solution)/shard_map/ppermute | solution.py:47
  10.7 34.1 %collective-permute-start = (bf16[128,2048]{1,0:T(8,128)(2,1)}, bf16[128,2048]{1,0:T(8,128)(2,1)}, u32[]{:S(2)}, u32[]{:S(2)}) collective-permute-start(bf16[128,2048]{1,0:T(8,128)(2,1)} %get-tuple-element.7), channel_id=1, source_target_pairs={{1,0},{2,1},{3,2},{5,4},{6,5},{7,6},{9,8},{10,9},{11,10},{13,12},{... | collective-permute-start | bytes 1572872 | tf_op jit(solution)/shard_map/ppermute | solution.py:46
  12.0 32.8 %collective-permute-start.1 = (bf16[128,2048]{1,0:T(8,128)(2,1)}, bf16[128,2048]{1,0:T(8,128)(2,1)}, u32[]{:S(2)}, u32[]{:S(2)}) collective-permute-start(bf16[128,2048]{1,0:T(8,128)(2,1)} %get-tuple-element.7), channel_id=1, source_target_pairs={{0,1},{1,2},{2,3},{4,5},{5,6},{6,7},{8,9},{9,10},{10,11},{12,13},{... | collective-permute-start | bytes 1572872 | tf_op jit(solution)/shard_map/ppermute | solution.py:47
  22.0 31.0 %collective-permute-start.12 = (f32[1024,128]{0,1:T(8,128)}, f32[1024,128]{0,1:T(8,128)}, u32[]{:S(2)}, u32[]{:S(2)}) collective-permute-start(f32[1024,128]{0,1:T(8,128)} %fusion.106), channel_id=1, source_target_pairs={{0,1},{3,2},{4,5},{7,6},{8,9},{11,10},{12,13},{15,14},{16,17},{19,... | collective-permute-start | bytes 1572872 | tf_op jit(solution)/shard_map/ppermute | solution.py:81
  26.7 1.2 copy-start.2
  34.3 9.7 %copy-start.18 = (bf16[2,1024,64]{1,2,0:T(8,128)(2,1)S(1)}, bf16[2,1024,64]{1,2,0:T(8,128)(2,1)}, u32[]{:S(2)}) copy-start(bf16[2,1024,64]{1,2,0:T(8,128)(2,1)} %param.10) | copy-start | bytes 786436
  40.6 2.0 %copy-start.3 = (bf16[8,128,2048]{2,1,0:T(8,128)(2,1)}, bf16[8,128,2048]{2,1,0:T(8,128)(2,1)S(1)}, u32[]{:S(2)}) copy-start(bf16[8,128,2048]{2,1,0:T(8,128)(2,1)S(1)} %fusion.3) | copy-start | bytes 12582916
  43.9 0.9 copy-start.6
  46.1 0.8 copy-start.4
  46.1 1.2 copy-start.8
  47.8 17.1 %collective-permute-start.6 = (bf16[128,2048]{1,0:T(8,128)(2,1)}, bf16[128,2048]{1,0:T(8,128)(2,1)}, u32[]{:S(2)}, u32[]{:S(2)}) collective-permute-start(bf16[128,2048]{1,0:T(8,128)(2,1)} %collective-permute-done.2), channel_id=1, source_target_pairs={{1,0},{2,1},{5,4},{6,5},{9,8},{10,9},{13,12},{14,13},{17,16},{18,1... | collective-permute-start | bytes 1572872 | tf_op jit(solution)/shard_map/ppermute | solution.py:46
  49.1 15.8 %collective-permute-start.7 = (bf16[128,2048]{1,0:T(8,128)(2,1)}, bf16[128,2048]{1,0:T(8,128)(2,1)}, u32[]{:S(2)}, u32[]{:S(2)}) collective-permute-start(bf16[128,2048]{1,0:T(8,128)(2,1)} %collective-permute-done.3), channel_id=1, source_target_pairs={{1,2},{2,3},{5,6},{6,7},{9,10},{10,11},{13,14},{14,15},{17,18},{18... | collective-permute-start | bytes 1572872 | tf_op jit(solution)/shard_map/ppermute | solution.py:47
  50.8 22.9 %copy-start.19 = (bf16[2,1024,64]{1,2,0:T(8,128)(2,1)S(1)}, bf16[2,1024,64]{1,2,0:T(8,128)(2,1)}, u32[]{:S(2)}) copy-start(bf16[2,1024,64]{1,2,0:T(8,128)(2,1)} %param.10) | copy-start | bytes 786436
  50.8 22.9 %collective-permute-start.4 = (bf16[128,2048]{1,0:T(8,128)(2,1)}, bf16[128,2048]{1,0:T(8,128)(2,1)S(1)}, u32[]{:S(2)}, u32[]{:S(2)}) collective-permute-start(bf16[128,2048]{1,0:T(8,128)(2,1)} %collective-permute-done), channel_id=1, source_target_pairs={{1,0},{2,1},{5,4},{6,5},{9,8},{10,9},{13,12},{14,13},{17,16},{18,1... | collective-permute-start | bytes 1572872 | tf_op jit(solution)/shard_map/ppermute | solution.py:46
  52.3 21.4 %collective-permute-start.5 = (bf16[128,2048]{1,0:T(8,128)(2,1)}, bf16[128,2048]{1,0:T(8,128)(2,1)S(1)}, u32[]{:S(2)}, u32[]{:S(2)}) collective-permute-start(bf16[128,2048]{1,0:T(8,128)(2,1)} %collective-permute-done.1), channel_id=1, source_target_pairs={{1,2},{2,3},{5,6},{6,7},{9,10},{10,11},{13,14},{14,15},{17,18},{18... | collective-permute-start | bytes 1572872 | tf_op jit(solution)/shard_map/ppermute | solution.py:47
  66.0 1.3 copy-start.9
  73.7 1.2 copy-start.13
  73.7 1.2 copy-start.15
  73.8 0.9 copy-start.11
  79.4 10.9 %collective-permute-start.13 = (f32[1,32,64]{2,1,0:T(8,128)S(1)}, f32[1,32,64]{2,1,0:T(8,128)S(1)}, u32[]{:S(2)}, u32[]{:S(2)}) collective-permute-start(f32[1,32,64]{2,1,0:T(8,128)S(1)} %get-tuple-element.8), channel_id=1, source_target_pairs={{1,2},{2,1},{5,6},{6,5},{9,10},{10,9},{13,14},{14,13},{17,18},{18,... | collective-permute-start | bytes 24584 | tf_op jit(solution)/shard_map/ppermute | solution.py:127
  80.0 10.2 %collective-permute-start.15 = (f32[1,32,64]{2,1,0:T(8,128)S(1)}, f32[1,32,64]{2,1,0:T(8,128)S(1)}, u32[]{:S(2)}, u32[]{:S(2)}) collective-permute-start(f32[1,32,64]{2,1,0:T(8,128)S(1)} %get-tuple-element.9), channel_id=1, source_target_pairs={{1,3},{2,0},{5,7},{6,4},{9,11},{10,8},{13,15},{14,12},{17,19},{18,... | collective-permute-start | bytes 24584 | tf_op jit(solution)/shard_map/ppermute | solution.py:127
  81.3 11.1 %copy-start.7 = (bf16[128,2048]{1,0:T(8,128)(2,1)S(1)}, bf16[128,2048]{1,0:T(8,128)(2,1)}, u32[]{:S(2)}) copy-start(bf16[128,2048]{1,0:T(8,128)(2,1)} %copy-done.6) | copy-start | bytes 1572868
  81.4 9.2 %collective-permute-start.14 = (f32[1,32,64]{2,1,0:T(8,128)S(1)}, f32[1,32,64]{2,1,0:T(8,128)S(1)}, u32[]{:S(2)}, u32[]{:S(2)}) collective-permute-start(f32[1,32,64]{2,1,0:T(8,128)S(1)} %get-tuple-element.10), channel_id=1, source_target_pairs={{1,0},{2,3},{5,4},{6,7},{9,8},{10,11},{13,12},{14,15},{17,16},{18,... | collective-permute-start | bytes 24584 | tf_op jit(solution)/shard_map/ppermute | solution.py:122
  90.6 11.5 %copy-start.12 = (bf16[128,2048]{1,0:T(8,128)(2,1)S(1)}, bf16[128,2048]{1,0:T(8,128)(2,1)}, u32[]{:S(2)}) copy-start(bf16[128,2048]{1,0:T(8,128)(2,1)} %copy-done.11) | copy-start | bytes 1572868
  90.6 9.0 %collective-permute-start.18 = (f32[1,2048]{1,0:T(1,128)S(1)}, f32[1,2048]{1,0:T(1,128)S(1)}, u32[]{:S(2)}, u32[]{:S(2)}) collective-permute-start(f32[1,2048]{1,0:T(1,128)S(1)} %reshape.69), channel_id=1, source_target_pairs={{0,12},{4,0},{8,4},{12,8},{1,13},{5,1},{9,5},{13,9},{2,14},{6,2},{... | collective-permute-start | bytes 24584 | tf_op jit(solution)/shard_map/ppermute | solution.py:138
  90.7 8.9 %collective-permute-start.17 = (f32[1,2048]{1,0:T(1,128)S(1)}, f32[1,2048]{1,0:T(1,128)S(1)}, u32[]{:S(2)}, u32[]{:S(2)}) collective-permute-start(f32[1,2048]{1,0:T(1,128)S(1)} %reshape.69), channel_id=1, source_target_pairs={{0,8},{4,12},{8,0},{12,4},{1,9},{5,13},{9,1},{13,5},{2,10},{6,14},... | collective-permute-start | bytes 24584 | tf_op jit(solution)/shard_map/ppermute | solution.py:138
  92.3 7.4 %collective-permute-start.16 = (f32[1,2048]{1,0:T(1,128)S(1)}, f32[1,2048]{1,0:T(1,128)S(1)}, u32[]{:S(2)}, u32[]{:S(2)}) collective-permute-start(f32[1,2048]{1,0:T(1,128)S(1)} %reshape.69), channel_id=1, source_target_pairs={{0,4},{4,8},{8,12},{12,0},{1,5},{5,9},{9,13},{13,1},{2,6},{6,10},{... | collective-permute-start | bytes 24584 | tf_op jit(solution)/shard_map/ppermute | solution.py:138
  92.4 30.4 %slice-start = ((s8[8388608]{0:T(1024)(128)(4,1)}), s8[4194304]{0:T(1024)(128)(4,1)S(1)}, s32[]{:S(2)}) async-start(s8[8388608]{0:T(1024)(128)(4,1)} %bitcast.130), calls=%async_computation | async-start | bytes 8388608
  99.7 23.1 %slice-start.1 = ((s8[8388608]{0:T(1024)(128)(4,1)}), s8[4194304]{0:T(1024)(128)(4,1)S(1)}, s32[]{:S(2)}) async-start(s8[8388608]{0:T(1024)(128)(4,1)} %bitcast.130), calls=%async_computation.1 | async-start | bytes 8388608
  100.4 8.8 %copy-start.14 = (bf16[128,2048]{1,0:T(8,128)(2,1)S(1)}, bf16[128,2048]{1,0:T(8,128)(2,1)}, u32[]{:S(2)}) copy-start(bf16[128,2048]{1,0:T(8,128)(2,1)} %copy-done.13) | copy-start | bytes 1572868
  100.5 10.0 %copy-start.16 = (bf16[128,2048]{1,0:T(8,128)(2,1)S(1)}, bf16[128,2048]{1,0:T(8,128)(2,1)}, u32[]{:S(2)}) copy-start(bf16[128,2048]{1,0:T(8,128)(2,1)} %copy-done.15) | copy-start | bytes 1572868
  100.5 22.4 %copy-start.10 = (bf16[128,2048]{1,0:T(8,128)(2,1)S(1)}, bf16[128,2048]{1,0:T(8,128)(2,1)}, u32[]{:S(2)}) copy-start(bf16[128,2048]{1,0:T(8,128)(2,1)} %copy-done.9) | copy-start | bytes 1572868
  100.5 11.7 %collective-permute-start.19 = (f32[1,512]{1,0:T(1,128)S(1)}, f32[1,512]{1,0:T(1,128)S(1)}, u32[]{:S(2)}, u32[]{:S(2)}) collective-permute-start(f32[1,512]{1,0:T(1,128)S(1)} %get-tuple-element.19), channel_id=1, source_target_pairs={{0,12},{4,0},{8,4},{12,8},{1,13},{5,1},{9,5},{13,9},{2,14},{6,2},{... | collective-permute-start | bytes 6152 | tf_op jit(solution)/shard_map/ppermute | solution.py:152
  109.2 20.2 %collective-permute-start.8 = (bf16[128,2048]{1,0:T(8,128)(2,1)S(1)}, bf16[128,2048]{1,0:T(8,128)(2,1)S(1)}, u32[]{:S(2)}, u32[]{:S(2)}) collective-permute-start(bf16[128,2048]{1,0:T(8,128)(2,1)S(1)} %copy-done.14), channel_id=1, source_target_pairs={{1,0},{5,4},{9,8},{13,12},{17,16},{21,20},{25,24},{29,28}} | collective-permute-start | bytes 1572872 | tf_op jit(solution)/shard_map/ppermute | solution.py:46
  110.5 18.9 %collective-permute-start.9 = (bf16[128,2048]{1,0:T(8,128)(2,1)S(1)}, bf16[128,2048]{1,0:T(8,128)(2,1)S(1)}, u32[]{:S(2)}, u32[]{:S(2)}) collective-permute-start(bf16[128,2048]{1,0:T(8,128)(2,1)S(1)} %copy-done.16), channel_id=1, source_target_pairs={{2,3},{6,7},{10,11},{14,15},{18,19},{22,23},{26,27},{30,31}} | collective-permute-start | bytes 1572872 | tf_op jit(solution)/shard_map/ppermute | solution.py:47
  111.2 3.7 %collective-permute-start.21 = (f32[1,512]{1,0:T(1,128)S(1)}, f32[1,512]{1,0:T(1,128)S(1)}, u32[]{:S(2)}, u32[]{:S(2)}) collective-permute-start(f32[1,512]{1,0:T(1,128)S(1)} %get-tuple-element.17), channel_id=1, source_target_pairs={{0,4},{4,8},{8,12},{12,0},{1,5},{5,9},{9,13},{13,1},{2,6},{6,10},{... | collective-permute-start | bytes 6152 | tf_op jit(solution)/shard_map/ppermute | solution.py:152
  111.3 3.7 %collective-permute-start.20 = (f32[1,512]{1,0:T(1,128)S(1)}, f32[1,512]{1,0:T(1,128)S(1)}, u32[]{:S(2)}, u32[]{:S(2)}) collective-permute-start(f32[1,512]{1,0:T(1,128)S(1)} %get-tuple-element.18), channel_id=1, source_target_pairs={{0,8},{4,12},{8,0},{12,4},{1,9},{5,13},{9,1},{13,5},{2,10},{6,14},... | collective-permute-start | bytes 6152 | tf_op jit(solution)/shard_map/ppermute | solution.py:152
  115.0 11.6 %collective-permute-start.22 = (f32[1,512]{1,0:T(1,128)S(1)}, f32[1,512]{1,0:T(1,128)S(1)}, u32[]{:S(2)}, u32[]{:S(2)}) collective-permute-start(f32[1,512]{1,0:T(1,128)S(1)} %get-tuple-element.14), channel_id=1, source_target_pairs={{0,1},{1,2},{2,3},{3,0},{4,5},{5,6},{6,7},{7,4},{8,9},{9,10},{10,1... | collective-permute-start | bytes 6152 | tf_op jit(solution)/shard_map/ppermute | solution.py:163
  120.8 7.1 %collective-permute-start.24 = (f32[1,512]{1,0:T(1,128)S(1)}, f32[1,512]{1,0:T(1,128)S(1)}, u32[]{:S(2)}, u32[]{:S(2)}) collective-permute-start(f32[1,512]{1,0:T(1,128)S(1)} %get-tuple-element.15), channel_id=1, source_target_pairs={{0,3},{1,0},{2,1},{3,2},{4,7},{5,4},{6,5},{7,6},{8,11},{9,8},{10,9... | collective-permute-start | bytes 6152 | tf_op jit(solution)/shard_map/ppermute | solution.py:163
  120.8 8.6 %copy-start.5 = (bf16[128,2048]{1,0:T(8,128)(2,1)S(1)}, bf16[128,2048]{1,0:T(8,128)(2,1)}, u32[]{:S(2)}) copy-start(bf16[128,2048]{1,0:T(8,128)(2,1)} %copy-done.4) | copy-start | bytes 1572868
  120.8 8.0 %collective-permute-start.23 = (f32[1,512]{1,0:T(1,128)S(1)}, f32[1,512]{1,0:T(1,128)S(1)}, u32[]{:S(2)}, u32[]{:S(2)}) collective-permute-start(f32[1,512]{1,0:T(1,128)S(1)} %get-tuple-element.16), channel_id=1, source_target_pairs={{0,2},{1,3},{2,0},{3,1},{4,6},{5,7},{6,4},{7,5},{8,10},{9,11},{10,... | collective-permute-start | bytes 6152 | tf_op jit(solution)/shard_map/ppermute | solution.py:163
  126.6 14.5 %collective-permute-start.10 = (bf16[128,2048]{1,0:T(8,128)(2,1)}, bf16[128,2048]{1,0:T(8,128)(2,1)S(1)}, u32[]{:S(2)}, u32[]{:S(2)}) collective-permute-start(bf16[128,2048]{1,0:T(8,128)(2,1)} %collective-permute-done.6), channel_id=1, source_target_pairs={{1,0},{5,4},{9,8},{13,12},{17,16},{21,20},{25,24},{29,28}} | collective-permute-start | bytes 1572872 | tf_op jit(solution)/shard_map/ppermute | solution.py:46
  127.9 13.2 %collective-permute-start.11 = (bf16[128,2048]{1,0:T(8,128)(2,1)}, bf16[128,2048]{1,0:T(8,128)(2,1)S(1)}, u32[]{:S(2)}, u32[]{:S(2)}) collective-permute-start(bf16[128,2048]{1,0:T(8,128)(2,1)} %collective-permute-done.7), channel_id=1, source_target_pairs={{2,3},{6,7},{10,11},{14,15},{18,19},{22,23},{26,27},{30,31}} | collective-permute-start | bytes 1572872 | tf_op jit(solution)/shard_map/ppermute | solution.py:47

commit v2 on v1

v2 whole, which is shorter than its diff:
```python
import jax
import jax.numpy as jnp
from jax import lax
from jax.sharding import PartitionSpec as P

SEQ = 1024


def three_terms(value):
    high = lax.reduce_precision(value, 8, 7)
    rest = value - high
    middle = lax.reduce_precision(rest, 8, 7)
    low = rest - middle
    return [term.astype(jnp.bfloat16) for term in (high, middle, low)]


def low_rank_rows(rows, proj_out):
    width = rows.shape[1] // 2
    parts = [
        jnp.dot(rows[:, layer * width : (layer + 1) * width], proj_out[layer], preferred_element_type=jnp.float32)
        for layer in range(2)
    ]
    return jnp.concatenate(parts, axis=1)


def times_width(rows, w_kv):
    return lax.dot_general(
        rows, w_kv, (((1,), (1,)), ((), ())), preferred_element_type=jnp.float32
    ).astype(jnp.bfloat16)


def sequence_sums(low_in, low_out, rank):
    count = low_in.shape[0] // SEQ
    left = low_in.reshape(count, SEQ, 2 * rank)
    right = low_out.reshape(count, SEQ, 2 * rank)
    return jnp.concatenate(
        [
            lax.dot_general(
                left[:, :, layer * rank : (layer + 1) * rank],
                right[:, :, layer * rank : (layer + 1) * rank],
                (((1,), (1,)), ((0,), (0,))),
                precision=lax.Precision.HIGHEST,
                preferred_element_type=jnp.float32,
            )
            for layer in range(2)
        ],
        axis=1,
    )


def slabs_of(sums, n):
    count, height, rank = sums.shape
    return lax.optimization_barrier(sums.reshape(count, n, height // n, rank).transpose(1, 0, 2, 3))


def put(whole, piece, index):
    return lax.dynamic_update_slice(whole, piece[None], (index,) + (jnp.int32(0),) * piece.ndim)


def take(whole, index):
    return lax.dynamic_index_in_dim(whole, index, axis=0, keepdims=False)


def gathered(hidden, w_kv, grad_kv, proj_in, proj_out):
    n = lax.axis_size("mp")
    rank = proj_out.shape[2]
    whole = lax.all_gather(grad_kv, "mp", axis=0, tiled=True)
    input_grad = times_width(whole, w_kv)
    low_in = jnp.dot(hidden, proj_in, preferred_element_type=jnp.float32)
    sums = slabs_of(sequence_sums(low_in, low_rank_rows(whole, proj_out), rank), n)
    features = lax.psum_scatter(sums, "mp", scatter_dimension=0, tiled=False)
    return input_grad, features


def line_of_four(hidden, w_kv, grad_kv, proj_in, proj_out):
    rank = proj_out.shape[2]
    local_rows = grad_kv.shape[0]
    me = lax.axis_index("mp")
    middle = (me == 1) | (me == 2)
    exchange_pairs = [(0, 1), (1, 0), (2, 3), (3, 2)]
    across = [(0, 0), (1, 2), (2, 1), (3, 3)]
    outward = [(1, 0), (2, 3)]
    inward = [(0, 1), (3, 2)]

    beside = lax.ppermute(grad_kv, "mp", exchange_pairs)
    facing = lax.ppermute(grad_kv, "mp", across)
    own_low = low_rank_rows(grad_kv, proj_out)
    far_low = lax.ppermute(own_low, "mp", [(3, 1), (0, 2)])
    low_in = jnp.dot(hidden, proj_in, preferred_element_type=jnp.float32)

    output = jnp.zeros((4, local_rows, w_kv.shape[0]), jnp.bfloat16)
    output = put(output, times_width(grad_kv, w_kv), me)

    beside, facing, low_in, output = lax.optimization_barrier((beside, facing, low_in, output))
    second = lax.ppermute(facing, "mp", outward)
    beside_across = lax.ppermute(beside, "mp", across)
    low_in_beside = lax.ppermute(low_in, "mp", inward)

    output = put(output, times_width(beside, w_kv), me ^ 1)

    low_out = jnp.zeros((4, local_rows, 2 * rank), jnp.float32)
    low_out = put(low_out, own_low, me)
    low_out = put(low_out, low_rank_rows(beside, proj_out), me ^ 1)
    low_out = put(low_out, low_rank_rows(facing, proj_out), me ^ 3)
    low_out = put(low_out, far_low, me ^ 2)
    sums = sequence_sums(low_in + low_in_beside, low_out.reshape(4 * local_rows, 2 * rank), rank)
    slabs = slabs_of(sums, 4)
    mine = jnp.where(middle, take(slabs, me), 0.0)
    mine = mine + lax.ppermute(take(slabs, me ^ 3), "mp", [(1, 2), (2, 1)])
    mine = mine + lax.ppermute(take(slabs, me ^ 1), "mp", outward)
    mine = mine + lax.ppermute(take(slabs, me ^ 2), "mp", [(1, 3), (2, 0)])

    beside_across, second, output = lax.optimization_barrier((beside_across, second, output))
    third = lax.ppermute(beside_across, "mp", outward)
    mine, beside_across = lax.optimization_barrier((mine, beside_across))
    output = put(
        output,
        times_width(jnp.where(middle, facing, second), w_kv),
        jnp.where(middle, me ^ 3, me ^ 2),
    )
    output = put(
        output,
        times_width(jnp.where(middle, beside_across, third), w_kv),
        jnp.where(middle, me ^ 2, me ^ 3),
    )
    return output.reshape(4 * local_rows, w_kv.shape[0]), mine


def on_device(hidden, w_kv, grad_kv, proj_in, proj_out, queries):
    n = lax.axis_size("mp")
    me = lax.axis_index("mp")
    input_grad, mine = (line_of_four if n == 4 else gathered)(hidden, w_kv, grad_kv, proj_in, proj_out)
    count = mine.shape[0]

    shards = lax.axis_size("dp")
    shard = lax.axis_index("dp")
    block_rows = queries.shape[0]
    mine = mine.reshape(count, queries.shape[1])
    all_features = [mine] + [
        lax.ppermute(mine, "dp", [(source, (source + step) % shards) for source in range(shards)])
        for step in range(1, shards)
    ]
    terms = jnp.concatenate(three_terms(jnp.concatenate(all_features, axis=0)), axis=0)
    products = lax.dot_general(
        terms, queries, (((1,), (1,)), ((), ())), preferred_element_type=jnp.float32
    ).reshape(3, shards, count, block_rows)
    partial_scores = products[0] + (products[1] + products[2])

    total = jnp.zeros((count, shards * block_rows), jnp.float32)
    for step in range(shards):
        back = partial_scores[step]
        if step > 0:
            back = lax.ppermute(back, "dp", [(source, (source - step) % shards) for source in range(shards)])
        total = lax.dynamic_update_slice(
            total, back, (jnp.int32(0), (shard + step) % shards * block_rows)
        )
    out_columns = shards * block_rows // n

    def columns_of(index):
        return lax.dynamic_slice(total, (jnp.int32(0), index * out_columns), (count, out_columns))

    scores = columns_of(me)
    for step in range(1, n):
        scores = scores + lax.ppermute(
            columns_of((me + step) % n), "mp", [(source, (source + step) % n) for source in range(n)]
        )
    return (input_grad, scores)


def solution(mesh):
    in_specs = (
        P(("groups", "dp"), "mp"),
        P("mp", None),
        P(("groups", "dp", "mp"), None),
        P("mp", None),
        P(),
        P("dp", "mp"),
    )
    out_specs = (P(("groups", "dp"), "mp"), P(("groups", "dp"), "mp"))
    return jax.shard_map(
        on_device, mesh=mesh, in_specs=in_specs, out_specs=out_specs, check_vma=False
    )
```

time: 146 us -> 121 us (0.83)
  matrix products: 59.8 us -> 41.3 us
  starting transfers between devices: 42.6 us -> 49 us
  waiting for transfers between devices: 26.2 us -> 21 us
  local copies, waits for them, and re-layouts: 7.94 us -> 4.15 us
  other arithmetic: 6.59 us -> 3.42 us
    dot_general x11 -> x7, matrix products: 53.9 us -> 31.3 us  [the longest x4 27.7 us: times_width(): lax.dot_general(rows, w_kv, (((1,), (1,)), ((), ())), preferred_element_t...]
    ppermute x16 -> x10, waiting for transfers between devices: 23.5 us -> 7.59 us  [the longest x1 6.44 us: line_of_four(): low_in_beside = lax.ppermute(low_in, 'mp', inward)]
    ppermute x3, waiting for transfers between devices: 0.02 us -> 8.96 us  [on_device(): lax.ppermute(columns_of((me + step) % n), 'mp', [(source, (source + step)...]
    ppermute x16 -> x10, starting transfers between devices: 30.4 us -> 35.4 us  [the longest x1 9.44 us: line_of_four(): facing = lax.ppermute(grad_kv, 'mp', across)]
    dot_general x16 -> x6, matrix products: 5.26 us -> 9.33 us  [low_rank_rows(): jnp.dot(rows[:, layer * width:(layer + 1) * width], proj_out[layer], pref...]
    unnamed x44 -> x8, local copies, waits for them, and re-layouts: 3.95 us -> 0.02 us
    select_n x4 -> x0, other arithmetic: 3.7 us -> none  [the longest x2 2.55 us: other(): return jnp.where(lower, up[step][c], down[step][c])]
    broadcast_in_dim x10 -> x6, local copies, waits for them, and re-layouts: 1.26 us -> 3.83 us  [the longest x1 2.54 us: line_of_four(): output = jnp.zeros((4, local_rows, w_kv.shape[0]), jnp.bfloat16)]
  transfers between devices with their start and end apart: 25 -> 19, of which waited for: 5 -> 7; matrix products, arithmetic and copies ran while one was open for 40% -> 29% of each run, Pallas kernels for 0% -> 0%
where the time goes in v2:
time: 121 us; the launch traced here: 120 us
  starting transfers between devices  49 us (40%)
  matrix products  41.3 us (34%)
  waiting for transfers between devices  21 us (17%)
  local copies, waits for them, and re-layouts  4.15 us (3%)
  other arithmetic  3.42 us (3%)
    dot_general x4, matrix products, times_width(): lax.dot_general(rows, w_kv, (((1,), (1,)), ((), ())), preferred_element_t...  27.7 us
    ppermute x1, starting transfers between devices, line_of_four(): facing = lax.ppermute(grad_kv, 'mp', across)  9.44 us
    ppermute x1, starting transfers between devices, line_of_four(): beside_across = lax.ppermute(beside, 'mp', across)  9.43 us
    dot_general x6, matrix products, low_rank_rows(): jnp.dot(rows[:, layer * width:(layer + 1) * width], proj_out[layer], pref...  9.33 us
    ppermute x3, waiting for transfers between devices, on_device(): lax.ppermute(columns_of((me + step) % n), 'mp', [(source, (source + step)...  8.96 us
    ppermute x3, starting transfers between devices, on_device(): lax.ppermute(columns_of((me + step) % n), 'mp', [(source, (source + step)...  8.34 us
    ppermute x1, waiting for transfers between devices, line_of_four(): low_in_beside = lax.ppermute(low_in, 'mp', inward)  6.44 us
    ppermute x1, starting transfers between devices, line_of_four(): low_in_beside = lax.ppermute(low_in, 'mp', inward)  6.3 us
  transfers between devices with their start and end apart: 19, of which 7 were waited for; matrix products, arithmetic and copies ran while one was open for 29% of the time, Pallas kernels for 0%

profile of v2, /device:TPU:0, one launch (start us, length us, event | category | flops | bytes accessed | tf_op | source)
XLA Modules:
  0.0 119.8 jit_solution(2897014294828928321)
XLA Ops:
  0.6 0.0 copy-start
  0.6 3.1 %collective-permute-start = (bf16[256,2048]{1,0:T(8,128)(2,1)}, bf16[256,2048]{1,0:T(8,128)(2,1)}, u32[]{:S(2)}, u32[]{:S(2)}) collective-permute-start(bf16[256,2048]{1,0:T(8,128)(2,1)} %param.8), channel_id=1, source_target_pairs={{0,1},{1,0},{2,3},{3,2},{4,5},{5,4},{6,7},{7,6},{8,9},{9,8},{10,11... | collective-permute-start | bytes 3145736 | tf_op jit(solution)/shard_map/ppermute | solution.py:85
  3.7 9.4 %collective-permute-start.1 = (bf16[256,2048]{1,0:T(8,128)(2,1)}, bf16[256,2048]{1,0:T(8,128)(2,1)}, u32[]{:S(2)}, u32[]{:S(2)}) collective-permute-start(bf16[256,2048]{1,0:T(8,128)(2,1)} %param.8), channel_id=1, source_target_pairs={{0,0},{1,2},{2,1},{3,3},{4,4},{5,6},{6,5},{7,7},{8,8},{9,10},{10,9... | collective-permute-start | bytes 3145736 | tf_op jit(solution)/shard_map/ppermute | solution.py:86
  13.2 1.3 %fusion.20 = f32[256,64]{0,1:T(8,128)S(1)} fusion(bf16[256,2048]{1,0:T(8,128)(2,1)} %param.8, bf16[2,1024,64]{1,2,0:T(8,128)(2,1)} %param.10), kind=kOutput, calls=%fused_computation.30 | convolution fusion | flops 33554432 | bytes 720896 | tf_op jit(solution)/shard_map/dot_general | solution.py:20
  14.5 1.4 %fusion.22 = f32[256,64]{0,1:T(8,128)S(1)} fusion(bf16[256,2048]{1,0:T(8,128)(2,1)} %param.8, bf16[2,1024,64]{1,2,0:T(8,128)(2,1)} %param.10), kind=kOutput, calls=%fused_computation.32 | convolution fusion | flops 33554432 | bytes 720896 | tf_op jit(solution)/shard_map/dot_general | solution.py:20
  15.9 1.3 %collective-permute-start.5 = (f32[256,128]{0,1:T(8,128)S(1)}, f32[256,128]{0,1:T(8,128)S(1)}, u32[]{:S(2)}, u32[]{:S(2)}) collective-permute-start(f32[256,128]{0,1:T(8,128)S(1)} %get-tuple-element.20), channel_id=1, source_target_pairs={{3,1},{0,2},{7,5},{4,6},{11,9},{8,10},{15,13},{12,14},{19,17},{16,... | collective-permute-start | bytes 393224 | tf_op jit(solution)/shard_map/ppermute | solution.py:88
  17.2 0.0 copy-start.3
  17.2 2.5 %broadcast_in_dim.37 = bf16[4,256,2048]{2,1,0:T(8,128)(2,1)} broadcast(bf16[]{:T(256)} %constant.59.clone.1), dimensions={} | broadcast | bytes 4194306 | tf_op jit(solution)/shard_map/broadcast_in_dim | solution.py:91
  19.8 6.9 %fusion.1 = bf16[4,256,2048]{2,1,0:T(8,128)(2,1)} fusion(bf16[4,256,2048]{2,1,0:T(8,128)(2,1)} %broadcast_in_dim.37, s32[]{:T(128)S(6)} %select_n.117, bf16[256,2048]{1,0:T(8,128)(2,1)S(1)} %copy-done.3, bf16[2048,2048]{1,0:T(8,128)(2,1)} %param.7), kind=kOutput, calls=%fused_computation.5 | convolution fusion | flops 2148007936 | bytes 10485764 | tf_op jit(solution)/shard_map/dot_general | solution.py:27
  26.6 1.2 %fusion.52 = f32[1024,128]{1,0:T(8,128)S(1)} fusion(bf16[1024,2048]{1,0:T(8,128)(2,1)S(1)} %copy-done.1, bf16[2048,128]{1,0:T(8,128)(2,1)S(1)} %copy-done.2), kind=kOutput, calls=%fused_computation.89 | convolution fusion | flops 536870912 | bytes 5242880 | tf_op jit(solution)/shard_map/dot_general | solution.py:89
  27.9 0.1 copy.8
  28.1 1.1 collective-permute-done.5
  29.2 0.1 copy.11
  29.3 0.0 collective-permute-done
  29.3 0.0 collective-permute-done.1
  29.3 1.3 %fusion.16 = f32[256,64]{0,1:T(8,128)S(1)} fusion(bf16[256,2048]{1,0:T(8,128)(2,1)} %collective-permute-done, bf16[2,1024,64]{1,2,0:T(8,128)(2,1)} %param.10), kind=kOutput, calls=%fused_computation.26 | convolution fusion | flops 33554432 | bytes 720896 | tf_op jit(solution)/shard_map/dot_general | solution.py:20
  30.7 1.3 %fusion.18 = f32[256,64]{0,1:T(8,128)S(1)} fusion(bf16[256,2048]{1,0:T(8,128)(2,1)} %collective-permute-done, bf16[2,1024,64]{1,2,0:T(8,128)(2,1)} %param.10), kind=kOutput, calls=%fused_computation.28 | convolution fusion | flops 33554432 | bytes 720896 | tf_op jit(solution)/shard_map/dot_general | solution.py:20
  32.0 2.0 %fusion.12 = f32[256,64]{0,1:T(8,128)} fusion(bf16[256,2048]{1,0:T(8,128)(2,1)} %collective-permute-done.1, bf16[2,1024,64]{1,2,0:T(8,128)(2,1)} %param.10), kind=kOutput, calls=%fused_computation.22 | convolution fusion | flops 33554432 | bytes 720896 | tf_op jit(solution)/shard_map/dot_general | solution.py:20
  34.0 2.0 %fusion.14 = f32[256,64]{0,1:T(8,128)} fusion(bf16[256,2048]{1,0:T(8,128)(2,1)} %collective-permute-done.1, bf16[2,1024,64]{1,2,0:T(8,128)(2,1)} %param.10), kind=kOutput, calls=%fused_computation.24 | convolution fusion | flops 33554432 | bytes 720896 | tf_op jit(solution)/shard_map/dot_general | solution.py:20
  36.0 9.4 %collective-permute-start.2 = (bf16[256,2048]{1,0:T(8,128)(2,1)}, bf16[256,2048]{1,0:T(8,128)(2,1)}, u32[]{:S(2)}, u32[]{:S(2)}) collective-permute-start(bf16[256,2048]{1,0:T(8,128)(2,1)} %collective-permute-done), channel_id=1, source_target_pairs={{0,0},{1,2},{2,1},{3,3},{4,4},{5,6},{6,5},{7,7},{8,8},{9,10},{10,9... | collective-permute-start | bytes 3145736 | tf_op jit(solution)/shard_map/ppermute | solution.py:96
  45.4 1.3 %collective-permute-start.3 = (bf16[256,2048]{1,0:T(8,128)(2,1)}, bf16[256,2048]{1,0:T(8,128)(2,1)}, u32[]{:S(2)}, u32[]{:S(2)}) collective-permute-start(bf16[256,2048]{1,0:T(8,128)(2,1)} %collective-permute-done.1), channel_id=1, source_target_pairs={{1,0},{2,3},{5,4},{6,7},{9,8},{10,11},{13,12},{14,15},{17,16},{18,... | collective-permute-start | bytes 3145736 | tf_op jit(solution)/shard_map/ppermute | solution.py:95
  46.7 6.3 %collective-permute-start.4 = (f32[1024,128]{1,0:T(8,128)S(1)}, f32[1024,128]{1,0:T(8,128)}, u32[]{:S(2)}, u32[]{:S(2)}) collective-permute-start(f32[1024,128]{1,0:T(8,128)S(1)} %fusion.52), channel_id=1, source_target_pairs={{0,1},{3,2},{4,5},{7,6},{8,9},{11,10},{12,13},{15,14},{16,17},{19,... | collective-permute-start | bytes 1572872 | tf_op jit(solution)/shard_map/ppermute | solution.py:97
  53.0 0.1 copy.9
  53.1 1.5 %maximum_bitcast_fusion.1 = f32[1,256,128]{1,2,0:T(8,128)} fusion(f32[256,64]{0,1:T(8,128)} %fusion.12, f32[256,64]{0,1:T(8,128)} %fusion.14), kind=kLoop, calls=%fused_computation.37 | loop fusion | flops 32768 | bytes 262144 | tf_op jit(solution)/shard_map/broadcast_in_dim | solution.py:57
  54.6 1.0 copy.10
  55.7 6.4 %collective-permute-done.4 = f32[1024,128]{1,0:T(8,128)} collective-permute-done((f32[1024,128]{1,0:T(8,128)S(1)}, f32[1024,128]{1,0:T(8,128)}, u32[]{:S(2)}, u32[]{:S(2)}) %collective-permute-start.4) | collective-permute-done | bytes 524320 | tf_op jit(solution)/shard_map/ppermute | solution.py:97
  62.1 1.1 add_bitcast_fusion
  63.2 1.0 convolution_bitcast_fusion.1
  64.3 1.3 %convolution_bitcast_fusion = f32[1,64,64]{1,2,0:T(8,128)S(1)} fusion(f32[1,1024,128]{2,1,0:T(8,128)S(1)} %bitcast.80, f32[1,1024,128]{2,1,0:T(8,128)S(1)} %add_bitcast_fusion), kind=kOutput, calls=%fused_computation.12 | convolution fusion | flops 50331648 | bytes 1064960 | tf_op jit(solution)/shard_map/dot_general | solution.py:38
  65.6 0.1 pad_maximum_fusion.1
  65.7 0.1 copy.12
  65.8 0.7 collective-permute-start.6
  66.5 1.3 %collective-permute-start.7 = (f32[1,32,64]{2,1,0:T(8,128)S(1)}, f32[1,32,64]{2,1,0:T(8,128)S(1)}, u32[]{:S(2)}, u32[]{:S(2)}) collective-permute-start(f32[1,32,64]{2,1,0:T(8,128)S(1)} %get-tuple-element.24), channel_id=1, source_target_pairs={{1,0},{2,3},{5,4},{6,7},{9,8},{10,11},{13,12},{14,15},{17,16},{18,... | collective-permute-start | bytes 24584 | tf_op jit(solution)/shard_map/ppermute | solution.py:110
  67.8 1.3 %collective-permute-start.8 = (f32[1,32,64]{2,1,0:T(8,128)S(1)}, f32[1,32,64]{2,1,0:T(8,128)S(1)}, u32[]{:S(2)}, u32[]{:S(2)}) collective-permute-start(f32[1,32,64]{2,1,0:T(8,128)S(1)} %get-tuple-element.23), channel_id=1, source_target_pairs={{1,3},{2,0},{5,7},{6,4},{9,11},{10,8},{13,15},{14,12},{17,19},{18,... | collective-permute-start | bytes 24584 | tf_op jit(solution)/shard_map/ppermute | solution.py:111
  69.1 7.1 %fusion.3 = bf16[4,256,2048]{2,1,0:T(8,128)(2,1)} fusion(bf16[4,256,2048]{2,1,0:T(8,128)(2,1)} %fusion.1, s32[]{:T(128)S(6)} %select_n.118, bf16[256,2048]{1,0:T(8,128)(2,1)} %collective-permute-done, bf16[2048,2048]{1,0:T(8,128)(2,1)} %param.7), kind=kOutput, calls=%fused_computation.7 | convolution fusion | flops 2148007936 | bytes 10485764 | tf_op jit(solution)/shard_map/dot_general | solution.py:27
  76.1 0.0 collective-permute-done.7
  76.1 0.0 collective-permute-done.8
  76.2 0.0 collective-permute-done.3
  76.2 0.1 reshape.65
  76.3 0.0 collective-permute-start.10
  76.3 1.6 %collective-permute-start.11 = (f32[1,2048]{1,0:T(1,128)S(1)}, f32[1,2048]{1,0:T(1,128)S(1)}, u32[]{:S(2)}, u32[]{:S(2)}) collective-permute-start(f32[1,2048]{1,0:T(1,128)S(1)} %reshape.65), channel_id=1, source_target_pairs={{0,8},{4,12},{8,0},{12,4},{1,9},{5,13},{9,1},{13,5},{2,10},{6,14},... | collective-permute-start | bytes 24584 | tf_op jit(solution)/shard_map/ppermute | solution.py:140
  77.8 1.4 %collective-permute-start.12 = (f32[1,2048]{1,0:T(1,128)S(1)}, f32[1,2048]{1,0:T(1,128)S(1)}, u32[]{:S(2)}, u32[]{:S(2)}) collective-permute-start(f32[1,2048]{1,0:T(1,128)S(1)} %reshape.65), channel_id=1, source_target_pairs={{0,12},{4,0},{8,4},{12,8},{1,13},{5,1},{9,5},{13,9},{2,14},{6,2},{... | collective-permute-start | bytes 24584 | tf_op jit(solution)/shard_map/ppermute | solution.py:140
  79.2 0.1 collective-permute-done.10
  79.3 0.7 collective-permute-done.11
  80.0 0.6 collective-permute-done.12
  80.6 0.1 reduce-precision_convert_fusion.1
  80.7 0.6 fusion.36
  81.4 1.8 %collective-permute-start.13 = (f32[1,512]{1,0:T(1,128)S(1)}, f32[1,512]{1,0:T(1,128)S(1)}, u32[]{:S(2)}, u32[]{:S(2)}) collective-permute-start(f32[1,512]{1,0:T(1,128)S(1)} %get-tuple-element.33), channel_id=1, source_target_pairs={{0,12},{4,0},{8,4},{12,8},{1,13},{5,1},{9,5},{13,9},{2,14},{6,2},{... | collective-permute-start | bytes 6152 | tf_op jit(solution)/shard_map/ppermute | solution.py:153
  83.1 1.3 %collective-permute-start.9 = (bf16[256,2048]{1,0:T(8,128)(2,1)}, bf16[256,2048]{1,0:T(8,128)(2,1)S(1)}, u32[]{:S(2)}, u32[]{:S(2)}) collective-permute-start(bf16[256,2048]{1,0:T(8,128)(2,1)} %collective-permute-done.2), channel_id=1, source_target_pairs={{1,0},{2,3},{5,4},{6,7},{9,8},{10,11},{13,12},{14,15},{17,16},{18,... | collective-permute-start | bytes 3145736 | tf_op jit(solution)/shard_map/ppermute | solution.py:114
  84.4 0.6 collective-permute-start.14
  85.0 0.0 collective-permute-start.15
  85.0 0.0 collective-permute-done.13
  85.0 3.0 %collective-permute-done.14 = f32[1,512]{1,0:T(1,128)S(1)} collective-permute-done((f32[1,512]{1,0:T(1,128)S(1)}, f32[1,512]{1,0:T(1,128)S(1)}, u32[]{:S(2)}, u32[]{:S(2)}) %collective-permute-start.14) | collective-permute-done | bytes 2080 | tf_op jit(solution)/shard_map/ppermute | solution.py:153
  88.1 0.0 collective-permute-done.15
  88.1 5.5 %collective-permute-start.16 = (f32[1,512]{1,0:T(1,128)S(1)}, f32[1,512]{1,0:T(1,128)S(1)}, u32[]{:S(2)}, u32[]{:S(2)}) collective-permute-start(f32[1,512]{1,0:T(1,128)S(1)} %get-tuple-element.28), channel_id=1, source_target_pairs={{0,1},{1,2},{2,3},{3,0},{4,5},{5,6},{6,7},{7,4},{8,9},{9,10},{10,1... | collective-permute-start | bytes 6152 | tf_op jit(solution)/shard_map/ppermute | solution.py:164
  93.6 0.0 collective-permute-start.17
  93.6 2.8 %collective-permute-start.18 = (f32[1,512]{1,0:T(1,128)S(1)}, f32[1,512]{1,0:T(1,128)S(1)}, u32[]{:S(2)}, u32[]{:S(2)}) collective-permute-start(f32[1,512]{1,0:T(1,128)S(1)} %get-tuple-element.29), channel_id=1, source_target_pairs={{0,3},{1,0},{2,1},{3,2},{4,7},{5,4},{6,5},{7,6},{8,11},{9,8},{10,9... | collective-permute-start | bytes 6152 | tf_op jit(solution)/shard_map/ppermute | solution.py:164
  96.4 7.1 %fusion.5 = bf16[4,256,2048]{2,1,0:T(8,128)(2,1)} fusion(bf16[4,256,2048]{2,1,0:T(8,128)(2,1)} %fusion.3, s32[]{:T(128)S(6)} %select_n.122, bf16[2048,2048]{1,0:T(8,128)(2,1)} %param.7, bf16[256,2048]{1,0:T(8,128)(2,1)} %collective-permute-done.1, bf16[256,2048]{1,0:T(8,128)(2,1)} %collective-permute-done.3, pred[]{:T(512)S(6)} %or.3), kind=kOutput, calls=%fused_computation.9 | convolution fusion | flops 2148532224 | bytes 11534341 | tf_op jit(solution)/shard_map/dot_general | solution.py:27
  103.5 0.0 collective-permute-done.16
  103.5 0.0 collective-permute-done.17
  103.5 9.0 %collective-permute-done.18 = f32[1,512]{1,0:T(1,128)S(1)} collective-permute-done((f32[1,512]{1,0:T(1,128)S(1)}, f32[1,512]{1,0:T(1,128)S(1)}, u32[]{:S(2)}, u32[]{:S(2)}) %collective-permute-start.18) | collective-permute-done | bytes 2080 | tf_op jit(solution)/shard_map/ppermute | solution.py:164
  112.5 0.6 fusion.48
  113.0 0.0 collective-permute-done.9
  113.0 6.7 %fusion.7 = bf16[4,256,2048]{2,1,0:T(8,128)(2,1)} fusion(bf16[4,256,2048]{2,1,0:T(8,128)(2,1)} %fusion.5, s32[]{:T(128)S(6)} %select_n.130, bf16[2048,2048]{1,0:T(8,128)(2,1)} %param.7, bf16[256,2048]{1,0:T(8,128)(2,1)} %collective-permute-done.2, bf16[256,2048]{1,0:T(8,128)(2,1)S(1)} %collective-permute-done.9, pred[]{:T(512)S(6)} %or.3), kind=kOutput, calls=%fused_computation.11 | convolution fusion | flops 2148532224 | bytes 11534341 | tf_op jit(solution)/shard_map/dot_general | solution.py:27
  (24 shorter events, 0.2 us)
Async XLA Ops:
  0.6 80.0 %copy-start = (bf16[512,2048]{1,0:T(8,128)(2,1)S(1)}, bf16[512,2048]{1,0:T(8,128)(2,1)}, u32[]{:S(2)}) copy-start(bf16[512,2048]{1,0:T(8,128)(2,1)} %param.11) | copy-start | bytes 6291460
  0.6 28.7 %collective-permute-start = (bf16[256,2048]{1,0:T(8,128)(2,1)}, bf16[256,2048]{1,0:T(8,128)(2,1)}, u32[]{:S(2)}, u32[]{:S(2)}) collective-permute-start(bf16[256,2048]{1,0:T(8,128)(2,1)} %param.8), channel_id=1, source_target_pairs={{0,1},{1,0},{2,3},{3,2},{4,5},{5,4},{6,7},{7,6},{8,9},{9,8},{10,11... | collective-permute-start | bytes 3145736 | tf_op jit(solution)/shard_map/ppermute | solution.py:85
  3.7 25.6 %collective-permute-start.1 = (bf16[256,2048]{1,0:T(8,128)(2,1)}, bf16[256,2048]{1,0:T(8,128)(2,1)}, u32[]{:S(2)}, u32[]{:S(2)}) collective-permute-start(bf16[256,2048]{1,0:T(8,128)(2,1)} %param.8), channel_id=1, source_target_pairs={{0,0},{1,2},{2,1},{3,3},{4,4},{5,6},{6,5},{7,7},{8,8},{9,10},{10,9... | collective-permute-start | bytes 3145736 | tf_op jit(solution)/shard_map/ppermute | solution.py:86
  15.9 13.3 %collective-permute-start.5 = (f32[256,128]{0,1:T(8,128)S(1)}, f32[256,128]{0,1:T(8,128)S(1)}, u32[]{:S(2)}, u32[]{:S(2)}) collective-permute-start(f32[256,128]{0,1:T(8,128)S(1)} %get-tuple-element.20), channel_id=1, source_target_pairs={{3,1},{0,2},{7,5},{4,6},{11,9},{8,10},{15,13},{12,14},{19,17},{16,... | collective-permute-start | bytes 393224 | tf_op jit(solution)/shard_map/ppermute | solution.py:88
  17.2 2.6 %copy-start.3 = (bf16[256,2048]{1,0:T(8,128)(2,1)S(1)}, bf16[256,2048]{1,0:T(8,128)(2,1)}, u32[]{:S(2)}) copy-start(bf16[256,2048]{1,0:T(8,128)(2,1)} %param.8) | copy-start | bytes 3145732
  19.8 6.9 %copy-start.1 = (bf16[1024,2048]{1,0:T(8,128)(2,1)S(1)}, bf16[1024,2048]{1,0:T(8,128)(2,1)}, u32[]{:S(2)}) copy-start(bf16[1024,2048]{1,0:T(8,128)(2,1)} %param.6) | copy-start | bytes 12582916
  19.8 6.9 %copy-start.2 = (bf16[2048,128]{1,0:T(8,128)(2,1)S(1)}, bf16[2048,128]{1,0:T(8,128)(2,1)}, u32[]{:S(2)}) copy-start(bf16[2048,128]{1,0:T(8,128)(2,1)} %param.9) | copy-start | bytes 1572868
  36.0 40.2 %collective-permute-start.2 = (bf16[256,2048]{1,0:T(8,128)(2,1)}, bf16[256,2048]{1,0:T(8,128)(2,1)}, u32[]{:S(2)}, u32[]{:S(2)}) collective-permute-start(bf16[256,2048]{1,0:T(8,128)(2,1)} %collective-permute-done), channel_id=1, source_target_pairs={{0,0},{1,2},{2,1},{3,3},{4,4},{5,6},{6,5},{7,7},{8,8},{9,10},{10,9... | collective-permute-start | bytes 3145736 | tf_op jit(solution)/shard_map/ppermute | solution.py:96
  45.4 30.8 %collective-permute-start.3 = (bf16[256,2048]{1,0:T(8,128)(2,1)}, bf16[256,2048]{1,0:T(8,128)(2,1)}, u32[]{:S(2)}, u32[]{:S(2)}) collective-permute-start(bf16[256,2048]{1,0:T(8,128)(2,1)} %collective-permute-done.1), channel_id=1, source_target_pairs={{1,0},{2,3},{5,4},{6,7},{9,8},{10,11},{13,12},{14,15},{17,16},{18,... | collective-permute-start | bytes 3145736 | tf_op jit(solution)/shard_map/ppermute | solution.py:95
  46.7 15.5 %collective-permute-start.4 = (f32[1024,128]{1,0:T(8,128)S(1)}, f32[1024,128]{1,0:T(8,128)}, u32[]{:S(2)}, u32[]{:S(2)}) collective-permute-start(f32[1024,128]{1,0:T(8,128)S(1)} %fusion.52), channel_id=1, source_target_pairs={{0,1},{3,2},{4,5},{7,6},{8,9},{11,10},{12,13},{15,14},{16,17},{19,... | collective-permute-start | bytes 1572872 | tf_op jit(solution)/shard_map/ppermute | solution.py:97
  65.8 10.3 %collective-permute-start.6 = (f32[1,32,64]{2,1,0:T(8,128)S(1)}, f32[1,32,64]{2,1,0:T(8,128)S(1)}, u32[]{:S(2)}, u32[]{:S(2)}) collective-permute-start(f32[1,32,64]{2,1,0:T(8,128)S(1)} %get-tuple-element.22), channel_id=1, source_target_pairs={{1,2},{2,1},{5,6},{6,5},{9,10},{10,9},{13,14},{14,13},{17,18},{18,... | collective-permute-start | bytes 24584 | tf_op jit(solution)/shard_map/ppermute | solution.py:109
  66.5 9.7 %collective-permute-start.7 = (f32[1,32,64]{2,1,0:T(8,128)S(1)}, f32[1,32,64]{2,1,0:T(8,128)S(1)}, u32[]{:S(2)}, u32[]{:S(2)}) collective-permute-start(f32[1,32,64]{2,1,0:T(8,128)S(1)} %get-tuple-element.24), channel_id=1, source_target_pairs={{1,0},{2,3},{5,4},{6,7},{9,8},{10,11},{13,12},{14,15},{17,16},{18,... | collective-permute-start | bytes 24584 | tf_op jit(solution)/shard_map/ppermute | solution.py:110
  67.8 8.4 %collective-permute-start.8 = (f32[1,32,64]{2,1,0:T(8,128)S(1)}, f32[1,32,64]{2,1,0:T(8,128)S(1)}, u32[]{:S(2)}, u32[]{:S(2)}) collective-permute-start(f32[1,32,64]{2,1,0:T(8,128)S(1)} %get-tuple-element.23), channel_id=1, source_target_pairs={{1,3},{2,0},{5,7},{6,4},{9,11},{10,8},{13,15},{14,12},{17,19},{18,... | collective-permute-start | bytes 24584 | tf_op jit(solution)/shard_map/ppermute | solution.py:111
  76.3 3.1 %collective-permute-start.10 = (f32[1,2048]{1,0:T(1,128)S(1)}, f32[1,2048]{1,0:T(1,128)S(1)}, u32[]{:S(2)}, u32[]{:S(2)}) collective-permute-start(f32[1,2048]{1,0:T(1,128)S(1)} %reshape.65), channel_id=1, source_target_pairs={{0,4},{4,8},{8,12},{12,0},{1,5},{5,9},{9,13},{13,1},{2,6},{6,10},{... | collective-permute-start | bytes 24584 | tf_op jit(solution)/shard_map/ppermute | solution.py:140
  76.3 3.7 %collective-permute-start.11 = (f32[1,2048]{1,0:T(1,128)S(1)}, f32[1,2048]{1,0:T(1,128)S(1)}, u32[]{:S(2)}, u32[]{:S(2)}) collective-permute-start(f32[1,2048]{1,0:T(1,128)S(1)} %reshape.65), channel_id=1, source_target_pairs={{0,8},{4,12},{8,0},{12,4},{1,9},{5,13},{9,1},{13,5},{2,10},{6,14},... | collective-permute-start | bytes 24584 | tf_op jit(solution)/shard_map/ppermute | solution.py:140
  77.8 2.8 %collective-permute-start.12 = (f32[1,2048]{1,0:T(1,128)S(1)}, f32[1,2048]{1,0:T(1,128)S(1)}, u32[]{:S(2)}, u32[]{:S(2)}) collective-permute-start(f32[1,2048]{1,0:T(1,128)S(1)} %reshape.65), channel_id=1, source_target_pairs={{0,12},{4,0},{8,4},{12,8},{1,13},{5,1},{9,5},{13,9},{2,14},{6,2},{... | collective-permute-start | bytes 24584 | tf_op jit(solution)/shard_map/ppermute | solution.py:140
  81.4 3.7 %collective-permute-start.13 = (f32[1,512]{1,0:T(1,128)S(1)}, f32[1,512]{1,0:T(1,128)S(1)}, u32[]{:S(2)}, u32[]{:S(2)}) collective-permute-start(f32[1,512]{1,0:T(1,128)S(1)} %get-tuple-element.33), channel_id=1, source_target_pairs={{0,12},{4,0},{8,4},{12,8},{1,13},{5,1},{9,5},{13,9},{2,14},{6,2},{... | collective-permute-start | bytes 6152 | tf_op jit(solution)/shard_map/ppermute | solution.py:153
  83.1 29.9 %collective-permute-start.9 = (bf16[256,2048]{1,0:T(8,128)(2,1)}, bf16[256,2048]{1,0:T(8,128)(2,1)S(1)}, u32[]{:S(2)}, u32[]{:S(2)}) collective-permute-start(bf16[256,2048]{1,0:T(8,128)(2,1)} %collective-permute-done.2), channel_id=1, source_target_pairs={{1,0},{2,3},{5,4},{6,7},{9,8},{10,11},{13,12},{14,15},{17,16},{18,... | collective-permute-start | bytes 3145736 | tf_op jit(solution)/shard_map/ppermute | solution.py:114
  84.4 3.7 %collective-permute-start.14 = (f32[1,512]{1,0:T(1,128)S(1)}, f32[1,512]{1,0:T(1,128)S(1)}, u32[]{:S(2)}, u32[]{:S(2)}) collective-permute-start(f32[1,512]{1,0:T(1,128)S(1)} %get-tuple-element.32), channel_id=1, source_target_pairs={{0,8},{4,12},{8,0},{12,4},{1,9},{5,13},{9,1},{13,5},{2,10},{6,14},... | collective-permute-start | bytes 6152 | tf_op jit(solution)/shard_map/ppermute | solution.py:153
  85.0 3.1 %collective-permute-start.15 = (f32[1,512]{1,0:T(1,128)S(1)}, f32[1,512]{1,0:T(1,128)S(1)}, u32[]{:S(2)}, u32[]{:S(2)}) collective-permute-start(f32[1,512]{1,0:T(1,128)S(1)} %get-tuple-element.31), channel_id=1, source_target_pairs={{0,4},{4,8},{8,12},{12,0},{1,5},{5,9},{9,13},{13,1},{2,6},{6,10},{... | collective-permute-start | bytes 6152 | tf_op jit(solution)/shard_map/ppermute | solution.py:153
  88.1 15.4 %collective-permute-start.16 = (f32[1,512]{1,0:T(1,128)S(1)}, f32[1,512]{1,0:T(1,128)S(1)}, u32[]{:S(2)}, u32[]{:S(2)}) collective-permute-start(f32[1,512]{1,0:T(1,128)S(1)} %get-tuple-element.28), channel_id=1, source_target_pairs={{0,1},{1,2},{2,3},{3,0},{4,5},{5,6},{6,7},{7,4},{8,9},{9,10},{10,1... | collective-permute-start | bytes 6152 | tf_op jit(solution)/shard_map/ppermute | solution.py:164
  93.6 9.9 %collective-permute-start.17 = (f32[1,512]{1,0:T(1,128)S(1)}, f32[1,512]{1,0:T(1,128)S(1)}, u32[]{:S(2)}, u32[]{:S(2)}) collective-permute-start(f32[1,512]{1,0:T(1,128)S(1)} %get-tuple-element.30), channel_id=1, source_target_pairs={{0,2},{1,3},{2,0},{3,1},{4,6},{5,7},{6,4},{7,5},{8,10},{9,11},{10,... | collective-permute-start | bytes 6152 | tf_op jit(solution)/shard_map/ppermute | solution.py:164
  93.6 18.8 %collective-permute-start.18 = (f32[1,512]{1,0:T(1,128)S(1)}, f32[1,512]{1,0:T(1,128)S(1)}, u32[]{:S(2)}, u32[]{:S(2)}) collective-permute-start(f32[1,512]{1,0:T(1,128)S(1)} %get-tuple-element.29), channel_id=1, source_target_pairs={{0,3},{1,0},{2,1},{3,2},{4,7},{5,4},{6,5},{7,6},{8,11},{9,8},{10,9... | collective-permute-start | bytes 6152 | tf_op jit(solution)/shard_map/ppermute | solution.py:164

commit v3 on v2

--- a/solution.py
+++ b/solution.py
@@ -1,6 +1,10 @@
+import functools
+
 import jax
 import jax.numpy as jnp
 from jax import lax
+from jax.experimental import pallas as pl
+from jax.experimental.pallas import tpu as pltpu
 from jax.sharding import PartitionSpec as P
 
 SEQ = 1024
@@ -14,19 +18,66 @@
     return [term.astype(jnp.bfloat16) for term in (high, middle, low)]
 
 
-def low_rank_rows(rows, proj_out):
-    width = rows.shape[1] // 2
-    parts = [
-        jnp.dot(rows[:, layer * width : (layer + 1) * width], proj_out[layer], preferred_element_type=jnp.float32)
-        for layer in range(2)
-    ]
-    return jnp.concatenate(parts, axis=1)
+def block_diagonal(proj_out):
+    layers, width, rank = proj_out.shape
+    zeros = jnp.zeros((width, rank), proj_out.dtype)
+    return jnp.concatenate(
+        [
+            jnp.concatenate([proj_out[layer] if column == layer else zeros for column in range(layers)], axis=1)
+            for layer in range(layers)
+        ],
+        axis=0,
+    )
 
 
 def times_width(rows, w_kv):
     return lax.dot_general(
         rows, w_kv, (((1,), (1,)), ((), ())), preferred_element_type=jnp.float32
     ).astype(jnp.bfloat16)
+
+
+def rows_kernel(part, place, first, second, w_tile, *refs):
+    out, held, arrived = refs[-3:]
+    rows = held.shape[0]
+
+    @pl.when(pl.program_id(0) == 0)
+    def _():
+        own_part = first.at[pl.ds(part * rows, rows)]
+        for source, chosen in ((own_part, place[1] == 0), (second, place[1] != 0)):
+
+            @pl.when(chosen)
+            def _():
+                copy = pltpu.make_async_copy(source, held, arrived)
+                copy.start()
+                copy.wait()
+
+    out[0] = lax.dot_general(
+        held[...], w_tile[...], (((1,), (1,)), ((), ())), preferred_element_type=jnp.float32
+    ).astype(out.dtype)
+
+
+def put_rows(output, blocks, first, second, w_kv, index, use_second=0, part=0):
+    rows, depth = second.shape
+    width = w_kv.shape[0]
+    tile = min(width, 512)
+    place = jnp.stack([index, use_second]).astype(jnp.int32)
+    anywhere = pl.BlockSpec(memory_space=pl.ANY)
+    earlier = [] if output is None else [output]
+    return pl.pallas_call(
+        functools.partial(rows_kernel, part),
+        grid_spec=pltpu.PrefetchScalarGridSpec(
+            num_scalar_prefetch=1,
+            grid=(width // tile,),
+            in_specs=[anywhere, anywhere, pl.BlockSpec((tile, depth), lambda j, place: (j, 0))] + [anywhere] * len(earlier),
+            out_specs=pl.BlockSpec((1, rows, tile), lambda j, place: (place[0], part, j)),
+            scratch_shapes=[pltpu.VMEM((rows, depth), first.dtype), pltpu.SemaphoreType.DMA],
+        ),
+        out_shape=jax.ShapeDtypeStruct((blocks, first.shape[0], width), jnp.bfloat16),
+        input_output_aliases={4: 0} if earlier else {},
+        compiler_params=pltpu.CompilerParams(vmem_limit_bytes=16 * 2**20),
+        cost_estimate=pl.CostEstimate(flops=rows * width, bytes_accessed=2 * rows * width, transcendentals=0),
+        name="input_grad_rows",
+    )(place, first, second, w_kv, *earlier)
 
 
 def sequence_sums(low_in, low_out, rank):
@@ -67,9 +118,9 @@
     whole = lax.all_gather(grad_kv, "mp", axis=0, tiled=True)
     input_grad = times_width(whole, w_kv)
     low_in = jnp.dot(hidden, proj_in, preferred_element_type=jnp.float32)
-    sums = slabs_of(sequence_sums(low_in, low_rank_rows(whole, proj_out), rank), n)
+    sums = slabs_of(sequence_sums(low_in, jnp.dot(whole, block_diagonal(proj_out), preferred_element_type=jnp.float32), rank), n)
     features = lax.psum_scatter(sums, "mp", scatter_dimension=0, tiled=False)
-    return input_grad, features
+    return features, lambda total: total, lambda: input_grad
 
 
 def line_of_four(hidden, w_kv, grad_kv, proj_in, proj_out):
@@ -78,30 +129,29 @@
     me = lax.axis_index("mp")
     middle = (me == 1) | (me == 2)
     exchange_pairs = [(0, 1), (1, 0), (2, 3), (3, 2)]
-    across = [(0, 0), (1, 2), (2, 1), (3, 3)]
+    across = [(1, 2), (2, 1)]
     outward = [(1, 0), (2, 3)]
     inward = [(0, 1), (3, 2)]
 
     beside = lax.ppermute(grad_kv, "mp", exchange_pairs)
     facing = lax.ppermute(grad_kv, "mp", across)
-    own_low = low_rank_rows(grad_kv, proj_out)
+    proj_both = block_diagonal(proj_out)
+    own_low = jnp.dot(grad_kv, proj_both, preferred_element_type=jnp.float32)
     far_low = lax.ppermute(own_low, "mp", [(3, 1), (0, 2)])
     low_in = jnp.dot(hidden, proj_in, preferred_element_type=jnp.float32)
-
-    output = jnp.zeros((4, local_rows, w_kv.shape[0]), jnp.bfloat16)
-    output = put(output, times_width(grad_kv, w_kv), me)
+    output = put_rows(None, 4, grad_kv, grad_kv, w_kv, me, 0)
 
     beside, facing, low_in, output = lax.optimization_barrier((beside, facing, low_in, output))
     second = lax.ppermute(facing, "mp", outward)
     beside_across = lax.ppermute(beside, "mp", across)
     low_in_beside = lax.ppermute(low_in, "mp", inward)
 
-    output = put(output, times_width(beside, w_kv), me ^ 1)
+    output = put_rows(output, 4, beside, beside, w_kv, me ^ 1, 0)
 
     low_out = jnp.zeros((4, local_rows, 2 * rank), jnp.float32)
     low_out = put(low_out, own_low, me)
-    low_out = put(low_out, low_rank_rows(beside, proj_out), me ^ 1)
-    low_out = put(low_out, low_rank_rows(facing, proj_out), me ^ 3)
+    low_out = put(low_out, jnp.dot(beside, proj_both, preferred_element_type=jnp.float32), me ^ 1)
+    low_out = put(low_out, jnp.dot(facing, proj_both, preferred_element_type=jnp.float32), me ^ 3)
     low_out = put(low_out, far_low, me ^ 2)
     sums = sequence_sums(low_in + low_in_beside, low_out.reshape(4 * local_rows, 2 * rank), rank)
     slabs = slabs_of(sums, 4)
@@ -111,25 +161,30 @@
     mine = mine + lax.ppermute(take(slabs, me ^ 2), "mp", [(1, 3), (2, 0)])
 
     beside_across, second, output = lax.optimization_barrier((beside_across, second, output))
-    third = lax.ppermute(beside_across, "mp", outward)
+    half = local_rows // 2
+    third = [lax.ppermute(beside_across[part * half : (part + 1) * half], "mp", outward) for part in range(2)]
     mine, beside_across = lax.optimization_barrier((mine, beside_across))
-    output = put(
-        output,
-        times_width(jnp.where(middle, facing, second), w_kv),
-        jnp.where(middle, me ^ 3, me ^ 2),
-    )
-    output = put(
-        output,
-        times_width(jnp.where(middle, beside_across, third), w_kv),
-        jnp.where(middle, me ^ 2, me ^ 3),
-    )
-    return output.reshape(4 * local_rows, w_kv.shape[0]), mine
+    ends = jnp.logical_not(middle).astype(jnp.int32)
+    output = put_rows(output, 4, facing, second, w_kv, jnp.where(middle, me ^ 3, me ^ 2), ends)
+    last = jnp.where(middle, me ^ 2, me ^ 3)
+    output = put_rows(output, 4, beside_across, third[0], w_kv, last, ends, 0)
+
+    def finish(total):
+        total, arrived = lax.optimization_barrier((total, third[0]))
+        return total
+
+    def rest():
+        return put_rows(output, 4, beside_across, third[1], w_kv, last, ends, 1).reshape(
+            4 * local_rows, w_kv.shape[0]
+        )
+
+    return mine, finish, rest
 
 
 def on_device(hidden, w_kv, grad_kv, proj_in, proj_out, queries):
     n = lax.axis_size("mp")
     me = lax.axis_index("mp")
-    input_grad, mine = (line_of_four if n == 4 else gathered)(hidden, w_kv, grad_kv, proj_in, proj_out)
+    mine, finish, rest = (line_of_four if n == 4 else gathered)(hidden, w_kv, grad_kv, proj_in, proj_out)
     count = mine.shape[0]
 
     shards = lax.axis_size("dp")
@@ -154,17 +209,25 @@
         total = lax.dynamic_update_slice(
             total, back, (jnp.int32(0), (shard + step) % shards * block_rows)
         )
+    total = finish(total)
     out_columns = shards * block_rows // n
 
     def columns_of(index):
         return lax.dynamic_slice(total, (jnp.int32(0), index * out_columns), (count, out_columns))
 
-    scores = columns_of(me)
-    for step in range(1, n):
-        scores = scores + lax.ppermute(
-            columns_of((me + step) % n), "mp", [(source, (source + step) % n) for source in range(n)]
-        )
-    return (input_grad, scores)
+    if n == 4:
+        pairs = [(source, source ^ 3) for source in range(n)]
+        away = lax.ppermute(jnp.concatenate([columns_of(me ^ 3), columns_of(me ^ 1)], axis=0), "mp", pairs)
+        kept = columns_of(me ^ 2) + away[count:]
+        scores = columns_of(me) + away[:count]
+        scores = scores + lax.ppermute(kept, "mp", [(source, source ^ 2) for source in range(n)])
+    else:
+        scores = columns_of(me)
+        for step in range(1, n):
+            scores = scores + lax.ppermute(
+                columns_of((me + step) % n), "mp", [(source, (source + step) % n) for source in range(n)]
+            )
+    return (rest(), scores)
 
 
 def solution(mesh):

time: 121 us -> 115 us (0.950)
  Pallas kernels: 0 us -> 26.7 us
  matrix products: 41.3 us -> 15.9 us
  starting transfers between devices: 49 us -> 26.4 us
  local copies, waits for them, and re-layouts: 4.15 us -> 13.4 us
  waiting for transfers between devices: 21 us -> 28.3 us
  other arithmetic: 3.42 us -> 2.19 us
    dot_general x10 -> x3, matrix products: 37 us -> 6.48 us  [the longest x1 2.34 us: line_of_four(): jnp.dot(beside, proj_both, preferred_element_type=jnp.float32)]
    pallas_call x0 -> x5, Pallas kernels: none -> 26.7 us  [put_rows(): pl.pallas_call(functools.partial(rows_kernel, part), grid_spec=pltpu.Pref...]
    unnamed x8 -> x16, local copies, waits for them, and re-layouts: 0.02 us -> 10.2 us
    ppermute x1, starting transfers between devices: 9.43 us -> 0.73 us  [line_of_four(): beside_across = lax.ppermute(beside, 'mp', across)]
    ppermute x1, starting transfers between devices: 9.44 us -> 1.78 us  [line_of_four(): facing = lax.ppermute(grad_kv, 'mp', across)]
    ppermute x1, waiting for transfers between devices: 1.13 us -> 7.31 us  [line_of_four(): far_low = lax.ppermute(own_low, 'mp', [(3, 1), (0, 2)])]
    ppermute x4, waiting for transfers between devices: 8.97 us -> 14.9 us  [the longest x2 10.8 us: line_of_four(): lax.ppermute(beside_across[part * half:(part + 1) * half], 'mp', outward)]
    ppermute x4, starting transfers between devices: 9.62 us -> 3.97 us  [the longest x2 2.56 us: line_of_four(): lax.ppermute(beside_across[part * half:(part + 1) * half], 'mp', outward)]
  transfers between devices with their start and end apart: 19 -> 19, of which waited for: 7 -> 6; matrix products, arithmetic and copies ran while one was open for 29% -> 18% of each run, Pallas kernels for 0% -> 23%
where the time goes in v3:
time: 115 us; the launch traced here: 114 us
  waiting for transfers between devices  28.3 us (25%)
  Pallas kernels  26.7 us (23%)
  starting transfers between devices  26.4 us (23%)
  matrix products  15.9 us (14%)
  local copies, waits for them, and re-layouts  13.4 us (12%)
  other arithmetic  2.19 us (2%)
    pallas_call x5, Pallas kernels, put_rows(): pl.pallas_call(functools.partial(rows_kernel, part), grid_spec=pltpu.Pref...  26.7 us
    ppermute x2, waiting for transfers between devices, line_of_four(): lax.ppermute(beside_across[part * half:(part + 1) * half], 'mp', outward)  10.8 us
    unnamed x16, local copies, waits for them, and re-layouts  10.2 us
    ppermute x1, waiting for transfers between devices, line_of_four(): far_low = lax.ppermute(own_low, 'mp', [(3, 1), (0, 2)])  7.31 us
    ppermute x1, starting transfers between devices, line_of_four(): beside = lax.ppermute(grad_kv, 'mp', exchange_pairs)  4.94 us
    dot_general x2, matrix products, sequence_sums(): lax.dot_general(left[:, :, layer * rank:(layer + 1) * rank], right[:, :,...  4.42 us
    dot_general x1, matrix products, line_of_four(): low_in = jnp.dot(hidden, proj_in, preferred_element_type=jnp.float32)  4.36 us
    ppermute x1, starting transfers between devices, line_of_four(): low_in_beside = lax.ppermute(low_in, 'mp', inward)  4.3 us
  transfers between devices with their start and end apart: 19, of which 6 were waited for; matrix products, arithmetic and copies ran while one was open for 18% of the time, Pallas kernels for 23%

profile of v3, /device:TPU:0, one launch (start us, length us, event | category | flops | bytes accessed | tf_op | source)
XLA Modules:
  0.0 114.0 jit_solution(14571633282521894310)
XLA Ops:
  0.6 0.0 copy-start
  0.6 1.8 %collective-permute-start.1 = (bf16[256,2048]{1,0:T(8,128)(2,1)}, bf16[256,2048]{1,0:T(8,128)(2,1)}, u32[]{:S(2)}, u32[]{:S(2)}) collective-permute-start(bf16[256,2048]{1,0:T(8,128)(2,1)} %second.1), channel_id=1, source_target_pairs={{1,2},{2,1},{5,6},{6,5},{9,10},{10,9},{13,14},{14,13},{17,18},{18,... | collective-permute-start | bytes 3145736 | tf_op jit(solution)/shard_map/ppermute | solution.py:137
  2.4 4.9 %collective-permute-start = (bf16[256,2048]{1,0:T(8,128)(2,1)}, bf16[256,2048]{1,0:T(8,128)(2,1)}, u32[]{:S(2)}, u32[]{:S(2)}) collective-permute-start(bf16[256,2048]{1,0:T(8,128)(2,1)} %second.1), channel_id=1, source_target_pairs={{0,1},{1,0},{2,3},{3,2},{4,5},{5,4},{6,7},{7,6},{8,9},{9,8},{10,11... | collective-permute-start | bytes 3145736 | tf_op jit(solution)/shard_map/ppermute | solution.py:136
  7.4 1.0 slice_bitcast_fusion.9
  8.4 0.0 copy-start.4
  8.4 1.8 %fusion.21 = f32[128,256]{1,0:T(8,128)S(1)} fusion(bf16[256,2048]{1,0:T(8,128)(2,1)} %second.1, bf16[1024,64]{0,1:T(8,128)(2,1)S(1)} %get-tuple-element.25, bf16[1024,64]{0,1:T(8,128)(2,1)S(1)} %get-tuple-element.24), kind=kOutput, calls=%fused_computation.58 | convolution fusion | flops 136314880 | bytes 1441792 | tf_op jit(solution)/shard_map/dot_general | solution.py:139
  10.2 2.6 %collective-permute-start.3 = (f32[256,128]{0,1:T(8,128)S(1)}, f32[256,128]{0,1:T(8,128)S(1)}, u32[]{:S(2)}, u32[]{:S(2)}) collective-permute-start(f32[256,128]{0,1:T(8,128)S(1)} %bitcast.66), channel_id=1, source_target_pairs={{3,1},{0,2},{7,5},{4,6},{11,9},{8,10},{15,13},{12,14},{19,17},{16,... | collective-permute-start | bytes 393224 | tf_op jit(solution)/shard_map/ppermute | solution.py:140
  12.8 4.4 %fusion.25 = f32[1024,128]{1,0:T(8,128)} fusion(bf16[1024,2048]{1,0:T(8,128)(2,1)} %param.6, bf16[2048,128]{1,0:T(8,128)(2,1)} %param.9), kind=kOutput, calls=%fused_computation.61 | convolution fusion | flops 536870912 | bytes 5242880 | tf_op jit(solution)/shard_map/dot_general | solution.py:141
  17.2 0.1 pad_add_fusion.1.place
  17.3 0.1 copy.14
  17.4 0.0 copy-start.1
  17.4 3.4 %copy-done.1 = bf16[2048,2048]{1,0:T(8,128)(2,1)S(1)} copy-done((bf16[2048,2048]{1,0:T(8,128)(2,1)S(1)}, bf16[2048,2048]{1,0:T(8,128)(2,1)}, u32[]{:S(2)}) %copy-start.1) | copy-done | bytes 8388632
  20.8 4.4 %input_grad_rows.5.refs_0_ = bf16[4,256,2048]{2,1,0:T(8,128)(2,1)} custom-call(s32[2]{0:T(128)S(1)} %pad_add_fusion.1.place, bf16[256,2048]{1,0:T(8,128)(2,1)S(1)} %copy-done.4, bf16[256,2048]{1,0:T(8,128)(2,1)S(1)} %copy-done.4, bf16[2048,2048]{1,0:T(8,128)(2,1)S(1)} %copy-done.1), custom_call_target="tpu_custom_call" | custom-call | flops 524288 | bytes 1048576 | tf_op jit(solution)/shard_map/input_grad_rows/pallas_call | solution.py:66
  25.2 7.3 %collective-permute-done.3 = f32[256,128]{0,1:T(8,128)S(1)} collective-permute-done((f32[256,128]{0,1:T(8,128)S(1)}, f32[256,128]{0,1:T(8,128)S(1)}, u32[]{:S(2)}, u32[]{:S(2)}) %collective-permute-start.3) | collective-permute-done | bytes 131104 | tf_op jit(solution)/shard_map/ppermute | solution.py:140
  32.5 0.1 copy.15
  32.6 0.0 collective-permute-done.1.first
  32.6 4.3 %collective-permute-start.2 = (f32[1024,128]{1,0:T(8,128)}, f32[1024,128]{1,0:T(8,128)S(1)}, u32[]{:S(2)}, u32[]{:S(2)}) collective-permute-start(f32[1024,128]{1,0:T(8,128)} %fusion.25), channel_id=1, source_target_pairs={{0,1},{3,2},{4,5},{7,6},{8,9},{11,10},{12,13},{15,14},{16,17},{19,... | collective-permute-start | bytes 1572872 | tf_op jit(solution)/shard_map/ppermute | solution.py:147
  37.0 0.7 collective-permute-start.7
  37.7 1.3 %collective-permute-start.8 = (bf16[256,2048]{1,0:T(8,128)(2,1)}, bf16[256,2048]{1,0:T(8,128)(2,1)}, u32[]{:S(2)}, u32[]{:S(2)}) collective-permute-start(bf16[256,2048]{1,0:T(8,128)(2,1)} %collective-permute-done.1.first), channel_id=1, source_target_pairs={{1,0},{2,3},{5,4},{6,7},{9,8},{10,11},{13,12},{14,15},{17,16},{18,... | collective-permute-start | bytes 3145736 | tf_op jit(solution)/shard_map/ppermute | solution.py:145
  39.0 2.3 %fusion.1 = f32[4,256,128]{2,1,0:T(8,128)} fusion(f32[4,256,128]{2,1,0:T(8,128)} %copy-done.5, s32[]{:T(128)S(6)} %select_n.88, bf16[256,2048]{1,0:T(8,128)(2,1)} %collective-permute-done.first.second, bf16[1024,64]{0,1:T(8,128)(2,1)} %copy-done.7, bf16[1024,64]{0,1:T(8,128)(2,1)} %copy-done.6), kind=kOutput, calls=%fused_computation.3 | convolution fusion | flops 136314880 | bytes 1441796 | tf_op jit(solution)/shard_map/dot_general | solution.py:153
  41.3 2.3 %fusion = f32[4,256,128]{2,1,0:T(8,128)} fusion(f32[4,256,128]{2,1,0:T(8,128)} %fusion.1, s32[]{:T(128)S(6)} %select_n.89, bf16[256,2048]{1,0:T(8,128)(2,1)} %collective-permute-done.1.first, bf16[1024,64]{0,1:T(8,128)(2,1)} %copy-done.7, bf16[1024,64]{0,1:T(8,128)(2,1)} %copy-done.6), kind=kOutput, calls=%fused_computation.1 | convolution fusion | flops 136314880 | bytes 1441796 | tf_op jit(solution)/shard_map/dot_general | solution.py:154
  43.7 0.7 constant_dynamic-update-slice_fusion.4
  44.3 2.6 %collective-permute-done.2 = f32[1024,128]{1,0:T(8,128)S(1)} collective-permute-done((f32[1024,128]{1,0:T(8,128)}, f32[1024,128]{1,0:T(8,128)S(1)}, u32[]{:S(2)}, u32[]{:S(2)}) %collective-permute-start.2) | collective-permute-done | bytes 524320 | tf_op jit(solution)/shard_map/ppermute | solution.py:147
  46.9 1.1 add_bitcast_fusion
  48.0 2.4 %convolution_bitcast_fusion.2 = f32[1,64,64]{1,2,0:T(8,128)S(1)} fusion(f32[1,1024,128]{2,1,0:T(8,128)} %bitcast.61, f32[1,1024,128]{2,1,0:T(8,128)S(1)} %add_bitcast_fusion), kind=kOutput, calls=%fused_computation.4 | convolution fusion | flops 50331648 | bytes 1064960 | tf_op jit(solution)/shard_map/dot_general | solution.py:89
  50.4 2.1 %convolution_bitcast_fusion.3 = f32[1,64,64]{1,2,0:T(8,128)S(1)} fusion(f32[1,1024,128]{2,1,0:T(8,128)} %bitcast.62, f32[1,1024,128]{2,1,0:T(8,128)S(1)} %add_bitcast_fusion), kind=kOutput, calls=%fused_computation.5 | convolution fusion | flops 50331648 | bytes 1064960 | tf_op jit(solution)/shard_map/dot_general | solution.py:89
  52.5 0.1 pad_maximum_fusion
  52.5 0.1 copy.16
  52.7 0.7 collective-permute-start.4
  53.3 1.3 %collective-permute-start.6 = (f32[1,32,64]{2,1,0:T(8,128)S(1)}, f32[1,32,64]{2,1,0:T(8,128)S(1)}, u32[]{:S(2)}, u32[]{:S(2)}) collective-permute-start(f32[1,32,64]{2,1,0:T(8,128)S(1)} %get-tuple-element.27), channel_id=1, source_target_pairs={{1,3},{2,0},{5,7},{6,4},{9,11},{10,8},{13,15},{14,12},{17,19},{18,... | collective-permute-start | bytes 24584 | tf_op jit(solution)/shard_map/ppermute | solution.py:161
  54.6 1.3 %collective-permute-start.5 = (f32[1,32,64]{2,1,0:T(8,128)S(1)}, f32[1,32,64]{2,1,0:T(8,128)S(1)}, u32[]{:S(2)}, u32[]{:S(2)}) collective-permute-start(f32[1,32,64]{2,1,0:T(8,128)S(1)} %get-tuple-element.28), channel_id=1, source_target_pairs={{1,0},{2,3},{5,4},{6,7},{9,8},{10,11},{13,12},{14,15},{17,16},{18,... | collective-permute-start | bytes 24584 | tf_op jit(solution)/shard_map/ppermute | solution.py:160
  55.9 0.1 pad_add_fusion.place
  56.0 3.4 %copy-done.2 = bf16[2048,2048]{1,0:T(8,128)(2,1)S(1)} copy-done((bf16[2048,2048]{1,0:T(8,128)(2,1)S(1)}, bf16[2048,2048]{1,0:T(8,128)(2,1)}, u32[]{:S(2)}) %copy-start.2) | copy-done | bytes 8388632
  59.4 5.5 %input_grad_rows.6.refs_0_ = bf16[4,256,2048]{2,1,0:T(8,128)(2,1)} custom-call(s32[2]{0:T(128)S(1)} %pad_add_fusion.place, bf16[256,2048]{1,0:T(8,128)(2,1)} %collective-permute-done.first.second, bf16[256,2048]{1,0:T(8,128)(2,1)} %collective-permute-done.first.second, bf16[2048,2048]{1,0:T(8,128)(2,1)S(1)} %copy-done.2, ...), custom_call_target="tpu_custom_call", output_to_operand_aliasing={{}: (4, {})} | custom-call | flops 524288 | bytes 1048576 | tf_op jit(solution)/shard_map/input_grad_rows/pallas_call | solution.py:66
  64.9 0.0 collective-permute-done.4
  64.9 0.0 collective-permute-done.5
  65.0 0.0 collective-permute-done.7.first
  65.0 0.1 reshape.65
  65.1 0.0 collective-permute-start.13
  65.1 1.6 %collective-permute-start.12 = (f32[1,2048]{1,0:T(1,128)S(1)}, f32[1,2048]{1,0:T(1,128)S(1)}, u32[]{:S(2)}, u32[]{:S(2)}) collective-permute-start(f32[1,2048]{1,0:T(1,128)S(1)} %reshape.65), channel_id=1, source_target_pairs={{0,8},{4,12},{8,0},{12,4},{1,9},{5,13},{9,1},{13,5},{2,10},{6,14},... | collective-permute-start | bytes 24584 | tf_op jit(solution)/shard_map/ppermute | solution.py:195
  66.6 0.2 collective-permute-start.11
  66.8 1.1 fusion.23
  67.9 1.3 %collective-permute-start.10 = (bf16[128,2048]{1,0:T(8,128)(2,1)}, bf16[128,2048]{1,0:T(8,128)(2,1)}, u32[]{:S(2)}, u32[]{:S(2)}) collective-permute-start(bf16[128,2048]{1,0:T(8,128)(2,1)} %get-tuple-element.22), channel_id=1, source_target_pairs={{1,0},{2,3},{5,4},{6,7},{9,8},{10,11},{13,12},{14,15},{17,16},{18,... | collective-permute-start | bytes 1572872 | tf_op jit(solution)/shard_map/ppermute | solution.py:165
  69.2 0.0 collective-permute-done.12
  69.2 0.5 collective-permute-done.11
  69.7 0.1 reduce-precision_convert_fusion.1
  69.8 0.6 fusion.5
  70.5 1.2 %collective-permute-start.14 = (f32[1,512]{1,0:T(1,128)S(1)}, f32[1,512]{1,0:T(1,128)S(1)}, u32[]{:S(2)}, u32[]{:S(2)}) collective-permute-start(f32[1,512]{1,0:T(1,128)S(1)} %get-tuple-element.36), channel_id=1, source_target_pairs={{0,12},{4,0},{8,4},{12,8},{1,13},{5,1},{9,5},{13,9},{2,14},{6,2},{... | collective-permute-start | bytes 6152 | tf_op jit(solution)/shard_map/ppermute | solution.py:208
  71.7 1.3 %collective-permute-start.9 = (bf16[128,2048]{1,0:T(8,128)(2,1)}, bf16[128,2048]{1,0:T(8,128)(2,1)}, u32[]{:S(2)}, u32[]{:S(2)}) collective-permute-start(bf16[128,2048]{1,0:T(8,128)(2,1)} %get-tuple-element.23), channel_id=1, source_target_pairs={{1,0},{2,3},{5,4},{6,7},{9,8},{10,11},{13,12},{14,15},{17,16},{18,... | collective-permute-start | bytes 1572872 | tf_op jit(solution)/shard_map/ppermute | solution.py:165
  73.0 0.1 collective-permute-start.16
  73.0 0.6 collective-permute-start.15
  73.6 0.0 collective-permute-done.14
  73.6 3.0 %collective-permute-done.15 = f32[1,512]{1,0:T(1,128)S(1)} collective-permute-done((f32[1,512]{1,0:T(1,128)S(1)}, f32[1,512]{1,0:T(1,128)S(1)}, u32[]{:S(2)}, u32[]{:S(2)}) %collective-permute-start.15) | collective-permute-done | bytes 2080 | tf_op jit(solution)/shard_map/ppermute | solution.py:208
  76.7 10.8 %collective-permute-done.10.second = bf16[128,2048]{1,0:T(8,128)(2,1)} collective-permute-done((bf16[128,2048]{1,0:T(8,128)(2,1)}, bf16[128,2048]{1,0:T(8,128)(2,1)}, u32[]{:S(2)}, u32[]{:S(2)}) %collective-permute-start.10) | collective-permute-done | bytes 524320 | tf_op jit(solution)/shard_map/ppermute | solution.py:165
  87.5 1.4 %collective-permute-start.17 = (f32[2,512]{1,0:T(2,128)S(1)}, f32[2,512]{1,0:T(2,128)S(1)}, u32[]{:S(2)}, u32[]{:S(2)}) collective-permute-start(f32[2,512]{1,0:T(2,128)S(1)} %pad_maximum_fusion.2), channel_id=1, source_target_pairs={{0,3},{1,2},{2,1},{3,0},{4,7},{5,6},{6,5},{7,4},{8,11},{9,10},{10,... | collective-permute-start | bytes 12296 | tf_op jit(solution)/shard_map/ppermute | solution.py:220
  88.9 0.1 pad_add_fusion.2.place
  89.0 4.1 %collective-permute-done.17 = f32[2,512]{1,0:T(2,128)S(1)} collective-permute-done((f32[2,512]{1,0:T(2,128)S(1)}, f32[2,512]{1,0:T(2,128)S(1)}, u32[]{:S(2)}, u32[]{:S(2)}) %collective-permute-start.17) | collective-permute-done | bytes 4128 | tf_op jit(solution)/shard_map/ppermute | solution.py:220
  93.1 0.1 pad_add_fusion.3.place
  93.2 3.4 %copy-done.3 = bf16[2048,2048]{1,0:T(8,128)(2,1)S(1)} copy-done((bf16[2048,2048]{1,0:T(8,128)(2,1)S(1)}, bf16[2048,2048]{1,0:T(8,128)(2,1)}, u32[]{:S(2)}) %copy-start.3) | copy-done | bytes 8388632
  96.6 5.5 %input_grad_rows.7.refs_0_ = bf16[4,256,2048]{2,1,0:T(8,128)(2,1)} custom-call(s32[2]{0:T(128)S(1)} %pad_add_fusion.3.place, bf16[256,2048]{1,0:T(8,128)(2,1)} %collective-permute-done.1.first, bf16[256,2048]{1,0:T(8,128)(2,1)} %collective-permute-done.8.second, bf16[2048,2048]{1,0:T(8,128)(2,1)S(1)} %copy-done.3, ...), custom_call_target="tpu_custom_call", output_to_operand_aliasing={{}: (4, {})} | custom-call | flops 524288 | bytes 1048576 | tf_op jit(solution)/shard_map/input_grad_rows/pallas_call | solution.py:66
  102.1 5.6 %input_grad_rows.8.refs_0_ = bf16[4,256,2048]{2,1,0:T(8,128)(2,1)} custom-call(s32[2]{0:T(128)S(1)} %pad_add_fusion.2.place, bf16[256,2048]{1,0:T(8,128)(2,1)S(1)} %collective-permute-done.7.first, bf16[128,2048]{1,0:T(8,128)(2,1)} %collective-permute-done.10.second, bf16[2048,2048]{1,0:T(8,128)(2,1)S(1)} %copy-done.3, ...), custom_call_target="tpu_custom_call", output_to_operand_aliasing={{}: (4, {})} | custom-call | flops 262144 | bytes 524288 | tf_op jit(solution)/shard_map/input_grad_rows/pallas_call | solution.py:66
  107.7 5.6 %input_grad_rows.9 = bf16[4,256,2048]{2,1,0:T(8,128)(2,1)} custom-call(s32[2]{0:T(128)S(1)} %pad_add_fusion.2.place, bf16[256,2048]{1,0:T(8,128)(2,1)S(1)} %collective-permute-done.7.first, bf16[128,2048]{1,0:T(8,128)(2,1)} %collective-permute-done.9.second, bf16[2048,2048]{1,0:T(8,128)(2,1)S(1)} %copy-done.3, ...), custom_call_target="tpu_custom_call", output_to_operand_aliasing={{}: (4, {})} | custom-call | flops 262144 | bytes 524288 | tf_op jit(solution)/shard_map/input_grad_rows/pallas_call | solution.py:66
  113.4 0.0 collective-permute-done.18
  113.4 0.6 fusion.16
  (30 shorter events, 0.2 us)
Async XLA Ops:
  0.6 69.2 %copy-start = (bf16[512,2048]{1,0:T(8,128)(2,1)S(1)}, bf16[512,2048]{1,0:T(8,128)(2,1)}, u32[]{:S(2)}) copy-start(bf16[512,2048]{1,0:T(8,128)(2,1)} %param.11) | copy-start | bytes 6291460
  0.6 32.0 %collective-permute-start.1 = (bf16[256,2048]{1,0:T(8,128)(2,1)}, bf16[256,2048]{1,0:T(8,128)(2,1)}, u32[]{:S(2)}, u32[]{:S(2)}) collective-permute-start(bf16[256,2048]{1,0:T(8,128)(2,1)} %second.1), channel_id=1, source_target_pairs={{1,2},{2,1},{5,6},{6,5},{9,10},{10,9},{13,14},{14,13},{17,18},{18,... | collective-permute-start | bytes 3145736 | tf_op jit(solution)/shard_map/ppermute | solution.py:137
  2.4 30.2 %collective-permute-start = (bf16[256,2048]{1,0:T(8,128)(2,1)}, bf16[256,2048]{1,0:T(8,128)(2,1)}, u32[]{:S(2)}, u32[]{:S(2)}) collective-permute-start(bf16[256,2048]{1,0:T(8,128)(2,1)} %second.1), channel_id=1, source_target_pairs={{0,1},{1,0},{2,3},{3,2},{4,5},{5,4},{6,7},{7,6},{8,9},{9,8},{10,11... | collective-permute-start | bytes 3145736 | tf_op jit(solution)/shard_map/ppermute | solution.py:136
  8.3 1.9 %copy-start.6 = (bf16[1024,64]{0,1:T(8,128)(2,1)}, bf16[1024,64]{0,1:T(8,128)(2,1)S(1)}, u32[]{:S(2)}) copy-start(bf16[1024,64]{0,1:T(8,128)(2,1)S(1)} %get-tuple-element.24) | copy-start | bytes 393220
  8.4 1.9 %copy-start.7 = (bf16[1024,64]{0,1:T(8,128)(2,1)}, bf16[1024,64]{0,1:T(8,128)(2,1)S(1)}, u32[]{:S(2)}) copy-start(bf16[1024,64]{0,1:T(8,128)(2,1)S(1)} %get-tuple-element.25) | copy-start | bytes 393220
  8.4 9.0 %copy-start.4 = (bf16[256,2048]{1,0:T(8,128)(2,1)S(1)}, bf16[256,2048]{1,0:T(8,128)(2,1)}, u32[]{:S(2)}) copy-start(bf16[256,2048]{1,0:T(8,128)(2,1)} %second.1) | copy-start | bytes 3145732
  10.2 22.3 %collective-permute-start.3 = (f32[256,128]{0,1:T(8,128)S(1)}, f32[256,128]{0,1:T(8,128)S(1)}, u32[]{:S(2)}, u32[]{:S(2)}) collective-permute-start(f32[256,128]{0,1:T(8,128)S(1)} %bitcast.66), channel_id=1, source_target_pairs={{3,1},{0,2},{7,5},{4,6},{11,9},{8,10},{15,13},{12,14},{19,17},{16,... | collective-permute-start | bytes 393224 | tf_op jit(solution)/shard_map/ppermute | solution.py:140
  17.4 3.4 %copy-start.1 = (bf16[2048,2048]{1,0:T(8,128)(2,1)S(1)}, bf16[2048,2048]{1,0:T(8,128)(2,1)}, u32[]{:S(2)}) copy-start(bf16[2048,2048]{1,0:T(8,128)(2,1)} %w_tile.9) | copy-start | bytes 25165828
  25.2 7.4 %copy-start.5 = (f32[4,256,128]{2,1,0:T(8,128)}, f32[4,256,128]{2,1,0:T(8,128)S(1)}, u32[]{:S(2)}) copy-start(f32[4,256,128]{2,1,0:T(8,128)S(1)} %constant_dynamic-update-slice_fusion.5) | copy-start | bytes 1572868
  32.6 14.3 %collective-permute-start.2 = (f32[1024,128]{1,0:T(8,128)}, f32[1024,128]{1,0:T(8,128)S(1)}, u32[]{:S(2)}, u32[]{:S(2)}) collective-permute-start(f32[1024,128]{1,0:T(8,128)} %fusion.25), channel_id=1, source_target_pairs={{0,1},{3,2},{4,5},{7,6},{8,9},{11,10},{12,13},{15,14},{16,17},{19,... | collective-permute-start | bytes 1572872 | tf_op jit(solution)/shard_map/ppermute | solution.py:147
  37.0 28.0 %collective-permute-start.7 = (bf16[256,2048]{1,0:T(8,128)(2,1)}, bf16[256,2048]{1,0:T(8,128)(2,1)S(1)}, u32[]{:S(2)}, u32[]{:S(2)}) collective-permute-start(bf16[256,2048]{1,0:T(8,128)(2,1)} %collective-permute-done.first.second), channel_id=1, source_target_pairs={{1,2},{2,1},{5,6},{6,5},{9,10},{10,9},{13,14},{14,13},{17,18},{18,... | collective-permute-start | bytes 3145736 | tf_op jit(solution)/shard_map/ppermute | solution.py:146
  37.7 27.3 %collective-permute-start.8 = (bf16[256,2048]{1,0:T(8,128)(2,1)}, bf16[256,2048]{1,0:T(8,128)(2,1)}, u32[]{:S(2)}, u32[]{:S(2)}) collective-permute-start(bf16[256,2048]{1,0:T(8,128)(2,1)} %collective-permute-done.1.first), channel_id=1, source_target_pairs={{1,0},{2,3},{5,4},{6,7},{9,8},{10,11},{13,12},{14,15},{17,16},{18,... | collective-permute-start | bytes 3145736 | tf_op jit(solution)/shard_map/ppermute | solution.py:145
  52.7 12.3 %collective-permute-start.4 = (f32[1,32,64]{2,1,0:T(8,128)S(1)}, f32[1,32,64]{2,1,0:T(8,128)S(1)}, u32[]{:S(2)}, u32[]{:S(2)}) collective-permute-start(f32[1,32,64]{2,1,0:T(8,128)S(1)} %get-tuple-element.26), channel_id=1, source_target_pairs={{1,2},{2,1},{5,6},{6,5},{9,10},{10,9},{13,14},{14,13},{17,18},{18,... | collective-permute-start | bytes 24584 | tf_op jit(solution)/shard_map/ppermute | solution.py:159
  53.3 11.6 %collective-permute-start.6 = (f32[1,32,64]{2,1,0:T(8,128)S(1)}, f32[1,32,64]{2,1,0:T(8,128)S(1)}, u32[]{:S(2)}, u32[]{:S(2)}) collective-permute-start(f32[1,32,64]{2,1,0:T(8,128)S(1)} %get-tuple-element.27), channel_id=1, source_target_pairs={{1,3},{2,0},{5,7},{6,4},{9,11},{10,8},{13,15},{14,12},{17,19},{18,... | collective-permute-start | bytes 24584 | tf_op jit(solution)/shard_map/ppermute | solution.py:161
  54.6 10.3 %collective-permute-start.5 = (f32[1,32,64]{2,1,0:T(8,128)S(1)}, f32[1,32,64]{2,1,0:T(8,128)S(1)}, u32[]{:S(2)}, u32[]{:S(2)}) collective-permute-start(f32[1,32,64]{2,1,0:T(8,128)S(1)} %get-tuple-element.28), channel_id=1, source_target_pairs={{1,0},{2,3},{5,4},{6,7},{9,8},{10,11},{13,12},{14,15},{17,16},{18,... | collective-permute-start | bytes 24584 | tf_op jit(solution)/shard_map/ppermute | solution.py:160
  56.0 3.4 %copy-start.2 = (bf16[2048,2048]{1,0:T(8,128)(2,1)S(1)}, bf16[2048,2048]{1,0:T(8,128)(2,1)}, u32[]{:S(2)}) copy-start(bf16[2048,2048]{1,0:T(8,128)(2,1)} %w_tile.9) | copy-start | bytes 25165828
  65.1 4.2 %collective-permute-start.13 = (f32[1,2048]{1,0:T(1,128)S(1)}, f32[1,2048]{1,0:T(1,128)S(1)}, u32[]{:S(2)}, u32[]{:S(2)}) collective-permute-start(f32[1,2048]{1,0:T(1,128)S(1)} %reshape.65), channel_id=1, source_target_pairs={{0,12},{4,0},{8,4},{12,8},{1,13},{5,1},{9,5},{13,9},{2,14},{6,2},{... | collective-permute-start | bytes 24584 | tf_op jit(solution)/shard_map/ppermute | solution.py:195
  65.1 4.1 %collective-permute-start.12 = (f32[1,2048]{1,0:T(1,128)S(1)}, f32[1,2048]{1,0:T(1,128)S(1)}, u32[]{:S(2)}, u32[]{:S(2)}) collective-permute-start(f32[1,2048]{1,0:T(1,128)S(1)} %reshape.65), channel_id=1, source_target_pairs={{0,8},{4,12},{8,0},{12,4},{1,9},{5,13},{9,1},{13,5},{2,10},{6,14},... | collective-permute-start | bytes 24584 | tf_op jit(solution)/shard_map/ppermute | solution.py:195
  66.6 3.1 %collective-permute-start.11 = (f32[1,2048]{1,0:T(1,128)S(1)}, f32[1,2048]{1,0:T(1,128)S(1)}, u32[]{:S(2)}, u32[]{:S(2)}) collective-permute-start(f32[1,2048]{1,0:T(1,128)S(1)} %reshape.65), channel_id=1, source_target_pairs={{0,4},{4,8},{8,12},{12,0},{1,5},{5,9},{9,13},{13,1},{2,6},{6,10},{... | collective-permute-start | bytes 24584 | tf_op jit(solution)/shard_map/ppermute | solution.py:195
  67.9 19.6 %collective-permute-start.10 = (bf16[128,2048]{1,0:T(8,128)(2,1)}, bf16[128,2048]{1,0:T(8,128)(2,1)}, u32[]{:S(2)}, u32[]{:S(2)}) collective-permute-start(bf16[128,2048]{1,0:T(8,128)(2,1)} %get-tuple-element.22), channel_id=1, source_target_pairs={{1,0},{2,3},{5,4},{6,7},{9,8},{10,11},{13,12},{14,15},{17,16},{18,... | collective-permute-start | bytes 1572872 | tf_op jit(solution)/shard_map/ppermute | solution.py:165
  70.5 3.1 %collective-permute-start.14 = (f32[1,512]{1,0:T(1,128)S(1)}, f32[1,512]{1,0:T(1,128)S(1)}, u32[]{:S(2)}, u32[]{:S(2)}) collective-permute-start(f32[1,512]{1,0:T(1,128)S(1)} %get-tuple-element.36), channel_id=1, source_target_pairs={{0,12},{4,0},{8,4},{12,8},{1,13},{5,1},{9,5},{13,9},{2,14},{6,2},{... | collective-permute-start | bytes 6152 | tf_op jit(solution)/shard_map/ppermute | solution.py:208
  71.7 36.1 %collective-permute-start.9 = (bf16[128,2048]{1,0:T(8,128)(2,1)}, bf16[128,2048]{1,0:T(8,128)(2,1)}, u32[]{:S(2)}, u32[]{:S(2)}) collective-permute-start(bf16[128,2048]{1,0:T(8,128)(2,1)} %get-tuple-element.23), channel_id=1, source_target_pairs={{1,0},{2,3},{5,4},{6,7},{9,8},{10,11},{13,12},{14,15},{17,16},{18,... | collective-permute-start | bytes 1572872 | tf_op jit(solution)/shard_map/ppermute | solution.py:165
  73.0 3.7 %collective-permute-start.16 = (f32[1,512]{1,0:T(1,128)S(1)}, f32[1,512]{1,0:T(1,128)S(1)}, u32[]{:S(2)}, u32[]{:S(2)}) collective-permute-start(f32[1,512]{1,0:T(1,128)S(1)} %get-tuple-element.34), channel_id=1, source_target_pairs={{0,4},{4,8},{8,12},{12,0},{1,5},{5,9},{9,13},{13,1},{2,6},{6,10},{... | collective-permute-start | bytes 6152 | tf_op jit(solution)/shard_map/ppermute | solution.py:208
  73.0 3.7 %collective-permute-start.15 = (f32[1,512]{1,0:T(1,128)S(1)}, f32[1,512]{1,0:T(1,128)S(1)}, u32[]{:S(2)}, u32[]{:S(2)}) collective-permute-start(f32[1,512]{1,0:T(1,128)S(1)} %get-tuple-element.35), channel_id=1, source_target_pairs={{0,8},{4,12},{8,0},{12,4},{1,9},{5,13},{9,1},{13,5},{2,10},{6,14},... | collective-permute-start | bytes 6152 | tf_op jit(solution)/shard_map/ppermute | solution.py:208
  87.5 5.6 %collective-permute-start.17 = (f32[2,512]{1,0:T(2,128)S(1)}, f32[2,512]{1,0:T(2,128)S(1)}, u32[]{:S(2)}, u32[]{:S(2)}) collective-permute-start(f32[2,512]{1,0:T(2,128)S(1)} %pad_maximum_fusion.2), channel_id=1, source_target_pairs={{0,3},{1,2},{2,1},{3,0},{4,7},{5,6},{6,5},{7,4},{8,11},{9,10},{10,... | collective-permute-start | bytes 12296 | tf_op jit(solution)/shard_map/ppermute | solution.py:220
  93.1 20.3 %collective-permute-start.18 = (f32[1,512]{1,0:T(1,128)S(1)}, f32[1,512]{1,0:T(1,128)S(1)}, u32[]{:S(2)}, u32[]{:S(2)}) collective-permute-start(f32[1,512]{1,0:T(1,128)S(1)} %fusion.17), channel_id=1, source_target_pairs={{0,2},{1,3},{2,0},{3,1},{4,6},{5,7},{6,4},{7,5},{8,10},{9,11},{10,... | collective-permute-start | bytes 6152 | tf_op jit(solution)/shard_map/ppermute | solution.py:223
  93.2 3.4 %copy-start.3 = (bf16[2048,2048]{1,0:T(8,128)(2,1)S(1)}, bf16[2048,2048]{1,0:T(8,128)(2,1)}, u32[]{:S(2)}) copy-start(bf16[2048,2048]{1,0:T(8,128)(2,1)} %w_tile.9) | copy-start | bytes 25165828

commit v4 on v3

--- a/solution.py
+++ b/solution.py
@@ -36,8 +36,47 @@
     ).astype(jnp.bfloat16)
 
 
-def rows_kernel(part, place, first, second, w_tile, *refs):
-    out, held, arrived = refs[-3:]
+TILE = 256
+GRANT = 56 * 2**20
+
+
+def first_rows_kernel(place, rows_in, w_tile, out, turned):
+    turned[...] = w_tile[...].T
+    out[0] = jnp.dot(rows_in[...], turned[...], preferred_element_type=jnp.float32).astype(out.dtype)
+
+
+def first_rows(blocks, rows_in, w_kv, index):
+    rows, depth = rows_in.shape
+    width = w_kv.shape[0]
+    return pl.pallas_call(
+        first_rows_kernel,
+        grid_spec=pltpu.PrefetchScalarGridSpec(
+            num_scalar_prefetch=1,
+            grid=(width // TILE,),
+            in_specs=[
+                pl.BlockSpec((rows, depth), lambda j, place: (0, 0)),
+                pl.BlockSpec((TILE, depth), lambda j, place: (j, 0)),
+            ],
+            out_specs=[
+                pl.BlockSpec((1, rows, TILE), lambda j, place: (place[0], 0, j)),
+                pl.BlockSpec((depth, TILE), lambda j, place: (0, j)),
+            ],
+        ),
+        out_shape=[
+            jax.ShapeDtypeStruct((blocks, rows, width), jnp.bfloat16),
+            jax.ShapeDtypeStruct((depth, width), w_kv.dtype),
+        ],
+        compiler_params=pltpu.CompilerParams(vmem_limit_bytes=GRANT),
+        cost_estimate=pl.CostEstimate(
+            flops=2 * rows * depth * width,
+            bytes_accessed=2 * (rows * depth + 2 * depth * width + rows * width),
+            transcendentals=0,
+        ),
+        name="input_grad_first_rows",
+    )(index.reshape(1).astype(jnp.int32), rows_in, w_kv)
+
+
+def rows_kernel(part, place, first, second, turned, earlier, out, held, arrived):
     rows = held.shape[0]
 
     @pl.when(pl.program_id(0) == 0)
@@ -51,33 +90,69 @@
                 copy.start()
                 copy.wait()
 
-    out[0] = lax.dot_general(
-        held[...], w_tile[...], (((1,), (1,)), ((), ())), preferred_element_type=jnp.float32
-    ).astype(out.dtype)
-
-
-def put_rows(output, blocks, first, second, w_kv, index, use_second=0, part=0):
+    out[0] = jnp.dot(held[...], turned[...], preferred_element_type=jnp.float32).astype(out.dtype)
+
+
+def put_rows(output, first, second, turned, index, use_second=0, part=0):
     rows, depth = second.shape
-    width = w_kv.shape[0]
-    tile = min(width, 512)
+    width = turned.shape[1]
     place = jnp.stack([index, use_second]).astype(jnp.int32)
     anywhere = pl.BlockSpec(memory_space=pl.ANY)
-    earlier = [] if output is None else [output]
     return pl.pallas_call(
         functools.partial(rows_kernel, part),
         grid_spec=pltpu.PrefetchScalarGridSpec(
             num_scalar_prefetch=1,
-            grid=(width // tile,),
-            in_specs=[anywhere, anywhere, pl.BlockSpec((tile, depth), lambda j, place: (j, 0))] + [anywhere] * len(earlier),
-            out_specs=pl.BlockSpec((1, rows, tile), lambda j, place: (place[0], part, j)),
+            grid=(width // TILE,),
+            in_specs=[anywhere, anywhere, pl.BlockSpec((depth, TILE), lambda j, place: (0, j)), anywhere],
+            out_specs=pl.BlockSpec((1, rows, TILE), lambda j, place: (place[0], part, j)),
             scratch_shapes=[pltpu.VMEM((rows, depth), first.dtype), pltpu.SemaphoreType.DMA],
         ),
-        out_shape=jax.ShapeDtypeStruct((blocks, first.shape[0], width), jnp.bfloat16),
-        input_output_aliases={4: 0} if earlier else {},
-        compiler_params=pltpu.CompilerParams(vmem_limit_bytes=16 * 2**20),
-        cost_estimate=pl.CostEstimate(flops=rows * width, bytes_accessed=2 * rows * width, transcendentals=0),
+        out_shape=jax.ShapeDtypeStruct(output.shape, output.dtype),
+        input_output_aliases={4: 0},
+        compiler_params=pltpu.CompilerParams(vmem_limit_bytes=GRANT),
+        cost_estimate=pl.CostEstimate(
+            flops=2 * rows * depth * width,
+            bytes_accessed=2 * (rows * depth + depth * width + rows * width),
+            transcendentals=0,
+        ),
         name="input_grad_rows",
-    )(place, first, second, w_kv, *earlier)
+    )(place, first, second, turned, output)
+
+
+def token_sums_kernel(me, low_in, low_in_beside, own_low, far_low, beside, facing, proj, out):
+    rows = own_low.shape[0]
+    rank = out.shape[2]
+    total = jnp.zeros((proj.shape[1], proj.shape[1]), jnp.float32)
+    for away, low_out in (
+        (0, own_low[...]),
+        (1, jnp.dot(beside[...], proj[...], preferred_element_type=jnp.float32)),
+        (3, jnp.dot(facing[...], proj[...], preferred_element_type=jnp.float32)),
+        (2, far_low[...]),
+    ):
+        here = pl.ds(pl.multiple_of((me[0] ^ away) * rows, rows), rows)
+        total += lax.dot_general(
+            low_in[here, :] + low_in_beside[here, :],
+            low_out,
+            (((0,), (0,)), ((), ())),
+            precision=lax.Precision.HIGHEST,
+            preferred_element_type=jnp.float32,
+        )
+    slab = out.shape[1]
+    for index in range(out.shape[0]):
+        layer = index * slab // rank
+        out[index] = total[index * slab : (index + 1) * slab, layer * rank : (layer + 1) * rank]
+
+
+def token_sums(me, low_in, low_in_beside, own_low, far_low, beside, facing, proj, rank):
+    whole = pl.BlockSpec(memory_space=pltpu.VMEM)
+    return pl.pallas_call(
+        token_sums_kernel,
+        in_specs=[pl.BlockSpec(memory_space=pltpu.SMEM)] + [whole] * 7,
+        out_specs=whole,
+        out_shape=jax.ShapeDtypeStruct((4, 2 * rank // 4, rank), jnp.float32),
+        compiler_params=pltpu.CompilerParams(vmem_limit_bytes=GRANT),
+        name="token_sums",
+    )(me.reshape(1).astype(jnp.int32), low_in, low_in_beside, own_low, far_low, beside, facing, proj)
 
 
 def sequence_sums(low_in, low_out, rank):
@@ -139,22 +214,25 @@
     own_low = jnp.dot(grad_kv, proj_both, preferred_element_type=jnp.float32)
     far_low = lax.ppermute(own_low, "mp", [(3, 1), (0, 2)])
     low_in = jnp.dot(hidden, proj_in, preferred_element_type=jnp.float32)
-    output = put_rows(None, 4, grad_kv, grad_kv, w_kv, me, 0)
+    output, turned = first_rows(4, grad_kv, w_kv, me)
 
     beside, facing, low_in, output = lax.optimization_barrier((beside, facing, low_in, output))
     second = lax.ppermute(facing, "mp", outward)
     beside_across = lax.ppermute(beside, "mp", across)
     low_in_beside = lax.ppermute(low_in, "mp", inward)
-
-    output = put_rows(output, 4, beside, beside, w_kv, me ^ 1, 0)
-
-    low_out = jnp.zeros((4, local_rows, 2 * rank), jnp.float32)
-    low_out = put(low_out, own_low, me)
-    low_out = put(low_out, jnp.dot(beside, proj_both, preferred_element_type=jnp.float32), me ^ 1)
-    low_out = put(low_out, jnp.dot(facing, proj_both, preferred_element_type=jnp.float32), me ^ 3)
-    low_out = put(low_out, far_low, me ^ 2)
-    sums = sequence_sums(low_in + low_in_beside, low_out.reshape(4 * local_rows, 2 * rank), rank)
-    slabs = slabs_of(sums, 4)
+    output = put_rows(output, beside, beside, turned, me ^ 1)
+
+    low_in_beside, far_low = lax.optimization_barrier((low_in_beside, far_low))
+    if low_in.shape[0] == SEQ:
+        slabs = token_sums(me, low_in, low_in_beside, own_low, far_low, beside, facing, proj_both, rank)[:, None]
+    else:
+        low_out = jnp.zeros((4, local_rows, 2 * rank), jnp.float32)
+        low_out = put(low_out, own_low, me)
+        low_out = put(low_out, jnp.dot(beside, proj_both, preferred_element_type=jnp.float32), me ^ 1)
+        low_out = put(low_out, jnp.dot(facing, proj_both, preferred_element_type=jnp.float32), me ^ 3)
+        low_out = put(low_out, far_low, me ^ 2)
+        sums = sequence_sums(low_in + low_in_beside, low_out.reshape(4 * local_rows, 2 * rank), rank)
+        slabs = slabs_of(sums, 4)
     mine = jnp.where(middle, take(slabs, me), 0.0)
     mine = mine + lax.ppermute(take(slabs, me ^ 3), "mp", [(1, 2), (2, 1)])
     mine = mine + lax.ppermute(take(slabs, me ^ 1), "mp", outward)
@@ -165,18 +243,15 @@
     third = [lax.ppermute(beside_across[part * half : (part + 1) * half], "mp", outward) for part in range(2)]
     mine, beside_across = lax.optimization_barrier((mine, beside_across))
     ends = jnp.logical_not(middle).astype(jnp.int32)
-    output = put_rows(output, 4, facing, second, w_kv, jnp.where(middle, me ^ 3, me ^ 2), ends)
+    output = put_rows(output, facing, second, turned, jnp.where(middle, me ^ 3, me ^ 2), ends)
     last = jnp.where(middle, me ^ 2, me ^ 3)
-    output = put_rows(output, 4, beside_across, third[0], w_kv, last, ends, 0)
 
     def finish(total):
-        total, arrived = lax.optimization_barrier((total, third[0]))
-        return total
+        return lax.optimization_barrier((total, third[0], output))[0]
 
     def rest():
-        return put_rows(output, 4, beside_across, third[1], w_kv, last, ends, 1).reshape(
-            4 * local_rows, w_kv.shape[0]
-        )
+        upper = put_rows(output, beside_across, third[0], turned, last, ends, 0)
+        return put_rows(upper, beside_across, third[1], turned, last, ends, 1).reshape(4 * local_rows, w_kv.shape[0])
 
     return mine, finish, rest
 

time: 115 us -> 114 us (level)
  Pallas kernels: 26.7 us -> 54.8 us
  waiting for transfers between devices: 28.3 us -> 7.67 us
  matrix products: 15.9 us -> 4.4 us
  local copies, waits for them, and re-layouts: 13.4 us -> 6.4 us
  starting transfers between devices: 26.4 us -> 32.9 us
  other arithmetic: 2.19 us -> 5.14 us
    pallas_call x0 -> x2, Pallas kernels: none -> 15.1 us  [the longest x1 11.2 us: first_rows(): pl.pallas_call(first_rows_kernel, grid_spec=pltpu.PrefetchScalarGridSpec(...]
    pallas_call x5 -> x4, Pallas kernels: 26.7 us -> 39.6 us  [put_rows(): pl.pallas_call(functools.partial(rows_kernel, part), grid_spec=pltpu.Pref...]
    ppermute x2, waiting for transfers between devices: 10.8 us -> 0.01 us  [line_of_four(): lax.ppermute(beside_across[part * half:(part + 1) * half], 'mp', outward)]
    dot_general x4 -> x0, matrix products: 9.09 us -> none  [the longest x2 4.42 us: sequence_sums(): lax.dot_general(left[:, :, layer * rank:(layer + 1) * rank], right[:, :,...]
    ppermute x1, waiting for transfers between devices: 7.31 us -> 0.01 us  [line_of_four(): far_low = lax.ppermute(own_low, 'mp', [(3, 1), (0, 2)])]
    unnamed x16 -> x18, local copies, waits for them, and re-layouts: 10.2 us -> 3.77 us
    ppermute x1, starting transfers between devices: 0.01 us -> 4.48 us  [on_device(): lax.ppermute(kept, 'mp', [(source, source ^ 2) for source in range(n)])]
    ppermute x1, waiting for transfers between devices: 4.09 us -> 0.01 us  [on_device(): lax.ppermute(jnp.concatenate([columns_of(me ^ 3), columns_of(me ^ 1)], ax...]
  transfers between devices with their start and end apart: 19 -> 19, of which waited for: 6 -> 4; matrix products, arithmetic and copies ran while one was open for 18% -> 12% of each run, Pallas kernels for 23% -> 49%
where the time goes in v4:
time: 114 us; the launch traced here: 112 us
  Pallas kernels  54.8 us (48%)
  starting transfers between devices  32.9 us (29%)
  waiting for transfers between devices  7.67 us (7%)
  local copies, waits for them, and re-layouts  6.4 us (6%)
  other arithmetic  5.14 us (5%)
  matrix products  4.4 us (4%)
    pallas_call x4, Pallas kernels, put_rows(): pl.pallas_call(functools.partial(rows_kernel, part), grid_spec=pltpu.Pref...  39.6 us
    pallas_call x1, Pallas kernels, first_rows(): pl.pallas_call(first_rows_kernel, grid_spec=pltpu.PrefetchScalarGridSpec(...  11.2 us
    ppermute x1, starting transfers between devices, line_of_four(): low_in_beside = lax.ppermute(low_in, 'mp', inward)  5.11 us
    ppermute x1, starting transfers between devices, line_of_four(): beside = lax.ppermute(grad_kv, 'mp', exchange_pairs)  4.89 us
    ppermute x1, starting transfers between devices, on_device(): lax.ppermute(kept, 'mp', [(source, source ^ 2) for source in range(n)])  4.48 us
    pallas_call x1, Pallas kernels, token_sums(): pl.pallas_call(token_sums_kernel, in_specs=[pl.BlockSpec(memory_space=plt...  3.9 us
    unnamed x18, local copies, waits for them, and re-layouts  3.77 us
    ppermute x1, starting transfers between devices, line_of_four(): far_low = lax.ppermute(own_low, 'mp', [(3, 1), (0, 2)])  3.28 us
  transfers between devices with their start and end apart: 19, of which 4 were waited for; matrix products, arithmetic and copies ran while one was open for 12% of the time, Pallas kernels for 49%

profile of v4, /device:TPU:0, one launch (start us, length us, event | category | flops | bytes accessed | tf_op | source)
XLA Modules:
  0.0 112.2 jit_solution(16390440277209701222)
XLA Ops:
  0.6 0.0 copy-start
  0.6 1.8 %collective-permute-start.1 = (bf16[256,2048]{1,0:T(8,128)(2,1)}, bf16[256,2048]{1,0:T(8,128)(2,1)}, u32[]{:S(2)}, u32[]{:S(2)}) collective-permute-start(bf16[256,2048]{1,0:T(8,128)(2,1)} %rows_in.1), channel_id=1, source_target_pairs={{1,2},{2,1},{5,6},{6,5},{9,10},{10,9},{13,14},{14,13},{17,18},{18,... | collective-permute-start | bytes 3145736 | tf_op jit(solution)/shard_map/ppermute | solution.py:212
  2.5 4.9 %collective-permute-start = (bf16[256,2048]{1,0:T(8,128)(2,1)}, bf16[256,2048]{1,0:T(8,128)(2,1)S(1)}, u32[]{:S(2)}, u32[]{:S(2)}) collective-permute-start(bf16[256,2048]{1,0:T(8,128)(2,1)} %rows_in.1), channel_id=1, source_target_pairs={{0,1},{1,0},{2,3},{3,2},{4,5},{5,4},{6,7},{7,6},{8,9},{9,8},{10,11... | collective-permute-start | bytes 3145736 | tf_op jit(solution)/shard_map/ppermute | solution.py:211
  7.4 1.6 %fusion.17 = (bf16[1,1024,64]{1,2,0:T(8,128)(2,1)}, bf16[1,1024,64]{1,2,0:T(8,128)(2,1)S(1)}) fusion(bf16[2,1024,64]{1,2,0:T(8,128)(2,1)} %param.10), kind=kLoop, calls=%fused_computation.41 | loop fusion | bytes 524288 | tf_op jit(solution)/shard_map/slice | solution.py:26
  9.0 1.1 copy.16
  10.1 0.8 copy.17
  10.9 1.7 %convolution_bitcast_fusion.own_low = f32[256,128]{1,0:T(8,128)S(1)} fusion(bf16[256,2048]{1,0:T(8,128)(2,1)} %rows_in.1, bf16[1024,64]{1,0:T(8,128)(2,1)} %bitcast.17, bf16[1024,64]{1,0:T(8,128)(2,1)S(1)} %bitcast.15), kind=kOutput, calls=%fused_computation | convolution fusion | flops 136314880 | bytes 1441792 | tf_op jit(solution)/shard_map/dot_general | solution.py:214
  12.6 3.3 %collective-permute-start.3 = (f32[256,128]{1,0:T(8,128)S(1)}, f32[256,128]{1,0:T(8,128)}, u32[]{:S(2)}, u32[]{:S(2)}) collective-permute-start(f32[256,128]{1,0:T(8,128)S(1)} %convolution_bitcast_fusion.own_low), channel_id=1, source_target_pairs={{3,1},{0,2},{7,5},{4,6},{11,9},{8,10},{15,13},{12,14},{19,17},{16,... | collective-permute-start | bytes 393224 | tf_op jit(solution)/shard_map/ppermute | solution.py:215
  15.9 11.2 %input_grad_first_rows.1 = (bf16[4,256,2048]{2,1,0:T(8,128)(2,1)}, bf16[2048,2048]{1,0:T(8,128)(2,1)}) custom-call(s32[1]{0:T(128)} %bitcast.2.place.me, bf16[256,2048]{1,0:T(8,128)(2,1)} %rows_in.1, bf16[2048,2048]{1,0:T(8,128)(2,1)} %w_tile.1), custom_call_target="tpu_custom_call" | custom-call | flops 2147483648 | bytes 18874368 | tf_op jit(solution)/shard_map/input_grad_first_rows/pallas_call | solution.py:51
  27.2 0.0 copy-done.3
  27.2 2.1 %fusion.19.low_in = f32[1024,128]{1,0:T(8,128)} fusion(bf16[1024,2048]{1,0:T(8,128)(2,1)S(1)} %copy-done.3, bf16[2048,128]{1,0:T(8,128)(2,1)S(1)} %copy-done.4), kind=kOutput, calls=%fused_computation.43 | convolution fusion | flops 536870912 | bytes 5242880 | tf_op jit(solution)/shard_map/dot_general | solution.py:216
  29.2 0.0 collective-permute-done.1.facing.first
  29.2 2.0 %collective-permute-done.beside.first.second = bf16[256,2048]{1,0:T(8,128)(2,1)S(1)} collective-permute-done((bf16[256,2048]{1,0:T(8,128)(2,1)}, bf16[256,2048]{1,0:T(8,128)(2,1)S(1)}, u32[]{:S(2)}, u32[]{:S(2)}) %collective-permute-start) | collective-permute-done | bytes 1048608 | tf_op jit(solution)/shard_map/ppermute | solution.py:211
  31.2 1.0 copy-done.2
  32.2 5.1 %collective-permute-start.2 = (f32[1024,128]{1,0:T(8,128)}, f32[1024,128]{1,0:T(8,128)}, u32[]{:S(2)}, u32[]{:S(2)}) collective-permute-start(f32[1024,128]{1,0:T(8,128)} %fusion.19.low_in), channel_id=1, source_target_pairs={{0,1},{3,2},{4,5},{7,6},{8,9},{11,10},{12,13},{15,14},{16,17},{19,... | collective-permute-start | bytes 1572872 | tf_op jit(solution)/shard_map/ppermute | solution.py:222
  37.3 0.7 collective-permute-start.7
  38.0 1.3 %collective-permute-start.8 = (bf16[256,2048]{1,0:T(8,128)(2,1)}, bf16[256,2048]{1,0:T(8,128)(2,1)}, u32[]{:S(2)}, u32[]{:S(2)}) collective-permute-start(bf16[256,2048]{1,0:T(8,128)(2,1)} %collective-permute-done.1.facing.first), channel_id=1, source_target_pairs={{1,0},{2,3},{5,4},{6,7},{9,8},{10,11},{13,12},{14,15},{17,16},{18,... | collective-permute-start | bytes 3145736 | tf_op jit(solution)/shard_map/ppermute | solution.py:220
  39.3 0.6 pad_add_fusion.place
  39.9 1.9 %fusion.2.proj = bf16[2048,128]{1,0:T(8,128)(2,1)} fusion(bf16[1024,64]{1,0:T(8,128)(2,1)} %bitcast.18, bf16[1024,64]{1,0:T(8,128)(2,1)S(1)} %bitcast.16), kind=kLoop, calls=%fused_computation.5 | loop fusion | flops 2097152 | bytes 786432 | tf_op jit(solution)/shard_map/concatenate | solution.py:24
  41.8 0.7 pad_add_fusion.2.place
  42.5 0.6 pad_add_fusion.1.place
  43.1 0.0 collective-permute-done.3.far_low
  43.1 2.4 %collective-permute-done.2.low_in_beside = f32[1024,128]{1,0:T(8,128)} collective-permute-done((f32[1024,128]{1,0:T(8,128)}, f32[1024,128]{1,0:T(8,128)}, u32[]{:S(2)}, u32[]{:S(2)}) %collective-permute-start.2) | collective-permute-done | bytes 524320 | tf_op jit(solution)/shard_map/ppermute | solution.py:222
  45.5 3.9 %token_sums.1 = f32[4,32,64]{2,1,0:T(8,128)} custom-call(s32[1]{0:T(128)} %bitcast.2.place.me, f32[1024,128]{1,0:T(8,128)} %fusion.19.low_in, f32[1024,128]{1,0:T(8,128)} %collective-permute-done.2.low_in_beside, f32[256,128]{1,0:T(8,128)} %copy-done.7, f32[256,128]{1,0:T(8,128)} %collective-permute-done.3.far_low, bf16[256,2048]{1,0:T(8,128)(2,1)} %copy-done.2, ...), custom_call_target="tpu_custom_call" | custom-call | tf_op jit(solution)/shard_map/token_sums/pallas_call | solution.py:148
  49.4 0.8 constant_dynamic-slice_fusion.6
  50.1 0.7 collective-permute-start.4
  50.8 1.3 %collective-permute-start.6 = (f32[1,32,64]{2,1,0:T(8,128)S(1)}, f32[1,32,64]{2,1,0:T(8,128)S(1)}, u32[]{:S(2)}, u32[]{:S(2)}) collective-permute-start(f32[1,32,64]{2,1,0:T(8,128)S(1)} %get-tuple-element.35), channel_id=1, source_target_pairs={{1,3},{2,0},{5,7},{6,4},{9,11},{10,8},{13,15},{14,12},{17,19},{18,... | collective-permute-start | bytes 24584 | tf_op jit(solution)/shard_map/ppermute | solution.py:239
  52.1 1.3 %collective-permute-start.5 = (f32[1,32,64]{2,1,0:T(8,128)S(1)}, f32[1,32,64]{2,1,0:T(8,128)S(1)}, u32[]{:S(2)}, u32[]{:S(2)}) collective-permute-start(f32[1,32,64]{2,1,0:T(8,128)S(1)} %get-tuple-element.36), channel_id=1, source_target_pairs={{1,0},{2,3},{5,4},{6,7},{9,8},{10,11},{13,12},{14,15},{17,16},{18,... | collective-permute-start | bytes 24584 | tf_op jit(solution)/shard_map/ppermute | solution.py:238
  53.4 10.3 %input_grad_rows.4.earlier = bf16[4,256,2048]{2,1,0:T(8,128)(2,1)} custom-call(s32[2]{0:T(128)} %pad_add_fusion.1.place, bf16[256,2048]{1,0:T(8,128)(2,1)} %copy-done.2, bf16[256,2048]{1,0:T(8,128)(2,1)} %copy-done.2, bf16[2048,2048]{1,0:T(8,128)(2,1)} %get-tuple-element.22.turned, ...), custom_call_target="tpu_custom_call", output_to_operand_aliasing={{}: (4, {})} | custom-call | flops 2147483648 | bytes 10485760 | tf_op jit(solution)/shard_map/input_grad_rows/pallas_call | solution.py:101
  63.7 0.0 collective-permute-done.4
  63.7 0.0 collective-permute-done.6
  63.7 0.0 collective-permute-done.5
  63.7 0.7 add_add_fusion
  64.5 0.0 collective-permute-done.7.first
  64.5 0.0 collective-permute-done.8.second
  64.5 0.1 reshape.43
  64.6 0.0 collective-permute-start.13
  64.6 1.6 %collective-permute-start.12 = (f32[1,2048]{1,0:T(1,128)S(1)}, f32[1,2048]{1,0:T(1,128)S(1)}, u32[]{:S(2)}, u32[]{:S(2)}) collective-permute-start(f32[1,2048]{1,0:T(1,128)S(1)} %reshape.43), channel_id=1, source_target_pairs={{0,8},{4,12},{8,0},{12,4},{1,9},{5,13},{9,1},{13,5},{2,10},{6,14},... | collective-permute-start | bytes 24584 | tf_op jit(solution)/shard_map/ppermute | solution.py:270
  66.1 0.2 collective-permute-start.11
  66.3 0.1 fusion.16
  66.4 1.3 %collective-permute-start.10 = (bf16[128,2048]{1,0:T(8,128)(2,1)S(1)}, bf16[128,2048]{1,0:T(8,128)(2,1)S(1)}, u32[]{:S(2)}, u32[]{:S(2)}) collective-permute-start(bf16[128,2048]{1,0:T(8,128)(2,1)S(1)} %get-tuple-element.30), channel_id=1, source_target_pairs={{1,0},{2,3},{5,4},{6,7},{9,8},{10,11},{13,12},{14,15},{17,16},{18,... | collective-permute-start | bytes 1572872 | tf_op jit(solution)/shard_map/ppermute | solution.py:243
  67.7 1.3 %collective-permute-start.9 = (bf16[128,2048]{1,0:T(8,128)(2,1)S(1)}, bf16[128,2048]{1,0:T(8,128)(2,1)S(1)}, u32[]{:S(2)}, u32[]{:S(2)}) collective-permute-start(bf16[128,2048]{1,0:T(8,128)(2,1)S(1)} %get-tuple-element.31), channel_id=1, source_target_pairs={{1,0},{2,3},{5,4},{6,7},{9,8},{10,11},{13,12},{14,15},{17,16},{18,... | collective-permute-start | bytes 1572872 | tf_op jit(solution)/shard_map/ppermute | solution.py:243
  69.0 0.0 collective-permute-done.13
  69.0 0.0 collective-permute-done.12
  69.0 0.2 collective-permute-done.11
  69.2 0.1 reduce-precision_convert_fusion.1
  69.3 0.6 fusion.3
  70.0 1.5 %collective-permute-start.14 = (f32[1,512]{1,0:T(1,128)S(1)}, f32[1,512]{1,0:T(1,128)S(1)}, u32[]{:S(2)}, u32[]{:S(2)}) collective-permute-start(f32[1,512]{1,0:T(1,128)S(1)} %get-tuple-element.44), channel_id=1, source_target_pairs={{0,12},{4,0},{8,4},{12,8},{1,13},{5,1},{9,5},{13,9},{2,14},{6,2},{... | collective-permute-start | bytes 6152 | tf_op jit(solution)/shard_map/ppermute | solution.py:283
  71.5 10.3 %input_grad_rows.5.earlier = bf16[4,256,2048]{2,1,0:T(8,128)(2,1)} custom-call(s32[2]{0:T(128)} %pad_add_fusion.2.place, bf16[256,2048]{1,0:T(8,128)(2,1)} %collective-permute-done.1.facing.first, bf16[256,2048]{1,0:T(8,128)(2,1)} %collective-permute-done.8.second, bf16[2048,2048]{1,0:T(8,128)(2,1)} %get-tuple-element.22.turned, ...), custom_call_target="tpu_custom_call", output_to_operand_aliasing={{}: (4, {})} | custom-call | flops 2147483648 | bytes 10485760 | tf_op jit(solution)/shard_map/input_grad_rows/pallas_call | solution.py:101
  81.8 0.1 collective-permute-start.16
  81.8 0.6 collective-permute-start.15
  82.4 0.0 collective-permute-done.14
  82.5 3.0 %collective-permute-done.15 = f32[1,512]{1,0:T(1,128)S(1)} collective-permute-done((f32[1,512]{1,0:T(1,128)S(1)}, f32[1,512]{1,0:T(1,128)S(1)}, u32[]{:S(2)}, u32[]{:S(2)}) %collective-permute-start.15) | collective-permute-done | bytes 2080 | tf_op jit(solution)/shard_map/ppermute | solution.py:283
  85.5 0.0 collective-permute-done.16
  85.5 0.0 collective-permute-done.10.second
  85.6 1.6 %collective-permute-start.17 = (f32[2,512]{1,0:T(2,128)S(1)}, f32[2,512]{1,0:T(2,128)S(1)}, u32[]{:S(2)}, u32[]{:S(2)}) collective-permute-start(f32[2,512]{1,0:T(2,128)S(1)} %pad_maximum_fusion.1), channel_id=1, source_target_pairs={{0,3},{1,2},{2,1},{3,0},{4,7},{5,6},{6,5},{7,4},{8,11},{9,10},{10,... | collective-permute-start | bytes 12296 | tf_op jit(solution)/shard_map/ppermute | solution.py:295
  87.2 9.5 %input_grad_rows.6.earlier = bf16[4,256,2048]{2,1,0:T(8,128)(2,1)} custom-call(s32[2]{0:T(128)} %pad_add_fusion.place, bf16[256,2048]{1,0:T(8,128)(2,1)} %copy-done.1, bf16[128,2048]{1,0:T(8,128)(2,1)} %copy-done.6, bf16[2048,2048]{1,0:T(8,128)(2,1)} %get-tuple-element.22.turned, ...), custom_call_target="tpu_custom_call", output_to_operand_aliasing={{}: (4, {})} | custom-call | flops 1073741824 | bytes 9437184 | tf_op jit(solution)/shard_map/input_grad_rows/pallas_call | solution.py:101
  96.7 0.0 collective-permute-done.17
  96.7 4.5 %collective-permute-start.18 = (f32[1,512]{1,0:T(1,128)S(1)}, f32[1,512]{1,0:T(1,128)S(1)}, u32[]{:S(2)}, u32[]{:S(2)}) collective-permute-start(f32[1,512]{1,0:T(1,128)S(1)} %fusion.13), channel_id=1, source_target_pairs={{0,2},{1,3},{2,0},{3,1},{4,6},{5,7},{6,4},{7,5},{8,10},{9,11},{10,... | collective-permute-start | bytes 6152 | tf_op jit(solution)/shard_map/ppermute | solution.py:298
  101.2 0.0 collective-permute-done.9.second
  101.2 0.8 copy-done.5
  102.1 9.5 %input_grad_rows.7 = bf16[4,256,2048]{2,1,0:T(8,128)(2,1)} custom-call(s32[2]{0:T(128)} %pad_add_fusion.place, bf16[256,2048]{1,0:T(8,128)(2,1)} %copy-done.1, bf16[128,2048]{1,0:T(8,128)(2,1)} %copy-done.5, bf16[2048,2048]{1,0:T(8,128)(2,1)} %get-tuple-element.22.turned, bf16[4,256,2048]{2,1,0:T(8,128)(2,1)} %input_grad_rows.6.earlier), custom_call_target="tpu_custom_call", output_to_operand_aliasing={{}: (4, {})} | custom-call | flops 1073741824 | bytes 9437184 | tf_op jit(solution)/shard_map/input_grad_rows/pallas_call | solution.py:101
  111.6 0.0 collective-permute-done.18
  111.6 0.6 fusion.12
  (21 shorter events, 0.1 us)
Async XLA Ops:
  0.6 68.6 %copy-start = (bf16[512,2048]{1,0:T(8,128)(2,1)S(1)}, bf16[512,2048]{1,0:T(8,128)(2,1)}, u32[]{:S(2)}) copy-start(bf16[512,2048]{1,0:T(8,128)(2,1)} %param.11) | copy-start | bytes 6291460
  0.6 28.6 %collective-permute-start.1 = (bf16[256,2048]{1,0:T(8,128)(2,1)}, bf16[256,2048]{1,0:T(8,128)(2,1)}, u32[]{:S(2)}, u32[]{:S(2)}) collective-permute-start(bf16[256,2048]{1,0:T(8,128)(2,1)} %rows_in.1), channel_id=1, source_target_pairs={{1,2},{2,1},{5,6},{6,5},{9,10},{10,9},{13,14},{14,13},{17,18},{18,... | collective-permute-start | bytes 3145736 | tf_op jit(solution)/shard_map/ppermute | solution.py:212
  2.5 28.7 %collective-permute-start = (bf16[256,2048]{1,0:T(8,128)(2,1)}, bf16[256,2048]{1,0:T(8,128)(2,1)S(1)}, u32[]{:S(2)}, u32[]{:S(2)}) collective-permute-start(bf16[256,2048]{1,0:T(8,128)(2,1)} %rows_in.1), channel_id=1, source_target_pairs={{0,1},{1,0},{2,3},{3,2},{4,5},{5,4},{6,7},{7,6},{8,9},{9,8},{10,11... | collective-permute-start | bytes 3145736 | tf_op jit(solution)/shard_map/ppermute | solution.py:211
  12.6 14.5 %copy-start.7 = (f32[256,128]{1,0:T(8,128)}, f32[256,128]{1,0:T(8,128)S(1)}, u32[]{:S(2)}) copy-start(f32[256,128]{1,0:T(8,128)S(1)} %convolution_bitcast_fusion.own_low) | copy-start | bytes 393220
  12.6 30.4 %collective-permute-start.3 = (f32[256,128]{1,0:T(8,128)S(1)}, f32[256,128]{1,0:T(8,128)}, u32[]{:S(2)}, u32[]{:S(2)}) collective-permute-start(f32[256,128]{1,0:T(8,128)S(1)} %convolution_bitcast_fusion.own_low), channel_id=1, source_target_pairs={{3,1},{0,2},{7,5},{4,6},{11,9},{8,10},{15,13},{12,14},{19,17},{16,... | collective-permute-start | bytes 393224 | tf_op jit(solution)/shard_map/ppermute | solution.py:215
  15.9 11.2 %copy-start.3 = (bf16[1024,2048]{1,0:T(8,128)(2,1)S(1)}, bf16[1024,2048]{1,0:T(8,128)(2,1)}, u32[]{:S(2)}) copy-start(bf16[1024,2048]{1,0:T(8,128)(2,1)} %param.6) | copy-start | bytes 12582916
  15.9 11.2 %copy-start.4 = (bf16[2048,128]{1,0:T(8,128)(2,1)S(1)}, bf16[2048,128]{1,0:T(8,128)(2,1)}, u32[]{:S(2)}) copy-start(bf16[2048,128]{1,0:T(8,128)(2,1)} %param.9) | copy-start | bytes 1572868
  31.2 1.0 copy-start.2
  32.2 13.3 %collective-permute-start.2 = (f32[1024,128]{1,0:T(8,128)}, f32[1024,128]{1,0:T(8,128)}, u32[]{:S(2)}, u32[]{:S(2)}) collective-permute-start(f32[1024,128]{1,0:T(8,128)} %fusion.19.low_in), channel_id=1, source_target_pairs={{0,1},{3,2},{4,5},{7,6},{8,9},{11,10},{12,13},{15,14},{16,17},{19,... | collective-permute-start | bytes 1572872 | tf_op jit(solution)/shard_map/ppermute | solution.py:222
  37.3 27.2 %collective-permute-start.7 = (bf16[256,2048]{1,0:T(8,128)(2,1)}, bf16[256,2048]{1,0:T(8,128)(2,1)S(1)}, u32[]{:S(2)}, u32[]{:S(2)}) collective-permute-start(bf16[256,2048]{1,0:T(8,128)(2,1)} %copy-done.2), channel_id=1, source_target_pairs={{1,2},{2,1},{5,6},{6,5},{9,10},{10,9},{13,14},{14,13},{17,18},{18,... | collective-permute-start | bytes 3145736 | tf_op jit(solution)/shard_map/ppermute | solution.py:221
  38.0 26.5 %collective-permute-start.8 = (bf16[256,2048]{1,0:T(8,128)(2,1)}, bf16[256,2048]{1,0:T(8,128)(2,1)}, u32[]{:S(2)}, u32[]{:S(2)}) collective-permute-start(bf16[256,2048]{1,0:T(8,128)(2,1)} %collective-permute-done.1.facing.first), channel_id=1, source_target_pairs={{1,0},{2,3},{5,4},{6,7},{9,8},{10,11},{13,12},{14,15},{17,16},{18,... | collective-permute-start | bytes 3145736 | tf_op jit(solution)/shard_map/ppermute | solution.py:220
  50.1 13.6 %collective-permute-start.4 = (f32[1,32,64]{2,1,0:T(8,128)S(1)}, f32[1,32,64]{2,1,0:T(8,128)S(1)}, u32[]{:S(2)}, u32[]{:S(2)}) collective-permute-start(f32[1,32,64]{2,1,0:T(8,128)S(1)} %get-tuple-element.34), channel_id=1, source_target_pairs={{1,2},{2,1},{5,6},{6,5},{9,10},{10,9},{13,14},{14,13},{17,18},{18,... | collective-permute-start | bytes 24584 | tf_op jit(solution)/shard_map/ppermute | solution.py:237
  50.8 12.9 %collective-permute-start.6 = (f32[1,32,64]{2,1,0:T(8,128)S(1)}, f32[1,32,64]{2,1,0:T(8,128)S(1)}, u32[]{:S(2)}, u32[]{:S(2)}) collective-permute-start(f32[1,32,64]{2,1,0:T(8,128)S(1)} %get-tuple-element.35), channel_id=1, source_target_pairs={{1,3},{2,0},{5,7},{6,4},{9,11},{10,8},{13,15},{14,12},{17,19},{18,... | collective-permute-start | bytes 24584 | tf_op jit(solution)/shard_map/ppermute | solution.py:239
  52.1 11.6 %collective-permute-start.5 = (f32[1,32,64]{2,1,0:T(8,128)S(1)}, f32[1,32,64]{2,1,0:T(8,128)S(1)}, u32[]{:S(2)}, u32[]{:S(2)}) collective-permute-start(f32[1,32,64]{2,1,0:T(8,128)S(1)} %get-tuple-element.36), channel_id=1, source_target_pairs={{1,0},{2,3},{5,4},{6,7},{9,8},{10,11},{13,12},{14,15},{17,16},{18,... | collective-permute-start | bytes 24584 | tf_op jit(solution)/shard_map/ppermute | solution.py:238
  64.5 17.3 %copy-start.1 = (bf16[256,2048]{1,0:T(8,128)(2,1)}, bf16[256,2048]{1,0:T(8,128)(2,1)S(1)}, u32[]{:S(2)}) copy-start(bf16[256,2048]{1,0:T(8,128)(2,1)S(1)} %collective-permute-done.7.first) | copy-start | bytes 3145732
  64.6 4.4 %collective-permute-start.13 = (f32[1,2048]{1,0:T(1,128)S(1)}, f32[1,2048]{1,0:T(1,128)S(1)}, u32[]{:S(2)}, u32[]{:S(2)}) collective-permute-start(f32[1,2048]{1,0:T(1,128)S(1)} %reshape.43), channel_id=1, source_target_pairs={{0,12},{4,0},{8,4},{12,8},{1,13},{5,1},{9,5},{13,9},{2,14},{6,2},{... | collective-permute-start | bytes 24584 | tf_op jit(solution)/shard_map/ppermute | solution.py:270
  64.6 4.4 %collective-permute-start.12 = (f32[1,2048]{1,0:T(1,128)S(1)}, f32[1,2048]{1,0:T(1,128)S(1)}, u32[]{:S(2)}, u32[]{:S(2)}) collective-permute-start(f32[1,2048]{1,0:T(1,128)S(1)} %reshape.43), channel_id=1, source_target_pairs={{0,8},{4,12},{8,0},{12,4},{1,9},{5,13},{9,1},{13,5},{2,10},{6,14},... | collective-permute-start | bytes 24584 | tf_op jit(solution)/shard_map/ppermute | solution.py:270
  66.1 3.1 %collective-permute-start.11 = (f32[1,2048]{1,0:T(1,128)S(1)}, f32[1,2048]{1,0:T(1,128)S(1)}, u32[]{:S(2)}, u32[]{:S(2)}) collective-permute-start(f32[1,2048]{1,0:T(1,128)S(1)} %reshape.43), channel_id=1, source_target_pairs={{0,4},{4,8},{8,12},{12,0},{1,5},{5,9},{9,13},{13,1},{2,6},{6,10},{... | collective-permute-start | bytes 24584 | tf_op jit(solution)/shard_map/ppermute | solution.py:270
  66.4 19.1 %collective-permute-start.10 = (bf16[128,2048]{1,0:T(8,128)(2,1)S(1)}, bf16[128,2048]{1,0:T(8,128)(2,1)S(1)}, u32[]{:S(2)}, u32[]{:S(2)}) collective-permute-start(bf16[128,2048]{1,0:T(8,128)(2,1)S(1)} %get-tuple-element.30), channel_id=1, source_target_pairs={{1,0},{2,3},{5,4},{6,7},{9,8},{10,11},{13,12},{14,15},{17,16},{18,... | collective-permute-start | bytes 1572872 | tf_op jit(solution)/shard_map/ppermute | solution.py:243
  67.7 33.5 %collective-permute-start.9 = (bf16[128,2048]{1,0:T(8,128)(2,1)S(1)}, bf16[128,2048]{1,0:T(8,128)(2,1)S(1)}, u32[]{:S(2)}, u32[]{:S(2)}) collective-permute-start(bf16[128,2048]{1,0:T(8,128)(2,1)S(1)} %get-tuple-element.31), channel_id=1, source_target_pairs={{1,0},{2,3},{5,4},{6,7},{9,8},{10,11},{13,12},{14,15},{17,16},{18,... | collective-permute-start | bytes 1572872 | tf_op jit(solution)/shard_map/ppermute | solution.py:243
  70.0 12.5 %collective-permute-start.14 = (f32[1,512]{1,0:T(1,128)S(1)}, f32[1,512]{1,0:T(1,128)S(1)}, u32[]{:S(2)}, u32[]{:S(2)}) collective-permute-start(f32[1,512]{1,0:T(1,128)S(1)} %get-tuple-element.44), channel_id=1, source_target_pairs={{0,12},{4,0},{8,4},{12,8},{1,13},{5,1},{9,5},{13,9},{2,14},{6,2},{... | collective-permute-start | bytes 6152 | tf_op jit(solution)/shard_map/ppermute | solution.py:283
  81.8 3.7 %collective-permute-start.16 = (f32[1,512]{1,0:T(1,128)S(1)}, f32[1,512]{1,0:T(1,128)S(1)}, u32[]{:S(2)}, u32[]{:S(2)}) collective-permute-start(f32[1,512]{1,0:T(1,128)S(1)} %get-tuple-element.42), channel_id=1, source_target_pairs={{0,4},{4,8},{8,12},{12,0},{1,5},{5,9},{9,13},{13,1},{2,6},{6,10},{... | collective-permute-start | bytes 6152 | tf_op jit(solution)/shard_map/ppermute | solution.py:283
  81.8 3.7 %collective-permute-start.15 = (f32[1,512]{1,0:T(1,128)S(1)}, f32[1,512]{1,0:T(1,128)S(1)}, u32[]{:S(2)}, u32[]{:S(2)}) collective-permute-start(f32[1,512]{1,0:T(1,128)S(1)} %get-tuple-element.43), channel_id=1, source_target_pairs={{0,8},{4,12},{8,0},{12,4},{1,9},{5,13},{9,1},{13,5},{2,10},{6,14},... | collective-permute-start | bytes 6152 | tf_op jit(solution)/shard_map/ppermute | solution.py:283
  85.5 1.7 %copy-start.6 = (bf16[128,2048]{1,0:T(8,128)(2,1)}, bf16[128,2048]{1,0:T(8,128)(2,1)S(1)}, u32[]{:S(2)}) copy-start(bf16[128,2048]{1,0:T(8,128)(2,1)S(1)} %collective-permute-done.10.second) | copy-start | bytes 1572868
  85.6 11.2 %collective-permute-start.17 = (f32[2,512]{1,0:T(2,128)S(1)}, f32[2,512]{1,0:T(2,128)S(1)}, u32[]{:S(2)}, u32[]{:S(2)}) collective-permute-start(f32[2,512]{1,0:T(2,128)S(1)} %pad_maximum_fusion.1), channel_id=1, source_target_pairs={{0,3},{1,2},{2,1},{3,0},{4,7},{5,6},{6,5},{7,4},{8,11},{9,10},{10,... | collective-permute-start | bytes 12296 | tf_op jit(solution)/shard_map/ppermute | solution.py:295
  96.7 14.8 %collective-permute-start.18 = (f32[1,512]{1,0:T(1,128)S(1)}, f32[1,512]{1,0:T(1,128)S(1)}, u32[]{:S(2)}, u32[]{:S(2)}) collective-permute-start(f32[1,512]{1,0:T(1,128)S(1)} %fusion.13), channel_id=1, source_target_pairs={{0,2},{1,3},{2,0},{3,1},{4,6},{5,7},{6,4},{7,5},{8,10},{9,11},{10,... | collective-permute-start | bytes 6152 | tf_op jit(solution)/shard_map/ppermute | solution.py:298
  101.2 0.8 copy-start.5

commit v5 on v4

--- a/solution.py
+++ b/solution.py
@@ -37,78 +37,72 @@
 
 
 TILE = 256
-GRANT = 56 * 2**20
-
-
-def first_rows_kernel(place, rows_in, w_tile, out, turned):
-    turned[...] = w_tile[...].T
-    out[0] = jnp.dot(rows_in[...], turned[...], preferred_element_type=jnp.float32).astype(out.dtype)
-
-
-def first_rows(blocks, rows_in, w_kv, index):
-    rows, depth = rows_in.shape
+GRANT = 24 * 2**20
+
+
+def rows_kernel(block, part, me, first, second, w_kv, *refs):
+    out, held, turned, weight, product, arrived, fetched, written = refs[-8:]
+    rows, depth = held.shape
+    tiles = weight.shape[0] // TILE
+    mine = me[0]
+    middle = (mine == 1) | (mine == 2)
+    index = [mine, mine ^ 1, jnp.where(middle, mine ^ 3, mine ^ 2), jnp.where(middle, mine ^ 2, mine ^ 3)][block]
+    use_second = jnp.logical_not(middle) if block > 1 else mine < 0
+
+    fetches = []
+    for tile in range(tiles):
+        here = pl.ds(tile * TILE, TILE)
+        fetches.append(pltpu.make_async_copy(w_kv.at[here], weight.at[here], fetched.at[tile]))
+    sources = [(first.at[pl.ds(part * rows, rows)], jnp.logical_not(use_second))]
+    if block > 1:
+        sources.append((second, use_second))
+    for source, chosen in sources:
+
+        @pl.when(chosen)
+        def _():
+            pltpu.make_async_copy(source, held, arrived).start()
+
+    for fetch in fetches:
+        fetch.start()
+    pltpu.make_async_copy(second, held, arrived).wait()
+    turned[...] = held[...].T
+    writes = []
+    for tile in range(tiles):
+        here = pl.ds(tile * TILE, TILE)
+        fetches[tile].wait()
+        columns = jnp.dot(weight[here, :], turned[...], preferred_element_type=jnp.float32)
+        product[:, here] = columns.astype(product.dtype).T
+        writes.append(
+            pltpu.make_async_copy(
+                product.at[:, here], out.at[index, pl.ds(part * rows, rows), here], written.at[tile]
+            )
+        )
+        writes[-1].start()
+    for write in writes:
+        write.wait()
+
+
+def put_rows(me, block, output, first, second, w_kv, part=0):
+    rows, depth = second.shape
     width = w_kv.shape[0]
+    anywhere = pl.BlockSpec(memory_space=pl.ANY)
+    earlier = [] if output is None else [output]
     return pl.pallas_call(
-        first_rows_kernel,
-        grid_spec=pltpu.PrefetchScalarGridSpec(
-            num_scalar_prefetch=1,
-            grid=(width // TILE,),
-            in_specs=[
-                pl.BlockSpec((rows, depth), lambda j, place: (0, 0)),
-                pl.BlockSpec((TILE, depth), lambda j, place: (j, 0)),
-            ],
-            out_specs=[
-                pl.BlockSpec((1, rows, TILE), lambda j, place: (place[0], 0, j)),
-                pl.BlockSpec((depth, TILE), lambda j, place: (0, j)),
-            ],
-        ),
-        out_shape=[
-            jax.ShapeDtypeStruct((blocks, rows, width), jnp.bfloat16),
-            jax.ShapeDtypeStruct((depth, width), w_kv.dtype),
+        functools.partial(rows_kernel, block, part),
+        in_specs=[pl.BlockSpec(memory_space=pltpu.SMEM), anywhere, anywhere, pl.BlockSpec(memory_space=pltpu.HBM)]
+        + [pl.BlockSpec(memory_space=pltpu.HBM)] * len(earlier),
+        out_specs=pl.BlockSpec(memory_space=pltpu.HBM),
+        scratch_shapes=[
+            pltpu.VMEM((rows, depth), first.dtype),
+            pltpu.VMEM((depth, rows), first.dtype),
+            pltpu.VMEM((width, depth), w_kv.dtype),
+            pltpu.VMEM((rows, width), jnp.bfloat16),
+            pltpu.SemaphoreType.DMA,
+            pltpu.SemaphoreType.DMA((width // TILE,)),
+            pltpu.SemaphoreType.DMA((width // TILE,)),
         ],
-        compiler_params=pltpu.CompilerParams(vmem_limit_bytes=GRANT),
-        cost_estimate=pl.CostEstimate(
-            flops=2 * rows * depth * width,
-            bytes_accessed=2 * (rows * depth + 2 * depth * width + rows * width),
-            transcendentals=0,
-        ),
-        name="input_grad_first_rows",
-    )(index.reshape(1).astype(jnp.int32), rows_in, w_kv)
-
-
-def rows_kernel(part, place, first, second, turned, earlier, out, held, arrived):
-    rows = held.shape[0]
-
-    @pl.when(pl.program_id(0) == 0)
-    def _():
-        own_part = first.at[pl.ds(part * rows, rows)]
-        for source, chosen in ((own_part, place[1] == 0), (second, place[1] != 0)):
-
-            @pl.when(chosen)
-            def _():
-                copy = pltpu.make_async_copy(source, held, arrived)
-                copy.start()
-                copy.wait()
-
-    out[0] = jnp.dot(held[...], turned[...], preferred_element_type=jnp.float32).astype(out.dtype)
-
-
-def put_rows(output, first, second, turned, index, use_second=0, part=0):
-    rows, depth = second.shape
-    width = turned.shape[1]
-    place = jnp.stack([index, use_second]).astype(jnp.int32)
-    anywhere = pl.BlockSpec(memory_space=pl.ANY)
-    return pl.pallas_call(
-        functools.partial(rows_kernel, part),
-        grid_spec=pltpu.PrefetchScalarGridSpec(
-            num_scalar_prefetch=1,
-            grid=(width // TILE,),
-            in_specs=[anywhere, anywhere, pl.BlockSpec((depth, TILE), lambda j, place: (0, j)), anywhere],
-            out_specs=pl.BlockSpec((1, rows, TILE), lambda j, place: (place[0], part, j)),
-            scratch_shapes=[pltpu.VMEM((rows, depth), first.dtype), pltpu.SemaphoreType.DMA],
-        ),
-        out_shape=jax.ShapeDtypeStruct(output.shape, output.dtype),
-        input_output_aliases={4: 0},
+        out_shape=jax.ShapeDtypeStruct((4, first.shape[0], width), jnp.bfloat16),
+        input_output_aliases={4: 0} if earlier else {},
         compiler_params=pltpu.CompilerParams(vmem_limit_bytes=GRANT),
         cost_estimate=pl.CostEstimate(
             flops=2 * rows * depth * width,
@@ -116,7 +110,7 @@
             transcendentals=0,
         ),
         name="input_grad_rows",
-    )(place, first, second, turned, output)
+    )(me.reshape(1).astype(jnp.int32), first, second, w_kv, *earlier)
 
 
 def token_sums_kernel(me, low_in, low_in_beside, own_low, far_low, beside, facing, proj, out):
@@ -209,20 +203,20 @@
     inward = [(0, 1), (3, 2)]
 
     beside = lax.ppermute(grad_kv, "mp", exchange_pairs)
-    facing = lax.ppermute(grad_kv, "mp", across)
-    proj_both = block_diagonal(proj_out)
+    proj_both, grad_after = lax.optimization_barrier((block_diagonal(proj_out), grad_kv))
+    facing = lax.ppermute(grad_after, "mp", across)
     own_low = jnp.dot(grad_kv, proj_both, preferred_element_type=jnp.float32)
-    far_low = lax.ppermute(own_low, "mp", [(3, 1), (0, 2)])
     low_in = jnp.dot(hidden, proj_in, preferred_element_type=jnp.float32)
-    output, turned = first_rows(4, grad_kv, w_kv, me)
-
-    beside, facing, low_in, output = lax.optimization_barrier((beside, facing, low_in, output))
+    output = put_rows(me, 0, None, grad_kv, grad_kv, w_kv)
+
+    beside, facing, low_in, own_low, output = lax.optimization_barrier((beside, facing, low_in, own_low, output))
     second = lax.ppermute(facing, "mp", outward)
     beside_across = lax.ppermute(beside, "mp", across)
+    far_low = lax.ppermute(own_low, "mp", [(3, 1), (0, 2)])
+    output = put_rows(me, 1, output, beside, beside, w_kv)
+    low_in, far_low, output = lax.optimization_barrier((low_in, far_low, output))
     low_in_beside = lax.ppermute(low_in, "mp", inward)
-    output = put_rows(output, beside, beside, turned, me ^ 1)
-
-    low_in_beside, far_low = lax.optimization_barrier((low_in_beside, far_low))
+
     if low_in.shape[0] == SEQ:
         slabs = token_sums(me, low_in, low_in_beside, own_low, far_low, beside, facing, proj_both, rank)[:, None]
     else:
@@ -242,16 +236,14 @@
     half = local_rows // 2
     third = [lax.ppermute(beside_across[part * half : (part + 1) * half], "mp", outward) for part in range(2)]
     mine, beside_across = lax.optimization_barrier((mine, beside_across))
-    ends = jnp.logical_not(middle).astype(jnp.int32)
-    output = put_rows(output, facing, second, turned, jnp.where(middle, me ^ 3, me ^ 2), ends)
-    last = jnp.where(middle, me ^ 2, me ^ 3)
+    output = put_rows(me, 2, output, facing, second, w_kv)
 
     def finish(total):
         return lax.optimization_barrier((total, third[0], output))[0]
 
     def rest():
-        upper = put_rows(output, beside_across, third[0], turned, last, ends, 0)
-        return put_rows(upper, beside_across, third[1], turned, last, ends, 1).reshape(4 * local_rows, w_kv.shape[0])
+        upper = put_rows(me, 3, output, beside_across, third[0], w_kv, 0)
+        return put_rows(me, 3, upper, beside_across, third[1], w_kv, 1).reshape(4 * local_rows, w_kv.shape[0])
 
     return mine, finish, rest
 

time: 114 us -> 120 us (1.053)
  waiting for transfers between devices: 7.67 us -> 28.7 us
  Pallas kernels: 54.8 us -> 38.3 us
  local copies, waits for them, and re-layouts: 6.4 us -> 10.6 us
  other arithmetic: 5.14 us -> 1.65 us
  starting transfers between devices: 32.9 us -> 35.6 us
  matrix products: 4.4 us -> 3.12 us
    pallas_call x5, Pallas kernels: 50.9 us -> 35.2 us  [put_rows(): pl.pallas_call(functools.partial(rows_kernel, block, part), in_specs=[pl....]
    ppermute x2, waiting for transfers between devices: 0.01 us -> 8.42 us  [line_of_four(): lax.ppermute(beside_across[part * half:(part + 1) * half], 'mp', outward)]
    ppermute x1, starting transfers between devices: 3.28 us -> 10.1 us  [line_of_four(): far_low = lax.ppermute(own_low, 'mp', [(3, 1), (0, 2)])]
    ppermute x1, waiting for transfers between devices: 2.41 us -> 8.92 us  [line_of_four(): low_in_beside = lax.ppermute(low_in, 'mp', inward)]
    unnamed x18 -> x20, local copies, waits for them, and re-layouts: 3.77 us -> 9.39 us
    ppermute x1, starting transfers between devices: 4.48 us -> 0.07 us  [on_device(): lax.ppermute(kept, 'mp', [(source, source ^ 2) for source in range(n)])]
    ppermute x1, waiting for transfers between devices: 0.01 us -> 3.29 us  [line_of_four(): mine = mine + lax.ppermute(take(slabs, me ^ 2), 'mp', [(1, 3), (2, 0)])]
    ppermute x1, waiting for transfers between devices: 2 us -> 4.67 us  [line_of_four(): beside = lax.ppermute(grad_kv, 'mp', exchange_pairs)]
  transfers between devices with their start and end apart: 19 -> 19, of which waited for: 4 -> 6; matrix products, arithmetic and copies ran while one was open for 12% -> 5% of each run, Pallas kernels for 49% -> 32%
where the time goes in v5:
time: 120 us; the launch traced here: 119 us
  Pallas kernels  38.3 us (32%)
  starting transfers between devices  35.6 us (30%)
  waiting for transfers between devices  28.7 us (24%)
  local copies, waits for them, and re-layouts  10.6 us (9%)
  matrix products  3.12 us (3%)
  other arithmetic  1.65 us (1%)
    pallas_call x5, Pallas kernels, put_rows(): pl.pallas_call(functools.partial(rows_kernel, block, part), in_specs=[pl....  35.2 us
    ppermute x1, starting transfers between devices, line_of_four(): far_low = lax.ppermute(own_low, 'mp', [(3, 1), (0, 2)])  10.1 us
    unnamed x20, local copies, waits for them, and re-layouts  9.39 us
    ppermute x1, waiting for transfers between devices, line_of_four(): low_in_beside = lax.ppermute(low_in, 'mp', inward)  8.92 us
    ppermute x2, waiting for transfers between devices, line_of_four(): lax.ppermute(beside_across[part * half:(part + 1) * half], 'mp', outward)  8.42 us
    ppermute x1, starting transfers between devices, line_of_four(): low_in_beside = lax.ppermute(low_in, 'mp', inward)  6.33 us
    ppermute x1, waiting for transfers between devices, line_of_four(): beside = lax.ppermute(grad_kv, 'mp', exchange_pairs)  4.67 us
    ppermute x1, waiting for transfers between devices, line_of_four(): mine = mine + lax.ppermute(take(slabs, me ^ 2), 'mp', [(1, 3), (2, 0)])  3.29 us
  transfers between devices with their start and end apart: 19, of which 6 were waited for; matrix products, arithmetic and copies ran while one was open for 5% of the time, Pallas kernels for 32%

profile of v5, /device:TPU:0, one launch (start us, length us, event | category | flops | bytes accessed | tf_op | source)
XLA Modules:
  0.0 119.1 jit_solution(11552856773628177923)
XLA Ops:
  0.6 0.0 copy-start
  0.6 3.1 %collective-permute-start = (bf16[256,2048]{1,0:T(8,128)(2,1)}, bf16[256,2048]{1,0:T(8,128)(2,1)}, u32[]{:S(2)}, u32[]{:S(2)}) collective-permute-start(bf16[256,2048]{1,0:T(8,128)(2,1)} %second.1), channel_id=1, source_target_pairs={{0,1},{1,0},{2,3},{3,2},{4,5},{5,4},{6,7},{7,6},{8,9},{9,8},{10,11... | collective-permute-start | bytes 3145736 | tf_op jit(solution)/shard_map/ppermute | solution.py:205
  3.7 1.0 fusion.16
  4.7 0.2 copy.17
  4.9 0.2 copy.16
  5.1 1.0 fusion.2.proj
  6.0 1.6 %collective-permute-start.1 = (bf16[256,2048]{1,0:T(8,128)(2,1)}, bf16[256,2048]{1,0:T(8,128)(2,1)}, u32[]{:S(2)}, u32[]{:S(2)}) collective-permute-start(bf16[256,2048]{1,0:T(8,128)(2,1)} %second.1), channel_id=1, source_target_pairs={{1,2},{2,1},{5,6},{6,5},{9,10},{10,9},{13,14},{14,13},{17,18},{18,... | collective-permute-start | bytes 3145736 | tf_op jit(solution)/shard_map/ppermute | solution.py:207
  7.7 3.4 %copy-done.1 = bf16[2048,2048]{1,0:T(8,128)(2,1)S(1)} copy-done((bf16[2048,2048]{1,0:T(8,128)(2,1)S(1)}, bf16[2048,2048]{1,0:T(8,128)(2,1)}, u32[]{:S(2)}) %copy-start.1) | copy-done | bytes 8388632
  11.0 1.2 %copy-done.4 = bf16[256,2048]{1,0:T(8,128)(2,1)S(1)} copy-done((bf16[256,2048]{1,0:T(8,128)(2,1)S(1)}, bf16[256,2048]{1,0:T(8,128)(2,1)}, u32[]{:S(2)}) %copy-start.4) | copy-done | bytes 1048600
  12.3 7.7 %input_grad_rows.5.refs_0_ = bf16[4,256,2048]{2,1,0:T(8,128)(2,1)} custom-call(s32[1]{0:T(128)} %bitcast.me, bf16[256,2048]{1,0:T(8,128)(2,1)S(1)} %copy-done.4, bf16[256,2048]{1,0:T(8,128)(2,1)S(1)} %copy-done.4, bf16[2048,2048]{1,0:T(8,128)(2,1)S(1)} %copy-done.1), custom_call_target="tpu_custom_call" | custom-call | flops 2147483648 | bytes 10485760 | tf_op jit(solution)/shard_map/input_grad_rows/pallas_call | solution.py:90
  20.0 0.0 copy-done.5
  20.0 0.4 convolution_bitcast_fusion.own_low
  20.5 0.0 copy-done.7
  20.5 2.0 %fusion.18.low_in = f32[1024,128]{1,0:T(8,128)} fusion(bf16[1024,2048]{1,0:T(8,128)(2,1)S(1)} %copy-done.7, bf16[2048,128]{1,0:T(8,128)(2,1)S(1)} %copy-done.8), kind=kOutput, calls=%fused_computation.40 | convolution fusion | flops 536870912 | bytes 5242880 | tf_op jit(solution)/shard_map/dot_general | solution.py:209
  22.5 4.7 %collective-permute-done.first.second.beside = bf16[256,2048]{1,0:T(8,128)(2,1)} collective-permute-done((bf16[256,2048]{1,0:T(8,128)(2,1)}, bf16[256,2048]{1,0:T(8,128)(2,1)}, u32[]{:S(2)}, u32[]{:S(2)}) %collective-permute-start) | collective-permute-done | bytes 1048608 | tf_op jit(solution)/shard_map/ppermute | solution.py:205
  27.2 0.0 collective-permute-done.1.facing.first
  27.2 10.1 %collective-permute-start.2 = (f32[256,128]{1,0:T(8,128)S(1)}, f32[256,128]{1,0:T(8,128)S(1)}, u32[]{:S(2)}, u32[]{:S(2)}) collective-permute-start(f32[256,128]{1,0:T(8,128)S(1)} %convolution_bitcast_fusion.own_low), channel_id=1, source_target_pairs={{3,1},{0,2},{7,5},{4,6},{11,9},{8,10},{15,13},{12,14},{19,17},{16,... | collective-permute-start | bytes 393224 | tf_op jit(solution)/shard_map/ppermute | solution.py:215
  37.4 0.7 collective-permute-start.7
  38.1 1.3 %collective-permute-start.8 = (bf16[256,2048]{1,0:T(8,128)(2,1)}, bf16[256,2048]{1,0:T(8,128)(2,1)}, u32[]{:S(2)}, u32[]{:S(2)}) collective-permute-start(bf16[256,2048]{1,0:T(8,128)(2,1)} %collective-permute-done.1.facing.first), channel_id=1, source_target_pairs={{1,0},{2,3},{5,4},{6,7},{9,8},{10,11},{13,12},{14,15},{17,16},{18,... | collective-permute-start | bytes 3145736 | tf_op jit(solution)/shard_map/ppermute | solution.py:213
  39.4 0.0 copy-done.2
  39.4 8.3 %input_grad_rows.6.refs_0_ = bf16[4,256,2048]{2,1,0:T(8,128)(2,1)} custom-call(s32[1]{0:T(128)} %bitcast.me, bf16[256,2048]{1,0:T(8,128)(2,1)} %collective-permute-done.first.second.beside, bf16[256,2048]{1,0:T(8,128)(2,1)} %collective-permute-done.first.second.beside, bf16[2048,2048]{1,0:T(8,128)(2,1)S(1)} %copy-done.2, ...), custom_call_target="tpu_custom_call", output_to_operand_aliasing={{}: (4, {})} | custom-call | flops 2147483648 | bytes 10485760 | tf_op jit(solution)/shard_map/input_grad_rows/pallas_call | solution.py:90
  47.7 0.0 collective-permute-done.2.far_low
  47.7 6.3 %collective-permute-start.3 = (f32[1024,128]{1,0:T(8,128)}, f32[1024,128]{1,0:T(8,128)}, u32[]{:S(2)}, u32[]{:S(2)}) collective-permute-start(f32[1024,128]{1,0:T(8,128)} %fusion.18.low_in), channel_id=1, source_target_pairs={{0,1},{3,2},{4,5},{7,6},{8,9},{11,10},{12,13},{15,14},{16,17},{19,... | collective-permute-start | bytes 1572872 | tf_op jit(solution)/shard_map/ppermute | solution.py:218
  54.1 8.9 %collective-permute-done.3.low_in_beside = f32[1024,128]{1,0:T(8,128)} collective-permute-done((f32[1024,128]{1,0:T(8,128)}, f32[1024,128]{1,0:T(8,128)}, u32[]{:S(2)}, u32[]{:S(2)}) %collective-permute-start.3) | collective-permute-done | bytes 524320 | tf_op jit(solution)/shard_map/ppermute | solution.py:218
  63.0 1.0 copy-done.6
  64.0 3.1 %token_sums.1 = f32[4,32,64]{2,1,0:T(8,128)S(1)} custom-call(s32[1]{0:T(128)} %bitcast.me, f32[1024,128]{1,0:T(8,128)} %fusion.18.low_in, f32[1024,128]{1,0:T(8,128)} %collective-permute-done.3.low_in_beside, f32[256,128]{1,0:T(8,128)S(1)} %convolution_bitcast_fusion.own_low, f32[256,128]{1,0:T(8,128)S(1)} %collective-permute-done.2.far_low, ...), custom_call_target="tpu_custom_call" | custom-call | tf_op jit(solution)/shard_map/token_sums/pallas_call | solution.py:142
  67.1 1.3 %collective-permute-start.6 = (f32[1,32,64]{2,1,0:T(8,128)S(1)}, f32[1,32,64]{2,1,0:T(8,128)S(1)}, u32[]{:S(2)}, u32[]{:S(2)}) collective-permute-start(f32[1,32,64]{2,1,0:T(8,128)S(1)} %get-tuple-element.39), channel_id=1, source_target_pairs={{1,3},{2,0},{5,7},{6,4},{9,11},{10,8},{13,15},{14,12},{17,19},{18,... | collective-permute-start | bytes 24584 | tf_op jit(solution)/shard_map/ppermute | solution.py:233
  68.4 1.3 %collective-permute-start.5 = (f32[1,32,64]{2,1,0:T(8,128)S(1)}, f32[1,32,64]{2,1,0:T(8,128)S(1)}, u32[]{:S(2)}, u32[]{:S(2)}) collective-permute-start(f32[1,32,64]{2,1,0:T(8,128)S(1)} %get-tuple-element.40), channel_id=1, source_target_pairs={{1,0},{2,3},{5,4},{6,7},{9,8},{10,11},{13,12},{14,15},{17,16},{18,... | collective-permute-start | bytes 24584 | tf_op jit(solution)/shard_map/ppermute | solution.py:232
  69.7 0.7 collective-permute-start.4
  70.5 3.3 %collective-permute-done.6 = f32[1,32,64]{2,1,0:T(8,128)S(1)} collective-permute-done((f32[1,32,64]{2,1,0:T(8,128)S(1)}, f32[1,32,64]{2,1,0:T(8,128)S(1)}, u32[]{:S(2)}, u32[]{:S(2)}) %collective-permute-start.6) | collective-permute-done | bytes 8224 | tf_op jit(solution)/shard_map/ppermute | solution.py:233
  73.8 0.3 collective-permute-done.5
  74.1 0.0 collective-permute-done.4
  74.1 0.0 collective-permute-done.7.first
  74.1 0.0 collective-permute-done.8.second
  74.1 0.1 reshape.47
  74.2 0.0 collective-permute-start.13
  74.2 1.6 %collective-permute-start.12 = (f32[1,2048]{1,0:T(1,128)S(1)}, f32[1,2048]{1,0:T(1,128)S(1)}, u32[]{:S(2)}, u32[]{:S(2)}) collective-permute-start(f32[1,2048]{1,0:T(1,128)S(1)} %reshape.47), channel_id=1, source_target_pairs={{0,8},{4,12},{8,0},{12,4},{1,9},{5,13},{9,1},{13,5},{2,10},{6,14},... | collective-permute-start | bytes 24584 | tf_op jit(solution)/shard_map/ppermute | solution.py:262
  75.8 0.2 collective-permute-start.11
  76.0 0.1 fusion.15
  76.1 1.3 %collective-permute-start.9 = (bf16[128,2048]{1,0:T(8,128)(2,1)S(1)}, bf16[128,2048]{1,0:T(8,128)(2,1)S(1)}, u32[]{:S(2)}, u32[]{:S(2)}) collective-permute-start(bf16[128,2048]{1,0:T(8,128)(2,1)S(1)} %get-tuple-element.35), channel_id=1, source_target_pairs={{1,0},{2,3},{5,4},{6,7},{9,8},{10,11},{13,12},{14,15},{17,16},{18,... | collective-permute-start | bytes 1572872 | tf_op jit(solution)/shard_map/ppermute | solution.py:237
  77.4 1.5 %collective-permute-start.10 = (bf16[128,2048]{1,0:T(8,128)(2,1)S(1)}, bf16[128,2048]{1,0:T(8,128)(2,1)S(1)}, u32[]{:S(2)}, u32[]{:S(2)}) collective-permute-start(bf16[128,2048]{1,0:T(8,128)(2,1)S(1)} %get-tuple-element.34), channel_id=1, source_target_pairs={{1,0},{2,3},{5,4},{6,7},{9,8},{10,11},{13,12},{14,15},{17,16},{18,... | collective-permute-start | bytes 1572872 | tf_op jit(solution)/shard_map/ppermute | solution.py:237
  78.9 0.0 collective-permute-done.13
  78.9 0.0 collective-permute-done.12
  78.9 0.0 collective-permute-done.11
  78.9 0.1 reduce-precision_convert_fusion.1
  78.9 0.0 copy-done
  79.0 0.6 fusion.3
  79.7 1.6 %collective-permute-start.14 = (f32[1,512]{1,0:T(1,128)S(1)}, f32[1,512]{1,0:T(1,128)S(1)}, u32[]{:S(2)}, u32[]{:S(2)}) collective-permute-start(f32[1,512]{1,0:T(1,128)S(1)} %get-tuple-element.48), channel_id=1, source_target_pairs={{0,12},{4,0},{8,4},{12,8},{1,13},{5,1},{9,5},{13,9},{2,14},{6,2},{... | collective-permute-start | bytes 6152 | tf_op jit(solution)/shard_map/ppermute | solution.py:275
  81.3 3.4 %copy-done.3 = bf16[2048,2048]{1,0:T(8,128)(2,1)S(1)} copy-done((bf16[2048,2048]{1,0:T(8,128)(2,1)S(1)}, bf16[2048,2048]{1,0:T(8,128)(2,1)}, u32[]{:S(2)}) %copy-start.3) | copy-done | bytes 8388632
  84.7 8.3 %input_grad_rows.7.refs_0_ = bf16[4,256,2048]{2,1,0:T(8,128)(2,1)} custom-call(s32[1]{0:T(128)} %bitcast.me, bf16[256,2048]{1,0:T(8,128)(2,1)} %collective-permute-done.1.facing.first, bf16[256,2048]{1,0:T(8,128)(2,1)} %collective-permute-done.8.second, bf16[2048,2048]{1,0:T(8,128)(2,1)S(1)} %copy-done.3, ...), custom_call_target="tpu_custom_call", output_to_operand_aliasing={{}: (4, {})} | custom-call | flops 2147483648 | bytes 10485760 | tf_op jit(solution)/shard_map/input_grad_rows/pallas_call | solution.py:90
  93.0 0.6 collective-permute-start.15
  93.6 0.0 collective-permute-start.16
  93.6 0.0 collective-permute-done.14
  93.6 3.0 %collective-permute-done.15 = f32[1,512]{1,0:T(1,128)S(1)} collective-permute-done((f32[1,512]{1,0:T(1,128)S(1)}, f32[1,512]{1,0:T(1,128)S(1)}, u32[]{:S(2)}, u32[]{:S(2)}) %collective-permute-start.15) | collective-permute-done | bytes 2080 | tf_op jit(solution)/shard_map/ppermute | solution.py:275
  96.7 0.0 collective-permute-done.16
  96.7 8.4 %collective-permute-done.10.second = bf16[128,2048]{1,0:T(8,128)(2,1)S(1)} collective-permute-done((bf16[128,2048]{1,0:T(8,128)(2,1)S(1)}, bf16[128,2048]{1,0:T(8,128)(2,1)S(1)}, u32[]{:S(2)}, u32[]{:S(2)}) %collective-permute-start.10) | collective-permute-done | bytes 524320 | tf_op jit(solution)/shard_map/ppermute | solution.py:237
  105.1 2.4 %collective-permute-start.17 = (f32[2,512]{1,0:T(2,128)S(1)}, f32[2,512]{1,0:T(2,128)S(1)}, u32[]{:S(2)}, u32[]{:S(2)}) collective-permute-start(f32[2,512]{1,0:T(2,128)S(1)} %pad_maximum_fusion.1), channel_id=1, source_target_pairs={{0,3},{1,2},{2,1},{3,0},{4,7},{5,6},{6,5},{7,4},{8,11},{9,10},{10,... | collective-permute-start | bytes 12296 | tf_op jit(solution)/shard_map/ppermute | solution.py:287
  107.5 5.4 %input_grad_rows.8.refs_0_ = bf16[4,256,2048]{2,1,0:T(8,128)(2,1)} custom-call(s32[1]{0:T(128)} %bitcast.me, bf16[256,2048]{1,0:T(8,128)(2,1)S(1)} %collective-permute-done.7.first, bf16[128,2048]{1,0:T(8,128)(2,1)S(1)} %collective-permute-done.10.second, bf16[2048,2048]{1,0:T(8,128)(2,1)S(1)} %copy-done.3, ...), custom_call_target="tpu_custom_call", output_to_operand_aliasing={{}: (4, {})} | custom-call | flops 1073741824 | bytes 9437184 | tf_op jit(solution)/shard_map/input_grad_rows/pallas_call | solution.py:90
  112.9 0.0 collective-permute-done.17
  112.9 0.1 collective-permute-start.18
  113.0 0.0 collective-permute-done.9.second
  113.0 5.4 %input_grad_rows.9 = bf16[4,256,2048]{2,1,0:T(8,128)(2,1)} custom-call(s32[1]{0:T(128)} %bitcast.me, bf16[256,2048]{1,0:T(8,128)(2,1)S(1)} %collective-permute-done.7.first, bf16[128,2048]{1,0:T(8,128)(2,1)S(1)} %collective-permute-done.9.second, bf16[2048,2048]{1,0:T(8,128)(2,1)S(1)} %copy-done.3, ...), custom_call_target="tpu_custom_call", output_to_operand_aliasing={{}: (4, {})} | custom-call | flops 1073741824 | bytes 9437184 | tf_op jit(solution)/shard_map/input_grad_rows/pallas_call | solution.py:90
  118.5 0.0 collective-permute-done.18
  118.5 0.6 fusion.12
  (20 shorter events, 0.1 us)
Async XLA Ops:
  0.6 78.3 %copy-start = (bf16[512,2048]{1,0:T(8,128)(2,1)S(1)}, bf16[512,2048]{1,0:T(8,128)(2,1)}, u32[]{:S(2)}) copy-start(bf16[512,2048]{1,0:T(8,128)(2,1)} %param.11) | copy-start | bytes 6291460
  0.6 26.6 %collective-permute-start = (bf16[256,2048]{1,0:T(8,128)(2,1)}, bf16[256,2048]{1,0:T(8,128)(2,1)}, u32[]{:S(2)}, u32[]{:S(2)}) collective-permute-start(bf16[256,2048]{1,0:T(8,128)(2,1)} %second.1), channel_id=1, source_target_pairs={{0,1},{1,0},{2,3},{3,2},{4,5},{5,4},{6,7},{7,6},{8,9},{9,8},{10,11... | collective-permute-start | bytes 3145736 | tf_op jit(solution)/shard_map/ppermute | solution.py:205
  6.0 21.2 %collective-permute-start.1 = (bf16[256,2048]{1,0:T(8,128)(2,1)}, bf16[256,2048]{1,0:T(8,128)(2,1)}, u32[]{:S(2)}, u32[]{:S(2)}) collective-permute-start(bf16[256,2048]{1,0:T(8,128)(2,1)} %second.1), channel_id=1, source_target_pairs={{1,2},{2,1},{5,6},{6,5},{9,10},{10,9},{13,14},{14,13},{17,18},{18,... | collective-permute-start | bytes 3145736 | tf_op jit(solution)/shard_map/ppermute | solution.py:207
  7.7 3.4 %copy-start.1 = (bf16[2048,2048]{1,0:T(8,128)(2,1)S(1)}, bf16[2048,2048]{1,0:T(8,128)(2,1)}, u32[]{:S(2)}) copy-start(bf16[2048,2048]{1,0:T(8,128)(2,1)} %w_kv.9) | copy-start | bytes 25165828
  11.0 1.2 %copy-start.4 = (bf16[256,2048]{1,0:T(8,128)(2,1)S(1)}, bf16[256,2048]{1,0:T(8,128)(2,1)}, u32[]{:S(2)}) copy-start(bf16[256,2048]{1,0:T(8,128)(2,1)} %second.1) | copy-start | bytes 3145732
  12.3 7.8 %copy-start.5 = (bf16[2048,128]{1,0:T(8,128)(2,1)S(1)}, bf16[2048,128]{1,0:T(8,128)(2,1)}, u32[]{:S(2)}) copy-start(bf16[2048,128]{1,0:T(8,128)(2,1)} %fusion.2.proj) | copy-start | bytes 1572868
  12.3 8.2 %copy-start.7 = (bf16[1024,2048]{1,0:T(8,128)(2,1)S(1)}, bf16[1024,2048]{1,0:T(8,128)(2,1)}, u32[]{:S(2)}) copy-start(bf16[1024,2048]{1,0:T(8,128)(2,1)} %param.6) | copy-start | bytes 12582916
  12.3 8.2 %copy-start.8 = (bf16[2048,128]{1,0:T(8,128)(2,1)S(1)}, bf16[2048,128]{1,0:T(8,128)(2,1)}, u32[]{:S(2)}) copy-start(bf16[2048,128]{1,0:T(8,128)(2,1)} %param.9) | copy-start | bytes 1572868
  12.3 27.1 %copy-start.2 = (bf16[2048,2048]{1,0:T(8,128)(2,1)S(1)}, bf16[2048,2048]{1,0:T(8,128)(2,1)}, u32[]{:S(2)}) copy-start(bf16[2048,2048]{1,0:T(8,128)(2,1)} %w_kv.9) | copy-start | bytes 25165828
  27.2 20.5 %collective-permute-start.2 = (f32[256,128]{1,0:T(8,128)S(1)}, f32[256,128]{1,0:T(8,128)S(1)}, u32[]{:S(2)}, u32[]{:S(2)}) collective-permute-start(f32[256,128]{1,0:T(8,128)S(1)} %convolution_bitcast_fusion.own_low), channel_id=1, source_target_pairs={{3,1},{0,2},{7,5},{4,6},{11,9},{8,10},{15,13},{12,14},{19,17},{16,... | collective-permute-start | bytes 393224 | tf_op jit(solution)/shard_map/ppermute | solution.py:215
  37.4 36.8 %collective-permute-start.7 = (bf16[256,2048]{1,0:T(8,128)(2,1)}, bf16[256,2048]{1,0:T(8,128)(2,1)S(1)}, u32[]{:S(2)}, u32[]{:S(2)}) collective-permute-start(bf16[256,2048]{1,0:T(8,128)(2,1)} %collective-permute-done.first.second.beside), channel_id=1, source_target_pairs={{1,2},{2,1},{5,6},{6,5},{9,10},{10,9},{13,14},{14,13},{17,18},{18,... | collective-permute-start | bytes 3145736 | tf_op jit(solution)/shard_map/ppermute | solution.py:214
  38.1 36.1 %collective-permute-start.8 = (bf16[256,2048]{1,0:T(8,128)(2,1)}, bf16[256,2048]{1,0:T(8,128)(2,1)}, u32[]{:S(2)}, u32[]{:S(2)}) collective-permute-start(bf16[256,2048]{1,0:T(8,128)(2,1)} %collective-permute-done.1.facing.first), channel_id=1, source_target_pairs={{1,0},{2,3},{5,4},{6,7},{9,8},{10,11},{13,12},{14,15},{17,16},{18,... | collective-permute-start | bytes 3145736 | tf_op jit(solution)/shard_map/ppermute | solution.py:213
  47.7 15.3 %collective-permute-start.3 = (f32[1024,128]{1,0:T(8,128)}, f32[1024,128]{1,0:T(8,128)}, u32[]{:S(2)}, u32[]{:S(2)}) collective-permute-start(f32[1024,128]{1,0:T(8,128)} %fusion.18.low_in), channel_id=1, source_target_pairs={{0,1},{3,2},{4,5},{7,6},{8,9},{11,10},{12,13},{15,14},{16,17},{19,... | collective-permute-start | bytes 1572872 | tf_op jit(solution)/shard_map/ppermute | solution.py:218
  63.0 1.0 copy-start.6
  67.1 6.7 %collective-permute-start.6 = (f32[1,32,64]{2,1,0:T(8,128)S(1)}, f32[1,32,64]{2,1,0:T(8,128)S(1)}, u32[]{:S(2)}, u32[]{:S(2)}) collective-permute-start(f32[1,32,64]{2,1,0:T(8,128)S(1)} %get-tuple-element.39), channel_id=1, source_target_pairs={{1,3},{2,0},{5,7},{6,4},{9,11},{10,8},{13,15},{14,12},{17,19},{18,... | collective-permute-start | bytes 24584 | tf_op jit(solution)/shard_map/ppermute | solution.py:233
  68.4 5.7 %collective-permute-start.5 = (f32[1,32,64]{2,1,0:T(8,128)S(1)}, f32[1,32,64]{2,1,0:T(8,128)S(1)}, u32[]{:S(2)}, u32[]{:S(2)}) collective-permute-start(f32[1,32,64]{2,1,0:T(8,128)S(1)} %get-tuple-element.40), channel_id=1, source_target_pairs={{1,0},{2,3},{5,4},{6,7},{9,8},{10,11},{13,12},{14,15},{17,16},{18,... | collective-permute-start | bytes 24584 | tf_op jit(solution)/shard_map/ppermute | solution.py:232
  69.7 4.4 %collective-permute-start.4 = (f32[1,32,64]{2,1,0:T(8,128)S(1)}, f32[1,32,64]{2,1,0:T(8,128)S(1)}, u32[]{:S(2)}, u32[]{:S(2)}) collective-permute-start(f32[1,32,64]{2,1,0:T(8,128)S(1)} %get-tuple-element.38), channel_id=1, source_target_pairs={{1,2},{2,1},{5,6},{6,5},{9,10},{10,9},{13,14},{14,13},{17,18},{18,... | collective-permute-start | bytes 24584 | tf_op jit(solution)/shard_map/ppermute | solution.py:231
  74.2 4.6 %collective-permute-start.13 = (f32[1,2048]{1,0:T(1,128)S(1)}, f32[1,2048]{1,0:T(1,128)S(1)}, u32[]{:S(2)}, u32[]{:S(2)}) collective-permute-start(f32[1,2048]{1,0:T(1,128)S(1)} %reshape.47), channel_id=1, source_target_pairs={{0,12},{4,0},{8,4},{12,8},{1,13},{5,1},{9,5},{13,9},{2,14},{6,2},{... | collective-permute-start | bytes 24584 | tf_op jit(solution)/shard_map/ppermute | solution.py:262
  74.2 4.6 %collective-permute-start.12 = (f32[1,2048]{1,0:T(1,128)S(1)}, f32[1,2048]{1,0:T(1,128)S(1)}, u32[]{:S(2)}, u32[]{:S(2)}) collective-permute-start(f32[1,2048]{1,0:T(1,128)S(1)} %reshape.47), channel_id=1, source_target_pairs={{0,8},{4,12},{8,0},{12,4},{1,9},{5,13},{9,1},{13,5},{2,10},{6,14},... | collective-permute-start | bytes 24584 | tf_op jit(solution)/shard_map/ppermute | solution.py:262
  75.8 3.1 %collective-permute-start.11 = (f32[1,2048]{1,0:T(1,128)S(1)}, f32[1,2048]{1,0:T(1,128)S(1)}, u32[]{:S(2)}, u32[]{:S(2)}) collective-permute-start(f32[1,2048]{1,0:T(1,128)S(1)} %reshape.47), channel_id=1, source_target_pairs={{0,4},{4,8},{8,12},{12,0},{1,5},{5,9},{9,13},{13,1},{2,6},{6,10},{... | collective-permute-start | bytes 24584 | tf_op jit(solution)/shard_map/ppermute | solution.py:262
  76.1 36.9 %collective-permute-start.9 = (bf16[128,2048]{1,0:T(8,128)(2,1)S(1)}, bf16[128,2048]{1,0:T(8,128)(2,1)S(1)}, u32[]{:S(2)}, u32[]{:S(2)}) collective-permute-start(bf16[128,2048]{1,0:T(8,128)(2,1)S(1)} %get-tuple-element.35), channel_id=1, source_target_pairs={{1,0},{2,3},{5,4},{6,7},{9,8},{10,11},{13,12},{14,15},{17,16},{18,... | collective-permute-start | bytes 1572872 | tf_op jit(solution)/shard_map/ppermute | solution.py:237
  77.4 27.7 %collective-permute-start.10 = (bf16[128,2048]{1,0:T(8,128)(2,1)S(1)}, bf16[128,2048]{1,0:T(8,128)(2,1)S(1)}, u32[]{:S(2)}, u32[]{:S(2)}) collective-permute-start(bf16[128,2048]{1,0:T(8,128)(2,1)S(1)} %get-tuple-element.34), channel_id=1, source_target_pairs={{1,0},{2,3},{5,4},{6,7},{9,8},{10,11},{13,12},{14,15},{17,16},{18,... | collective-permute-start | bytes 1572872 | tf_op jit(solution)/shard_map/ppermute | solution.py:237
  79.7 13.9 %collective-permute-start.14 = (f32[1,512]{1,0:T(1,128)S(1)}, f32[1,512]{1,0:T(1,128)S(1)}, u32[]{:S(2)}, u32[]{:S(2)}) collective-permute-start(f32[1,512]{1,0:T(1,128)S(1)} %get-tuple-element.48), channel_id=1, source_target_pairs={{0,12},{4,0},{8,4},{12,8},{1,13},{5,1},{9,5},{13,9},{2,14},{6,2},{... | collective-permute-start | bytes 6152 | tf_op jit(solution)/shard_map/ppermute | solution.py:275
  81.3 3.4 %copy-start.3 = (bf16[2048,2048]{1,0:T(8,128)(2,1)S(1)}, bf16[2048,2048]{1,0:T(8,128)(2,1)}, u32[]{:S(2)}) copy-start(bf16[2048,2048]{1,0:T(8,128)(2,1)} %w_kv.9) | copy-start | bytes 25165828
  93.0 3.7 %collective-permute-start.15 = (f32[1,512]{1,0:T(1,128)S(1)}, f32[1,512]{1,0:T(1,128)S(1)}, u32[]{:S(2)}, u32[]{:S(2)}) collective-permute-start(f32[1,512]{1,0:T(1,128)S(1)} %get-tuple-element.47), channel_id=1, source_target_pairs={{0,8},{4,12},{8,0},{12,4},{1,9},{5,13},{9,1},{13,5},{2,10},{6,14},... | collective-permute-start | bytes 6152 | tf_op jit(solution)/shard_map/ppermute | solution.py:275
  93.6 3.1 %collective-permute-start.16 = (f32[1,512]{1,0:T(1,128)S(1)}, f32[1,512]{1,0:T(1,128)S(1)}, u32[]{:S(2)}, u32[]{:S(2)}) collective-permute-start(f32[1,512]{1,0:T(1,128)S(1)} %get-tuple-element.46), channel_id=1, source_target_pairs={{0,4},{4,8},{8,12},{12,0},{1,5},{5,9},{9,13},{13,1},{2,6},{6,10},{... | collective-permute-start | bytes 6152 | tf_op jit(solution)/shard_map/ppermute | solution.py:275
  105.1 7.8 %collective-permute-start.17 = (f32[2,512]{1,0:T(2,128)S(1)}, f32[2,512]{1,0:T(2,128)S(1)}, u32[]{:S(2)}, u32[]{:S(2)}) collective-permute-start(f32[2,512]{1,0:T(2,128)S(1)} %pad_maximum_fusion.1), channel_id=1, source_target_pairs={{0,3},{1,2},{2,1},{3,0},{4,7},{5,6},{6,5},{7,4},{8,11},{9,10},{10,... | collective-permute-start | bytes 12296 | tf_op jit(solution)/shard_map/ppermute | solution.py:287
  112.9 5.5 %collective-permute-start.18 = (f32[1,512]{1,0:T(1,128)S(1)}, f32[1,512]{1,0:T(1,128)S(1)}, u32[]{:S(2)}, u32[]{:S(2)}) collective-permute-start(f32[1,512]{1,0:T(1,128)S(1)} %fusion.13), channel_id=1, source_target_pairs={{0,2},{1,3},{2,0},{3,1},{4,6},{5,7},{6,4},{7,5},{8,10},{9,11},{10,... | collective-permute-start | bytes 6152 | tf_op jit(solution)/shard_map/ppermute | solution.py:290

commit v6 on v5

v6 whole, which is shorter than its diff:
```python
import functools

import jax
import jax.numpy as jnp
from jax import lax
from jax.experimental import pallas as pl
from jax.experimental.pallas import tpu as pltpu
from jax.sharding import PartitionSpec as P

SEQ = 1024


def three_terms(value):
    high = lax.reduce_precision(value, 8, 7)
    rest = value - high
    middle = lax.reduce_precision(rest, 8, 7)
    low = rest - middle
    return [term.astype(jnp.bfloat16) for term in (high, middle, low)]


def block_diagonal(proj_out):
    layers, width, rank = proj_out.shape
    zeros = jnp.zeros((width, rank), proj_out.dtype)
    return jnp.concatenate(
        [
            jnp.concatenate([proj_out[layer] if column == layer else zeros for column in range(layers)], axis=1)
            for layer in range(layers)
        ],
        axis=0,
    )


def times_width(rows, w_kv):
    return lax.dot_general(
        rows, w_kv, (((1,), (1,)), ((), ())), preferred_element_type=jnp.float32
    ).astype(jnp.bfloat16)


FETCH = 256
TILE = 512
GRANT = 24 * 2**20


def rows_kernel(block, start, count, me, *refs):
    firsts, seconds = refs[:count], refs[count : 2 * count]
    w_kv = refs[2 * count]
    out, held, weight, product, arrived, fetched, written = refs[-7:]
    mine = me[0]
    middle = (mine == 1) | (mine == 2)
    index = [mine, mine ^ 1, jnp.where(middle, mine ^ 3, mine ^ 2), jnp.where(middle, mine ^ 2, mine ^ 3)][block]
    use_second = jnp.logical_not(middle) if block > 1 else mine < 0

    fetches = []
    for piece in range(weight.shape[0] // FETCH):
        here = pl.ds(piece * FETCH, FETCH)
        fetches.append(pltpu.make_async_copy(w_kv.at[here], weight.at[here], fetched.at[piece]))
    loads = []
    filled = 0
    for part in range(count):
        rows = firsts[part].shape[0]
        here = held.at[pl.ds(filled, rows)]
        filled += rows
        loads.append(pltpu.make_async_copy(firsts[part], here, arrived.at[part]))
        late = pltpu.make_async_copy(seconds[part], here, arrived.at[part])
        if block > 1:
            pl.when(jnp.logical_not(use_second))(loads[-1].start)
            pl.when(use_second)(late.start)
        else:
            loads[-1].start()
    for fetch in fetches:
        fetch.start()
    for load in loads:
        load.wait()
    writes = []
    for tile in range(weight.shape[0] // TILE):
        here = pl.ds(tile * TILE, TILE)
        for piece in range(tile * TILE // FETCH, (tile + 1) * TILE // FETCH):
            fetches[piece].wait()
        product[:, here] = lax.dot_general(
            held[...], weight[here, :], (((1,), (1,)), ((), ())), preferred_element_type=jnp.float32
        ).astype(product.dtype)
        writes.append(
            pltpu.make_async_copy(
                product.at[:, here], out.at[index, pl.ds(start, product.shape[0]), here], written.at[tile]
            )
        )
        writes[-1].start()
    for write in writes:
        write.wait()


def put_rows(me, block, output, firsts, seconds, w_kv, block_rows, start=0):
    count = len(firsts)
    depth = firsts[0].shape[1]
    rows = sum(part.shape[0] for part in firsts)
    width = w_kv.shape[0]
    earlier = [] if output is None else [output]
    return pl.pallas_call(
        functools.partial(rows_kernel, block, start, count),
        in_specs=[pl.BlockSpec(memory_space=pltpu.SMEM)]
        + [pl.BlockSpec(memory_space=pl.ANY)] * (2 * count)
        + [pl.BlockSpec(memory_space=pltpu.HBM)] * (1 + len(earlier)),
        out_specs=pl.BlockSpec(memory_space=pltpu.HBM),
        scratch_shapes=[
            pltpu.VMEM((rows, depth), firsts[0].dtype),
            pltpu.VMEM((width, depth), w_kv.dtype),
            pltpu.VMEM((rows, width), jnp.bfloat16),
            pltpu.SemaphoreType.DMA((count,)),
            pltpu.SemaphoreType.DMA((width // FETCH,)),
            pltpu.SemaphoreType.DMA((width // TILE,)),
        ],
        out_shape=jax.ShapeDtypeStruct((4, block_rows, width), jnp.bfloat16),
        input_output_aliases={2 * count + 2: 0} if earlier else {},
        compiler_params=pltpu.CompilerParams(vmem_limit_bytes=GRANT),
        cost_estimate=pl.CostEstimate(flops=rows * width, bytes_accessed=rows * width, transcendentals=0),
        name="input_grad_rows",
    )(me.reshape(1).astype(jnp.int32), *firsts, *seconds, w_kv, *earlier)


def token_sums_kernel(me, low_in, low_in_beside, own_low, beside_low, facing_low, far_low, out):
    rows = own_low.shape[0]
    rank = out.shape[2]
    total = jnp.zeros((own_low.shape[1], own_low.shape[1]), jnp.float32)
    for away, low_out in (
        (0, own_low[...]),
        (1, beside_low[...]),
        (3, facing_low[...]),
        (2, far_low[...]),
    ):
        here = pl.ds(pl.multiple_of((me[0] ^ away) * rows, rows), rows)
        total += lax.dot_general(
            low_in[here, :] + low_in_beside[here, :],
            low_out,
            (((0,), (0,)), ((), ())),
            precision=lax.Precision.HIGHEST,
            preferred_element_type=jnp.float32,
        )
    slab = out.shape[1]
    for index in range(out.shape[0]):
        layer = index * slab // rank
        out[index] = total[index * slab : (index + 1) * slab, layer * rank : (layer + 1) * rank]


def token_sums(me, low_in, low_in_beside, own_low, beside_low, facing_low, far_low, rank):
    whole = pl.BlockSpec(memory_space=pltpu.VMEM)
    return pl.pallas_call(
        token_sums_kernel,
        in_specs=[pl.BlockSpec(memory_space=pltpu.SMEM)] + [whole] * 6,
        out_specs=whole,
        out_shape=jax.ShapeDtypeStruct((4, 2 * rank // 4, rank), jnp.float32),
        compiler_params=pltpu.CompilerParams(vmem_limit_bytes=GRANT),
        name="token_sums",
    )(me.reshape(1).astype(jnp.int32), low_in, low_in_beside, own_low, beside_low, facing_low, far_low)


def sequence_sums(low_in, low_out, rank):
    count = low_in.shape[0] // SEQ
    left = low_in.reshape(count, SEQ, 2 * rank)
    right = low_out.reshape(count, SEQ, 2 * rank)
    return jnp.concatenate(
        [
            lax.dot_general(
                left[:, :, layer * rank : (layer + 1) * rank],
                right[:, :, layer * rank : (layer + 1) * rank],
                (((1,), (1,)), ((0,), (0,))),
                precision=lax.Precision.HIGHEST,
                preferred_element_type=jnp.float32,
            )
            for layer in range(2)
        ],
        axis=1,
    )


def slabs_of(sums, n):
    count, height, rank = sums.shape
    return lax.optimization_barrier(sums.reshape(count, n, height // n, rank).transpose(1, 0, 2, 3))


def put(whole, piece, index):
    return lax.dynamic_update_slice(whole, piece[None], (index,) + (jnp.int32(0),) * piece.ndim)


def take(whole, index):
    return lax.dynamic_index_in_dim(whole, index, axis=0, keepdims=False)


def gathered(hidden, w_kv, grad_kv, proj_in, proj_out):
    n = lax.axis_size("mp")
    rank = proj_out.shape[2]
    whole = lax.all_gather(grad_kv, "mp", axis=0, tiled=True)
    input_grad = times_width(whole, w_kv)
    low_in = jnp.dot(hidden, proj_in, preferred_element_type=jnp.float32)
    sums = slabs_of(sequence_sums(low_in, jnp.dot(whole, block_diagonal(proj_out), preferred_element_type=jnp.float32), rank), n)
    features = lax.psum_scatter(sums, "mp", scatter_dimension=0, tiled=False)
    return features, lambda scores: scores, lambda: input_grad


def line_of_four(hidden, w_kv, grad_kv, proj_in, proj_out):
    rank = proj_out.shape[2]
    local_rows = grad_kv.shape[0]
    cut = local_rows * 5 // 8 // 16 * 16
    me = lax.axis_index("mp")
    middle = (me == 1) | (me == 2)
    exchange_pairs = [(0, 1), (1, 0), (2, 3), (3, 2)]
    across = [(1, 2), (2, 1)]
    outward = [(1, 0), (2, 3)]
    inward = [(0, 1), (3, 2)]
    tied = lax.optimization_barrier

    def pieces(rows):
        return [rows[:cut], rows[cut:]]

    def low_rank(rows):
        return jnp.dot(rows, proj_both, preferred_element_type=jnp.float32)

    beside = lax.ppermute(grad_kv, "mp", exchange_pairs)
    facing = [lax.ppermute(part, "mp", across) for part in pieces(grad_kv)]
    proj_both = tied(block_diagonal(proj_out))
    own_low = low_rank(grad_kv)
    low_in = jnp.dot(hidden, proj_in, preferred_element_type=jnp.float32)

    facing[0], own_low, low_in = tied((facing[0], own_low, low_in))
    second = [lax.ppermute(facing[0], "mp", outward)]
    far_low = lax.ppermute(own_low, "mp", [(3, 1), (0, 2)])
    low_in_beside = lax.ppermute(low_in, "mp", inward)
    output = put_rows(me, 0, None, [grad_kv], [grad_kv], w_kv, local_rows)

    beside, facing[1], output = tied((beside, facing[1], output))
    second.append(lax.ppermute(facing[1], "mp", outward))
    beside_across = [lax.ppermute(part, "mp", across) for part in pieces(beside)]
    output = put_rows(me, 1, output, [beside], [beside], w_kv, local_rows)

    beside_across[0], second[0], far_low, low_in_beside, output = tied(
        (beside_across[0], second[0], far_low, low_in_beside, output)
    )
    third = [lax.ppermute(beside_across[0], "mp", outward)]

    beside_low = low_rank(beside)
    facing_low = jnp.concatenate([low_rank(part) for part in facing], axis=0)
    if low_in.shape[0] == SEQ:
        slabs = token_sums(me, low_in, low_in_beside, own_low, beside_low, facing_low, far_low, rank)[:, None]
    else:
        low_out = jnp.zeros((4, local_rows, 2 * rank), jnp.float32)
        for away, rows in ((0, own_low), (1, beside_low), (3, facing_low), (2, far_low)):
            low_out = put(low_out, rows, me ^ away)
        sums = sequence_sums(low_in + low_in_beside, low_out.reshape(4 * local_rows, 2 * rank), rank)
        slabs = slabs_of(sums, 4)
    slabs_across = lax.ppermute(slabs, "mp", across)

    beside_across[1], second[1], slabs_across = tied((beside_across[1], second[1], slabs_across))
    third.append(lax.ppermute(beside_across[1], "mp", outward))
    slabs = slabs + slabs_across
    mine = lax.ppermute(take(slabs, me ^ 2), "mp", [(2, 0), (1, 3)])
    mine = jnp.where(middle, take(slabs, me), mine)
    output = put_rows(me, 2, output, facing, second, w_kv, local_rows)

    def finish(scores):
        return tied((scores, third[0], output))[0]

    def rest():
        done = output
        for part in range(2):
            done = put_rows(me, 3, done, [beside_across[part]], [third[part]], w_kv, local_rows, part * cut)
        return done.reshape(4 * local_rows, w_kv.shape[0])

    return mine, finish, rest


def on_device(hidden, w_kv, grad_kv, proj_in, proj_out, queries):
    n = lax.axis_size("mp")
    me = lax.axis_index("mp")
    mine, finish, rest = (line_of_four if n == 4 else gathered)(hidden, w_kv, grad_kv, proj_in, proj_out)
    count = mine.shape[0]

    shards = lax.axis_size("dp")
    shard = lax.axis_index("dp")
    block_rows = queries.shape[0]
    mine = mine.reshape(count, queries.shape[1])
    all_features = [mine] + [
        lax.ppermute(mine, "dp", [(source, (source + step) % shards) for source in range(shards)])
        for step in range(1, shards)
    ]
    terms = jnp.concatenate(three_terms(jnp.concatenate(all_features, axis=0)), axis=0)
    products = lax.dot_general(
        terms, queries, (((1,), (1,)), ((), ())), preferred_element_type=jnp.float32
    ).reshape(3, shards, count, block_rows)
    partial_scores = finish(products[0] + (products[1] + products[2]))

    total = jnp.zeros((count, shards * block_rows), jnp.float32)
    for step in range(shards):
        back = partial_scores[step]
        if step > 0:
            back = lax.ppermute(back, "dp", [(source, (source - step) % shards) for source in range(shards)])
        total = lax.dynamic_update_slice(
            total, back, (jnp.int32(0), (shard + step) % shards * block_rows)
        )
    out_columns = shards * block_rows // n

    def columns_of(index):
        return lax.dynamic_slice(total, (jnp.int32(0), index * out_columns), (count, out_columns))

    if n == 4:
        pairs = [(source, source ^ 3) for source in range(n)]
        away = lax.ppermute(jnp.concatenate([columns_of(me ^ 3), columns_of(me ^ 1)], axis=0), "mp", pairs)
        kept = columns_of(me ^ 2) + away[count:]
        scores = columns_of(me) + away[:count]
        scores = scores + lax.ppermute(kept, "mp", [(source, source ^ 2) for source in range(n)])
    else:
        scores = columns_of(me)
        for step in range(1, n):
            scores = scores + lax.ppermute(
                columns_of((me + step) % n), "mp", [(source, (source + step) % n) for source in range(n)]
            )
    return (rest(), scores)


def solution(mesh):
    in_specs = (
        P(("groups", "dp"), "mp"),
        P("mp", None),
        P(("groups", "dp", "mp"), None),
        P("mp", None),
        P(),
        P("dp", "mp"),
    )
    out_specs = (P(("groups", "dp"), "mp"), P(("groups", "dp"), "mp"))
    return jax.shard_map(
        on_device, mesh=mesh, in_specs=in_specs, out_specs=out_specs, check_vma=False
    )
```

time: 120 us -> 123 us (1.025)
  Pallas kernels: 38.3 us -> 24.7 us
  local copies, waits for them, and re-layouts: 10.6 us -> 21.9 us
  matrix products: 3.12 us -> 7.57 us
  waiting for transfers between devices: 28.7 us -> 31.2 us
    pallas_call x5, Pallas kernels: 35.2 us -> 24 us  [put_rows(): pl.pallas_call(functools.partial(rows_kernel, block, start, count), in_sp...]
    ppermute x1, waiting for transfers between devices: 8.92 us -> 0.01 us  [line_of_four(): low_in_beside = lax.ppermute(low_in, 'mp', inward)]
    ppermute x1, starting transfers between devices: 10.1 us -> 1.3 us  [line_of_four(): far_low = lax.ppermute(own_low, 'mp', [(3, 1), (0, 2)])]
    ppermute x8 -> x10, waiting for transfers between devices: 12 us -> 19.4 us  [the longest x1 12.1 us: line_of_four(): mine = lax.ppermute(take(slabs, me ^ 2), 'mp', [(2, 0), (1, 3)])]
    ppermute x1, starting transfers between devices: 6.33 us -> 12.8 us  [line_of_four(): low_in_beside = lax.ppermute(low_in, 'mp', inward)]
    slice x3 -> x4, local copies, waits for them, and re-layouts: 1.1 us -> 6.67 us  [pieces(): return [rows[:cut], rows[cut:]]]
    dot_general x1 -> x4, matrix products: 0.43 us -> 5.68 us  [low_rank(): return jnp.dot(rows, proj_both, preferred_element_type=jnp.float32)]
    unnamed x20 -> x30, local copies, waits for them, and re-layouts: 9.39 us -> 14.1 us
  transfers between devices with their start and end apart: 19 -> 21, of which waited for: 6 -> 7; matrix products, arithmetic and copies ran while one was open for 5% -> 13% of each run, Pallas kernels for 32% -> 20%
where the time goes in v6:
time: 123 us; the launch traced here: 122 us
  starting transfers between devices  34.6 us (28%)
  waiting for transfers between devices  31.2 us (25%)
  Pallas kernels  24.7 us (20%)
  local copies, waits for them, and re-layouts  21.9 us (18%)
  matrix products  7.57 us (6%)
  other arithmetic  1.45 us (1%)
    pallas_call x5, Pallas kernels, put_rows(): pl.pallas_call(functools.partial(rows_kernel, block, start, count), in_sp...  24 us
    unnamed x30, local copies, waits for them, and re-layouts  14.1 us
    ppermute x1, starting transfers between devices, line_of_four(): low_in_beside = lax.ppermute(low_in, 'mp', inward)  12.8 us
    ppermute x1, waiting for transfers between devices, line_of_four(): mine = lax.ppermute(take(slabs, me ^ 2), 'mp', [(2, 0), (1, 3)])  12.1 us
    ppermute x1, waiting for transfers between devices, line_of_four(): third = [lax.ppermute(beside_across[0], 'mp', outward)]  7.31 us
    slice x4, local copies, waits for them, and re-layouts, pieces(): return [rows[:cut], rows[cut:]]  6.67 us
    dot_general x4, matrix products, low_rank(): return jnp.dot(rows, proj_both, preferred_element_type=jnp.float32)  5.68 us
    ppermute x1, waiting for transfers between devices, on_device(): lax.ppermute(jnp.concatenate([columns_of(me ^ 3), columns_of(me ^ 1)], ax...  3.38 us
  transfers between devices with their start and end apart: 21, of which 7 were waited for; matrix products, arithmetic and copies ran while one was open for 13% of the time, Pallas kernels for 20%

profile of v6, /device:TPU:0, one launch (start us, length us, event | category | flops | bytes accessed | tf_op | source)
XLA Modules:
  0.0 122.5 jit_solution(14933547780718321074)
XLA Ops:
  0.6 0.0 copy-start
  0.6 0.0 copy-start.5
  0.7 3.1 %collective-permute-start = (bf16[256,2048]{1,0:T(8,128)(2,1)}, bf16[256,2048]{1,0:T(8,128)(2,1)}, u32[]{:S(2)}, u32[]{:S(2)}) collective-permute-start(bf16[256,2048]{1,0:T(8,128)(2,1)} %refs_1_.1), channel_id=1, source_target_pairs={{0,1},{1,0},{2,3},{3,2},{4,5},{5,4},{6,7},{7,6},{8,9},{9,8},{10,11... | collective-permute-start | bytes 3145736 | tf_op jit(solution)/shard_map/ppermute | solution.py:217
  3.7 1.8 %slice.48 = bf16[96,2048]{1,0:T(8,128)(2,1)} slice(bf16[256,2048]{1,0:T(8,128)(2,1)} %refs_1_.1), slice={[160:256], [0:2048]} | slice | bytes 786432 | tf_op jit(solution)/shard_map/slice | solution.py:212
  5.5 0.7 collective-permute-start.1
  6.2 2.0 %slice.50 = bf16[160,2048]{1,0:T(8,128)(2,1)} slice(bf16[256,2048]{1,0:T(8,128)(2,1)} %refs_1_.1), slice={[0:160], [0:2048]} | slice | bytes 1310720 | tf_op jit(solution)/shard_map/slice | solution.py:212
  8.2 1.5 %collective-permute-start.4 = (bf16[160,2048]{1,0:T(8,128)(2,1)}, bf16[160,2048]{1,0:T(8,128)(2,1)}, u32[]{:S(2)}, u32[]{:S(2)}) collective-permute-start(bf16[160,2048]{1,0:T(8,128)(2,1)} %slice.50), channel_id=1, source_target_pairs={{1,2},{2,1},{5,6},{6,5},{9,10},{10,9},{13,14},{14,13},{17,18},{18,... | collective-permute-start | bytes 1966088 | tf_op jit(solution)/shard_map/ppermute | solution.py:218
  9.7 1.0 slice_bitcast_fusion.1
  10.7 0.8 copy-done.11
  11.5 2.3 %convolution_bitcast_fusion.own_low = f32[256,128]{1,0:T(8,128)} fusion(bf16[2048,128]{0,1:T(8,128)(2,1)S(1)} %fusion.2, bf16[256,2048]{1,0:T(8,128)(2,1)} %refs_1_.1), kind=kOutput, calls=%fused_computation | convolution fusion | flops 134217728 | bytes 1703936 | tf_op jit(solution)/shard_map/dot_general | solution.py:215
  13.8 3.4 %copy-done.1 = bf16[2048,2048]{1,0:T(8,128)(2,1)S(1)} copy-done((bf16[2048,2048]{1,0:T(8,128)(2,1)S(1)}, bf16[2048,2048]{1,0:T(8,128)(2,1)}, u32[]{:S(2)}) %copy-start.1) | copy-done | bytes 8388632
  17.2 4.4 %input_grad_rows.5.refs_3_ = bf16[4,256,2048]{2,1,0:T(8,128)(2,1)} custom-call(s32[1]{0:T(128)} %bitcast.me, bf16[256,2048]{1,0:T(8,128)(2,1)S(1)} %copy-done.5, bf16[256,2048]{1,0:T(8,128)(2,1)S(1)} %copy-done.5, bf16[2048,2048]{1,0:T(8,128)(2,1)S(1)} %copy-done.1), custom_call_target="tpu_custom_call" | custom-call | flops 524288 | bytes 524288 | tf_op jit(solution)/shard_map/input_grad_rows/pallas_call | solution.py:98
  21.7 0.0 copy-start.2
  21.7 1.2 %fusion.16.low_in = f32[1024,128]{1,0:T(8,128)S(1)} fusion(bf16[1024,2048]{1,0:T(8,128)(2,1)S(1)} %copy-done.13, bf16[2048,128]{1,0:T(8,128)(2,1)S(1)} %copy-done.14), kind=kOutput, calls=%fused_computation.43 | convolution fusion | flops 536870912 | bytes 5242880 | tf_op jit(solution)/shard_map/dot_general | solution.py:221
  22.9 1.6 %collective-permute-start.6 = (bf16[160,2048]{1,0:T(8,128)(2,1)}, bf16[160,2048]{1,0:T(8,128)(2,1)S(1)}, u32[]{:S(2)}, u32[]{:S(2)}) collective-permute-start(bf16[160,2048]{1,0:T(8,128)(2,1)} %collective-permute-done.4.refs_0_), channel_id=1, source_target_pairs={{1,0},{2,3},{5,4},{6,7},{9,8},{10,11},{13,12},{14,15},{17,16},{18,... | collective-permute-start | bytes 1966088 | tf_op jit(solution)/shard_map/ppermute | solution.py:224
  24.5 2.7 %collective-permute-done.refs_0_.refs_1_ = bf16[256,2048]{1,0:T(8,128)(2,1)} collective-permute-done((bf16[256,2048]{1,0:T(8,128)(2,1)}, bf16[256,2048]{1,0:T(8,128)(2,1)}, u32[]{:S(2)}, u32[]{:S(2)}) %collective-permute-start) | collective-permute-done | bytes 1048608 | tf_op jit(solution)/shard_map/ppermute | solution.py:217
  27.2 1.1 slice.53
  28.4 0.7 collective-permute-start.5
  29.1 1.4 %fusion.18 = f32[160,128]{1,0:T(8,128)S(1)} fusion(bf16[160,2048]{1,0:T(8,128)(2,1)} %collective-permute-done.4.refs_0_, bf16[2048,128]{0,1:T(8,128)(2,1)S(1)} %copy-done.12), kind=kOutput, calls=%fused_computation.45 | convolution fusion | flops 83886080 | bytes 1261568 | tf_op jit(solution)/shard_map/dot_general | solution.py:215
  30.5 12.8 %collective-permute-start.8 = (f32[1024,128]{1,0:T(8,128)S(1)}, f32[1024,128]{1,0:T(8,128)S(1)}, u32[]{:S(2)}, u32[]{:S(2)}) collective-permute-start(f32[1024,128]{1,0:T(8,128)S(1)} %fusion.16.low_in), channel_id=1, source_target_pairs={{0,1},{3,2},{4,5},{7,6},{8,9},{11,10},{12,13},{15,14},{16,17},{19,... | collective-permute-start | bytes 1572872 | tf_op jit(solution)/shard_map/ppermute | solution.py:226
  43.3 1.3 %collective-permute-start.7 = (f32[256,128]{1,0:T(8,128)S(1)}, f32[256,128]{1,0:T(8,128)S(1)}, u32[]{:S(2)}, u32[]{:S(2)}) collective-permute-start(f32[256,128]{1,0:T(8,128)S(1)} %copy-done.10), channel_id=1, source_target_pairs={{3,1},{0,2},{7,5},{4,6},{11,9},{8,10},{15,13},{12,14},{19,17},{16,... | collective-permute-start | bytes 393224 | tf_op jit(solution)/shard_map/ppermute | solution.py:225
  44.6 1.8 %slice.49 = bf16[96,2048]{1,0:T(8,128)(2,1)} slice(bf16[256,2048]{1,0:T(8,128)(2,1)} %collective-permute-done.refs_0_.refs_1_), slice={[160:256], [0:2048]} | slice | bytes 786432 | tf_op jit(solution)/shard_map/slice | solution.py:212
  46.4 1.3 %collective-permute-start.3 = (bf16[96,2048]{1,0:T(8,128)(2,1)S(1)}, bf16[96,2048]{1,0:T(8,128)(2,1)}, u32[]{:S(2)}, u32[]{:S(2)}) collective-permute-start(bf16[96,2048]{1,0:T(8,128)(2,1)S(1)} %collective-permute-done.1.refs_1_), channel_id=1, source_target_pairs={{1,0},{2,3},{5,4},{6,7},{9,8},{10,11},{13,12},{14,15},{17,16},{18,... | collective-permute-start | bytes 1179656 | tf_op jit(solution)/shard_map/ppermute | solution.py:230
  47.7 5.0 %input_grad_rows.6.refs_5_ = bf16[4,256,2048]{2,1,0:T(8,128)(2,1)} custom-call(s32[1]{0:T(128)} %bitcast.me, bf16[256,2048]{1,0:T(8,128)(2,1)} %collective-permute-done.refs_0_.refs_1_, bf16[256,2048]{1,0:T(8,128)(2,1)} %collective-permute-done.refs_0_.refs_1_, bf16[2048,2048]{1,0:T(8,128)(2,1)S(1)} %copy-done.2, ...), custom_call_target="tpu_custom_call", output_to_operand_aliasing={{}: (4, {})} | custom-call | flops 524288 | bytes 524288 | tf_op jit(solution)/shard_map/input_grad_rows/pallas_call | solution.py:98
  52.7 0.3 fusion.19
  53.0 2.8 %collective-permute-done.7.far_low = f32[256,128]{1,0:T(8,128)S(1)} collective-permute-done((f32[256,128]{1,0:T(8,128)S(1)}, f32[256,128]{1,0:T(8,128)S(1)}, u32[]{:S(2)}, u32[]{:S(2)}) %collective-permute-start.7) | collective-permute-done | bytes 131104 | tf_op jit(solution)/shard_map/ppermute | solution.py:225
  55.8 1.4 %collective-permute-start.2 = (bf16[96,2048]{1,0:T(8,128)(2,1)}, bf16[96,2048]{1,0:T(8,128)(2,1)}, u32[]{:S(2)}, u32[]{:S(2)}) collective-permute-start(bf16[96,2048]{1,0:T(8,128)(2,1)} %slice.49), channel_id=1, source_target_pairs={{1,2},{2,1},{5,6},{6,5},{9,10},{10,9},{13,14},{14,13},{17,18},{18,... | collective-permute-start | bytes 1179656 | tf_op jit(solution)/shard_map/ppermute | solution.py:231
  57.2 1.7 %fusion.17.beside_low = f32[256,128]{1,0:T(8,128)S(1)} fusion(bf16[256,2048]{1,0:T(8,128)(2,1)} %collective-permute-done.refs_0_.refs_1_, bf16[2048,128]{0,1:T(8,128)(2,1)S(1)} %copy-done.12), kind=kOutput, calls=%fused_computation.44 | convolution fusion | flops 134217728 | bytes 1703936 | tf_op jit(solution)/shard_map/dot_general | solution.py:215
  58.9 0.0 collective-permute-done.6.refs_2_
  58.9 0.0 collective-permute-done.5.refs_0_
  58.9 0.7 token_sums.1
  59.6 0.1 copy-done.6
  59.7 0.7 collective-permute-start.9
  60.4 0.0 collective-permute-done.2.refs_0_
  60.4 0.0 collective-permute-done.9
  60.5 1.3 %collective-permute-start.12 = (f32[1,32,64]{2,1,0:T(8,128)S(1)}, f32[1,32,64]{2,1,0:T(8,128)S(1)}, u32[]{:S(2)}, u32[]{:S(2)}) collective-permute-start(f32[1,32,64]{2,1,0:T(8,128)S(1)} %dynamic-slice_bitcast_fusion), channel_id=1, source_target_pairs={{2,0},{1,3},{6,4},{5,7},{10,8},{9,11},{14,12},{13,15},{18,16},{17,... | collective-permute-start | bytes 24584 | tf_op jit(solution)/shard_map/ppermute | solution.py:254
  61.8 12.1 %collective-permute-done.12 = f32[1,32,64]{2,1,0:T(8,128)S(1)} collective-permute-done((f32[1,32,64]{2,1,0:T(8,128)S(1)}, f32[1,32,64]{2,1,0:T(8,128)S(1)}, u32[]{:S(2)}, u32[]{:S(2)}) %collective-permute-start.12) | collective-permute-done | bytes 8224 | tf_op jit(solution)/shard_map/ppermute | solution.py:254
  73.8 0.1 reshape.29
  73.9 0.0 collective-permute-start.13
  73.9 1.5 %collective-permute-start.14 = (f32[1,2048]{1,0:T(1,128)S(1)}, f32[1,2048]{1,0:T(1,128)}, u32[]{:S(2)}, u32[]{:S(2)}) collective-permute-start(f32[1,2048]{1,0:T(1,128)S(1)} %reshape.29), channel_id=1, source_target_pairs={{0,8},{4,12},{8,0},{12,4},{1,9},{5,13},{9,1},{13,5},{2,10},{6,14},... | collective-permute-start | bytes 24584 | tf_op jit(solution)/shard_map/ppermute | solution.py:281
  75.5 1.4 %collective-permute-start.15 = (f32[1,2048]{1,0:T(1,128)S(1)}, f32[1,2048]{1,0:T(1,128)}, u32[]{:S(2)}, u32[]{:S(2)}) collective-permute-start(f32[1,2048]{1,0:T(1,128)S(1)} %reshape.29), channel_id=1, source_target_pairs={{0,12},{4,0},{8,4},{12,8},{1,13},{5,1},{9,5},{13,9},{2,14},{6,2},{... | collective-permute-start | bytes 24584 | tf_op jit(solution)/shard_map/ppermute | solution.py:281
  76.9 1.3 %collective-permute-start.11 = (bf16[160,2048]{1,0:T(8,128)(2,1)}, bf16[160,2048]{1,0:T(8,128)(2,1)S(1)}, u32[]{:S(2)}, u32[]{:S(2)}) collective-permute-start(bf16[160,2048]{1,0:T(8,128)(2,1)} %copy-done.6), channel_id=1, source_target_pairs={{1,0},{2,3},{5,4},{6,7},{9,8},{10,11},{13,12},{14,15},{17,16},{18,... | collective-permute-start | bytes 1966088 | tf_op jit(solution)/shard_map/ppermute | solution.py:237
  78.2 1.3 %collective-permute-start.10 = (bf16[96,2048]{1,0:T(8,128)(2,1)}, bf16[96,2048]{1,0:T(8,128)(2,1)S(1)}, u32[]{:S(2)}, u32[]{:S(2)}) collective-permute-start(bf16[96,2048]{1,0:T(8,128)(2,1)} %collective-permute-done.2.refs_0_), channel_id=1, source_target_pairs={{1,0},{2,3},{5,4},{6,7},{9,8},{10,11},{13,12},{14,15},{17,16},{18,... | collective-permute-start | bytes 1179656 | tf_op jit(solution)/shard_map/ppermute | solution.py:252
  79.5 0.0 copy-start.3
  79.5 3.4 %copy-done.3 = bf16[2048,2048]{1,0:T(8,128)(2,1)S(1)} copy-done((bf16[2048,2048]{1,0:T(8,128)(2,1)S(1)}, bf16[2048,2048]{1,0:T(8,128)(2,1)}, u32[]{:S(2)}) %copy-start.3) | copy-done | bytes 8388632
  82.9 5.0 %input_grad_rows.7.refs_3_ = bf16[4,256,2048]{2,1,0:T(8,128)(2,1)} custom-call(s32[1]{0:T(128)} %bitcast.me, bf16[160,2048]{1,0:T(8,128)(2,1)} %collective-permute-done.4.refs_0_, bf16[96,2048]{1,0:T(8,128)(2,1)S(1)} %collective-permute-done.1.refs_1_, bf16[160,2048]{1,0:T(8,128)(2,1)S(1)} %collective-permute-done.6.refs_2_, ...), custom_call_target="tpu_custom_call", output_to_operand_aliasing={{}: (6, {})} | custom-call | flops 524288 | bytes 524288 | tf_op jit(solution)/shard_map/input_grad_rows/pallas_call | solution.py:98
  87.9 0.0 collective-permute-done.14
  87.9 0.8 reduce-precision_convert_fusion.1
  88.7 0.6 fusion.3
  89.3 7.3 %collective-permute-done.11.refs_1_ = bf16[160,2048]{1,0:T(8,128)(2,1)S(1)} collective-permute-done((bf16[160,2048]{1,0:T(8,128)(2,1)}, bf16[160,2048]{1,0:T(8,128)(2,1)S(1)}, u32[]{:S(2)}, u32[]{:S(2)}) %collective-permute-start.11) | collective-permute-done | bytes 655392 | tf_op jit(solution)/shard_map/ppermute | solution.py:237
  96.6 0.9 copy-done.8
  97.5 0.6 collective-permute-start.17
  98.1 0.2 collective-permute-start.18
  98.3 0.6 collective-permute-done.16
  98.8 2.3 %collective-permute-done.17 = f32[1,512]{1,0:T(1,128)S(1)} collective-permute-done((f32[1,512]{1,0:T(1,128)S(1)}, f32[1,512]{1,0:T(1,128)S(1)}, u32[]{:S(2)}, u32[]{:S(2)}) %collective-permute-start.17) | collective-permute-done | bytes 2080 | tf_op jit(solution)/shard_map/ppermute | solution.py:294
  101.2 2.1 %collective-permute-start.19 = (f32[2,512]{1,0:T(2,128)S(1)}, f32[2,512]{1,0:T(2,128)S(1)}, u32[]{:S(2)}, u32[]{:S(2)}) collective-permute-start(f32[2,512]{1,0:T(2,128)S(1)} %pad_maximum_fusion.2), channel_id=1, source_target_pairs={{0,3},{1,2},{2,1},{3,0},{4,7},{5,6},{6,5},{7,4},{8,11},{9,10},{10,... | collective-permute-start | bytes 12296 | tf_op jit(solution)/shard_map/ppermute | solution.py:305
  103.3 3.4 %collective-permute-done.19 = f32[2,512]{1,0:T(2,128)S(1)} collective-permute-done((f32[2,512]{1,0:T(2,128)S(1)}, f32[2,512]{1,0:T(2,128)S(1)}, u32[]{:S(2)}, u32[]{:S(2)}) %collective-permute-start.19) | collective-permute-done | bytes 4128 | tf_op jit(solution)/shard_map/ppermute | solution.py:305
  106.7 0.0 copy-start.4
  106.7 3.4 %copy-done.4 = bf16[2048,2048]{1,0:T(8,128)(2,1)S(1)} copy-done((bf16[2048,2048]{1,0:T(8,128)(2,1)S(1)}, bf16[2048,2048]{1,0:T(8,128)(2,1)}, u32[]{:S(2)}) %copy-start.4) | copy-done | bytes 8388632
  110.1 1.1 copy-done.7
  111.2 1.1 copy-done.9
  112.3 4.9 %input_grad_rows.8.refs_3_ = bf16[4,256,2048]{2,1,0:T(8,128)(2,1)} custom-call(s32[1]{0:T(128)} %bitcast.me, bf16[160,2048]{1,0:T(8,128)(2,1)S(1)} %copy-done.7, bf16[160,2048]{1,0:T(8,128)(2,1)S(1)} %copy-done.9, bf16[2048,2048]{1,0:T(8,128)(2,1)S(1)} %copy-done.4, bf16[4,256,2048]{2,1,0:T(8,128)(2,1)} %input_grad_rows.7.refs_3_), custom_call_target="tpu_custom_call", output_to_operand_aliasing={{}: (4, {})} | custom-call | flops 327680 | bytes 327680 | tf_op jit(solution)/shard_map/input_grad_rows/pallas_call | solution.py:98
  117.2 4.6 %input_grad_rows.9 = bf16[4,256,2048]{2,1,0:T(8,128)(2,1)} custom-call(s32[1]{0:T(128)} %bitcast.me, bf16[96,2048]{1,0:T(8,128)(2,1)} %collective-permute-done.2.refs_0_, bf16[96,2048]{1,0:T(8,128)(2,1)S(1)} %collective-permute-done.10.refs_1_, bf16[2048,2048]{1,0:T(8,128)(2,1)S(1)} %copy-done.4, ...), custom_call_target="tpu_custom_call", output_to_operand_aliasing={{}: (4, {})} | custom-call | flops 196608 | bytes 196608 | tf_op jit(solution)/shard_map/input_grad_rows/pallas_call | solution.py:98
  121.9 0.6 fusion.13
  (43 shorter events, 0.2 us)
Async XLA Ops:
  0.6 88.0 %copy-start = (bf16[512,2048]{1,0:T(8,128)(2,1)S(1)}, bf16[512,2048]{1,0:T(8,128)(2,1)}, u32[]{:S(2)}) copy-start(bf16[512,2048]{1,0:T(8,128)(2,1)} %param.11) | copy-start | bytes 6291460
  0.6 13.2 %copy-start.5 = (bf16[256,2048]{1,0:T(8,128)(2,1)S(1)}, bf16[256,2048]{1,0:T(8,128)(2,1)}, u32[]{:S(2)}) copy-start(bf16[256,2048]{1,0:T(8,128)(2,1)} %refs_1_.1) | copy-start | bytes 3145732
  0.7 26.6 %collective-permute-start = (bf16[256,2048]{1,0:T(8,128)(2,1)}, bf16[256,2048]{1,0:T(8,128)(2,1)}, u32[]{:S(2)}, u32[]{:S(2)}) collective-permute-start(bf16[256,2048]{1,0:T(8,128)(2,1)} %refs_1_.1), channel_id=1, source_target_pairs={{0,1},{1,0},{2,3},{3,2},{4,5},{5,4},{6,7},{7,6},{8,9},{9,8},{10,11... | collective-permute-start | bytes 3145736 | tf_op jit(solution)/shard_map/ppermute | solution.py:217
  5.5 19.0 %collective-permute-start.1 = (bf16[96,2048]{1,0:T(8,128)(2,1)}, bf16[96,2048]{1,0:T(8,128)(2,1)S(1)}, u32[]{:S(2)}, u32[]{:S(2)}) collective-permute-start(bf16[96,2048]{1,0:T(8,128)(2,1)} %slice.48), channel_id=1, source_target_pairs={{1,2},{2,1},{5,6},{6,5},{9,10},{10,9},{13,14},{14,13},{17,18},{18,... | collective-permute-start | bytes 1179656 | tf_op jit(solution)/shard_map/ppermute | solution.py:218
  8.2 14.7 %collective-permute-start.4 = (bf16[160,2048]{1,0:T(8,128)(2,1)}, bf16[160,2048]{1,0:T(8,128)(2,1)}, u32[]{:S(2)}, u32[]{:S(2)}) collective-permute-start(bf16[160,2048]{1,0:T(8,128)(2,1)} %slice.50), channel_id=1, source_target_pairs={{1,2},{2,1},{5,6},{6,5},{9,10},{10,9},{13,14},{14,13},{17,18},{18,... | collective-permute-start | bytes 1966088 | tf_op jit(solution)/shard_map/ppermute | solution.py:218
  10.7 0.8 copy-start.11
  13.8 3.4 %copy-start.1 = (bf16[2048,2048]{1,0:T(8,128)(2,1)S(1)}, bf16[2048,2048]{1,0:T(8,128)(2,1)}, u32[]{:S(2)}) copy-start(bf16[2048,2048]{1,0:T(8,128)(2,1)} %refs_2_.7) | copy-start | bytes 25165828
  17.2 4.4 %copy-start.13 = (bf16[1024,2048]{1,0:T(8,128)(2,1)S(1)}, bf16[1024,2048]{1,0:T(8,128)(2,1)}, u32[]{:S(2)}) copy-start(bf16[1024,2048]{1,0:T(8,128)(2,1)} %param.6) | copy-start | bytes 12582916
  17.2 4.4 %copy-start.14 = (bf16[2048,128]{1,0:T(8,128)(2,1)S(1)}, bf16[2048,128]{1,0:T(8,128)(2,1)}, u32[]{:S(2)}) copy-start(bf16[2048,128]{1,0:T(8,128)(2,1)} %param.9) | copy-start | bytes 1572868
  17.2 11.9 %copy-start.12 = (bf16[2048,128]{0,1:T(8,128)(2,1)S(1)}, bf16[2048,128]{0,1:T(8,128)(2,1)}, u32[]{:S(2)}) copy-start(bf16[2048,128]{0,1:T(8,128)(2,1)} %copy-done.11) | copy-start | bytes 1572868
  21.7 21.6 %copy-start.10 = (f32[256,128]{1,0:T(8,128)S(1)}, f32[256,128]{1,0:T(8,128)}, u32[]{:S(2)}) copy-start(f32[256,128]{1,0:T(8,128)} %convolution_bitcast_fusion.own_low) | copy-start | bytes 393220
  21.7 26.0 %copy-start.2 = (bf16[2048,2048]{1,0:T(8,128)(2,1)S(1)}, bf16[2048,2048]{1,0:T(8,128)(2,1)}, u32[]{:S(2)}) copy-start(bf16[2048,2048]{1,0:T(8,128)(2,1)} %refs_2_.7) | copy-start | bytes 25165828
  22.9 35.9 %collective-permute-start.6 = (bf16[160,2048]{1,0:T(8,128)(2,1)}, bf16[160,2048]{1,0:T(8,128)(2,1)S(1)}, u32[]{:S(2)}, u32[]{:S(2)}) collective-permute-start(bf16[160,2048]{1,0:T(8,128)(2,1)} %collective-permute-done.4.refs_0_), channel_id=1, source_target_pairs={{1,0},{2,3},{5,4},{6,7},{9,8},{10,11},{13,12},{14,15},{17,16},{18,... | collective-permute-start | bytes 1966088 | tf_op jit(solution)/shard_map/ppermute | solution.py:224
  28.4 30.5 %collective-permute-start.5 = (bf16[160,2048]{1,0:T(8,128)(2,1)S(1)}, bf16[160,2048]{1,0:T(8,128)(2,1)S(1)}, u32[]{:S(2)}, u32[]{:S(2)}) collective-permute-start(bf16[160,2048]{1,0:T(8,128)(2,1)S(1)} %slice.53), channel_id=1, source_target_pairs={{1,2},{2,1},{5,6},{6,5},{9,10},{10,9},{13,14},{14,13},{17,18},{18,... | collective-permute-start | bytes 1966088 | tf_op jit(solution)/shard_map/ppermute | solution.py:231
  30.5 28.3 %collective-permute-start.8 = (f32[1024,128]{1,0:T(8,128)S(1)}, f32[1024,128]{1,0:T(8,128)S(1)}, u32[]{:S(2)}, u32[]{:S(2)}) collective-permute-start(f32[1024,128]{1,0:T(8,128)S(1)} %fusion.16.low_in), channel_id=1, source_target_pairs={{0,1},{3,2},{4,5},{7,6},{8,9},{11,10},{12,13},{15,14},{16,17},{19,... | collective-permute-start | bytes 1572872 | tf_op jit(solution)/shard_map/ppermute | solution.py:226
  43.3 12.5 %collective-permute-start.7 = (f32[256,128]{1,0:T(8,128)S(1)}, f32[256,128]{1,0:T(8,128)S(1)}, u32[]{:S(2)}, u32[]{:S(2)}) collective-permute-start(f32[256,128]{1,0:T(8,128)S(1)} %copy-done.10), channel_id=1, source_target_pairs={{3,1},{0,2},{7,5},{4,6},{11,9},{8,10},{15,13},{12,14},{19,17},{16,... | collective-permute-start | bytes 393224 | tf_op jit(solution)/shard_map/ppermute | solution.py:225
  46.4 14.0 %collective-permute-start.3 = (bf16[96,2048]{1,0:T(8,128)(2,1)S(1)}, bf16[96,2048]{1,0:T(8,128)(2,1)}, u32[]{:S(2)}, u32[]{:S(2)}) collective-permute-start(bf16[96,2048]{1,0:T(8,128)(2,1)S(1)} %collective-permute-done.1.refs_1_), channel_id=1, source_target_pairs={{1,0},{2,3},{5,4},{6,7},{9,8},{10,11},{13,12},{14,15},{17,16},{18,... | collective-permute-start | bytes 1179656 | tf_op jit(solution)/shard_map/ppermute | solution.py:230
  55.8 4.6 %collective-permute-start.2 = (bf16[96,2048]{1,0:T(8,128)(2,1)}, bf16[96,2048]{1,0:T(8,128)(2,1)}, u32[]{:S(2)}, u32[]{:S(2)}) collective-permute-start(bf16[96,2048]{1,0:T(8,128)(2,1)} %slice.49), channel_id=1, source_target_pairs={{1,2},{2,1},{5,6},{6,5},{9,10},{10,9},{13,14},{14,13},{17,18},{18,... | collective-permute-start | bytes 1179656 | tf_op jit(solution)/shard_map/ppermute | solution.py:231
  58.9 0.9 copy-start.6
  59.7 0.7 collective-permute-start.9
  60.5 13.4 %collective-permute-start.12 = (f32[1,32,64]{2,1,0:T(8,128)S(1)}, f32[1,32,64]{2,1,0:T(8,128)S(1)}, u32[]{:S(2)}, u32[]{:S(2)}) collective-permute-start(f32[1,32,64]{2,1,0:T(8,128)S(1)} %dynamic-slice_bitcast_fusion), channel_id=1, source_target_pairs={{2,0},{1,3},{6,4},{5,7},{10,8},{9,11},{14,12},{13,15},{18,16},{17,... | collective-permute-start | bytes 24584 | tf_op jit(solution)/shard_map/ppermute | solution.py:254
  73.9 13.9 %collective-permute-start.13 = (f32[1,2048]{1,0:T(1,128)S(1)}, f32[1,2048]{1,0:T(1,128)S(1)}, u32[]{:S(2)}, u32[]{:S(2)}) collective-permute-start(f32[1,2048]{1,0:T(1,128)S(1)} %reshape.29), channel_id=1, source_target_pairs={{0,4},{4,8},{8,12},{12,0},{1,5},{5,9},{9,13},{13,1},{2,6},{6,10},{... | collective-permute-start | bytes 24584 | tf_op jit(solution)/shard_map/ppermute | solution.py:281
  73.9 13.9 %collective-permute-start.14 = (f32[1,2048]{1,0:T(1,128)S(1)}, f32[1,2048]{1,0:T(1,128)}, u32[]{:S(2)}, u32[]{:S(2)}) collective-permute-start(f32[1,2048]{1,0:T(1,128)S(1)} %reshape.29), channel_id=1, source_target_pairs={{0,8},{4,12},{8,0},{12,4},{1,9},{5,13},{9,1},{13,5},{2,10},{6,14},... | collective-permute-start | bytes 24584 | tf_op jit(solution)/shard_map/ppermute | solution.py:281
  75.5 12.4 %collective-permute-start.15 = (f32[1,2048]{1,0:T(1,128)S(1)}, f32[1,2048]{1,0:T(1,128)}, u32[]{:S(2)}, u32[]{:S(2)}) collective-permute-start(f32[1,2048]{1,0:T(1,128)S(1)} %reshape.29), channel_id=1, source_target_pairs={{0,12},{4,0},{8,4},{12,8},{1,13},{5,1},{9,5},{13,9},{2,14},{6,2},{... | collective-permute-start | bytes 24584 | tf_op jit(solution)/shard_map/ppermute | solution.py:281
  76.9 19.8 %collective-permute-start.11 = (bf16[160,2048]{1,0:T(8,128)(2,1)}, bf16[160,2048]{1,0:T(8,128)(2,1)S(1)}, u32[]{:S(2)}, u32[]{:S(2)}) collective-permute-start(bf16[160,2048]{1,0:T(8,128)(2,1)} %copy-done.6), channel_id=1, source_target_pairs={{1,0},{2,3},{5,4},{6,7},{9,8},{10,11},{13,12},{14,15},{17,16},{18,... | collective-permute-start | bytes 1966088 | tf_op jit(solution)/shard_map/ppermute | solution.py:237
  78.2 39.1 %collective-permute-start.10 = (bf16[96,2048]{1,0:T(8,128)(2,1)}, bf16[96,2048]{1,0:T(8,128)(2,1)S(1)}, u32[]{:S(2)}, u32[]{:S(2)}) collective-permute-start(bf16[96,2048]{1,0:T(8,128)(2,1)} %collective-permute-done.2.refs_0_), channel_id=1, source_target_pairs={{1,0},{2,3},{5,4},{6,7},{9,8},{10,11},{13,12},{14,15},{17,16},{18,... | collective-permute-start | bytes 1179656 | tf_op jit(solution)/shard_map/ppermute | solution.py:252
  79.5 3.4 %copy-start.3 = (bf16[2048,2048]{1,0:T(8,128)(2,1)S(1)}, bf16[2048,2048]{1,0:T(8,128)(2,1)}, u32[]{:S(2)}) copy-start(bf16[2048,2048]{1,0:T(8,128)(2,1)} %refs_2_.7) | copy-start | bytes 25165828
  96.6 0.9 copy-start.8
  97.5 1.3 %collective-permute-start.16 = (f32[1,512]{1,0:T(1,128)S(1)}, f32[1,512]{1,0:T(1,128)S(1)}, u32[]{:S(2)}, u32[]{:S(2)}) collective-permute-start(f32[1,512]{1,0:T(1,128)S(1)} %get-tuple-element.41), channel_id=1, source_target_pairs={{0,12},{4,0},{8,4},{12,8},{1,13},{5,1},{9,5},{13,9},{2,14},{6,2},{... | collective-permute-start | bytes 6152 | tf_op jit(solution)/shard_map/ppermute | solution.py:294
  97.5 3.7 %collective-permute-start.17 = (f32[1,512]{1,0:T(1,128)S(1)}, f32[1,512]{1,0:T(1,128)S(1)}, u32[]{:S(2)}, u32[]{:S(2)}) collective-permute-start(f32[1,512]{1,0:T(1,128)S(1)} %get-tuple-element.40), channel_id=1, source_target_pairs={{0,8},{4,12},{8,0},{12,4},{1,9},{5,13},{9,1},{13,5},{2,10},{6,14},... | collective-permute-start | bytes 6152 | tf_op jit(solution)/shard_map/ppermute | solution.py:294
  98.1 3.1 %collective-permute-start.18 = (f32[1,512]{1,0:T(1,128)S(1)}, f32[1,512]{1,0:T(1,128)S(1)}, u32[]{:S(2)}, u32[]{:S(2)}) collective-permute-start(f32[1,512]{1,0:T(1,128)S(1)} %get-tuple-element.39), channel_id=1, source_target_pairs={{0,4},{4,8},{8,12},{12,0},{1,5},{5,9},{9,13},{13,1},{2,6},{6,10},{... | collective-permute-start | bytes 6152 | tf_op jit(solution)/shard_map/ppermute | solution.py:294
  101.2 5.5 %collective-permute-start.19 = (f32[2,512]{1,0:T(2,128)S(1)}, f32[2,512]{1,0:T(2,128)S(1)}, u32[]{:S(2)}, u32[]{:S(2)}) collective-permute-start(f32[2,512]{1,0:T(2,128)S(1)} %pad_maximum_fusion.2), channel_id=1, source_target_pairs={{0,3},{1,2},{2,1},{3,0},{4,7},{5,6},{6,5},{7,4},{8,11},{9,10},{10,... | collective-permute-start | bytes 12296 | tf_op jit(solution)/shard_map/ppermute | solution.py:305
  106.7 15.2 %collective-permute-start.20 = (f32[1,512]{1,0:T(1,128)S(1)}, f32[1,512]{1,0:T(1,128)S(1)}, u32[]{:S(2)}, u32[]{:S(2)}) collective-permute-start(f32[1,512]{1,0:T(1,128)S(1)} %fusion.14), channel_id=1, source_target_pairs={{0,2},{1,3},{2,0},{3,1},{4,6},{5,7},{6,4},{7,5},{8,10},{9,11},{10,... | collective-permute-start | bytes 6152 | tf_op jit(solution)/shard_map/ppermute | solution.py:308
  106.7 3.4 %copy-start.4 = (bf16[2048,2048]{1,0:T(8,128)(2,1)S(1)}, bf16[2048,2048]{1,0:T(8,128)(2,1)}, u32[]{:S(2)}) copy-start(bf16[2048,2048]{1,0:T(8,128)(2,1)} %refs_2_.7) | copy-start | bytes 25165828
  110.1 1.1 copy-start.7
  111.2 1.1 copy-start.9

commit v7 on v6

--- a/solution.py
+++ b/solution.py
@@ -117,7 +117,7 @@
     )(me.reshape(1).astype(jnp.int32), *firsts, *seconds, w_kv, *earlier)
 
 
-def token_sums_kernel(me, low_in, low_in_beside, own_low, beside_low, facing_low, far_low, out):
+def token_sums_kernel(me, low_in, low_in_beside, own_low, beside_low, facing_low, far_low, note, out):
     rows = own_low.shape[0]
     rank = out.shape[2]
     total = jnp.zeros((own_low.shape[1], own_low.shape[1]), jnp.float32)
@@ -141,16 +141,16 @@
         out[index] = total[index * slab : (index + 1) * slab, layer * rank : (layer + 1) * rank]
 
 
-def token_sums(me, low_in, low_in_beside, own_low, beside_low, facing_low, far_low, rank):
+def token_sums(me, low_in, low_in_beside, own_low, beside_low, facing_low, far_low, note, rank):
     whole = pl.BlockSpec(memory_space=pltpu.VMEM)
     return pl.pallas_call(
         token_sums_kernel,
-        in_specs=[pl.BlockSpec(memory_space=pltpu.SMEM)] + [whole] * 6,
+        in_specs=[pl.BlockSpec(memory_space=pltpu.SMEM)] + [whole] * 7,
         out_specs=whole,
         out_shape=jax.ShapeDtypeStruct((4, 2 * rank // 4, rank), jnp.float32),
         compiler_params=pltpu.CompilerParams(vmem_limit_bytes=GRANT),
         name="token_sums",
-    )(me.reshape(1).astype(jnp.int32), low_in, low_in_beside, own_low, beside_low, facing_low, far_low)
+    )(me.reshape(1).astype(jnp.int32), low_in, low_in_beside, own_low, beside_low, facing_low, far_low, note)
 
 
 def sequence_sums(low_in, low_out, rank):
@@ -199,7 +199,6 @@
 def line_of_four(hidden, w_kv, grad_kv, proj_in, proj_out):
     rank = proj_out.shape[2]
     local_rows = grad_kv.shape[0]
-    cut = local_rows * 5 // 8 // 16 * 16
     me = lax.axis_index("mp")
     middle = (me == 1) | (me == 2)
     exchange_pairs = [(0, 1), (1, 0), (2, 3), (3, 2)]
@@ -208,60 +207,50 @@
     inward = [(0, 1), (3, 2)]
     tied = lax.optimization_barrier
 
-    def pieces(rows):
-        return [rows[:cut], rows[cut:]]
-
     def low_rank(rows):
         return jnp.dot(rows, proj_both, preferred_element_type=jnp.float32)
 
+    facing = lax.ppermute(grad_kv, "mp", across)
     beside = lax.ppermute(grad_kv, "mp", exchange_pairs)
-    facing = [lax.ppermute(part, "mp", across) for part in pieces(grad_kv)]
     proj_both = tied(block_diagonal(proj_out))
     own_low = low_rank(grad_kv)
     low_in = jnp.dot(hidden, proj_in, preferred_element_type=jnp.float32)
-
-    facing[0], own_low, low_in = tied((facing[0], own_low, low_in))
-    second = [lax.ppermute(facing[0], "mp", outward)]
-    far_low = lax.ppermute(own_low, "mp", [(3, 1), (0, 2)])
+    output = put_rows(me, 0, None, [grad_kv], [grad_kv], w_kv, local_rows)
+
+    beside, facing, low_in, output = tied((beside, facing, low_in, output))
+    beside_across = lax.ppermute(beside, "mp", across)
+    second = lax.ppermute(facing, "mp", outward)
+    output = put_rows(me, 1, output, [beside], [beside], w_kv, local_rows)
+    low_in, output = tied((low_in, output))
     low_in_beside = lax.ppermute(low_in, "mp", inward)
-    output = put_rows(me, 0, None, [grad_kv], [grad_kv], w_kv, local_rows)
-
-    beside, facing[1], output = tied((beside, facing[1], output))
-    second.append(lax.ppermute(facing[1], "mp", outward))
-    beside_across = [lax.ppermute(part, "mp", across) for part in pieces(beside)]
-    output = put_rows(me, 1, output, [beside], [beside], w_kv, local_rows)
-
-    beside_across[0], second[0], far_low, low_in_beside, output = tied(
-        (beside_across[0], second[0], far_low, low_in_beside, output)
-    )
-    third = [lax.ppermute(beside_across[0], "mp", outward)]
 
     beside_low = low_rank(beside)
-    facing_low = jnp.concatenate([low_rank(part) for part in facing], axis=0)
+    facing_low = low_rank(facing)
+
+    beside_across, second, low_in_beside, output = tied((beside_across, second, low_in_beside, output))
+    third = lax.ppermute(beside_across, "mp", outward)
+    shards = lax.axis_size("dp")
+    note = lax.ppermute(low_in_beside[:1], "dp", [(source, (source + 1) % shards) for source in range(shards)])
+
+    far_low = low_rank(beside_across)
     if low_in.shape[0] == SEQ:
-        slabs = token_sums(me, low_in, low_in_beside, own_low, beside_low, facing_low, far_low, rank)[:, None]
+        slabs = token_sums(me, low_in, low_in_beside, own_low, beside_low, facing_low, far_low, note, rank)[:, None]
     else:
         low_out = jnp.zeros((4, local_rows, 2 * rank), jnp.float32)
         for away, rows in ((0, own_low), (1, beside_low), (3, facing_low), (2, far_low)):
             low_out = put(low_out, rows, me ^ away)
         sums = sequence_sums(low_in + low_in_beside, low_out.reshape(4 * local_rows, 2 * rank), rank)
         slabs = slabs_of(sums, 4)
-    slabs_across = lax.ppermute(slabs, "mp", across)
-
-    beside_across[1], second[1], slabs_across = tied((beside_across[1], second[1], slabs_across))
-    third.append(lax.ppermute(beside_across[1], "mp", outward))
-    slabs = slabs + slabs_across
+    slabs = slabs + lax.ppermute(slabs, "mp", across)
     mine = lax.ppermute(take(slabs, me ^ 2), "mp", [(2, 0), (1, 3)])
     mine = jnp.where(middle, take(slabs, me), mine)
-    output = put_rows(me, 2, output, facing, second, w_kv, local_rows)
+    output = put_rows(me, 2, output, [facing], [second], w_kv, local_rows)
 
     def finish(scores):
-        return tied((scores, third[0], output))[0]
+        return tied((scores, output))[0]
 
     def rest():
-        done = output
-        for part in range(2):
-            done = put_rows(me, 3, done, [beside_across[part]], [third[part]], w_kv, local_rows, part * cut)
+        done = put_rows(me, 3, output, [beside_across], [third], w_kv, local_rows)
         return done.reshape(4 * local_rows, w_kv.shape[0])
 
     return mine, finish, rest
@@ -287,6 +276,16 @@
     ).reshape(3, shards, count, block_rows)
     partial_scores = finish(products[0] + (products[1] + products[2]))
 
+    if shards == n:
+        scores = jnp.zeros((count, block_rows), jnp.float32)
+        for step in range(n):
+            pairs = [
+                (q * n + slab, (slab + step) % n * n + q) for q in range(n) for slab in range(n)
+            ]
+            row = take(partial_scores, (shard - me - step + 2 * n) % n)
+            scores = scores + lax.ppermute(row, ("dp", "mp"), pairs)
+        return (rest(), scores)
+
     total = jnp.zeros((count, shards * block_rows), jnp.float32)
     for step in range(shards):
         back = partial_scores[step]
@@ -300,18 +299,11 @@
     def columns_of(index):
         return lax.dynamic_slice(total, (jnp.int32(0), index * out_columns), (count, out_columns))
 
-    if n == 4:
-        pairs = [(source, source ^ 3) for source in range(n)]
-        away = lax.ppermute(jnp.concatenate([columns_of(me ^ 3), columns_of(me ^ 1)], axis=0), "mp", pairs)
-        kept = columns_of(me ^ 2) + away[count:]
-        scores = columns_of(me) + away[:count]
-        scores = scores + lax.ppermute(kept, "mp", [(source, source ^ 2) for source in range(n)])
-    else:
-        scores = columns_of(me)
-        for step in range(1, n):
-            scores = scores + lax.ppermute(
-                columns_of((me + step) % n), "mp", [(source, (source + step) % n) for source in range(n)]
-            )
+    scores = columns_of(me)
+    for step in range(1, n):
+        scores = scores + lax.ppermute(
+            columns_of((me + step) % n), "mp", [(source, (source + step) % n) for source in range(n)]
+        )
     return (rest(), scores)
 
 

time: 123 us -> 107 us (0.87)
  local copies, waits for them, and re-layouts: 21.9 us -> 9.38 us
  waiting for transfers between devices: 31.2 us -> 43 us
  Pallas kernels: 24.7 us -> 18.6 us
  starting transfers between devices: 34.6 us -> 28.8 us
  matrix products: 7.57 us -> 4.85 us
    ppermute x1, waiting for transfers between devices: 2.7 us -> 11.4 us  [line_of_four(): beside = lax.ppermute(grad_kv, 'mp', exchange_pairs)]
    ppermute x1, waiting for transfers between devices: 0.01 us -> 7.55 us  [line_of_four(): low_in_beside = lax.ppermute(low_in, 'mp', inward)]
    slice x4 -> x1, local copies, waits for them, and re-layouts: 6.67 us -> 0.01 us  [line_of_four(): low_in_beside[:1]]
    pallas_call x5 -> x4, Pallas kernels: 24 us -> 17.9 us  [put_rows(): pl.pallas_call(functools.partial(rows_kernel, block, start, count), in_sp...]
    ppermute x1, waiting for transfers between devices: 12.1 us -> 7.16 us  [line_of_four(): mine = lax.ppermute(take(slabs, me ^ 2), 'mp', [(2, 0), (1, 3)])]
    unnamed x30 -> x26, local copies, waits for them, and re-layouts: 14.1 us -> 9.25 us
    ppermute x1, starting transfers between devices: 12.8 us -> 9.79 us  [line_of_four(): low_in_beside = lax.ppermute(low_in, 'mp', inward)]
    dot_general x4, matrix products: 5.68 us -> 2.96 us  [low_rank(): return jnp.dot(rows, proj_both, preferred_element_type=jnp.float32)]
  transfers between devices with their start and end apart: 21 -> 16, of which waited for: 7 -> 6; matrix products, arithmetic and copies ran while one was open for 13% -> 5% of each run, Pallas kernels for 20% -> 13%
where the time goes in v7:
time: 107 us
  waiting for transfers between devices  43 us (40%)
  starting transfers between devices  28.8 us (27%)
  Pallas kernels  18.6 us (17%)
  local copies, waits for them, and re-layouts  9.38 us (9%)
  matrix products  4.85 us (5%)
  between operations  1.12 us (1%)
    pallas_call x4, Pallas kernels, put_rows(): pl.pallas_call(functools.partial(rows_kernel, block, start, count), in_sp...  17.9 us
    ppermute x1, waiting for transfers between devices, line_of_four(): beside = lax.ppermute(grad_kv, 'mp', exchange_pairs)  11.4 us
    ppermute x1, starting transfers between devices, line_of_four(): low_in_beside = lax.ppermute(low_in, 'mp', inward)  9.79 us
    unnamed x26, local copies, waits for them, and re-layouts  9.25 us
    ppermute x4, waiting for transfers between devices, on_device(): scores = scores + lax.ppermute(row, ('dp', 'mp'), pairs)  9.18 us
    ppermute x1, waiting for transfers between devices, line_of_four(): low_in_beside = lax.ppermute(low_in, 'mp', inward)  7.55 us
    ppermute x4, starting transfers between devices, on_device(): scores = scores + lax.ppermute(row, ('dp', 'mp'), pairs)  7.35 us
    ppermute x1, waiting for transfers between devices, line_of_four(): mine = lax.ppermute(take(slabs, me ^ 2), 'mp', [(2, 0), (1, 3)])  7.16 us
  transfers between devices with their start and end apart: 16, of which 6 were waited for; matrix products, arithmetic and copies ran while one was open for 5% of the time, Pallas kernels for 13%

profile of v7, /device:TPU:0, one launch (start us, length us, event | category | flops | bytes accessed | tf_op | source)
XLA Modules:
  0.0 106.5 jit_solution(8005322031855274939)
XLA Ops:
  0.6 0.0 copy-start
  0.6 3.1 %collective-permute-start = (bf16[256,2048]{1,0:T(8,128)(2,1)}, bf16[256,2048]{1,0:T(8,128)(2,1)S(1)}, u32[]{:S(2)}, u32[]{:S(2)}) collective-permute-start(bf16[256,2048]{1,0:T(8,128)(2,1)} %refs_1_.1), channel_id=1, source_target_pairs={{0,1},{1,0},{2,3},{3,2},{4,5},{5,4},{6,7},{7,6},{8,9},{9,8},{10,11... | collective-permute-start | bytes 3145736 | tf_op jit(solution)/shard_map/ppermute | solution.py:214
  3.7 1.6 %collective-permute-start.1 = (bf16[256,2048]{1,0:T(8,128)(2,1)}, bf16[256,2048]{1,0:T(8,128)(2,1)}, u32[]{:S(2)}, u32[]{:S(2)}) collective-permute-start(bf16[256,2048]{1,0:T(8,128)(2,1)} %refs_1_.1), channel_id=1, source_target_pairs={{1,2},{2,1},{5,6},{6,5},{9,10},{10,9},{13,14},{14,13},{17,18},{18,... | collective-permute-start | bytes 3145736 | tf_op jit(solution)/shard_map/ppermute | solution.py:213
  5.4 0.0 copy-start.1
  5.4 3.4 %copy-done.1 = bf16[2048,2048]{1,0:T(8,128)(2,1)S(1)} copy-done((bf16[2048,2048]{1,0:T(8,128)(2,1)S(1)}, bf16[2048,2048]{1,0:T(8,128)(2,1)}, u32[]{:S(2)}) %copy-start.1) | copy-done | bytes 8388632
  8.8 0.0 copy-start.4
  8.8 1.2 %copy-done.4 = bf16[256,2048]{1,0:T(8,128)(2,1)S(1)} copy-done((bf16[256,2048]{1,0:T(8,128)(2,1)S(1)}, bf16[256,2048]{1,0:T(8,128)(2,1)}, u32[]{:S(2)}) %copy-start.4) | copy-done | bytes 1048600
  10.0 4.4 %input_grad_rows.4.refs_3_ = bf16[4,256,2048]{2,1,0:T(8,128)(2,1)} custom-call(s32[1]{0:T(128)} %bitcast.me, bf16[256,2048]{1,0:T(8,128)(2,1)S(1)} %copy-done.4, bf16[256,2048]{1,0:T(8,128)(2,1)S(1)} %copy-done.4, bf16[2048,2048]{1,0:T(8,128)(2,1)S(1)} %copy-done.1), custom_call_target="tpu_custom_call" | custom-call | flops 524288 | bytes 524288 | tf_op jit(solution)/shard_map/input_grad_rows/pallas_call | solution.py:98
  14.4 0.0 copy-done.10
  14.4 0.0 copy-done.11
  14.5 0.0 copy-start.2
  14.5 1.2 %fusion.13.low_in = f32[1024,128]{1,0:T(8,128)S(1)} fusion(bf16[1024,2048]{1,0:T(8,128)(2,1)S(1)} %copy-done.10, bf16[2048,128]{1,0:T(8,128)(2,1)S(1)} %copy-done.11), kind=kOutput, calls=%fused_computation.32 | convolution fusion | flops 536870912 | bytes 5242880 | tf_op jit(solution)/shard_map/dot_general | solution.py:217
  15.7 11.4 %collective-permute-done.refs_0_.refs_1_ = bf16[256,2048]{1,0:T(8,128)(2,1)S(1)} collective-permute-done((bf16[256,2048]{1,0:T(8,128)(2,1)}, bf16[256,2048]{1,0:T(8,128)(2,1)S(1)}, u32[]{:S(2)}, u32[]{:S(2)}) %collective-permute-start) | collective-permute-done | bytes 1048608 | tf_op jit(solution)/shard_map/ppermute | solution.py:214
  27.1 0.0 collective-permute-done.1.refs_0_
  27.1 0.7 collective-permute-start.2
  27.8 1.3 %collective-permute-start.3 = (bf16[256,2048]{1,0:T(8,128)(2,1)}, bf16[256,2048]{1,0:T(8,128)(2,1)S(1)}, u32[]{:S(2)}, u32[]{:S(2)}) collective-permute-start(bf16[256,2048]{1,0:T(8,128)(2,1)} %collective-permute-done.1.refs_0_), channel_id=1, source_target_pairs={{1,0},{2,3},{5,4},{6,7},{9,8},{10,11},{13,12},{14,15},{17,16},{18,... | collective-permute-start | bytes 3145736 | tf_op jit(solution)/shard_map/ppermute | solution.py:222
  29.1 0.0 copy-done.12
  29.2 0.0 copy-done.5
  29.2 0.4 convolution_bitcast_fusion.own_low
  29.7 0.0 copy-done.2
  29.7 4.4 %input_grad_rows.5.refs_3_ = bf16[4,256,2048]{2,1,0:T(8,128)(2,1)} custom-call(s32[1]{0:T(128)} %bitcast.me, bf16[256,2048]{1,0:T(8,128)(2,1)S(1)} %collective-permute-done.refs_0_.refs_1_, bf16[256,2048]{1,0:T(8,128)(2,1)S(1)} %collective-permute-done.refs_0_.refs_1_, bf16[2048,2048]{1,0:T(8,128)(2,1)S(1)} %copy-done.2, ...), custom_call_target="tpu_custom_call", output_to_operand_aliasing={{}: (4, {})} | custom-call | flops 524288 | bytes 524288 | tf_op jit(solution)/shard_map/input_grad_rows/pallas_call | solution.py:98
  34.1 9.8 %collective-permute-start.4 = (f32[1024,128]{1,0:T(8,128)S(1)}, f32[1024,128]{1,0:T(8,128)S(1)}, u32[]{:S(2)}, u32[]{:S(2)}) collective-permute-start(f32[1024,128]{1,0:T(8,128)S(1)} %fusion.13.low_in), channel_id=1, source_target_pairs={{0,1},{3,2},{4,5},{7,6},{8,9},{11,10},{12,13},{15,14},{16,17},{19,... | collective-permute-start | bytes 1572872 | tf_op jit(solution)/shard_map/ppermute | solution.py:225
  43.9 0.4 fusion.14.beside_low
  44.3 1.7 %fusion.15.facing_low = f32[256,128]{1,0:T(8,128)S(1)} fusion(bf16[256,2048]{1,0:T(8,128)(2,1)} %collective-permute-done.1.refs_0_, bf16[2048,128]{0,1:T(8,128)(2,1)S(1)} %fusion.2), kind=kOutput, calls=%fused_computation.34 | convolution fusion | flops 134217728 | bytes 1703936 | tf_op jit(solution)/shard_map/dot_general | solution.py:211
  46.0 7.6 %collective-permute-done.4.low_in_beside = f32[1024,128]{1,0:T(8,128)S(1)} collective-permute-done((f32[1024,128]{1,0:T(8,128)S(1)}, f32[1024,128]{1,0:T(8,128)S(1)}, u32[]{:S(2)}, u32[]{:S(2)}) %collective-permute-start.4) | collective-permute-done | bytes 524320 | tf_op jit(solution)/shard_map/ppermute | solution.py:225
  53.6 0.0 collective-permute-done.2.refs_0_
  53.6 5.2 %collective-permute-done.3.refs_1_ = bf16[256,2048]{1,0:T(8,128)(2,1)S(1)} collective-permute-done((bf16[256,2048]{1,0:T(8,128)(2,1)}, bf16[256,2048]{1,0:T(8,128)(2,1)S(1)}, u32[]{:S(2)}, u32[]{:S(2)}) %collective-permute-start.3) | collective-permute-done | bytes 1048608 | tf_op jit(solution)/shard_map/ppermute | solution.py:222
  58.8 0.0 collective-permute-start.6
  58.8 0.0 copy-done.6
  58.8 0.4 fusion.16.far_low
  59.2 2.5 %collective-permute-done.6.note = f32[1,128]{1,0:T(1,128)S(1)} collective-permute-done((f32[1,128]{1,0:T(1,128)S(1)}, f32[1,128]{1,0:T(1,128)S(1)}, u32[]{:S(2)}, u32[]{:S(2)}) %collective-permute-start.6) | collective-permute-done | bytes 544 | tf_op jit(solution)/shard_map/ppermute | solution.py:233
  61.8 0.7 token_sums.1
  62.5 0.0 copy-done.8
  62.5 0.7 collective-permute-start.7
  63.2 0.0 collective-permute-done.7
  63.2 1.3 %collective-permute-start.8 = (f32[1,32,64]{2,1,0:T(8,128)S(1)}, f32[1,32,64]{2,1,0:T(8,128)S(1)}, u32[]{:S(2)}, u32[]{:S(2)}) collective-permute-start(f32[1,32,64]{2,1,0:T(8,128)S(1)} %dynamic-slice_bitcast_fusion), channel_id=1, source_target_pairs={{2,0},{1,3},{6,4},{5,7},{10,8},{9,11},{14,12},{13,15},{18,16},{17,... | collective-permute-start | bytes 24584 | tf_op jit(solution)/shard_map/ppermute | solution.py:245
  64.5 7.2 %collective-permute-done.8 = f32[1,32,64]{2,1,0:T(8,128)S(1)} collective-permute-done((f32[1,32,64]{2,1,0:T(8,128)S(1)}, f32[1,32,64]{2,1,0:T(8,128)S(1)}, u32[]{:S(2)}, u32[]{:S(2)}) %collective-permute-start.8) | collective-permute-done | bytes 8224 | tf_op jit(solution)/shard_map/ppermute | solution.py:245
  71.7 0.1 reshape.28
  71.8 0.0 collective-permute-start.11
  71.8 1.6 %collective-permute-start.10 = (f32[1,2048]{1,0:T(1,128)S(1)}, f32[1,2048]{1,0:T(1,128)S(1)}, u32[]{:S(2)}, u32[]{:S(2)}) collective-permute-start(f32[1,2048]{1,0:T(1,128)S(1)} %reshape.28), channel_id=1, source_target_pairs={{0,8},{4,12},{8,0},{12,4},{1,9},{5,13},{9,1},{13,5},{2,10},{6,14},... | collective-permute-start | bytes 24584 | tf_op jit(solution)/shard_map/ppermute | solution.py:270
  73.3 0.2 collective-permute-start.9
  73.5 1.3 %collective-permute-start.5 = (bf16[256,2048]{1,0:T(8,128)(2,1)}, bf16[256,2048]{1,0:T(8,128)(2,1)S(1)}, u32[]{:S(2)}, u32[]{:S(2)}) collective-permute-start(bf16[256,2048]{1,0:T(8,128)(2,1)} %copy-done.6), channel_id=1, source_target_pairs={{1,0},{2,3},{5,4},{6,7},{9,8},{10,11},{13,12},{14,15},{17,16},{18,... | collective-permute-start | bytes 3145736 | tf_op jit(solution)/shard_map/ppermute | solution.py:231
  74.8 0.0 copy-start.3
  74.8 3.4 %copy-done.3 = bf16[2048,2048]{1,0:T(8,128)(2,1)S(1)} copy-done((bf16[2048,2048]{1,0:T(8,128)(2,1)S(1)}, bf16[2048,2048]{1,0:T(8,128)(2,1)}, u32[]{:S(2)}) %copy-start.3) | copy-done | bytes 8388632
  78.2 1.2 %copy-done.9 = bf16[256,2048]{1,0:T(8,128)(2,1)S(1)} copy-done((bf16[256,2048]{1,0:T(8,128)(2,1)S(1)}, bf16[256,2048]{1,0:T(8,128)(2,1)}, u32[]{:S(2)}) %copy-start.9) | copy-done | bytes 1048600
  79.4 4.6 %input_grad_rows.6.refs_3_ = bf16[4,256,2048]{2,1,0:T(8,128)(2,1)} custom-call(s32[1]{0:T(128)} %bitcast.me, bf16[256,2048]{1,0:T(8,128)(2,1)} %collective-permute-done.1.refs_0_, bf16[256,2048]{1,0:T(8,128)(2,1)S(1)} %copy-done.9, bf16[2048,2048]{1,0:T(8,128)(2,1)S(1)} %copy-done.3, ...), custom_call_target="tpu_custom_call", output_to_operand_aliasing={{}: (4, {})} | custom-call | flops 524288 | bytes 524288 | tf_op jit(solution)/shard_map/input_grad_rows/pallas_call | solution.py:98
  84.0 0.0 collective-permute-done.11
  84.0 0.0 collective-permute-done.10
  84.0 0.0 collective-permute-done.9
  84.0 0.1 reduce-precision_convert_fusion.1
  84.1 0.0 copy-done
  84.1 0.6 fusion.3
  84.8 1.6 %collective-permute-start.15 = (f32[1,512]{1,0:T(1,128)S(1)}, f32[1,512]{1,0:T(1,128)S(1)}, u32[]{:S(2)}, u32[]{:S(2)}) collective-permute-start(f32[1,512]{1,0:T(1,128)S(1)} %get-tuple-element.30), channel_id=1, source_target_pairs={{0,12},{1,0},{2,4},{3,8},{4,13},{5,1},{6,5},{7,9},{8,14},{9,2},{10... | collective-permute-start | bytes 6152 | tf_op jit(solution)/shard_map/ppermute | solution.py:286
  86.4 3.5 %collective-permute-start.14 = (f32[1,512]{1,0:T(1,128)S(1)}, f32[1,512]{1,0:T(1,128)S(1)}, u32[]{:S(2)}, u32[]{:S(2)}) collective-permute-start(f32[1,512]{1,0:T(1,128)S(1)} %get-tuple-element.31), channel_id=1, source_target_pairs={{0,8},{1,12},{2,0},{3,4},{4,9},{5,13},{6,1},{7,5},{8,10},{9,14},{1... | collective-permute-start | bytes 6152 | tf_op jit(solution)/shard_map/ppermute | solution.py:286
  89.9 0.6 collective-permute-start.12
  90.6 1.6 %collective-permute-start.13 = (f32[1,512]{1,0:T(1,128)S(1)}, f32[1,512]{1,0:T(1,128)S(1)}, u32[]{:S(2)}, u32[]{:S(2)}) collective-permute-start(f32[1,512]{1,0:T(1,128)S(1)} %get-tuple-element.29), channel_id=1, source_target_pairs={{0,4},{1,8},{2,12},{3,0},{4,5},{5,9},{6,13},{7,1},{8,6},{9,10},{10... | collective-permute-start | bytes 6152 | tf_op jit(solution)/shard_map/ppermute | solution.py:286
  92.2 9.2 %collective-permute-done.15 = f32[1,512]{1,0:T(1,128)S(1)} collective-permute-done((f32[1,512]{1,0:T(1,128)S(1)}, f32[1,512]{1,0:T(1,128)S(1)}, u32[]{:S(2)}, u32[]{:S(2)}) %collective-permute-start.15) | collective-permute-done | bytes 2080 | tf_op jit(solution)/shard_map/ppermute | solution.py:286
  101.3 0.0 collective-permute-done.14
  101.3 0.0 collective-permute-done.12
  101.3 0.0 collective-permute-done.13
  101.3 0.6 add_add_fusion
  101.9 0.0 collective-permute-done.5.refs_1_
  101.9 0.0 copy-done.7
  101.9 4.4 %input_grad_rows.7 = bf16[4,256,2048]{2,1,0:T(8,128)(2,1)} custom-call(s32[1]{0:T(128)} %bitcast.me, bf16[256,2048]{1,0:T(8,128)(2,1)S(1)} %copy-done.7, bf16[256,2048]{1,0:T(8,128)(2,1)S(1)} %collective-permute-done.5.refs_1_, bf16[2048,2048]{1,0:T(8,128)(2,1)S(1)} %copy-done.3, ...), custom_call_target="tpu_custom_call", output_to_operand_aliasing={{}: (4, {})} | custom-call | flops 524288 | bytes 524288 | tf_op jit(solution)/shard_map/input_grad_rows/pallas_call | solution.py:98
  (16 shorter events, 0.1 us)
Async XLA Ops:
  0.6 83.5 %copy-start = (bf16[512,2048]{1,0:T(8,128)(2,1)S(1)}, bf16[512,2048]{1,0:T(8,128)(2,1)}, u32[]{:S(2)}) copy-start(bf16[512,2048]{1,0:T(8,128)(2,1)} %param.11) | copy-start | bytes 6291460
  0.6 26.5 %collective-permute-start = (bf16[256,2048]{1,0:T(8,128)(2,1)}, bf16[256,2048]{1,0:T(8,128)(2,1)S(1)}, u32[]{:S(2)}, u32[]{:S(2)}) collective-permute-start(bf16[256,2048]{1,0:T(8,128)(2,1)} %refs_1_.1), channel_id=1, source_target_pairs={{0,1},{1,0},{2,3},{3,2},{4,5},{5,4},{6,7},{7,6},{8,9},{9,8},{10,11... | collective-permute-start | bytes 3145736 | tf_op jit(solution)/shard_map/ppermute | solution.py:214
  3.7 23.4 %collective-permute-start.1 = (bf16[256,2048]{1,0:T(8,128)(2,1)}, bf16[256,2048]{1,0:T(8,128)(2,1)}, u32[]{:S(2)}, u32[]{:S(2)}) collective-permute-start(bf16[256,2048]{1,0:T(8,128)(2,1)} %refs_1_.1), channel_id=1, source_target_pairs={{1,2},{2,1},{5,6},{6,5},{9,10},{10,9},{13,14},{14,13},{17,18},{18,... | collective-permute-start | bytes 3145736 | tf_op jit(solution)/shard_map/ppermute | solution.py:213
  5.4 3.4 %copy-start.1 = (bf16[2048,2048]{1,0:T(8,128)(2,1)S(1)}, bf16[2048,2048]{1,0:T(8,128)(2,1)}, u32[]{:S(2)}) copy-start(bf16[2048,2048]{1,0:T(8,128)(2,1)} %refs_2_.7) | copy-start | bytes 25165828
  8.8 1.2 %copy-start.4 = (bf16[256,2048]{1,0:T(8,128)(2,1)S(1)}, bf16[256,2048]{1,0:T(8,128)(2,1)}, u32[]{:S(2)}) copy-start(bf16[256,2048]{1,0:T(8,128)(2,1)} %refs_1_.1) | copy-start | bytes 3145732
  10.0 4.5 %copy-start.10 = (bf16[1024,2048]{1,0:T(8,128)(2,1)S(1)}, bf16[1024,2048]{1,0:T(8,128)(2,1)}, u32[]{:S(2)}) copy-start(bf16[1024,2048]{1,0:T(8,128)(2,1)} %param.6) | copy-start | bytes 12582916
  10.0 4.5 %copy-start.11 = (bf16[2048,128]{1,0:T(8,128)(2,1)S(1)}, bf16[2048,128]{1,0:T(8,128)(2,1)}, u32[]{:S(2)}) copy-start(bf16[2048,128]{1,0:T(8,128)(2,1)} %param.9) | copy-start | bytes 1572868
  10.0 19.1 %copy-start.12 = (bf16[2,1024,64]{1,2,0:T(8,128)(2,1)S(1)}, bf16[2,1024,64]{1,2,0:T(8,128)(2,1)}, u32[]{:S(2)}) copy-start(bf16[2,1024,64]{1,2,0:T(8,128)(2,1)} %param.10) | copy-start | bytes 786436
  10.0 19.2 %copy-start.5 = (bf16[256,2048]{1,0:T(8,128)(2,1)S(1)}, bf16[256,2048]{1,0:T(8,128)(2,1)}, u32[]{:S(2)}) copy-start(bf16[256,2048]{1,0:T(8,128)(2,1)} %refs_1_.1) | copy-start | bytes 3145732
  14.5 15.2 %copy-start.2 = (bf16[2048,2048]{1,0:T(8,128)(2,1)S(1)}, bf16[2048,2048]{1,0:T(8,128)(2,1)}, u32[]{:S(2)}) copy-start(bf16[2048,2048]{1,0:T(8,128)(2,1)} %refs_2_.7) | copy-start | bytes 25165828
  27.1 26.5 %collective-permute-start.2 = (bf16[256,2048]{1,0:T(8,128)(2,1)S(1)}, bf16[256,2048]{1,0:T(8,128)(2,1)S(1)}, u32[]{:S(2)}, u32[]{:S(2)}) collective-permute-start(bf16[256,2048]{1,0:T(8,128)(2,1)S(1)} %collective-permute-done.refs_0_.refs_1_), channel_id=1, source_target_pairs={{1,2},{2,1},{5,6},{6,5},{9,10},{10,9},{13,14},{14,13},{17,18},{18,... | collective-permute-start | bytes 3145736 | tf_op jit(solution)/shard_map/ppermute | solution.py:221
  27.8 31.0 %collective-permute-start.3 = (bf16[256,2048]{1,0:T(8,128)(2,1)}, bf16[256,2048]{1,0:T(8,128)(2,1)S(1)}, u32[]{:S(2)}, u32[]{:S(2)}) collective-permute-start(bf16[256,2048]{1,0:T(8,128)(2,1)} %collective-permute-done.1.refs_0_), channel_id=1, source_target_pairs={{1,0},{2,3},{5,4},{6,7},{9,8},{10,11},{13,12},{14,15},{17,16},{18,... | collective-permute-start | bytes 3145736 | tf_op jit(solution)/shard_map/ppermute | solution.py:222
  34.1 19.4 %collective-permute-start.4 = (f32[1024,128]{1,0:T(8,128)S(1)}, f32[1024,128]{1,0:T(8,128)S(1)}, u32[]{:S(2)}, u32[]{:S(2)}) collective-permute-start(f32[1024,128]{1,0:T(8,128)S(1)} %fusion.13.low_in), channel_id=1, source_target_pairs={{0,1},{3,2},{4,5},{7,6},{8,9},{11,10},{12,13},{15,14},{16,17},{19,... | collective-permute-start | bytes 1572872 | tf_op jit(solution)/shard_map/ppermute | solution.py:225
  53.6 5.2 %copy-start.6 = (bf16[256,2048]{1,0:T(8,128)(2,1)}, bf16[256,2048]{1,0:T(8,128)(2,1)S(1)}, u32[]{:S(2)}) copy-start(bf16[256,2048]{1,0:T(8,128)(2,1)S(1)} %collective-permute-done.2.refs_0_) | copy-start | bytes 3145732
  58.8 3.7 %copy-start.8 = (bf16[256,2048]{1,0:T(8,128)(2,1)}, bf16[256,2048]{1,0:T(8,128)(2,1)S(1)}, u32[]{:S(2)}) copy-start(bf16[256,2048]{1,0:T(8,128)(2,1)S(1)} %collective-permute-done.3.refs_1_) | copy-start | bytes 3145732
  58.8 3.0 %collective-permute-start.6 = (f32[1,128]{1,0:T(1,128)S(1)}, f32[1,128]{1,0:T(1,128)S(1)}, u32[]{:S(2)}, u32[]{:S(2)}) collective-permute-start(f32[1,128]{1,0:T(1,128)S(1)} %slice.23), channel_id=1, source_target_pairs={{0,4},{4,8},{8,12},{12,0},{1,5},{5,9},{9,13},{13,1},{2,6},{6,10},{... | collective-permute-start | bytes 1544 | tf_op jit(solution)/shard_map/ppermute | solution.py:233
  62.5 0.7 collective-permute-start.7
  63.2 8.5 %collective-permute-start.8 = (f32[1,32,64]{2,1,0:T(8,128)S(1)}, f32[1,32,64]{2,1,0:T(8,128)S(1)}, u32[]{:S(2)}, u32[]{:S(2)}) collective-permute-start(f32[1,32,64]{2,1,0:T(8,128)S(1)} %dynamic-slice_bitcast_fusion), channel_id=1, source_target_pairs={{2,0},{1,3},{6,4},{5,7},{10,8},{9,11},{14,12},{13,15},{18,16},{17,... | collective-permute-start | bytes 24584 | tf_op jit(solution)/shard_map/ppermute | solution.py:245
  71.8 12.3 %collective-permute-start.11 = (f32[1,2048]{1,0:T(1,128)S(1)}, f32[1,2048]{1,0:T(1,128)S(1)}, u32[]{:S(2)}, u32[]{:S(2)}) collective-permute-start(f32[1,2048]{1,0:T(1,128)S(1)} %reshape.28), channel_id=1, source_target_pairs={{0,12},{4,0},{8,4},{12,8},{1,13},{5,1},{9,5},{13,9},{2,14},{6,2},{... | collective-permute-start | bytes 24584 | tf_op jit(solution)/shard_map/ppermute | solution.py:270
  71.8 12.3 %collective-permute-start.10 = (f32[1,2048]{1,0:T(1,128)S(1)}, f32[1,2048]{1,0:T(1,128)S(1)}, u32[]{:S(2)}, u32[]{:S(2)}) collective-permute-start(f32[1,2048]{1,0:T(1,128)S(1)} %reshape.28), channel_id=1, source_target_pairs={{0,8},{4,12},{8,0},{12,4},{1,9},{5,13},{9,1},{13,5},{2,10},{6,14},... | collective-permute-start | bytes 24584 | tf_op jit(solution)/shard_map/ppermute | solution.py:270
  73.3 10.7 %collective-permute-start.9 = (f32[1,2048]{1,0:T(1,128)S(1)}, f32[1,2048]{1,0:T(1,128)S(1)}, u32[]{:S(2)}, u32[]{:S(2)}) collective-permute-start(f32[1,2048]{1,0:T(1,128)S(1)} %reshape.28), channel_id=1, source_target_pairs={{0,4},{4,8},{8,12},{12,0},{1,5},{5,9},{9,13},{13,1},{2,6},{6,10},{... | collective-permute-start | bytes 24584 | tf_op jit(solution)/shard_map/ppermute | solution.py:270
  73.5 28.4 %collective-permute-start.5 = (bf16[256,2048]{1,0:T(8,128)(2,1)}, bf16[256,2048]{1,0:T(8,128)(2,1)S(1)}, u32[]{:S(2)}, u32[]{:S(2)}) collective-permute-start(bf16[256,2048]{1,0:T(8,128)(2,1)} %copy-done.6), channel_id=1, source_target_pairs={{1,0},{2,3},{5,4},{6,7},{9,8},{10,11},{13,12},{14,15},{17,16},{18,... | collective-permute-start | bytes 3145736 | tf_op jit(solution)/shard_map/ppermute | solution.py:231
  74.8 3.4 %copy-start.3 = (bf16[2048,2048]{1,0:T(8,128)(2,1)S(1)}, bf16[2048,2048]{1,0:T(8,128)(2,1)}, u32[]{:S(2)}) copy-start(bf16[2048,2048]{1,0:T(8,128)(2,1)} %refs_2_.7) | copy-start | bytes 25165828
  78.2 1.2 %copy-start.9 = (bf16[256,2048]{1,0:T(8,128)(2,1)S(1)}, bf16[256,2048]{1,0:T(8,128)(2,1)}, u32[]{:S(2)}) copy-start(bf16[256,2048]{1,0:T(8,128)(2,1)} %copy-done.8) | copy-start | bytes 3145732
  79.4 22.5 %copy-start.7 = (bf16[256,2048]{1,0:T(8,128)(2,1)S(1)}, bf16[256,2048]{1,0:T(8,128)(2,1)}, u32[]{:S(2)}) copy-start(bf16[256,2048]{1,0:T(8,128)(2,1)} %copy-done.6) | copy-start | bytes 3145732
  84.8 16.5 %collective-permute-start.15 = (f32[1,512]{1,0:T(1,128)S(1)}, f32[1,512]{1,0:T(1,128)S(1)}, u32[]{:S(2)}, u32[]{:S(2)}) collective-permute-start(f32[1,512]{1,0:T(1,128)S(1)} %get-tuple-element.30), channel_id=1, source_target_pairs={{0,12},{1,0},{2,4},{3,8},{4,13},{5,1},{6,5},{7,9},{8,14},{9,2},{10... | collective-permute-start | bytes 6152 | tf_op jit(solution)/shard_map/ppermute | solution.py:286
  86.4 14.9 %collective-permute-start.14 = (f32[1,512]{1,0:T(1,128)S(1)}, f32[1,512]{1,0:T(1,128)S(1)}, u32[]{:S(2)}, u32[]{:S(2)}) collective-permute-start(f32[1,512]{1,0:T(1,128)S(1)} %get-tuple-element.31), channel_id=1, source_target_pairs={{0,8},{1,12},{2,0},{3,4},{4,9},{5,13},{6,1},{7,5},{8,10},{9,14},{1... | collective-permute-start | bytes 6152 | tf_op jit(solution)/shard_map/ppermute | solution.py:286
  89.9 11.4 %collective-permute-start.12 = (f32[1,512]{1,0:T(1,128)S(1)}, f32[1,512]{1,0:T(1,128)S(1)}, u32[]{:S(2)}, u32[]{:S(2)}) collective-permute-start(f32[1,512]{1,0:T(1,128)S(1)} %get-tuple-element.32), channel_id=1, source_target_pairs={{0,0},{1,4},{2,8},{3,12},{4,1},{5,5},{6,9},{7,13},{8,2},{9,6},{10,... | collective-permute-start | bytes 6152 | tf_op jit(solution)/shard_map/ppermute | solution.py:286
  90.6 10.8 %collective-permute-start.13 = (f32[1,512]{1,0:T(1,128)S(1)}, f32[1,512]{1,0:T(1,128)S(1)}, u32[]{:S(2)}, u32[]{:S(2)}) collective-permute-start(f32[1,512]{1,0:T(1,128)S(1)} %get-tuple-element.29), channel_id=1, source_target_pairs={{0,4},{1,8},{2,12},{3,0},{4,5},{5,9},{6,13},{7,1},{8,6},{9,10},{10... | collective-permute-start | bytes 6152 | tf_op jit(solution)/shard_map/ppermute | solution.py:286

commit v8 on v7

--- a/solution.py
+++ b/solution.py
@@ -117,7 +117,7 @@
     )(me.reshape(1).astype(jnp.int32), *firsts, *seconds, w_kv, *earlier)
 
 
-def token_sums_kernel(me, low_in, low_in_beside, own_low, beside_low, facing_low, far_low, note, out):
+def token_sums_kernel(me, low_in, low_in_beside, own_low, beside_low, facing_low, far_low, out):
     rows = own_low.shape[0]
     rank = out.shape[2]
     total = jnp.zeros((own_low.shape[1], own_low.shape[1]), jnp.float32)
@@ -141,16 +141,16 @@
         out[index] = total[index * slab : (index + 1) * slab, layer * rank : (layer + 1) * rank]
 
 
-def token_sums(me, low_in, low_in_beside, own_low, beside_low, facing_low, far_low, note, rank):
+def token_sums(me, low_in, low_in_beside, own_low, beside_low, facing_low, far_low, rank):
     whole = pl.BlockSpec(memory_space=pltpu.VMEM)
     return pl.pallas_call(
         token_sums_kernel,
-        in_specs=[pl.BlockSpec(memory_space=pltpu.SMEM)] + [whole] * 7,
+        in_specs=[pl.BlockSpec(memory_space=pltpu.SMEM)] + [whole] * 6,
         out_specs=whole,
         out_shape=jax.ShapeDtypeStruct((4, 2 * rank // 4, rank), jnp.float32),
         compiler_params=pltpu.CompilerParams(vmem_limit_bytes=GRANT),
         name="token_sums",
-    )(me.reshape(1).astype(jnp.int32), low_in, low_in_beside, own_low, beside_low, facing_low, far_low, note)
+    )(me.reshape(1).astype(jnp.int32), low_in, low_in_beside, own_low, beside_low, facing_low, far_low)
 
 
 def sequence_sums(low_in, low_out, rank):
@@ -193,7 +193,7 @@
     low_in = jnp.dot(hidden, proj_in, preferred_element_type=jnp.float32)
     sums = slabs_of(sequence_sums(low_in, jnp.dot(whole, block_diagonal(proj_out), preferred_element_type=jnp.float32), rank), n)
     features = lax.psum_scatter(sums, "mp", scatter_dimension=0, tiled=False)
-    return features, lambda scores: scores, lambda: input_grad
+    return features, lambda scores: (scores, scores), lambda: input_grad
 
 
 def line_of_four(hidden, w_kv, grad_kv, proj_in, proj_out):
@@ -229,12 +229,9 @@
 
     beside_across, second, low_in_beside, output = tied((beside_across, second, low_in_beside, output))
     third = lax.ppermute(beside_across, "mp", outward)
-    shards = lax.axis_size("dp")
-    note = lax.ppermute(low_in_beside[:1], "dp", [(source, (source + 1) % shards) for source in range(shards)])
-
     far_low = low_rank(beside_across)
     if low_in.shape[0] == SEQ:
-        slabs = token_sums(me, low_in, low_in_beside, own_low, beside_low, facing_low, far_low, note, rank)[:, None]
+        slabs = token_sums(me, low_in, low_in_beside, own_low, beside_low, facing_low, far_low, rank)[:, None]
     else:
         low_out = jnp.zeros((4, local_rows, 2 * rank), jnp.float32)
         for away, rows in ((0, own_low), (1, beside_low), (3, facing_low), (2, far_low)):
@@ -247,7 +244,8 @@
     output = put_rows(me, 2, output, [facing], [second], w_kv, local_rows)
 
     def finish(scores):
-        return tied((scores, output))[0]
+        scores = tied((scores, output))[0]
+        return scores, tied((scores, third))[0]
 
     def rest():
         done = put_rows(me, 3, output, [beside_across], [third], w_kv, local_rows)
@@ -274,7 +272,7 @@
     products = lax.dot_general(
         terms, queries, (((1,), (1,)), ((), ())), preferred_element_type=jnp.float32
     ).reshape(3, shards, count, block_rows)
-    partial_scores = finish(products[0] + (products[1] + products[2]))
+    partial_scores, last_scores = finish(products[0] + (products[1] + products[2]))
 
     if shards == n:
         scores = jnp.zeros((count, block_rows), jnp.float32)
@@ -282,7 +280,7 @@
             pairs = [
                 (q * n + slab, (slab + step) % n * n + q) for q in range(n) for slab in range(n)
             ]
-            row = take(partial_scores, (shard - me - step + 2 * n) % n)
+            row = take(partial_scores if step < n - 1 else last_scores, (shard - me - step + 2 * n) % n)
             scores = scores + lax.ppermute(row, ("dp", "mp"), pairs)
         return (rest(), scores)
 

time: 107 us -> 95.7 us (0.89)
  waiting for transfers between devices: 43 us -> 33.4 us
  starting transfers between devices: 28.8 us -> 27.4 us
    ppermute x4, waiting for transfers between devices: 9.18 us -> 0.01 us  [on_device(): scores = scores + lax.ppermute(row, ('dp', 'mp'), pairs)]
    ppermute x1 -> x0, waiting for transfers between devices: 2.51 us -> none  [line_of_four(): lax.ppermute(low_in_beside[:1], 'dp', [(source, (source + 1) % shards) fo...]
    ppermute x1, waiting for transfers between devices: 0.01 us -> 2.11 us  [line_of_four(): third = lax.ppermute(beside_across, 'mp', outward)]
    ppermute x4, starting transfers between devices: 7.35 us -> 5.86 us  [on_device(): scores = scores + lax.ppermute(row, ('dp', 'mp'), pairs)]
  transfers between devices with their start and end apart: 16 -> 15, of which waited for: 6 -> 5; matrix products, arithmetic and copies ran while one was open for 5% -> 5% of each run, Pallas kernels for 13% -> 19%
where the time goes in v8:
time: 95.7 us; the launch traced here: 95.2 us
  waiting for transfers between devices  33.4 us (35%)
  starting transfers between devices  27.4 us (29%)
  Pallas kernels  18.6 us (19%)
  local copies, waits for them, and re-layouts  9.38 us (10%)
  matrix products  4.85 us (5%)
  between operations  0.98 us (1%)
    pallas_call x4, Pallas kernels, put_rows(): pl.pallas_call(functools.partial(rows_kernel, block, start, count), in_sp...  17.9 us
    ppermute x1, waiting for transfers between devices, line_of_four(): beside = lax.ppermute(grad_kv, 'mp', exchange_pairs)  11.4 us
    ppermute x1, starting transfers between devices, line_of_four(): low_in_beside = lax.ppermute(low_in, 'mp', inward)  9.79 us
    unnamed x26, local copies, waits for them, and re-layouts  9.25 us
    ppermute x1, waiting for transfers between devices, line_of_four(): low_in_beside = lax.ppermute(low_in, 'mp', inward)  7.55 us
    ppermute x1, waiting for transfers between devices, line_of_four(): mine = lax.ppermute(take(slabs, me ^ 2), 'mp', [(2, 0), (1, 3)])  7.06 us
    ppermute x4, starting transfers between devices, on_device(): scores = scores + lax.ppermute(row, ('dp', 'mp'), pairs)  5.86 us
    ppermute x1, waiting for transfers between devices, line_of_four(): second = lax.ppermute(facing, 'mp', outward)  5.22 us
  transfers between devices with their start and end apart: 15, of which 5 were waited for; matrix products, arithmetic and copies ran while one was open for 5% of the time, Pallas kernels for 19%

profile of v8, /device:TPU:0, one launch (start us, length us, event | category | flops | bytes accessed | tf_op | source)
XLA Modules:
  0.0 95.2 jit_solution(13396908952575775291)
XLA Ops:
  0.6 0.0 copy-start
  0.6 3.1 %collective-permute-start = (bf16[256,2048]{1,0:T(8,128)(2,1)}, bf16[256,2048]{1,0:T(8,128)(2,1)S(1)}, u32[]{:S(2)}, u32[]{:S(2)}) collective-permute-start(bf16[256,2048]{1,0:T(8,128)(2,1)} %refs_1_.1), channel_id=1, source_target_pairs={{0,1},{1,0},{2,3},{3,2},{4,5},{5,4},{6,7},{7,6},{8,9},{9,8},{10,11... | collective-permute-start | bytes 3145736 | tf_op jit(solution)/shard_map/ppermute | solution.py:214
  3.7 1.6 %collective-permute-start.1 = (bf16[256,2048]{1,0:T(8,128)(2,1)}, bf16[256,2048]{1,0:T(8,128)(2,1)}, u32[]{:S(2)}, u32[]{:S(2)}) collective-permute-start(bf16[256,2048]{1,0:T(8,128)(2,1)} %refs_1_.1), channel_id=1, source_target_pairs={{1,2},{2,1},{5,6},{6,5},{9,10},{10,9},{13,14},{14,13},{17,18},{18,... | collective-permute-start | bytes 3145736 | tf_op jit(solution)/shard_map/ppermute | solution.py:213
  5.4 0.0 copy-start.1
  5.4 3.4 %copy-done.1 = bf16[2048,2048]{1,0:T(8,128)(2,1)S(1)} copy-done((bf16[2048,2048]{1,0:T(8,128)(2,1)S(1)}, bf16[2048,2048]{1,0:T(8,128)(2,1)}, u32[]{:S(2)}) %copy-start.1) | copy-done | bytes 8388632
  8.7 0.0 copy-start.4
  8.7 1.2 %copy-done.4 = bf16[256,2048]{1,0:T(8,128)(2,1)S(1)} copy-done((bf16[256,2048]{1,0:T(8,128)(2,1)S(1)}, bf16[256,2048]{1,0:T(8,128)(2,1)}, u32[]{:S(2)}) %copy-start.4) | copy-done | bytes 1048600
  10.0 0.0 copy-start.10
  10.0 0.0 copy-start.11
  10.0 0.0 copy-start.12
  10.0 4.4 %input_grad_rows.4.refs_3_ = bf16[4,256,2048]{2,1,0:T(8,128)(2,1)} custom-call(s32[1]{0:T(128)} %bitcast.me, bf16[256,2048]{1,0:T(8,128)(2,1)S(1)} %copy-done.4, bf16[256,2048]{1,0:T(8,128)(2,1)S(1)} %copy-done.4, bf16[2048,2048]{1,0:T(8,128)(2,1)S(1)} %copy-done.1), custom_call_target="tpu_custom_call" | custom-call | flops 524288 | bytes 524288 | tf_op jit(solution)/shard_map/input_grad_rows/pallas_call | solution.py:98
  14.4 0.0 copy-done.10
  14.4 0.0 copy-done.11
  14.4 0.0 copy-start.2
  14.4 1.2 %fusion.13.low_in = f32[1024,128]{1,0:T(8,128)S(1)} fusion(bf16[1024,2048]{1,0:T(8,128)(2,1)S(1)} %copy-done.10, bf16[2048,128]{1,0:T(8,128)(2,1)S(1)} %copy-done.11), kind=kOutput, calls=%fused_computation.32 | convolution fusion | flops 536870912 | bytes 5242880 | tf_op jit(solution)/shard_map/dot_general | solution.py:217
  15.7 11.4 %collective-permute-done.refs_0_.refs_1_ = bf16[256,2048]{1,0:T(8,128)(2,1)S(1)} collective-permute-done((bf16[256,2048]{1,0:T(8,128)(2,1)}, bf16[256,2048]{1,0:T(8,128)(2,1)S(1)}, u32[]{:S(2)}, u32[]{:S(2)}) %collective-permute-start) | collective-permute-done | bytes 1048608 | tf_op jit(solution)/shard_map/ppermute | solution.py:214
  27.1 0.0 collective-permute-done.1.refs_0_
  27.1 0.7 collective-permute-start.2
  27.8 1.3 %collective-permute-start.3 = (bf16[256,2048]{1,0:T(8,128)(2,1)}, bf16[256,2048]{1,0:T(8,128)(2,1)S(1)}, u32[]{:S(2)}, u32[]{:S(2)}) collective-permute-start(bf16[256,2048]{1,0:T(8,128)(2,1)} %collective-permute-done.1.refs_0_), channel_id=1, source_target_pairs={{1,0},{2,3},{5,4},{6,7},{9,8},{10,11},{13,12},{14,15},{17,16},{18,... | collective-permute-start | bytes 3145736 | tf_op jit(solution)/shard_map/ppermute | solution.py:222
  29.1 0.0 copy-done.12
  29.2 0.0 copy-done.5
  29.2 0.4 convolution_bitcast_fusion.own_low
  29.7 0.0 copy-done.2
  29.7 4.4 %input_grad_rows.5.refs_3_ = bf16[4,256,2048]{2,1,0:T(8,128)(2,1)} custom-call(s32[1]{0:T(128)} %bitcast.me, bf16[256,2048]{1,0:T(8,128)(2,1)S(1)} %collective-permute-done.refs_0_.refs_1_, bf16[256,2048]{1,0:T(8,128)(2,1)S(1)} %collective-permute-done.refs_0_.refs_1_, bf16[2048,2048]{1,0:T(8,128)(2,1)S(1)} %copy-done.2, ...), custom_call_target="tpu_custom_call", output_to_operand_aliasing={{}: (4, {})} | custom-call | flops 524288 | bytes 524288 | tf_op jit(solution)/shard_map/input_grad_rows/pallas_call | solution.py:98
  34.1 9.8 %collective-permute-start.4 = (f32[1024,128]{1,0:T(8,128)S(1)}, f32[1024,128]{1,0:T(8,128)S(1)}, u32[]{:S(2)}, u32[]{:S(2)}) collective-permute-start(f32[1024,128]{1,0:T(8,128)S(1)} %fusion.13.low_in), channel_id=1, source_target_pairs={{0,1},{3,2},{4,5},{7,6},{8,9},{11,10},{12,13},{15,14},{16,17},{19,... | collective-permute-start | bytes 1572872 | tf_op jit(solution)/shard_map/ppermute | solution.py:225
  43.9 0.4 fusion.14.beside_low
  44.3 1.7 %fusion.15.facing_low = f32[256,128]{1,0:T(8,128)S(1)} fusion(bf16[256,2048]{1,0:T(8,128)(2,1)} %collective-permute-done.1.refs_0_, bf16[2048,128]{0,1:T(8,128)(2,1)S(1)} %fusion.2), kind=kOutput, calls=%fused_computation.34 | convolution fusion | flops 134217728 | bytes 1703936 | tf_op jit(solution)/shard_map/dot_general | solution.py:211
  46.0 7.6 %collective-permute-done.4.low_in_beside = f32[1024,128]{1,0:T(8,128)S(1)} collective-permute-done((f32[1024,128]{1,0:T(8,128)S(1)}, f32[1024,128]{1,0:T(8,128)S(1)}, u32[]{:S(2)}, u32[]{:S(2)}) %collective-permute-start.4) | collective-permute-done | bytes 524320 | tf_op jit(solution)/shard_map/ppermute | solution.py:225
  53.6 0.0 collective-permute-done.2.refs_0_
  53.6 5.2 %collective-permute-done.3.refs_1_ = bf16[256,2048]{1,0:T(8,128)(2,1)S(1)} collective-permute-done((bf16[256,2048]{1,0:T(8,128)(2,1)}, bf16[256,2048]{1,0:T(8,128)(2,1)S(1)}, u32[]{:S(2)}, u32[]{:S(2)}) %collective-permute-start.3) | collective-permute-done | bytes 1048608 | tf_op jit(solution)/shard_map/ppermute | solution.py:222
  58.8 0.0 copy-done.6
  58.8 0.4 fusion.16.far_low
  59.2 0.7 token_sums.1
  59.9 0.0 copy-done.8
  60.0 0.7 collective-permute-start.6
  60.6 0.0 collective-permute-done.6
  60.7 1.3 %collective-permute-start.7 = (f32[1,32,64]{2,1,0:T(8,128)S(1)}, f32[1,32,64]{2,1,0:T(8,128)S(1)}, u32[]{:S(2)}, u32[]{:S(2)}) collective-permute-start(f32[1,32,64]{2,1,0:T(8,128)S(1)} %dynamic-slice_bitcast_fusion), channel_id=1, source_target_pairs={{2,0},{1,3},{6,4},{5,7},{10,8},{9,11},{14,12},{13,15},{18,16},{17,... | collective-permute-start | bytes 24584 | tf_op jit(solution)/shard_map/ppermute | solution.py:242
  62.0 1.3 %collective-permute-start.5 = (bf16[256,2048]{1,0:T(8,128)(2,1)}, bf16[256,2048]{1,0:T(8,128)(2,1)S(1)}, u32[]{:S(2)}, u32[]{:S(2)}) collective-permute-start(bf16[256,2048]{1,0:T(8,128)(2,1)} %copy-done.6), channel_id=1, source_target_pairs={{1,0},{2,3},{5,4},{6,7},{9,8},{10,11},{13,12},{14,15},{17,16},{18,... | collective-permute-start | bytes 3145736 | tf_op jit(solution)/shard_map/ppermute | solution.py:231
  63.3 7.1 %collective-permute-done.7 = f32[1,32,64]{2,1,0:T(8,128)S(1)} collective-permute-done((f32[1,32,64]{2,1,0:T(8,128)S(1)}, f32[1,32,64]{2,1,0:T(8,128)S(1)}, u32[]{:S(2)}, u32[]{:S(2)}) %collective-permute-start.7) | collective-permute-done | bytes 8224 | tf_op jit(solution)/shard_map/ppermute | solution.py:242
  70.4 0.1 reshape.28
  70.4 0.0 collective-permute-start.10
  70.4 1.6 %collective-permute-start.9 = (f32[1,2048]{1,0:T(1,128)S(1)}, f32[1,2048]{1,0:T(1,128)S(1)}, u32[]{:S(2)}, u32[]{:S(2)}) collective-permute-start(f32[1,2048]{1,0:T(1,128)S(1)} %reshape.28), channel_id=1, source_target_pairs={{0,8},{4,12},{8,0},{12,4},{1,9},{5,13},{9,1},{13,5},{2,10},{6,14},... | collective-permute-start | bytes 24584 | tf_op jit(solution)/shard_map/ppermute | solution.py:268
  72.0 0.2 collective-permute-start.8
  72.2 3.4 %copy-done.3 = bf16[2048,2048]{1,0:T(8,128)(2,1)S(1)} copy-done((bf16[2048,2048]{1,0:T(8,128)(2,1)S(1)}, bf16[2048,2048]{1,0:T(8,128)(2,1)}, u32[]{:S(2)}) %copy-start.3) | copy-done | bytes 8388632
  75.6 1.2 %copy-done.9 = bf16[256,2048]{1,0:T(8,128)(2,1)S(1)} copy-done((bf16[256,2048]{1,0:T(8,128)(2,1)S(1)}, bf16[256,2048]{1,0:T(8,128)(2,1)}, u32[]{:S(2)}) %copy-start.9) | copy-done | bytes 1048600
  76.8 4.6 %input_grad_rows.6.refs_3_ = bf16[4,256,2048]{2,1,0:T(8,128)(2,1)} custom-call(s32[1]{0:T(128)} %bitcast.me, bf16[256,2048]{1,0:T(8,128)(2,1)} %collective-permute-done.1.refs_0_, bf16[256,2048]{1,0:T(8,128)(2,1)S(1)} %copy-done.9, bf16[2048,2048]{1,0:T(8,128)(2,1)S(1)} %copy-done.3, ...), custom_call_target="tpu_custom_call", output_to_operand_aliasing={{}: (4, {})} | custom-call | flops 524288 | bytes 524288 | tf_op jit(solution)/shard_map/input_grad_rows/pallas_call | solution.py:98
  81.4 0.0 collective-permute-done.10
  81.4 0.0 collective-permute-done.9
  81.4 0.0 collective-permute-done.8
  81.4 0.1 reduce-precision_convert_fusion.1
  81.5 0.0 copy-done
  81.5 0.6 fusion.3
  82.2 0.6 collective-permute-start.13
  82.8 0.6 collective-permute-start.11
  83.4 3.9 %collective-permute-start.12 = (f32[1,512]{1,0:T(1,128)S(1)}, f32[1,512]{1,0:T(1,128)S(1)}, u32[]{:S(2)}, u32[]{:S(2)}) collective-permute-start(f32[1,512]{1,0:T(1,128)S(1)} %get-tuple-element.31), channel_id=1, source_target_pairs={{0,4},{1,8},{2,12},{3,0},{4,5},{5,9},{6,13},{7,1},{8,6},{9,10},{10... | collective-permute-start | bytes 6152 | tf_op jit(solution)/shard_map/ppermute | solution.py:284
  87.4 2.1 %collective-permute-done.5.refs_1_ = bf16[256,2048]{1,0:T(8,128)(2,1)S(1)} collective-permute-done((bf16[256,2048]{1,0:T(8,128)(2,1)}, bf16[256,2048]{1,0:T(8,128)(2,1)S(1)}, u32[]{:S(2)}, u32[]{:S(2)}) %collective-permute-start.5) | collective-permute-done | bytes 1048608 | tf_op jit(solution)/shard_map/ppermute | solution.py:231
  89.5 0.7 collective-permute-start.14
  90.2 0.0 copy-done.7
  90.2 4.4 %input_grad_rows.7 = bf16[4,256,2048]{2,1,0:T(8,128)(2,1)} custom-call(s32[1]{0:T(128)} %bitcast.me, bf16[256,2048]{1,0:T(8,128)(2,1)S(1)} %copy-done.7, bf16[256,2048]{1,0:T(8,128)(2,1)S(1)} %collective-permute-done.5.refs_1_, bf16[2048,2048]{1,0:T(8,128)(2,1)S(1)} %copy-done.3, ...), custom_call_target="tpu_custom_call", output_to_operand_aliasing={{}: (4, {})} | custom-call | flops 524288 | bytes 524288 | tf_op jit(solution)/shard_map/input_grad_rows/pallas_call | solution.py:98
  94.6 0.0 collective-permute-done.13
  94.6 0.0 collective-permute-done.11
  94.6 0.0 collective-permute-done.12
  94.6 0.0 collective-permute-done.14
  94.7 0.6 add_add_fusion
  (14 shorter events, 0.1 us)
Async XLA Ops:
  0.6 80.9 %copy-start = (bf16[512,2048]{1,0:T(8,128)(2,1)S(1)}, bf16[512,2048]{1,0:T(8,128)(2,1)}, u32[]{:S(2)}) copy-start(bf16[512,2048]{1,0:T(8,128)(2,1)} %param.11) | copy-start | bytes 6291460
  0.6 26.5 %collective-permute-start = (bf16[256,2048]{1,0:T(8,128)(2,1)}, bf16[256,2048]{1,0:T(8,128)(2,1)S(1)}, u32[]{:S(2)}, u32[]{:S(2)}) collective-permute-start(bf16[256,2048]{1,0:T(8,128)(2,1)} %refs_1_.1), channel_id=1, source_target_pairs={{0,1},{1,0},{2,3},{3,2},{4,5},{5,4},{6,7},{7,6},{8,9},{9,8},{10,11... | collective-permute-start | bytes 3145736 | tf_op jit(solution)/shard_map/ppermute | solution.py:214
  3.7 23.4 %collective-permute-start.1 = (bf16[256,2048]{1,0:T(8,128)(2,1)}, bf16[256,2048]{1,0:T(8,128)(2,1)}, u32[]{:S(2)}, u32[]{:S(2)}) collective-permute-start(bf16[256,2048]{1,0:T(8,128)(2,1)} %refs_1_.1), channel_id=1, source_target_pairs={{1,2},{2,1},{5,6},{6,5},{9,10},{10,9},{13,14},{14,13},{17,18},{18,... | collective-permute-start | bytes 3145736 | tf_op jit(solution)/shard_map/ppermute | solution.py:213
  5.4 3.4 %copy-start.1 = (bf16[2048,2048]{1,0:T(8,128)(2,1)S(1)}, bf16[2048,2048]{1,0:T(8,128)(2,1)}, u32[]{:S(2)}) copy-start(bf16[2048,2048]{1,0:T(8,128)(2,1)} %refs_2_.7) | copy-start | bytes 25165828
  8.7 1.2 %copy-start.4 = (bf16[256,2048]{1,0:T(8,128)(2,1)S(1)}, bf16[256,2048]{1,0:T(8,128)(2,1)}, u32[]{:S(2)}) copy-start(bf16[256,2048]{1,0:T(8,128)(2,1)} %refs_1_.1) | copy-start | bytes 3145732
  10.0 4.5 %copy-start.10 = (bf16[1024,2048]{1,0:T(8,128)(2,1)S(1)}, bf16[1024,2048]{1,0:T(8,128)(2,1)}, u32[]{:S(2)}) copy-start(bf16[1024,2048]{1,0:T(8,128)(2,1)} %param.6) | copy-start | bytes 12582916
  10.0 4.5 %copy-start.11 = (bf16[2048,128]{1,0:T(8,128)(2,1)S(1)}, bf16[2048,128]{1,0:T(8,128)(2,1)}, u32[]{:S(2)}) copy-start(bf16[2048,128]{1,0:T(8,128)(2,1)} %param.9) | copy-start | bytes 1572868
  10.0 19.2 %copy-start.12 = (bf16[2,1024,64]{1,2,0:T(8,128)(2,1)S(1)}, bf16[2,1024,64]{1,2,0:T(8,128)(2,1)}, u32[]{:S(2)}) copy-start(bf16[2,1024,64]{1,2,0:T(8,128)(2,1)} %param.10) | copy-start | bytes 786436
  10.0 19.2 %copy-start.5 = (bf16[256,2048]{1,0:T(8,128)(2,1)S(1)}, bf16[256,2048]{1,0:T(8,128)(2,1)}, u32[]{:S(2)}) copy-start(bf16[256,2048]{1,0:T(8,128)(2,1)} %refs_1_.1) | copy-start | bytes 3145732
  14.4 15.2 %copy-start.2 = (bf16[2048,2048]{1,0:T(8,128)(2,1)S(1)}, bf16[2048,2048]{1,0:T(8,128)(2,1)}, u32[]{:S(2)}) copy-start(bf16[2048,2048]{1,0:T(8,128)(2,1)} %refs_2_.7) | copy-start | bytes 25165828
  27.1 26.5 %collective-permute-start.2 = (bf16[256,2048]{1,0:T(8,128)(2,1)S(1)}, bf16[256,2048]{1,0:T(8,128)(2,1)S(1)}, u32[]{:S(2)}, u32[]{:S(2)}) collective-permute-start(bf16[256,2048]{1,0:T(8,128)(2,1)S(1)} %collective-permute-done.refs_0_.refs_1_), channel_id=1, source_target_pairs={{1,2},{2,1},{5,6},{6,5},{9,10},{10,9},{13,14},{14,13},{17,18},{18,... | collective-permute-start | bytes 3145736 | tf_op jit(solution)/shard_map/ppermute | solution.py:221
  27.8 31.0 %collective-permute-start.3 = (bf16[256,2048]{1,0:T(8,128)(2,1)}, bf16[256,2048]{1,0:T(8,128)(2,1)S(1)}, u32[]{:S(2)}, u32[]{:S(2)}) collective-permute-start(bf16[256,2048]{1,0:T(8,128)(2,1)} %collective-permute-done.1.refs_0_), channel_id=1, source_target_pairs={{1,0},{2,3},{5,4},{6,7},{9,8},{10,11},{13,12},{14,15},{17,16},{18,... | collective-permute-start | bytes 3145736 | tf_op jit(solution)/shard_map/ppermute | solution.py:222
  34.1 19.4 %collective-permute-start.4 = (f32[1024,128]{1,0:T(8,128)S(1)}, f32[1024,128]{1,0:T(8,128)S(1)}, u32[]{:S(2)}, u32[]{:S(2)}) collective-permute-start(f32[1024,128]{1,0:T(8,128)S(1)} %fusion.13.low_in), channel_id=1, source_target_pairs={{0,1},{3,2},{4,5},{7,6},{8,9},{11,10},{12,13},{15,14},{16,17},{19,... | collective-permute-start | bytes 1572872 | tf_op jit(solution)/shard_map/ppermute | solution.py:225
  53.6 5.2 %copy-start.6 = (bf16[256,2048]{1,0:T(8,128)(2,1)}, bf16[256,2048]{1,0:T(8,128)(2,1)S(1)}, u32[]{:S(2)}) copy-start(bf16[256,2048]{1,0:T(8,128)(2,1)S(1)} %collective-permute-done.2.refs_0_) | copy-start | bytes 3145732
  58.8 1.2 %copy-start.8 = (bf16[256,2048]{1,0:T(8,128)(2,1)}, bf16[256,2048]{1,0:T(8,128)(2,1)S(1)}, u32[]{:S(2)}) copy-start(bf16[256,2048]{1,0:T(8,128)(2,1)S(1)} %collective-permute-done.3.refs_1_) | copy-start | bytes 3145732
  60.0 0.7 collective-permute-start.6
  60.7 9.7 %collective-permute-start.7 = (f32[1,32,64]{2,1,0:T(8,128)S(1)}, f32[1,32,64]{2,1,0:T(8,128)S(1)}, u32[]{:S(2)}, u32[]{:S(2)}) collective-permute-start(f32[1,32,64]{2,1,0:T(8,128)S(1)} %dynamic-slice_bitcast_fusion), channel_id=1, source_target_pairs={{2,0},{1,3},{6,4},{5,7},{10,8},{9,11},{14,12},{13,15},{18,16},{17,... | collective-permute-start | bytes 24584 | tf_op jit(solution)/shard_map/ppermute | solution.py:242
  62.0 27.5 %collective-permute-start.5 = (bf16[256,2048]{1,0:T(8,128)(2,1)}, bf16[256,2048]{1,0:T(8,128)(2,1)S(1)}, u32[]{:S(2)}, u32[]{:S(2)}) collective-permute-start(bf16[256,2048]{1,0:T(8,128)(2,1)} %copy-done.6), channel_id=1, source_target_pairs={{1,0},{2,3},{5,4},{6,7},{9,8},{10,11},{13,12},{14,15},{17,16},{18,... | collective-permute-start | bytes 3145736 | tf_op jit(solution)/shard_map/ppermute | solution.py:231
  70.4 11.0 %collective-permute-start.10 = (f32[1,2048]{1,0:T(1,128)S(1)}, f32[1,2048]{1,0:T(1,128)S(1)}, u32[]{:S(2)}, u32[]{:S(2)}) collective-permute-start(f32[1,2048]{1,0:T(1,128)S(1)} %reshape.28), channel_id=1, source_target_pairs={{0,12},{4,0},{8,4},{12,8},{1,13},{5,1},{9,5},{13,9},{2,14},{6,2},{... | collective-permute-start | bytes 24584 | tf_op jit(solution)/shard_map/ppermute | solution.py:268
  70.4 11.0 %collective-permute-start.9 = (f32[1,2048]{1,0:T(1,128)S(1)}, f32[1,2048]{1,0:T(1,128)S(1)}, u32[]{:S(2)}, u32[]{:S(2)}) collective-permute-start(f32[1,2048]{1,0:T(1,128)S(1)} %reshape.28), channel_id=1, source_target_pairs={{0,8},{4,12},{8,0},{12,4},{1,9},{5,13},{9,1},{13,5},{2,10},{6,14},... | collective-permute-start | bytes 24584 | tf_op jit(solution)/shard_map/ppermute | solution.py:268
  72.0 9.4 %collective-permute-start.8 = (f32[1,2048]{1,0:T(1,128)S(1)}, f32[1,2048]{1,0:T(1,128)S(1)}, u32[]{:S(2)}, u32[]{:S(2)}) collective-permute-start(f32[1,2048]{1,0:T(1,128)S(1)} %reshape.28), channel_id=1, source_target_pairs={{0,4},{4,8},{8,12},{12,0},{1,5},{5,9},{9,13},{13,1},{2,6},{6,10},{... | collective-permute-start | bytes 24584 | tf_op jit(solution)/shard_map/ppermute | solution.py:268
  72.2 3.4 %copy-start.3 = (bf16[2048,2048]{1,0:T(8,128)(2,1)S(1)}, bf16[2048,2048]{1,0:T(8,128)(2,1)}, u32[]{:S(2)}) copy-start(bf16[2048,2048]{1,0:T(8,128)(2,1)} %refs_2_.7) | copy-start | bytes 25165828
  75.6 1.2 %copy-start.9 = (bf16[256,2048]{1,0:T(8,128)(2,1)S(1)}, bf16[256,2048]{1,0:T(8,128)(2,1)}, u32[]{:S(2)}) copy-start(bf16[256,2048]{1,0:T(8,128)(2,1)} %copy-done.8) | copy-start | bytes 3145732
  76.8 13.4 %copy-start.7 = (bf16[256,2048]{1,0:T(8,128)(2,1)S(1)}, bf16[256,2048]{1,0:T(8,128)(2,1)}, u32[]{:S(2)}) copy-start(bf16[256,2048]{1,0:T(8,128)(2,1)} %copy-done.6) | copy-start | bytes 3145732
  82.2 12.4 %collective-permute-start.13 = (f32[1,512]{1,0:T(1,128)S(1)}, f32[1,512]{1,0:T(1,128)S(1)}, u32[]{:S(2)}, u32[]{:S(2)}) collective-permute-start(f32[1,512]{1,0:T(1,128)S(1)} %get-tuple-element.32), channel_id=1, source_target_pairs={{0,8},{1,12},{2,0},{3,4},{4,9},{5,13},{6,1},{7,5},{8,10},{9,14},{1... | collective-permute-start | bytes 6152 | tf_op jit(solution)/shard_map/ppermute | solution.py:284
  82.8 11.9 %collective-permute-start.11 = (f32[1,512]{1,0:T(1,128)S(1)}, f32[1,512]{1,0:T(1,128)S(1)}, u32[]{:S(2)}, u32[]{:S(2)}) collective-permute-start(f32[1,512]{1,0:T(1,128)S(1)} %get-tuple-element.33), channel_id=1, source_target_pairs={{0,0},{1,4},{2,8},{3,12},{4,1},{5,5},{6,9},{7,13},{8,2},{9,6},{10,... | collective-permute-start | bytes 6152 | tf_op jit(solution)/shard_map/ppermute | solution.py:284
  83.4 11.2 %collective-permute-start.12 = (f32[1,512]{1,0:T(1,128)S(1)}, f32[1,512]{1,0:T(1,128)S(1)}, u32[]{:S(2)}, u32[]{:S(2)}) collective-permute-start(f32[1,512]{1,0:T(1,128)S(1)} %get-tuple-element.31), channel_id=1, source_target_pairs={{0,4},{1,8},{2,12},{3,0},{4,5},{5,9},{6,13},{7,1},{8,6},{9,10},{10... | collective-permute-start | bytes 6152 | tf_op jit(solution)/shard_map/ppermute | solution.py:284
  89.5 5.2 %collective-permute-start.14 = (f32[1,512]{1,0:T(1,128)S(1)}, f32[1,512]{1,0:T(1,128)S(1)}, u32[]{:S(2)}, u32[]{:S(2)}) collective-permute-start(f32[1,512]{1,0:T(1,128)S(1)} %dynamic-slice_bitcast_fusion.1), channel_id=1, source_target_pairs={{0,12},{1,0},{2,4},{3,8},{4,13},{5,1},{6,5},{7,9},{8,14},{9,2},{10... | collective-permute-start | bytes 6152 | tf_op jit(solution)/shard_map/ppermute | solution.py:284

commit v9 on v8

--- a/solution.py
+++ b/solution.py
@@ -217,19 +217,16 @@
     low_in = jnp.dot(hidden, proj_in, preferred_element_type=jnp.float32)
     output = put_rows(me, 0, None, [grad_kv], [grad_kv], w_kv, local_rows)
 
+    far_low = lax.ppermute(own_low, "mp", [(3, 1), (0, 2)])
+
     beside, facing, low_in, output = tied((beside, facing, low_in, output))
     beside_across = lax.ppermute(beside, "mp", across)
     second = lax.ppermute(facing, "mp", outward)
+    low_in_beside = lax.ppermute(low_in, "mp", inward)
     output = put_rows(me, 1, output, [beside], [beside], w_kv, local_rows)
-    low_in, output = tied((low_in, output))
-    low_in_beside = lax.ppermute(low_in, "mp", inward)
 
     beside_low = low_rank(beside)
     facing_low = low_rank(facing)
-
-    beside_across, second, low_in_beside, output = tied((beside_across, second, low_in_beside, output))
-    third = lax.ppermute(beside_across, "mp", outward)
-    far_low = low_rank(beside_across)
     if low_in.shape[0] == SEQ:
         slabs = token_sums(me, low_in, low_in_beside, own_low, beside_low, facing_low, far_low, rank)[:, None]
     else:
@@ -239,6 +236,9 @@
         sums = sequence_sums(low_in + low_in_beside, low_out.reshape(4 * local_rows, 2 * rank), rank)
         slabs = slabs_of(sums, 4)
     slabs = slabs + lax.ppermute(slabs, "mp", across)
+
+    beside_across, second, slabs, output = tied((beside_across, second, slabs, output))
+    third = lax.ppermute(beside_across, "mp", outward)
     mine = lax.ppermute(take(slabs, me ^ 2), "mp", [(2, 0), (1, 3)])
     mine = jnp.where(middle, take(slabs, me), mine)
     output = put_rows(me, 2, output, [facing], [second], w_kv, local_rows)

time: 95.7 us -> 96.9 us (1.013)
  local copies, waits for them, and re-layouts: 9.38 us -> 12.5 us
  waiting for transfers between devices: 33.4 us -> 30.3 us
    ppermute x0 -> x1, starting transfers between devices: none -> 9.48 us  [line_of_four(): far_low = lax.ppermute(own_low, 'mp', [(3, 1), (0, 2)])]
    ppermute x1, starting transfers between devices: 9.79 us -> 1.59 us  [line_of_four(): low_in_beside = lax.ppermute(low_in, 'mp', inward)]
    ppermute x1, waiting for transfers between devices: 5.22 us -> 0.01 us  [line_of_four(): second = lax.ppermute(facing, 'mp', outward)]
    ppermute x1, waiting for transfers between devices: 2.11 us -> 5.07 us  [line_of_four(): third = lax.ppermute(beside_across, 'mp', outward)]
    unnamed x26 -> x14, local copies, waits for them, and re-layouts: 9.25 us -> 11.4 us
    ppermute x4, starting transfers between devices: 5.86 us -> 4.16 us  [on_device(): scores = scores + lax.ppermute(row, ('dp', 'mp'), pairs)]
    ppermute x1, waiting for transfers between devices: 7.06 us -> 5.67 us  [line_of_four(): mine = lax.ppermute(take(slabs, me ^ 2), 'mp', [(2, 0), (1, 3)])]
    ppermute x1, waiting for transfers between devices: 7.55 us -> 8.93 us  [line_of_four(): low_in_beside = lax.ppermute(low_in, 'mp', inward)]
  transfers between devices with their start and end apart: 15 -> 16, of which waited for: 5 -> 5; matrix products, arithmetic and copies ran while one was open for 5% -> 6% of each run, Pallas kernels for 19% -> 20%
where the time goes in v9:
time: 96.9 us; the launch traced here: 96.1 us
  waiting for transfers between devices  30.3 us (31%)
  starting transfers between devices  28.2 us (29%)
  Pallas kernels  19 us (20%)
  local copies, waits for them, and re-layouts  12.5 us (13%)
  matrix products  4.41 us (5%)
    pallas_call x4, Pallas kernels, put_rows(): pl.pallas_call(functools.partial(rows_kernel, block, start, count), in_sp...  18.3 us
    unnamed x14, local copies, waits for them, and re-layouts  11.4 us
    ppermute x1, waiting for transfers between devices, line_of_four(): beside = lax.ppermute(grad_kv, 'mp', exchange_pairs)  10.4 us
    ppermute x1, starting transfers between devices, line_of_four(): far_low = lax.ppermute(own_low, 'mp', [(3, 1), (0, 2)])  9.48 us
    ppermute x1, waiting for transfers between devices, line_of_four(): low_in_beside = lax.ppermute(low_in, 'mp', inward)  8.93 us
    ppermute x1, waiting for transfers between devices, line_of_four(): mine = lax.ppermute(take(slabs, me ^ 2), 'mp', [(2, 0), (1, 3)])  5.67 us
    ppermute x1, waiting for transfers between devices, line_of_four(): third = lax.ppermute(beside_across, 'mp', outward)  5.07 us
    ppermute x4, starting transfers between devices, on_device(): scores = scores + lax.ppermute(row, ('dp', 'mp'), pairs)  4.16 us
  transfers between devices with their start and end apart: 16, of which 5 were waited for; matrix products, arithmetic and copies ran while one was open for 6% of the time, Pallas kernels for 20%

profile of v9, /device:TPU:0, one launch (start us, length us, event | category | flops | bytes accessed | tf_op | source)
XLA Modules:
  0.0 96.1 jit_solution(7813052446838086068)
XLA Ops:
  0.6 0.0 copy-start
  0.6 3.1 %collective-permute-start = (bf16[256,2048]{1,0:T(8,128)(2,1)}, bf16[256,2048]{1,0:T(8,128)(2,1)S(1)}, u32[]{:S(2)}, u32[]{:S(2)}) collective-permute-start(bf16[256,2048]{1,0:T(8,128)(2,1)} %refs_1_.1), channel_id=1, source_target_pairs={{0,1},{1,0},{2,3},{3,2},{4,5},{5,4},{6,7},{7,6},{8,9},{9,8},{10,11... | collective-permute-start | bytes 3145736 | tf_op jit(solution)/shard_map/ppermute | solution.py:214
  3.7 1.6 %collective-permute-start.1 = (bf16[256,2048]{1,0:T(8,128)(2,1)}, bf16[256,2048]{1,0:T(8,128)(2,1)}, u32[]{:S(2)}, u32[]{:S(2)}) collective-permute-start(bf16[256,2048]{1,0:T(8,128)(2,1)} %refs_1_.1), channel_id=1, source_target_pairs={{1,2},{2,1},{5,6},{6,5},{9,10},{10,9},{13,14},{14,13},{17,18},{18,... | collective-permute-start | bytes 3145736 | tf_op jit(solution)/shard_map/ppermute | solution.py:213
  5.4 1.0 %slice_bitcast_fusion.1 = (bf16[1024,64]{0,1:T(8,128)(2,1)S(1)}, bf16[1024,64]{0,1:T(8,128)(2,1)S(1)}) fusion(bf16[2,1024,64]{1,2,0:T(8,128)(2,1)} %param.10), kind=kLoop, calls=%fused_computation.7 | loop fusion | bytes 524288 | tf_op jit(solution)/shard_map/squeeze | solution.py:26
  6.4 0.0 copy-start.1
  6.4 3.4 %copy-done.1 = bf16[2048,2048]{1,0:T(8,128)(2,1)S(1)} copy-done((bf16[2048,2048]{1,0:T(8,128)(2,1)S(1)}, bf16[2048,2048]{1,0:T(8,128)(2,1)}, u32[]{:S(2)}) %copy-start.1) | copy-done | bytes 8388632
  9.8 0.0 copy-start.4
  9.8 1.2 %copy-done.4 = bf16[256,2048]{1,0:T(8,128)(2,1)S(1)} copy-done((bf16[256,2048]{1,0:T(8,128)(2,1)S(1)}, bf16[256,2048]{1,0:T(8,128)(2,1)}, u32[]{:S(2)}) %copy-start.4) | copy-done | bytes 1048600
  11.0 0.0 copy-start.5
  11.0 0.0 copy-start.6
  11.0 4.4 %input_grad_rows.4.refs_3_ = bf16[4,256,2048]{2,1,0:T(8,128)(2,1)} custom-call(s32[1]{0:T(128)} %bitcast.me, bf16[256,2048]{1,0:T(8,128)(2,1)S(1)} %copy-done.4, bf16[256,2048]{1,0:T(8,128)(2,1)S(1)} %copy-done.4, bf16[2048,2048]{1,0:T(8,128)(2,1)S(1)} %copy-done.1), custom_call_target="tpu_custom_call" | custom-call | flops 524288 | bytes 524288 | tf_op jit(solution)/shard_map/input_grad_rows/pallas_call | solution.py:98
  15.4 0.0 copy-done.5
  15.4 0.0 copy-done.6
  15.5 1.2 %fusion.13.low_in = f32[1024,128]{1,0:T(8,128)S(1)} fusion(bf16[1024,2048]{1,0:T(8,128)(2,1)S(1)} %copy-done.5, bf16[2048,128]{1,0:T(8,128)(2,1)S(1)} %copy-done.6), kind=kOutput, calls=%fused_computation.32 | convolution fusion | flops 536870912 | bytes 5242880 | tf_op jit(solution)/shard_map/dot_general | solution.py:217
  16.7 10.4 %collective-permute-done.refs_0_.refs_1_ = bf16[256,2048]{1,0:T(8,128)(2,1)S(1)} collective-permute-done((bf16[256,2048]{1,0:T(8,128)(2,1)}, bf16[256,2048]{1,0:T(8,128)(2,1)S(1)}, u32[]{:S(2)}, u32[]{:S(2)}) %collective-permute-start) | collective-permute-done | bytes 1048608 | tf_op jit(solution)/shard_map/ppermute | solution.py:214
  27.1 0.0 collective-permute-done.1.refs_0_
  27.1 1.7 %collective-permute-start.2 = (bf16[256,2048]{1,0:T(8,128)(2,1)S(1)}, bf16[256,2048]{1,0:T(8,128)(2,1)}, u32[]{:S(2)}, u32[]{:S(2)}) collective-permute-start(bf16[256,2048]{1,0:T(8,128)(2,1)S(1)} %collective-permute-done.refs_0_.refs_1_), channel_id=1, source_target_pairs={{1,2},{2,1},{5,6},{6,5},{9,10},{10,9},{13,14},{14,13},{17,18},{18,... | collective-permute-start | bytes 3145736 | tf_op jit(solution)/shard_map/ppermute | solution.py:223
  28.8 1.3 %collective-permute-start.3 = (bf16[256,2048]{1,0:T(8,128)(2,1)}, bf16[256,2048]{1,0:T(8,128)(2,1)}, u32[]{:S(2)}, u32[]{:S(2)}) collective-permute-start(bf16[256,2048]{1,0:T(8,128)(2,1)} %collective-permute-done.1.refs_0_), channel_id=1, source_target_pairs={{1,0},{2,3},{5,4},{6,7},{9,8},{10,11},{13,12},{14,15},{17,16},{18,... | collective-permute-start | bytes 3145736 | tf_op jit(solution)/shard_map/ppermute | solution.py:224
  30.1 0.4 convolution_bitcast_fusion.own_low
  30.5 9.5 %collective-permute-start.5 = (f32[256,128]{1,0:T(8,128)S(1)}, f32[256,128]{1,0:T(8,128)S(1)}, u32[]{:S(2)}, u32[]{:S(2)}) collective-permute-start(f32[256,128]{1,0:T(8,128)S(1)} %convolution_bitcast_fusion.own_low), channel_id=1, source_target_pairs={{3,1},{0,2},{7,5},{4,6},{11,9},{8,10},{15,13},{12,14},{19,17},{16,... | collective-permute-start | bytes 393224 | tf_op jit(solution)/shard_map/ppermute | solution.py:220
  40.0 1.6 %collective-permute-start.4 = (f32[1024,128]{1,0:T(8,128)S(1)}, f32[1024,128]{1,0:T(8,128)S(1)}, u32[]{:S(2)}, u32[]{:S(2)}) collective-permute-start(f32[1024,128]{1,0:T(8,128)S(1)} %fusion.13.low_in), channel_id=1, source_target_pairs={{0,1},{3,2},{4,5},{7,6},{8,9},{11,10},{12,13},{15,14},{16,17},{19,... | collective-permute-start | bytes 1572872 | tf_op jit(solution)/shard_map/ppermute | solution.py:225
  41.6 0.4 fusion.14.beside_low
  42.0 1.7 %fusion.15.facing_low = f32[256,128]{1,0:T(8,128)S(1)} fusion(bf16[256,2048]{1,0:T(8,128)(2,1)} %collective-permute-done.1.refs_0_, bf16[2048,128]{0,1:T(8,128)(2,1)S(1)} %fusion.2), kind=kOutput, calls=%fused_computation.34 | convolution fusion | flops 134217728 | bytes 1703936 | tf_op jit(solution)/shard_map/dot_general | solution.py:211
  43.7 0.2 collective-permute-done.5.far_low
  43.9 8.9 %collective-permute-done.4.low_in_beside = f32[1024,128]{1,0:T(8,128)S(1)} collective-permute-done((f32[1024,128]{1,0:T(8,128)S(1)}, f32[1024,128]{1,0:T(8,128)S(1)}, u32[]{:S(2)}, u32[]{:S(2)}) %collective-permute-start.4) | collective-permute-done | bytes 524320 | tf_op jit(solution)/shard_map/ppermute | solution.py:225
  52.8 0.7 token_sums.1
  53.6 0.7 collective-permute-start.6
  54.2 0.0 copy-start.2
  54.3 3.4 %copy-done.2 = bf16[2048,2048]{1,0:T(8,128)(2,1)S(1)} copy-done((bf16[2048,2048]{1,0:T(8,128)(2,1)S(1)}, bf16[2048,2048]{1,0:T(8,128)(2,1)}, u32[]{:S(2)}) %copy-start.2) | copy-done | bytes 8388632
  57.6 4.4 %input_grad_rows.5.refs_3_ = bf16[4,256,2048]{2,1,0:T(8,128)(2,1)} custom-call(s32[1]{0:T(128)} %bitcast.me, bf16[256,2048]{1,0:T(8,128)(2,1)S(1)} %collective-permute-done.refs_0_.refs_1_, bf16[256,2048]{1,0:T(8,128)(2,1)S(1)} %collective-permute-done.refs_0_.refs_1_, bf16[2048,2048]{1,0:T(8,128)(2,1)S(1)} %copy-done.2, ...), custom_call_target="tpu_custom_call", output_to_operand_aliasing={{}: (4, {})} | custom-call | flops 524288 | bytes 524288 | tf_op jit(solution)/shard_map/input_grad_rows/pallas_call | solution.py:98
  62.1 0.0 collective-permute-done.6
  62.1 0.0 collective-permute-done.2.refs_0_
  62.1 0.0 collective-permute-done.3.refs_1_
  62.1 1.3 %collective-permute-start.8 = (f32[1,32,64]{2,1,0:T(8,128)S(1)}, f32[1,32,64]{2,1,0:T(8,128)S(1)}, u32[]{:S(2)}, u32[]{:S(2)}) collective-permute-start(f32[1,32,64]{2,1,0:T(8,128)S(1)} %dynamic-slice_bitcast_fusion), channel_id=1, source_target_pairs={{2,0},{1,3},{6,4},{5,7},{10,8},{9,11},{14,12},{13,15},{18,16},{17,... | collective-permute-start | bytes 24584 | tf_op jit(solution)/shard_map/ppermute | solution.py:242
  63.4 1.3 %collective-permute-start.7 = (bf16[256,2048]{1,0:T(8,128)(2,1)}, bf16[256,2048]{1,0:T(8,128)(2,1)S(1)}, u32[]{:S(2)}, u32[]{:S(2)}) collective-permute-start(bf16[256,2048]{1,0:T(8,128)(2,1)} %collective-permute-done.2.refs_0_), channel_id=1, source_target_pairs={{1,0},{2,3},{5,4},{6,7},{9,8},{10,11},{13,12},{14,15},{17,16},{18,... | collective-permute-start | bytes 3145736 | tf_op jit(solution)/shard_map/ppermute | solution.py:241
  64.7 5.7 %collective-permute-done.8 = f32[1,32,64]{2,1,0:T(8,128)S(1)} collective-permute-done((f32[1,32,64]{2,1,0:T(8,128)S(1)}, f32[1,32,64]{2,1,0:T(8,128)S(1)}, u32[]{:S(2)}, u32[]{:S(2)}) %collective-permute-start.8) | collective-permute-done | bytes 8224 | tf_op jit(solution)/shard_map/ppermute | solution.py:242
  70.4 0.1 reshape.28
  70.5 1.5 %collective-permute-start.10 = (f32[1,2048]{1,0:T(1,128)S(1)}, f32[1,2048]{1,0:T(1,128)S(1)}, u32[]{:S(2)}, u32[]{:S(2)}) collective-permute-start(f32[1,2048]{1,0:T(1,128)S(1)} %reshape.28), channel_id=1, source_target_pairs={{0,8},{4,12},{8,0},{12,4},{1,9},{5,13},{9,1},{13,5},{2,10},{6,14},... | collective-permute-start | bytes 24584 | tf_op jit(solution)/shard_map/ppermute | solution.py:268
  72.0 0.0 collective-permute-start.11
  72.0 0.5 collective-permute-start.9
  72.5 0.0 copy-start.3
  72.5 3.4 %copy-done.3 = bf16[2048,2048]{1,0:T(8,128)(2,1)S(1)} copy-done((bf16[2048,2048]{1,0:T(8,128)(2,1)S(1)}, bf16[2048,2048]{1,0:T(8,128)(2,1)}, u32[]{:S(2)}) %copy-start.3) | copy-done | bytes 8388632
  75.9 5.0 %input_grad_rows.6.refs_3_ = bf16[4,256,2048]{2,1,0:T(8,128)(2,1)} custom-call(s32[1]{0:T(128)} %bitcast.me, bf16[256,2048]{1,0:T(8,128)(2,1)} %collective-permute-done.1.refs_0_, bf16[256,2048]{1,0:T(8,128)(2,1)} %collective-permute-done.3.refs_1_, bf16[2048,2048]{1,0:T(8,128)(2,1)S(1)} %copy-done.3, ...), custom_call_target="tpu_custom_call", output_to_operand_aliasing={{}: (4, {})} | custom-call | flops 524288 | bytes 524288 | tf_op jit(solution)/shard_map/input_grad_rows/pallas_call | solution.py:98
  80.9 0.0 collective-permute-done.10
  80.9 0.0 collective-permute-done.11
  81.0 0.0 collective-permute-done.9
  81.0 0.1 reduce-precision_convert_fusion.1
  81.0 0.0 copy-done
  81.0 0.6 fusion.3
  81.7 0.7 collective-permute-start.12
  82.4 1.5 %collective-permute-start.13 = (f32[1,512]{1,0:T(1,128)S(1)}, f32[1,512]{1,0:T(1,128)S(1)}, u32[]{:S(2)}, u32[]{:S(2)}) collective-permute-start(f32[1,512]{1,0:T(1,128)S(1)} %get-tuple-element.27), channel_id=1, source_target_pairs={{0,4},{1,8},{2,12},{3,0},{4,5},{5,9},{6,13},{7,1},{8,6},{9,10},{10... | collective-permute-start | bytes 6152 | tf_op jit(solution)/shard_map/ppermute | solution.py:284
  83.9 2.0 %collective-permute-start.14 = (f32[1,512]{1,0:T(1,128)S(1)}, f32[1,512]{1,0:T(1,128)S(1)}, u32[]{:S(2)}, u32[]{:S(2)}) collective-permute-start(f32[1,512]{1,0:T(1,128)S(1)} %get-tuple-element.28), channel_id=1, source_target_pairs={{0,8},{1,12},{2,0},{3,4},{4,9},{5,13},{6,1},{7,5},{8,10},{9,14},{1... | collective-permute-start | bytes 6152 | tf_op jit(solution)/shard_map/ppermute | solution.py:284
  85.9 5.1 %collective-permute-done.7.refs_1_ = bf16[256,2048]{1,0:T(8,128)(2,1)S(1)} collective-permute-done((bf16[256,2048]{1,0:T(8,128)(2,1)}, bf16[256,2048]{1,0:T(8,128)(2,1)S(1)}, u32[]{:S(2)}, u32[]{:S(2)}) %collective-permute-start.7) | collective-permute-done | bytes 1048608 | tf_op jit(solution)/shard_map/ppermute | solution.py:241
  91.0 0.0 collective-permute-start.15
  91.0 4.4 %input_grad_rows.7 = bf16[4,256,2048]{2,1,0:T(8,128)(2,1)} custom-call(s32[1]{0:T(128)} %bitcast.me, bf16[256,2048]{1,0:T(8,128)(2,1)} %collective-permute-done.2.refs_0_, bf16[256,2048]{1,0:T(8,128)(2,1)S(1)} %collective-permute-done.7.refs_1_, bf16[2048,2048]{1,0:T(8,128)(2,1)S(1)} %copy-done.3, ...), custom_call_target="tpu_custom_call", output_to_operand_aliasing={{}: (4, {})} | custom-call | flops 524288 | bytes 524288 | tf_op jit(solution)/shard_map/input_grad_rows/pallas_call | solution.py:98
  95.4 0.0 collective-permute-done.12
  95.4 0.0 collective-permute-done.13
  95.4 0.0 collective-permute-done.14
  95.5 0.0 collective-permute-done.15
  95.5 0.6 add_add_fusion
  (7 shorter events, 0.1 us)
Async XLA Ops:
  0.6 80.4 %copy-start = (bf16[512,2048]{1,0:T(8,128)(2,1)S(1)}, bf16[512,2048]{1,0:T(8,128)(2,1)}, u32[]{:S(2)}) copy-start(bf16[512,2048]{1,0:T(8,128)(2,1)} %param.11) | copy-start | bytes 6291460
  0.6 26.5 %collective-permute-start = (bf16[256,2048]{1,0:T(8,128)(2,1)}, bf16[256,2048]{1,0:T(8,128)(2,1)S(1)}, u32[]{:S(2)}, u32[]{:S(2)}) collective-permute-start(bf16[256,2048]{1,0:T(8,128)(2,1)} %refs_1_.1), channel_id=1, source_target_pairs={{0,1},{1,0},{2,3},{3,2},{4,5},{5,4},{6,7},{7,6},{8,9},{9,8},{10,11... | collective-permute-start | bytes 3145736 | tf_op jit(solution)/shard_map/ppermute | solution.py:214
  3.7 23.4 %collective-permute-start.1 = (bf16[256,2048]{1,0:T(8,128)(2,1)}, bf16[256,2048]{1,0:T(8,128)(2,1)}, u32[]{:S(2)}, u32[]{:S(2)}) collective-permute-start(bf16[256,2048]{1,0:T(8,128)(2,1)} %refs_1_.1), channel_id=1, source_target_pairs={{1,2},{2,1},{5,6},{6,5},{9,10},{10,9},{13,14},{14,13},{17,18},{18,... | collective-permute-start | bytes 3145736 | tf_op jit(solution)/shard_map/ppermute | solution.py:213
  6.4 3.4 %copy-start.1 = (bf16[2048,2048]{1,0:T(8,128)(2,1)S(1)}, bf16[2048,2048]{1,0:T(8,128)(2,1)}, u32[]{:S(2)}) copy-start(bf16[2048,2048]{1,0:T(8,128)(2,1)} %refs_2_.7) | copy-start | bytes 25165828
  9.8 1.2 %copy-start.4 = (bf16[256,2048]{1,0:T(8,128)(2,1)S(1)}, bf16[256,2048]{1,0:T(8,128)(2,1)}, u32[]{:S(2)}) copy-start(bf16[256,2048]{1,0:T(8,128)(2,1)} %refs_1_.1) | copy-start | bytes 3145732
  11.0 4.4 %copy-start.5 = (bf16[1024,2048]{1,0:T(8,128)(2,1)S(1)}, bf16[1024,2048]{1,0:T(8,128)(2,1)}, u32[]{:S(2)}) copy-start(bf16[1024,2048]{1,0:T(8,128)(2,1)} %param.6) | copy-start | bytes 12582916
  11.0 4.4 %copy-start.6 = (bf16[2048,128]{1,0:T(8,128)(2,1)S(1)}, bf16[2048,128]{1,0:T(8,128)(2,1)}, u32[]{:S(2)}) copy-start(bf16[2048,128]{1,0:T(8,128)(2,1)} %param.9) | copy-start | bytes 1572868
  27.1 35.0 %collective-permute-start.2 = (bf16[256,2048]{1,0:T(8,128)(2,1)S(1)}, bf16[256,2048]{1,0:T(8,128)(2,1)}, u32[]{:S(2)}, u32[]{:S(2)}) collective-permute-start(bf16[256,2048]{1,0:T(8,128)(2,1)S(1)} %collective-permute-done.refs_0_.refs_1_), channel_id=1, source_target_pairs={{1,2},{2,1},{5,6},{6,5},{9,10},{10,9},{13,14},{14,13},{17,18},{18,... | collective-permute-start | bytes 3145736 | tf_op jit(solution)/shard_map/ppermute | solution.py:223
  28.8 33.3 %collective-permute-start.3 = (bf16[256,2048]{1,0:T(8,128)(2,1)}, bf16[256,2048]{1,0:T(8,128)(2,1)}, u32[]{:S(2)}, u32[]{:S(2)}) collective-permute-start(bf16[256,2048]{1,0:T(8,128)(2,1)} %collective-permute-done.1.refs_0_), channel_id=1, source_target_pairs={{1,0},{2,3},{5,4},{6,7},{9,8},{10,11},{13,12},{14,15},{17,16},{18,... | collective-permute-start | bytes 3145736 | tf_op jit(solution)/shard_map/ppermute | solution.py:224
  30.5 13.4 %collective-permute-start.5 = (f32[256,128]{1,0:T(8,128)S(1)}, f32[256,128]{1,0:T(8,128)S(1)}, u32[]{:S(2)}, u32[]{:S(2)}) collective-permute-start(f32[256,128]{1,0:T(8,128)S(1)} %convolution_bitcast_fusion.own_low), channel_id=1, source_target_pairs={{3,1},{0,2},{7,5},{4,6},{11,9},{8,10},{15,13},{12,14},{19,17},{16,... | collective-permute-start | bytes 393224 | tf_op jit(solution)/shard_map/ppermute | solution.py:220
  40.0 12.9 %collective-permute-start.4 = (f32[1024,128]{1,0:T(8,128)S(1)}, f32[1024,128]{1,0:T(8,128)S(1)}, u32[]{:S(2)}, u32[]{:S(2)}) collective-permute-start(f32[1024,128]{1,0:T(8,128)S(1)} %fusion.13.low_in), channel_id=1, source_target_pairs={{0,1},{3,2},{4,5},{7,6},{8,9},{11,10},{12,13},{15,14},{16,17},{19,... | collective-permute-start | bytes 1572872 | tf_op jit(solution)/shard_map/ppermute | solution.py:225
  53.6 8.5 %collective-permute-start.6 = (f32[4,1,32,64]{3,2,0,1:T(8,128)S(1)}, f32[4,1,32,64]{3,2,0,1:T(8,128)S(1)}, u32[]{:S(2)}, u32[]{:S(2)}) collective-permute-start(f32[4,1,32,64]{3,2,0,1:T(8,128)S(1)} %bitcast.33), channel_id=1, source_target_pairs={{1,2},{2,1},{5,6},{6,5},{9,10},{10,9},{13,14},{14,13},{17,18},{18,... | collective-permute-start | bytes 98312 | tf_op jit(solution)/shard_map/ppermute | solution.py:238
  54.2 3.4 %copy-start.2 = (bf16[2048,2048]{1,0:T(8,128)(2,1)S(1)}, bf16[2048,2048]{1,0:T(8,128)(2,1)}, u32[]{:S(2)}) copy-start(bf16[2048,2048]{1,0:T(8,128)(2,1)} %refs_2_.7) | copy-start | bytes 25165828
  62.1 8.3 %collective-permute-start.8 = (f32[1,32,64]{2,1,0:T(8,128)S(1)}, f32[1,32,64]{2,1,0:T(8,128)S(1)}, u32[]{:S(2)}, u32[]{:S(2)}) collective-permute-start(f32[1,32,64]{2,1,0:T(8,128)S(1)} %dynamic-slice_bitcast_fusion), channel_id=1, source_target_pairs={{2,0},{1,3},{6,4},{5,7},{10,8},{9,11},{14,12},{13,15},{18,16},{17,... | collective-permute-start | bytes 24584 | tf_op jit(solution)/shard_map/ppermute | solution.py:242
  63.4 27.5 %collective-permute-start.7 = (bf16[256,2048]{1,0:T(8,128)(2,1)}, bf16[256,2048]{1,0:T(8,128)(2,1)S(1)}, u32[]{:S(2)}, u32[]{:S(2)}) collective-permute-start(bf16[256,2048]{1,0:T(8,128)(2,1)} %collective-permute-done.2.refs_0_), channel_id=1, source_target_pairs={{1,0},{2,3},{5,4},{6,7},{9,8},{10,11},{13,12},{14,15},{17,16},{18,... | collective-permute-start | bytes 3145736 | tf_op jit(solution)/shard_map/ppermute | solution.py:241
  70.5 10.4 %collective-permute-start.10 = (f32[1,2048]{1,0:T(1,128)S(1)}, f32[1,2048]{1,0:T(1,128)S(1)}, u32[]{:S(2)}, u32[]{:S(2)}) collective-permute-start(f32[1,2048]{1,0:T(1,128)S(1)} %reshape.28), channel_id=1, source_target_pairs={{0,8},{4,12},{8,0},{12,4},{1,9},{5,13},{9,1},{13,5},{2,10},{6,14},... | collective-permute-start | bytes 24584 | tf_op jit(solution)/shard_map/ppermute | solution.py:268
  72.0 8.9 %collective-permute-start.11 = (f32[1,2048]{1,0:T(1,128)S(1)}, f32[1,2048]{1,0:T(1,128)S(1)}, u32[]{:S(2)}, u32[]{:S(2)}) collective-permute-start(f32[1,2048]{1,0:T(1,128)S(1)} %reshape.28), channel_id=1, source_target_pairs={{0,12},{4,0},{8,4},{12,8},{1,13},{5,1},{9,5},{13,9},{2,14},{6,2},{... | collective-permute-start | bytes 24584 | tf_op jit(solution)/shard_map/ppermute | solution.py:268
  72.0 8.9 %collective-permute-start.9 = (f32[1,2048]{1,0:T(1,128)S(1)}, f32[1,2048]{1,0:T(1,128)S(1)}, u32[]{:S(2)}, u32[]{:S(2)}) collective-permute-start(f32[1,2048]{1,0:T(1,128)S(1)} %reshape.28), channel_id=1, source_target_pairs={{0,4},{4,8},{8,12},{12,0},{1,5},{5,9},{9,13},{13,1},{2,6},{6,10},{... | collective-permute-start | bytes 24584 | tf_op jit(solution)/shard_map/ppermute | solution.py:268
  72.5 3.4 %copy-start.3 = (bf16[2048,2048]{1,0:T(8,128)(2,1)S(1)}, bf16[2048,2048]{1,0:T(8,128)(2,1)}, u32[]{:S(2)}) copy-start(bf16[2048,2048]{1,0:T(8,128)(2,1)} %refs_2_.7) | copy-start | bytes 25165828
  81.7 13.7 %collective-permute-start.12 = (f32[1,512]{1,0:T(1,128)S(1)}, f32[1,512]{1,0:T(1,128)S(1)}, u32[]{:S(2)}, u32[]{:S(2)}) collective-permute-start(f32[1,512]{1,0:T(1,128)S(1)} %get-tuple-element.29), channel_id=1, source_target_pairs={{0,0},{1,4},{2,8},{3,12},{4,1},{5,5},{6,9},{7,13},{8,2},{9,6},{10,... | collective-permute-start | bytes 6152 | tf_op jit(solution)/shard_map/ppermute | solution.py:284
  82.4 13.0 %collective-permute-start.13 = (f32[1,512]{1,0:T(1,128)S(1)}, f32[1,512]{1,0:T(1,128)S(1)}, u32[]{:S(2)}, u32[]{:S(2)}) collective-permute-start(f32[1,512]{1,0:T(1,128)S(1)} %get-tuple-element.27), channel_id=1, source_target_pairs={{0,4},{1,8},{2,12},{3,0},{4,5},{5,9},{6,13},{7,1},{8,6},{9,10},{10... | collective-permute-start | bytes 6152 | tf_op jit(solution)/shard_map/ppermute | solution.py:284
  83.9 11.6 %collective-permute-start.14 = (f32[1,512]{1,0:T(1,128)S(1)}, f32[1,512]{1,0:T(1,128)S(1)}, u32[]{:S(2)}, u32[]{:S(2)}) collective-permute-start(f32[1,512]{1,0:T(1,128)S(1)} %get-tuple-element.28), channel_id=1, source_target_pairs={{0,8},{1,12},{2,0},{3,4},{4,9},{5,13},{6,1},{7,5},{8,10},{9,14},{1... | collective-permute-start | bytes 6152 | tf_op jit(solution)/shard_map/ppermute | solution.py:284
  91.0 4.5 %collective-permute-start.15 = (f32[1,512]{1,0:T(1,128)S(1)}, f32[1,512]{1,0:T(1,128)S(1)}, u32[]{:S(2)}, u32[]{:S(2)}) collective-permute-start(f32[1,512]{1,0:T(1,128)S(1)} %dynamic-slice_bitcast_fusion.1), channel_id=1, source_target_pairs={{0,12},{1,0},{2,4},{3,8},{4,13},{5,1},{6,5},{7,9},{8,14},{9,2},{10... | collective-permute-start | bytes 6152 | tf_op jit(solution)/shard_map/ppermute | solution.py:284

commit v10 on v9

--- a/solution.py
+++ b/solution.py
@@ -219,12 +219,13 @@
 
     far_low = lax.ppermute(own_low, "mp", [(3, 1), (0, 2)])
 
-    beside, facing, low_in, output = tied((beside, facing, low_in, output))
+    beside, low_in, output = tied((beside, low_in, output))
     beside_across = lax.ppermute(beside, "mp", across)
     second = lax.ppermute(facing, "mp", outward)
     low_in_beside = lax.ppermute(low_in, "mp", inward)
     output = put_rows(me, 1, output, [beside], [beside], w_kv, local_rows)
 
+    far_low, output = tied((far_low, output))
     beside_low = low_rank(beside)
     facing_low = low_rank(facing)
     if low_in.shape[0] == SEQ:

time: 96.9 us -> 92.2 us (0.951)
  local copies, waits for them, and re-layouts: 12.5 us -> 9.09 us
  starting transfers between devices: 28.2 us -> 26.8 us
    unnamed x14, local copies, waits for them, and re-layouts: 11.4 us -> 8 us
    ppermute x1, waiting for transfers between devices: 5.67 us -> 8.93 us  [line_of_four(): mine = lax.ppermute(take(slabs, me ^ 2), 'mp', [(2, 0), (1, 3)])]
    ppermute x1, waiting for transfers between devices: 8.93 us -> 7.15 us  [line_of_four(): low_in_beside = lax.ppermute(low_in, 'mp', inward)]
    ppermute x1, starting transfers between devices: 9.48 us -> 7.84 us  [line_of_four(): far_low = lax.ppermute(own_low, 'mp', [(3, 1), (0, 2)])]
    ppermute x1, waiting for transfers between devices: 5.07 us -> 3.55 us  [line_of_four(): third = lax.ppermute(beside_across, 'mp', outward)]
  transfers between devices with their start and end apart: 16 -> 16, of which waited for: 5 -> 5; matrix products, arithmetic and copies ran while one was open for 6% -> 6% of each run, Pallas kernels for 20% -> 21%
where the time goes in v10:
time: 92.2 us; the launch traced here: 91.5 us
  waiting for transfers between devices  30.5 us (33%)
  starting transfers between devices  26.8 us (29%)
  Pallas kernels  19 us (21%)
  local copies, waits for them, and re-layouts  9.09 us (10%)
  matrix products  4.41 us (5%)
  between operations  0.94 us (1%)
    pallas_call x4, Pallas kernels, put_rows(): pl.pallas_call(functools.partial(rows_kernel, block, start, count), in_sp...  18.3 us
    ppermute x1, waiting for transfers between devices, line_of_four(): beside = lax.ppermute(grad_kv, 'mp', exchange_pairs)  10.4 us
    ppermute x1, waiting for transfers between devices, line_of_four(): mine = lax.ppermute(take(slabs, me ^ 2), 'mp', [(2, 0), (1, 3)])  8.93 us
    unnamed x14, local copies, waits for them, and re-layouts  8 us
    ppermute x1, starting transfers between devices, line_of_four(): far_low = lax.ppermute(own_low, 'mp', [(3, 1), (0, 2)])  7.84 us
    ppermute x1, waiting for transfers between devices, line_of_four(): low_in_beside = lax.ppermute(low_in, 'mp', inward)  7.15 us
    ppermute x4, starting transfers between devices, on_device(): scores = scores + lax.ppermute(row, ('dp', 'mp'), pairs)  4.03 us
    ppermute x1, waiting for transfers between devices, line_of_four(): third = lax.ppermute(beside_across, 'mp', outward)  3.55 us
  transfers between devices with their start and end apart: 16, of which 5 were waited for; matrix products, arithmetic and copies ran while one was open for 6% of the time, Pallas kernels for 21%

profile of v10, /device:TPU:0, one launch (start us, length us, event | category | flops | bytes accessed | tf_op | source)
XLA Modules:
  0.0 91.5 jit_solution(1152772478083104260)
XLA Ops:
  0.6 0.0 copy-start
  0.6 3.1 %collective-permute-start = (bf16[256,2048]{1,0:T(8,128)(2,1)}, bf16[256,2048]{1,0:T(8,128)(2,1)S(1)}, u32[]{:S(2)}, u32[]{:S(2)}) collective-permute-start(bf16[256,2048]{1,0:T(8,128)(2,1)} %refs_1_.1), channel_id=1, source_target_pairs={{0,1},{1,0},{2,3},{3,2},{4,5},{5,4},{6,7},{7,6},{8,9},{9,8},{10,11... | collective-permute-start | bytes 3145736 | tf_op jit(solution)/shard_map/ppermute | solution.py:214
  3.7 1.6 %collective-permute-start.2 = (bf16[256,2048]{1,0:T(8,128)(2,1)}, bf16[256,2048]{1,0:T(8,128)(2,1)}, u32[]{:S(2)}, u32[]{:S(2)}) collective-permute-start(bf16[256,2048]{1,0:T(8,128)(2,1)} %refs_1_.1), channel_id=1, source_target_pairs={{1,2},{2,1},{5,6},{6,5},{9,10},{10,9},{13,14},{14,13},{17,18},{18,... | collective-permute-start | bytes 3145736 | tf_op jit(solution)/shard_map/ppermute | solution.py:213
  5.4 1.0 %slice_bitcast_fusion.1 = (bf16[1024,64]{0,1:T(8,128)(2,1)S(1)}, bf16[1024,64]{0,1:T(8,128)(2,1)S(1)}) fusion(bf16[2,1024,64]{1,2,0:T(8,128)(2,1)} %param.10), kind=kLoop, calls=%fused_computation.8 | loop fusion | bytes 524288 | tf_op jit(solution)/shard_map/squeeze | solution.py:26
  6.4 0.0 copy-start.1
  6.4 3.4 %copy-done.1 = bf16[2048,2048]{1,0:T(8,128)(2,1)S(1)} copy-done((bf16[2048,2048]{1,0:T(8,128)(2,1)S(1)}, bf16[2048,2048]{1,0:T(8,128)(2,1)}, u32[]{:S(2)}) %copy-start.1) | copy-done | bytes 8388632
  9.8 0.0 copy-start.4
  9.8 1.2 %copy-done.4 = bf16[256,2048]{1,0:T(8,128)(2,1)S(1)} copy-done((bf16[256,2048]{1,0:T(8,128)(2,1)S(1)}, bf16[256,2048]{1,0:T(8,128)(2,1)}, u32[]{:S(2)}) %copy-start.4) | copy-done | bytes 1048600
  11.0 0.0 copy-start.5
  11.0 0.0 copy-start.6
  11.0 0.0 copy-start.2
  11.0 4.4 %input_grad_rows.4.refs_3_ = bf16[4,256,2048]{2,1,0:T(8,128)(2,1)} custom-call(s32[1]{0:T(128)} %bitcast.me, bf16[256,2048]{1,0:T(8,128)(2,1)S(1)} %copy-done.4, bf16[256,2048]{1,0:T(8,128)(2,1)S(1)} %copy-done.4, bf16[2048,2048]{1,0:T(8,128)(2,1)S(1)} %copy-done.1), custom_call_target="tpu_custom_call" | custom-call | flops 524288 | bytes 524288 | tf_op jit(solution)/shard_map/input_grad_rows/pallas_call | solution.py:98
  15.4 0.0 copy-done.5
  15.4 0.0 copy-done.6
  15.5 1.2 %fusion.13.low_in = f32[1024,128]{1,0:T(8,128)S(1)} fusion(bf16[1024,2048]{1,0:T(8,128)(2,1)S(1)} %copy-done.5, bf16[2048,128]{1,0:T(8,128)(2,1)S(1)} %copy-done.6), kind=kOutput, calls=%fused_computation.33 | convolution fusion | flops 536870912 | bytes 5242880 | tf_op jit(solution)/shard_map/dot_general | solution.py:217
  16.7 10.4 %collective-permute-done.refs_0_.refs_1_ = bf16[256,2048]{1,0:T(8,128)(2,1)S(1)} collective-permute-done((bf16[256,2048]{1,0:T(8,128)(2,1)}, bf16[256,2048]{1,0:T(8,128)(2,1)S(1)}, u32[]{:S(2)}, u32[]{:S(2)}) %collective-permute-start) | collective-permute-done | bytes 1048608 | tf_op jit(solution)/shard_map/ppermute | solution.py:214
  27.1 1.7 %collective-permute-start.1 = (bf16[256,2048]{1,0:T(8,128)(2,1)S(1)}, bf16[256,2048]{1,0:T(8,128)(2,1)}, u32[]{:S(2)}, u32[]{:S(2)}) collective-permute-start(bf16[256,2048]{1,0:T(8,128)(2,1)S(1)} %collective-permute-done.refs_0_.refs_1_), channel_id=1, source_target_pairs={{1,2},{2,1},{5,6},{6,5},{9,10},{10,9},{13,14},{14,13},{17,18},{18,... | collective-permute-start | bytes 3145736 | tf_op jit(solution)/shard_map/ppermute | solution.py:223
  28.8 0.0 collective-permute-done.2.refs_0_
  28.8 1.3 %collective-permute-start.3 = (bf16[256,2048]{1,0:T(8,128)(2,1)}, bf16[256,2048]{1,0:T(8,128)(2,1)}, u32[]{:S(2)}, u32[]{:S(2)}) collective-permute-start(bf16[256,2048]{1,0:T(8,128)(2,1)} %collective-permute-done.2.refs_0_), channel_id=1, source_target_pairs={{1,0},{2,3},{5,4},{6,7},{9,8},{10,11},{13,12},{14,15},{17,16},{18,... | collective-permute-start | bytes 3145736 | tf_op jit(solution)/shard_map/ppermute | solution.py:224
  30.1 0.4 convolution_bitcast_fusion.1.own_low
  30.5 7.8 %collective-permute-start.5 = (f32[256,128]{1,0:T(8,128)S(1)}, f32[256,128]{1,0:T(8,128)S(1)}, u32[]{:S(2)}, u32[]{:S(2)}) collective-permute-start(f32[256,128]{1,0:T(8,128)S(1)} %convolution_bitcast_fusion.1.own_low), channel_id=1, source_target_pairs={{3,1},{0,2},{7,5},{4,6},{11,9},{8,10},{15,13},{12,14},{19,17},{16,... | collective-permute-start | bytes 393224 | tf_op jit(solution)/shard_map/ppermute | solution.py:220
  38.3 0.0 copy-done.2
  38.4 4.4 %input_grad_rows.5.refs_3_ = bf16[4,256,2048]{2,1,0:T(8,128)(2,1)} custom-call(s32[1]{0:T(128)} %bitcast.me, bf16[256,2048]{1,0:T(8,128)(2,1)S(1)} %collective-permute-done.refs_0_.refs_1_, bf16[256,2048]{1,0:T(8,128)(2,1)S(1)} %collective-permute-done.refs_0_.refs_1_, bf16[2048,2048]{1,0:T(8,128)(2,1)S(1)} %copy-done.2, ...), custom_call_target="tpu_custom_call", output_to_operand_aliasing={{}: (4, {})} | custom-call | flops 524288 | bytes 524288 | tf_op jit(solution)/shard_map/input_grad_rows/pallas_call | solution.py:98
  42.8 0.0 collective-permute-done.5.far_low
  42.8 2.1 %collective-permute-start.4 = (f32[1024,128]{1,0:T(8,128)S(1)}, f32[1024,128]{1,0:T(8,128)S(1)}, u32[]{:S(2)}, u32[]{:S(2)}) collective-permute-start(f32[1024,128]{1,0:T(8,128)S(1)} %fusion.13.low_in), channel_id=1, source_target_pairs={{0,1},{3,2},{4,5},{7,6},{8,9},{11,10},{12,13},{15,14},{16,17},{19,... | collective-permute-start | bytes 1572872 | tf_op jit(solution)/shard_map/ppermute | solution.py:225
  44.9 0.4 fusion.14.beside_low
  45.3 1.7 %convolution_bitcast_fusion.facing_low = f32[256,128]{1,0:T(8,128)S(1)} fusion(bf16[2048,128]{0,1:T(8,128)(2,1)S(1)} %fusion.2, bf16[256,2048]{1,0:T(8,128)(2,1)} %collective-permute-done.2.refs_0_), kind=kOutput, calls=%fused_computation | convolution fusion | flops 134217728 | bytes 1703936 | tf_op jit(solution)/shard_map/dot_general | solution.py:211
  47.0 7.1 %collective-permute-done.4.low_in_beside = f32[1024,128]{1,0:T(8,128)S(1)} collective-permute-done((f32[1024,128]{1,0:T(8,128)S(1)}, f32[1024,128]{1,0:T(8,128)S(1)}, u32[]{:S(2)}, u32[]{:S(2)}) %collective-permute-start.4) | collective-permute-done | bytes 524320 | tf_op jit(solution)/shard_map/ppermute | solution.py:225
  54.1 0.7 token_sums.1
  54.8 0.7 collective-permute-start.6
  55.5 0.0 collective-permute-done.6
  55.5 0.0 collective-permute-done.1.refs_0_
  55.6 0.5 collective-permute-done.3.refs_1_
  56.0 1.3 %collective-permute-start.8 = (f32[1,32,64]{2,1,0:T(8,128)S(1)}, f32[1,32,64]{2,1,0:T(8,128)S(1)}, u32[]{:S(2)}, u32[]{:S(2)}) collective-permute-start(f32[1,32,64]{2,1,0:T(8,128)S(1)} %dynamic-slice_bitcast_fusion), channel_id=1, source_target_pairs={{2,0},{1,3},{6,4},{5,7},{10,8},{9,11},{14,12},{13,15},{18,16},{17,... | collective-permute-start | bytes 24584 | tf_op jit(solution)/shard_map/ppermute | solution.py:243
  57.3 1.3 %collective-permute-start.7 = (bf16[256,2048]{1,0:T(8,128)(2,1)}, bf16[256,2048]{1,0:T(8,128)(2,1)S(1)}, u32[]{:S(2)}, u32[]{:S(2)}) collective-permute-start(bf16[256,2048]{1,0:T(8,128)(2,1)} %collective-permute-done.1.refs_0_), channel_id=1, source_target_pairs={{1,0},{2,3},{5,4},{6,7},{9,8},{10,11},{13,12},{14,15},{17,16},{18,... | collective-permute-start | bytes 3145736 | tf_op jit(solution)/shard_map/ppermute | solution.py:242
  58.6 8.9 %collective-permute-done.8 = f32[1,32,64]{2,1,0:T(8,128)S(1)} collective-permute-done((f32[1,32,64]{2,1,0:T(8,128)S(1)}, f32[1,32,64]{2,1,0:T(8,128)S(1)}, u32[]{:S(2)}, u32[]{:S(2)}) %collective-permute-start.8) | collective-permute-done | bytes 8224 | tf_op jit(solution)/shard_map/ppermute | solution.py:243
  67.6 0.1 reshape.28
  67.7 1.5 %collective-permute-start.10 = (f32[1,2048]{1,0:T(1,128)S(1)}, f32[1,2048]{1,0:T(1,128)S(1)}, u32[]{:S(2)}, u32[]{:S(2)}) collective-permute-start(f32[1,2048]{1,0:T(1,128)S(1)} %reshape.28), channel_id=1, source_target_pairs={{0,8},{4,12},{8,0},{12,4},{1,9},{5,13},{9,1},{13,5},{2,10},{6,14},... | collective-permute-start | bytes 24584 | tf_op jit(solution)/shard_map/ppermute | solution.py:269
  69.2 0.0 collective-permute-start.11
  69.2 0.5 collective-permute-start.9
  69.7 0.0 copy-start.3
  69.7 3.4 %copy-done.3 = bf16[2048,2048]{1,0:T(8,128)(2,1)S(1)} copy-done((bf16[2048,2048]{1,0:T(8,128)(2,1)S(1)}, bf16[2048,2048]{1,0:T(8,128)(2,1)}, u32[]{:S(2)}) %copy-start.3) | copy-done | bytes 8388632
  73.1 5.0 %input_grad_rows.6.refs_3_ = bf16[4,256,2048]{2,1,0:T(8,128)(2,1)} custom-call(s32[1]{0:T(128)} %bitcast.me, bf16[256,2048]{1,0:T(8,128)(2,1)} %collective-permute-done.2.refs_0_, bf16[256,2048]{1,0:T(8,128)(2,1)} %collective-permute-done.3.refs_1_, bf16[2048,2048]{1,0:T(8,128)(2,1)S(1)} %copy-done.3, ...), custom_call_target="tpu_custom_call", output_to_operand_aliasing={{}: (4, {})} | custom-call | flops 524288 | bytes 524288 | tf_op jit(solution)/shard_map/input_grad_rows/pallas_call | solution.py:98
  78.1 0.0 collective-permute-done.10
  78.1 0.0 collective-permute-done.11
  78.1 0.0 collective-permute-done.9
  78.1 0.1 reduce-precision_convert_fusion.1
  78.2 0.0 copy-done
  78.2 0.6 fusion.3
  78.9 0.7 collective-permute-start.12
  79.5 1.5 %collective-permute-start.13 = (f32[1,512]{1,0:T(1,128)S(1)}, f32[1,512]{1,0:T(1,128)S(1)}, u32[]{:S(2)}, u32[]{:S(2)}) collective-permute-start(f32[1,512]{1,0:T(1,128)S(1)} %get-tuple-element.29), channel_id=1, source_target_pairs={{0,4},{1,8},{2,12},{3,0},{4,5},{5,9},{6,13},{7,1},{8,6},{9,10},{10... | collective-permute-start | bytes 6152 | tf_op jit(solution)/shard_map/ppermute | solution.py:285
  81.0 1.3 %collective-permute-start.14 = (f32[1,512]{1,0:T(1,128)S(1)}, f32[1,512]{1,0:T(1,128)S(1)}, u32[]{:S(2)}, u32[]{:S(2)}) collective-permute-start(f32[1,512]{1,0:T(1,128)S(1)} %get-tuple-element.30), channel_id=1, source_target_pairs={{0,8},{1,12},{2,0},{3,4},{4,9},{5,13},{6,1},{7,5},{8,10},{9,14},{1... | collective-permute-start | bytes 6152 | tf_op jit(solution)/shard_map/ppermute | solution.py:285
  82.3 3.5 %collective-permute-done.7.refs_1_ = bf16[256,2048]{1,0:T(8,128)(2,1)S(1)} collective-permute-done((bf16[256,2048]{1,0:T(8,128)(2,1)}, bf16[256,2048]{1,0:T(8,128)(2,1)S(1)}, u32[]{:S(2)}, u32[]{:S(2)}) %collective-permute-start.7) | collective-permute-done | bytes 1048608 | tf_op jit(solution)/shard_map/ppermute | solution.py:242
  85.8 0.6 collective-permute-start.15
  86.5 4.4 %input_grad_rows.7 = bf16[4,256,2048]{2,1,0:T(8,128)(2,1)} custom-call(s32[1]{0:T(128)} %bitcast.me, bf16[256,2048]{1,0:T(8,128)(2,1)} %collective-permute-done.1.refs_0_, bf16[256,2048]{1,0:T(8,128)(2,1)S(1)} %collective-permute-done.7.refs_1_, bf16[2048,2048]{1,0:T(8,128)(2,1)S(1)} %copy-done.3, ...), custom_call_target="tpu_custom_call", output_to_operand_aliasing={{}: (4, {})} | custom-call | flops 524288 | bytes 524288 | tf_op jit(solution)/shard_map/input_grad_rows/pallas_call | solution.py:98
  90.9 0.0 collective-permute-done.12
  90.9 0.0 collective-permute-done.13
  90.9 0.0 collective-permute-done.14
  90.9 0.0 collective-permute-done.15
  90.9 0.6 add_add_fusion
  (7 shorter events, 0.1 us)
Async XLA Ops:
  0.6 77.5 %copy-start = (bf16[512,2048]{1,0:T(8,128)(2,1)S(1)}, bf16[512,2048]{1,0:T(8,128)(2,1)}, u32[]{:S(2)}) copy-start(bf16[512,2048]{1,0:T(8,128)(2,1)} %param.11) | copy-start | bytes 6291460
  0.6 26.5 %collective-permute-start = (bf16[256,2048]{1,0:T(8,128)(2,1)}, bf16[256,2048]{1,0:T(8,128)(2,1)S(1)}, u32[]{:S(2)}, u32[]{:S(2)}) collective-permute-start(bf16[256,2048]{1,0:T(8,128)(2,1)} %refs_1_.1), channel_id=1, source_target_pairs={{0,1},{1,0},{2,3},{3,2},{4,5},{5,4},{6,7},{7,6},{8,9},{9,8},{10,11... | collective-permute-start | bytes 3145736 | tf_op jit(solution)/shard_map/ppermute | solution.py:214
  3.7 25.0 %collective-permute-start.2 = (bf16[256,2048]{1,0:T(8,128)(2,1)}, bf16[256,2048]{1,0:T(8,128)(2,1)}, u32[]{:S(2)}, u32[]{:S(2)}) collective-permute-start(bf16[256,2048]{1,0:T(8,128)(2,1)} %refs_1_.1), channel_id=1, source_target_pairs={{1,2},{2,1},{5,6},{6,5},{9,10},{10,9},{13,14},{14,13},{17,18},{18,... | collective-permute-start | bytes 3145736 | tf_op jit(solution)/shard_map/ppermute | solution.py:213
  6.4 3.4 %copy-start.1 = (bf16[2048,2048]{1,0:T(8,128)(2,1)S(1)}, bf16[2048,2048]{1,0:T(8,128)(2,1)}, u32[]{:S(2)}) copy-start(bf16[2048,2048]{1,0:T(8,128)(2,1)} %refs_2_.7) | copy-start | bytes 25165828
  9.8 1.2 %copy-start.4 = (bf16[256,2048]{1,0:T(8,128)(2,1)S(1)}, bf16[256,2048]{1,0:T(8,128)(2,1)}, u32[]{:S(2)}) copy-start(bf16[256,2048]{1,0:T(8,128)(2,1)} %refs_1_.1) | copy-start | bytes 3145732
  11.0 4.4 %copy-start.5 = (bf16[1024,2048]{1,0:T(8,128)(2,1)S(1)}, bf16[1024,2048]{1,0:T(8,128)(2,1)}, u32[]{:S(2)}) copy-start(bf16[1024,2048]{1,0:T(8,128)(2,1)} %param.6) | copy-start | bytes 12582916
  11.0 4.4 %copy-start.6 = (bf16[2048,128]{1,0:T(8,128)(2,1)S(1)}, bf16[2048,128]{1,0:T(8,128)(2,1)}, u32[]{:S(2)}) copy-start(bf16[2048,128]{1,0:T(8,128)(2,1)} %param.9) | copy-start | bytes 1572868
  11.0 27.3 %copy-start.2 = (bf16[2048,2048]{1,0:T(8,128)(2,1)S(1)}, bf16[2048,2048]{1,0:T(8,128)(2,1)}, u32[]{:S(2)}) copy-start(bf16[2048,2048]{1,0:T(8,128)(2,1)} %refs_2_.7) | copy-start | bytes 25165828
  27.1 28.4 %collective-permute-start.1 = (bf16[256,2048]{1,0:T(8,128)(2,1)S(1)}, bf16[256,2048]{1,0:T(8,128)(2,1)}, u32[]{:S(2)}, u32[]{:S(2)}) collective-permute-start(bf16[256,2048]{1,0:T(8,128)(2,1)S(1)} %collective-permute-done.refs_0_.refs_1_), channel_id=1, source_target_pairs={{1,2},{2,1},{5,6},{6,5},{9,10},{10,9},{13,14},{14,13},{17,18},{18,... | collective-permute-start | bytes 3145736 | tf_op jit(solution)/shard_map/ppermute | solution.py:223
  28.8 27.3 %collective-permute-start.3 = (bf16[256,2048]{1,0:T(8,128)(2,1)}, bf16[256,2048]{1,0:T(8,128)(2,1)}, u32[]{:S(2)}, u32[]{:S(2)}) collective-permute-start(bf16[256,2048]{1,0:T(8,128)(2,1)} %collective-permute-done.2.refs_0_), channel_id=1, source_target_pairs={{1,0},{2,3},{5,4},{6,7},{9,8},{10,11},{13,12},{14,15},{17,16},{18,... | collective-permute-start | bytes 3145736 | tf_op jit(solution)/shard_map/ppermute | solution.py:224
  30.5 12.3 %collective-permute-start.5 = (f32[256,128]{1,0:T(8,128)S(1)}, f32[256,128]{1,0:T(8,128)S(1)}, u32[]{:S(2)}, u32[]{:S(2)}) collective-permute-start(f32[256,128]{1,0:T(8,128)S(1)} %convolution_bitcast_fusion.1.own_low), channel_id=1, source_target_pairs={{3,1},{0,2},{7,5},{4,6},{11,9},{8,10},{15,13},{12,14},{19,17},{16,... | collective-permute-start | bytes 393224 | tf_op jit(solution)/shard_map/ppermute | solution.py:220
  42.8 11.3 %collective-permute-start.4 = (f32[1024,128]{1,0:T(8,128)S(1)}, f32[1024,128]{1,0:T(8,128)S(1)}, u32[]{:S(2)}, u32[]{:S(2)}) collective-permute-start(f32[1024,128]{1,0:T(8,128)S(1)} %fusion.13.low_in), channel_id=1, source_target_pairs={{0,1},{3,2},{4,5},{7,6},{8,9},{11,10},{12,13},{15,14},{16,17},{19,... | collective-permute-start | bytes 1572872 | tf_op jit(solution)/shard_map/ppermute | solution.py:225
  54.8 0.7 collective-permute-start.6
  56.0 11.5 %collective-permute-start.8 = (f32[1,32,64]{2,1,0:T(8,128)S(1)}, f32[1,32,64]{2,1,0:T(8,128)S(1)}, u32[]{:S(2)}, u32[]{:S(2)}) collective-permute-start(f32[1,32,64]{2,1,0:T(8,128)S(1)} %dynamic-slice_bitcast_fusion), channel_id=1, source_target_pairs={{2,0},{1,3},{6,4},{5,7},{10,8},{9,11},{14,12},{13,15},{18,16},{17,... | collective-permute-start | bytes 24584 | tf_op jit(solution)/shard_map/ppermute | solution.py:243
  57.3 28.5 %collective-permute-start.7 = (bf16[256,2048]{1,0:T(8,128)(2,1)}, bf16[256,2048]{1,0:T(8,128)(2,1)S(1)}, u32[]{:S(2)}, u32[]{:S(2)}) collective-permute-start(bf16[256,2048]{1,0:T(8,128)(2,1)} %collective-permute-done.1.refs_0_), channel_id=1, source_target_pairs={{1,0},{2,3},{5,4},{6,7},{9,8},{10,11},{13,12},{14,15},{17,16},{18,... | collective-permute-start | bytes 3145736 | tf_op jit(solution)/shard_map/ppermute | solution.py:242
  67.7 10.4 %collective-permute-start.10 = (f32[1,2048]{1,0:T(1,128)S(1)}, f32[1,2048]{1,0:T(1,128)S(1)}, u32[]{:S(2)}, u32[]{:S(2)}) collective-permute-start(f32[1,2048]{1,0:T(1,128)S(1)} %reshape.28), channel_id=1, source_target_pairs={{0,8},{4,12},{8,0},{12,4},{1,9},{5,13},{9,1},{13,5},{2,10},{6,14},... | collective-permute-start | bytes 24584 | tf_op jit(solution)/shard_map/ppermute | solution.py:269
  69.2 8.9 %collective-permute-start.11 = (f32[1,2048]{1,0:T(1,128)S(1)}, f32[1,2048]{1,0:T(1,128)S(1)}, u32[]{:S(2)}, u32[]{:S(2)}) collective-permute-start(f32[1,2048]{1,0:T(1,128)S(1)} %reshape.28), channel_id=1, source_target_pairs={{0,12},{4,0},{8,4},{12,8},{1,13},{5,1},{9,5},{13,9},{2,14},{6,2},{... | collective-permute-start | bytes 24584 | tf_op jit(solution)/shard_map/ppermute | solution.py:269
  69.2 8.9 %collective-permute-start.9 = (f32[1,2048]{1,0:T(1,128)S(1)}, f32[1,2048]{1,0:T(1,128)S(1)}, u32[]{:S(2)}, u32[]{:S(2)}) collective-permute-start(f32[1,2048]{1,0:T(1,128)S(1)} %reshape.28), channel_id=1, source_target_pairs={{0,4},{4,8},{8,12},{12,0},{1,5},{5,9},{9,13},{13,1},{2,6},{6,10},{... | collective-permute-start | bytes 24584 | tf_op jit(solution)/shard_map/ppermute | solution.py:269
  69.7 3.4 %copy-start.3 = (bf16[2048,2048]{1,0:T(8,128)(2,1)S(1)}, bf16[2048,2048]{1,0:T(8,128)(2,1)}, u32[]{:S(2)}) copy-start(bf16[2048,2048]{1,0:T(8,128)(2,1)} %refs_2_.7) | copy-start | bytes 25165828
  78.9 12.0 %collective-permute-start.12 = (f32[1,512]{1,0:T(1,128)S(1)}, f32[1,512]{1,0:T(1,128)S(1)}, u32[]{:S(2)}, u32[]{:S(2)}) collective-permute-start(f32[1,512]{1,0:T(1,128)S(1)} %get-tuple-element.31), channel_id=1, source_target_pairs={{0,0},{1,4},{2,8},{3,12},{4,1},{5,5},{6,9},{7,13},{8,2},{9,6},{10,... | collective-permute-start | bytes 6152 | tf_op jit(solution)/shard_map/ppermute | solution.py:285
  79.5 11.4 %collective-permute-start.13 = (f32[1,512]{1,0:T(1,128)S(1)}, f32[1,512]{1,0:T(1,128)S(1)}, u32[]{:S(2)}, u32[]{:S(2)}) collective-permute-start(f32[1,512]{1,0:T(1,128)S(1)} %get-tuple-element.29), channel_id=1, source_target_pairs={{0,4},{1,8},{2,12},{3,0},{4,5},{5,9},{6,13},{7,1},{8,6},{9,10},{10... | collective-permute-start | bytes 6152 | tf_op jit(solution)/shard_map/ppermute | solution.py:285
  81.0 9.9 %collective-permute-start.14 = (f32[1,512]{1,0:T(1,128)S(1)}, f32[1,512]{1,0:T(1,128)S(1)}, u32[]{:S(2)}, u32[]{:S(2)}) collective-permute-start(f32[1,512]{1,0:T(1,128)S(1)} %get-tuple-element.30), channel_id=1, source_target_pairs={{0,8},{1,12},{2,0},{3,4},{4,9},{5,13},{6,1},{7,5},{8,10},{9,14},{1... | collective-permute-start | bytes 6152 | tf_op jit(solution)/shard_map/ppermute | solution.py:285
  85.8 5.1 %collective-permute-start.15 = (f32[1,512]{1,0:T(1,128)S(1)}, f32[1,512]{1,0:T(1,128)S(1)}, u32[]{:S(2)}, u32[]{:S(2)}) collective-permute-start(f32[1,512]{1,0:T(1,128)S(1)} %dynamic-slice_bitcast_fusion.1), channel_id=1, source_target_pairs={{0,12},{1,0},{2,4},{3,8},{4,13},{5,1},{6,5},{7,9},{8,14},{9,2},{10... | collective-permute-start | bytes 6152 | tf_op jit(solution)/shard_map/ppermute | solution.py:285

commit v11 on v9

--- a/solution.py
+++ b/solution.py
@@ -219,12 +219,13 @@
 
     far_low = lax.ppermute(own_low, "mp", [(3, 1), (0, 2)])
 
-    beside, facing, low_in, output = tied((beside, facing, low_in, output))
+    beside, low_in, far_low, output = tied((beside, low_in, far_low, output))
     beside_across = lax.ppermute(beside, "mp", across)
     second = lax.ppermute(facing, "mp", outward)
     low_in_beside = lax.ppermute(low_in, "mp", inward)
     output = put_rows(me, 1, output, [beside], [beside], w_kv, local_rows)
 
+    low_in_beside, output = tied((low_in_beside, output))
     beside_low = low_rank(beside)
     facing_low = low_rank(facing)
     if low_in.shape[0] == SEQ:

time: 96.9 us -> 92.5 us (0.955)
  waiting for transfers between devices: 30.3 us -> 17.9 us
  matrix products: 4.41 us -> 10 us
  starting transfers between devices: 28.2 us -> 30 us
  Pallas kernels: 19 us -> 20.2 us
    ppermute x1, waiting for transfers between devices: 10.4 us -> 0.01 us  [line_of_four(): beside = lax.ppermute(grad_kv, 'mp', exchange_pairs)]
    ppermute x1, waiting for transfers between devices: 8.93 us -> 0.01 us  [line_of_four(): low_in_beside = lax.ppermute(low_in, 'mp', inward)]
    ppermute x1, starting transfers between devices: 1.59 us -> 8.08 us  [line_of_four(): low_in_beside = lax.ppermute(low_in, 'mp', inward)]
    ppermute x1, waiting for transfers between devices: 0.01 us -> 6.09 us  [line_of_four(): second = lax.ppermute(facing, 'mp', outward)]
    ppermute x1, starting transfers between devices: 9.48 us -> 4.75 us  [line_of_four(): far_low = lax.ppermute(own_low, 'mp', [(3, 1), (0, 2)])]
    ppermute x1, waiting for transfers between devices: 0.22 us -> 3.32 us  [line_of_four(): far_low = lax.ppermute(own_low, 'mp', [(3, 1), (0, 2)])]
    dot_general x1, matrix products: 1.24 us -> 4.33 us  [line_of_four(): low_in = jnp.dot(hidden, proj_in, preferred_element_type=jnp.float32)]
    dot_general x3, matrix products: 2.52 us -> 5.05 us  [low_rank(): return jnp.dot(rows, proj_both, preferred_element_type=jnp.float32)]
  transfers between devices with their start and end apart: 16 -> 16, of which waited for: 5 -> 4; matrix products, arithmetic and copies ran while one was open for 6% -> 12% of each run, Pallas kernels for 20% -> 22%
where the time goes in v11:
time: 92.5 us; the launch traced here: 91.9 us
  starting transfers between devices  30 us (32%)
  Pallas kernels  20.2 us (22%)
  waiting for transfers between devices  17.9 us (19%)
  local copies, waits for them, and re-layouts  12 us (13%)
  matrix products  10 us (11%)
  between operations  0.96 us (1%)
    pallas_call x4, Pallas kernels, put_rows(): pl.pallas_call(functools.partial(rows_kernel, block, start, count), in_sp...  19.5 us
    unnamed x16, local copies, waits for them, and re-layouts  11 us
    ppermute x1, starting transfers between devices, line_of_four(): low_in_beside = lax.ppermute(low_in, 'mp', inward)  8.08 us
    ppermute x1, waiting for transfers between devices, line_of_four(): second = lax.ppermute(facing, 'mp', outward)  6.09 us
    ppermute x4, starting transfers between devices, on_device(): scores = scores + lax.ppermute(row, ('dp', 'mp'), pairs)  5.17 us
    dot_general x3, matrix products, low_rank(): return jnp.dot(rows, proj_both, preferred_element_type=jnp.float32)  5.05 us
    ppermute x1, starting transfers between devices, line_of_four(): far_low = lax.ppermute(own_low, 'mp', [(3, 1), (0, 2)])  4.75 us
    ppermute x1, waiting for transfers between devices, line_of_four(): third = lax.ppermute(beside_across, 'mp', outward)  4.45 us
  transfers between devices with their start and end apart: 16, of which 4 were waited for; matrix products, arithmetic and copies ran while one was open for 12% of the time, Pallas kernels for 22%

profile of v11, /device:TPU:0, one launch (start us, length us, event | category | flops | bytes accessed | tf_op | source)
XLA Modules:
  0.0 91.9 jit_solution(9487874917550530161)
XLA Ops:
  0.6 0.0 copy-start
  0.6 3.1 %collective-permute-start = (bf16[256,2048]{1,0:T(8,128)(2,1)}, bf16[256,2048]{1,0:T(8,128)(2,1)}, u32[]{:S(2)}, u32[]{:S(2)}) collective-permute-start(bf16[256,2048]{1,0:T(8,128)(2,1)} %refs_1_.1), channel_id=1, source_target_pairs={{0,1},{1,0},{2,3},{3,2},{4,5},{5,4},{6,7},{7,6},{8,9},{9,8},{10,11... | collective-permute-start | bytes 3145736 | tf_op jit(solution)/shard_map/ppermute | solution.py:214
  3.7 1.7 %collective-permute-start.3 = (bf16[256,2048]{1,0:T(8,128)(2,1)}, bf16[256,2048]{1,0:T(8,128)(2,1)}, u32[]{:S(2)}, u32[]{:S(2)}) collective-permute-start(bf16[256,2048]{1,0:T(8,128)(2,1)} %refs_1_.1), channel_id=1, source_target_pairs={{1,2},{2,1},{5,6},{6,5},{9,10},{10,9},{13,14},{14,13},{17,18},{18,... | collective-permute-start | bytes 3145736 | tf_op jit(solution)/shard_map/ppermute | solution.py:213
  5.4 1.0 %slice_bitcast_fusion.1 = (bf16[1024,64]{0,1:T(8,128)(2,1)S(1)}, bf16[1024,64]{0,1:T(8,128)(2,1)S(1)}) fusion(bf16[2,1024,64]{1,2,0:T(8,128)(2,1)} %param.10), kind=kLoop, calls=%fused_computation.8 | loop fusion | bytes 524288 | tf_op jit(solution)/shard_map/squeeze | solution.py:26
  6.4 0.0 copy-start.6
  6.5 0.8 copy-done.6
  7.2 0.0 copy-start.4
  7.2 1.7 %convolution_bitcast_fusion.1.own_low = f32[256,128]{1,0:T(8,128)S(1)} fusion(bf16[2048,128]{0,1:T(8,128)(2,1)S(1)} %fusion.2, bf16[256,2048]{1,0:T(8,128)(2,1)} %refs_1_.1), kind=kOutput, calls=%fused_computation.1 | convolution fusion | flops 134217728 | bytes 1703936 | tf_op jit(solution)/shard_map/dot_general | solution.py:211
  9.0 4.7 %collective-permute-start.1 = (f32[256,128]{1,0:T(8,128)S(1)}, f32[256,128]{1,0:T(8,128)S(1)}, u32[]{:S(2)}, u32[]{:S(2)}) collective-permute-start(f32[256,128]{1,0:T(8,128)S(1)} %convolution_bitcast_fusion.1.own_low), channel_id=1, source_target_pairs={{3,1},{0,2},{7,5},{4,6},{11,9},{8,10},{15,13},{12,14},{19,17},{16,... | collective-permute-start | bytes 393224 | tf_op jit(solution)/shard_map/ppermute | solution.py:220
  13.7 4.3 %fusion.13.low_in = f32[1024,128]{1,0:T(8,128)} fusion(bf16[1024,2048]{1,0:T(8,128)(2,1)} %param.6, bf16[2048,128]{1,0:T(8,128)(2,1)} %param.9), kind=kOutput, calls=%fused_computation.33 | convolution fusion | flops 536870912 | bytes 5242880 | tf_op jit(solution)/shard_map/dot_general | solution.py:217
  18.1 0.0 copy-done.4
  18.1 0.0 copy-start.1
  18.1 3.4 %copy-done.1 = bf16[2048,2048]{1,0:T(8,128)(2,1)S(1)} copy-done((bf16[2048,2048]{1,0:T(8,128)(2,1)S(1)}, bf16[2048,2048]{1,0:T(8,128)(2,1)}, u32[]{:S(2)}) %copy-start.1) | copy-done | bytes 8388632
  21.5 0.0 copy-start.5
  21.5 0.0 copy-start.7
  21.5 4.4 %input_grad_rows.4.refs_3_ = bf16[4,256,2048]{2,1,0:T(8,128)(2,1)} custom-call(s32[1]{0:T(128)} %bitcast.me, bf16[256,2048]{1,0:T(8,128)(2,1)S(1)} %copy-done.4, bf16[256,2048]{1,0:T(8,128)(2,1)S(1)} %copy-done.4, bf16[2048,2048]{1,0:T(8,128)(2,1)S(1)} %copy-done.1), custom_call_target="tpu_custom_call" | custom-call | flops 524288 | bytes 524288 | tf_op jit(solution)/shard_map/input_grad_rows/pallas_call | solution.py:98
  25.9 3.3 %collective-permute-done.1.far_low = f32[256,128]{1,0:T(8,128)S(1)} collective-permute-done((f32[256,128]{1,0:T(8,128)S(1)}, f32[256,128]{1,0:T(8,128)S(1)}, u32[]{:S(2)}, u32[]{:S(2)}) %collective-permute-start.1) | collective-permute-done | bytes 131104 | tf_op jit(solution)/shard_map/ppermute | solution.py:220
  29.2 0.0 collective-permute-done.refs_0_.refs_1_
  29.2 0.7 collective-permute-start.2
  29.9 0.0 collective-permute-done.3.refs_0_
  30.0 1.3 %collective-permute-start.4 = (bf16[256,2048]{1,0:T(8,128)(2,1)}, bf16[256,2048]{1,0:T(8,128)(2,1)}, u32[]{:S(2)}, u32[]{:S(2)}) collective-permute-start(bf16[256,2048]{1,0:T(8,128)(2,1)} %collective-permute-done.3.refs_0_), channel_id=1, source_target_pairs={{1,0},{2,3},{5,4},{6,7},{9,8},{10,11},{13,12},{14,15},{17,16},{18,... | collective-permute-start | bytes 3145736 | tf_op jit(solution)/shard_map/ppermute | solution.py:224
  31.3 0.0 copy-done.5
  31.3 8.1 %collective-permute-start.5 = (f32[1024,128]{1,0:T(8,128)S(1)}, f32[1024,128]{1,0:T(8,128)S(1)}, u32[]{:S(2)}, u32[]{:S(2)}) collective-permute-start(f32[1024,128]{1,0:T(8,128)S(1)} %copy-done.5), channel_id=1, source_target_pairs={{0,1},{3,2},{4,5},{7,6},{8,9},{11,10},{12,13},{15,14},{16,17},{19,... | collective-permute-start | bytes 1572872 | tf_op jit(solution)/shard_map/ppermute | solution.py:225
  39.4 0.0 copy-start.2
  39.4 3.4 %copy-done.2 = bf16[2048,2048]{1,0:T(8,128)(2,1)S(1)} copy-done((bf16[2048,2048]{1,0:T(8,128)(2,1)S(1)}, bf16[2048,2048]{1,0:T(8,128)(2,1)}, u32[]{:S(2)}) %copy-start.2) | copy-done | bytes 8388632
  42.7 5.0 %input_grad_rows.5.refs_3_ = bf16[4,256,2048]{2,1,0:T(8,128)(2,1)} custom-call(s32[1]{0:T(128)} %bitcast.me, bf16[256,2048]{1,0:T(8,128)(2,1)} %collective-permute-done.refs_0_.refs_1_, bf16[256,2048]{1,0:T(8,128)(2,1)} %collective-permute-done.refs_0_.refs_1_, bf16[2048,2048]{1,0:T(8,128)(2,1)S(1)} %copy-done.2, ...), custom_call_target="tpu_custom_call", output_to_operand_aliasing={{}: (4, {})} | custom-call | flops 524288 | bytes 524288 | tf_op jit(solution)/shard_map/input_grad_rows/pallas_call | solution.py:98
  47.8 0.0 copy-done.7
  47.8 1.7 %fusion.14.beside_low = f32[256,128]{1,0:T(8,128)S(1)} fusion(bf16[256,2048]{1,0:T(8,128)(2,1)} %collective-permute-done.refs_0_.refs_1_, bf16[2048,128]{0,1:T(8,128)(2,1)S(1)} %copy-done.7), kind=kOutput, calls=%fused_computation.34 | convolution fusion | flops 134217728 | bytes 1703936 | tf_op jit(solution)/shard_map/dot_general | solution.py:211
  49.4 1.7 %convolution_bitcast_fusion.facing_low = f32[256,128]{1,0:T(8,128)S(1)} fusion(bf16[2048,128]{0,1:T(8,128)(2,1)S(1)} %copy-done.7, bf16[256,2048]{1,0:T(8,128)(2,1)} %collective-permute-done.3.refs_0_), kind=kOutput, calls=%fused_computation | convolution fusion | flops 134217728 | bytes 1703936 | tf_op jit(solution)/shard_map/dot_general | solution.py:211
  51.1 0.0 collective-permute-done.5.low_in_beside
  51.1 0.7 token_sums.1
  51.8 0.7 collective-permute-start.6
  52.5 0.0 collective-permute-done.6
  52.5 0.0 collective-permute-done.2.refs_0_
  52.6 6.1 %collective-permute-done.4.refs_1_ = bf16[256,2048]{1,0:T(8,128)(2,1)} collective-permute-done((bf16[256,2048]{1,0:T(8,128)(2,1)}, bf16[256,2048]{1,0:T(8,128)(2,1)}, u32[]{:S(2)}, u32[]{:S(2)}) %collective-permute-start.4) | collective-permute-done | bytes 1048608 | tf_op jit(solution)/shard_map/ppermute | solution.py:224
  58.7 1.3 %collective-permute-start.8 = (f32[1,32,64]{2,1,0:T(8,128)S(1)}, f32[1,32,64]{2,1,0:T(8,128)S(1)}, u32[]{:S(2)}, u32[]{:S(2)}) collective-permute-start(f32[1,32,64]{2,1,0:T(8,128)S(1)} %dynamic-slice_bitcast_fusion), channel_id=1, source_target_pairs={{2,0},{1,3},{6,4},{5,7},{10,8},{9,11},{14,12},{13,15},{18,16},{17,... | collective-permute-start | bytes 24584 | tf_op jit(solution)/shard_map/ppermute | solution.py:243
  59.9 1.3 %collective-permute-start.7 = (bf16[256,2048]{1,0:T(8,128)(2,1)S(1)}, bf16[256,2048]{1,0:T(8,128)(2,1)}, u32[]{:S(2)}, u32[]{:S(2)}) collective-permute-start(bf16[256,2048]{1,0:T(8,128)(2,1)S(1)} %collective-permute-done.2.refs_0_), channel_id=1, source_target_pairs={{1,0},{2,3},{5,4},{6,7},{9,8},{10,11},{13,12},{14,15},{17,16},{18,... | collective-permute-start | bytes 3145736 | tf_op jit(solution)/shard_map/ppermute | solution.py:242
  61.2 4.0 %collective-permute-done.8 = f32[1,32,64]{2,1,0:T(8,128)S(1)} collective-permute-done((f32[1,32,64]{2,1,0:T(8,128)S(1)}, f32[1,32,64]{2,1,0:T(8,128)S(1)}, u32[]{:S(2)}, u32[]{:S(2)}) %collective-permute-start.8) | collective-permute-done | bytes 8224 | tf_op jit(solution)/shard_map/ppermute | solution.py:243
  65.3 0.1 reshape.28
  65.4 1.5 %collective-permute-start.10 = (f32[1,2048]{1,0:T(1,128)S(1)}, f32[1,2048]{1,0:T(1,128)S(1)}, u32[]{:S(2)}, u32[]{:S(2)}) collective-permute-start(f32[1,2048]{1,0:T(1,128)S(1)} %reshape.28), channel_id=1, source_target_pairs={{0,8},{4,12},{8,0},{12,4},{1,9},{5,13},{9,1},{13,5},{2,10},{6,14},... | collective-permute-start | bytes 24584 | tf_op jit(solution)/shard_map/ppermute | solution.py:269
  66.9 0.0 collective-permute-start.11
  66.9 0.5 collective-permute-start.9
  67.4 0.0 copy-start.3
  67.4 3.4 %copy-done.3 = bf16[2048,2048]{1,0:T(8,128)(2,1)S(1)} copy-done((bf16[2048,2048]{1,0:T(8,128)(2,1)S(1)}, bf16[2048,2048]{1,0:T(8,128)(2,1)}, u32[]{:S(2)}) %copy-start.3) | copy-done | bytes 8388632
  70.8 5.0 %input_grad_rows.6.refs_3_ = bf16[4,256,2048]{2,1,0:T(8,128)(2,1)} custom-call(s32[1]{0:T(128)} %bitcast.me, bf16[256,2048]{1,0:T(8,128)(2,1)} %collective-permute-done.3.refs_0_, bf16[256,2048]{1,0:T(8,128)(2,1)} %collective-permute-done.4.refs_1_, bf16[2048,2048]{1,0:T(8,128)(2,1)S(1)} %copy-done.3, ...), custom_call_target="tpu_custom_call", output_to_operand_aliasing={{}: (4, {})} | custom-call | flops 524288 | bytes 524288 | tf_op jit(solution)/shard_map/input_grad_rows/pallas_call | solution.py:98
  75.8 0.0 collective-permute-done.10
  75.8 0.0 collective-permute-done.11
  75.8 0.0 collective-permute-done.9
  75.8 0.1 reduce-precision_convert_fusion.1
  75.9 0.0 copy-done
  75.9 0.6 fusion.3
  76.6 0.7 collective-permute-start.12
  77.2 2.0 %collective-permute-start.13 = (f32[1,512]{1,0:T(1,128)S(1)}, f32[1,512]{1,0:T(1,128)S(1)}, u32[]{:S(2)}, u32[]{:S(2)}) collective-permute-start(f32[1,512]{1,0:T(1,128)S(1)} %get-tuple-element.31), channel_id=1, source_target_pairs={{0,4},{1,8},{2,12},{3,0},{4,5},{5,9},{6,13},{7,1},{8,6},{9,10},{10... | collective-permute-start | bytes 6152 | tf_op jit(solution)/shard_map/ppermute | solution.py:285
  79.2 2.5 %collective-permute-start.14 = (f32[1,512]{1,0:T(1,128)S(1)}, f32[1,512]{1,0:T(1,128)S(1)}, u32[]{:S(2)}, u32[]{:S(2)}) collective-permute-start(f32[1,512]{1,0:T(1,128)S(1)} %get-tuple-element.32), channel_id=1, source_target_pairs={{0,8},{1,12},{2,0},{3,4},{4,9},{5,13},{6,1},{7,5},{8,10},{9,14},{1... | collective-permute-start | bytes 6152 | tf_op jit(solution)/shard_map/ppermute | solution.py:285
  81.8 4.4 %collective-permute-done.7.refs_1_ = bf16[256,2048]{1,0:T(8,128)(2,1)} collective-permute-done((bf16[256,2048]{1,0:T(8,128)(2,1)S(1)}, bf16[256,2048]{1,0:T(8,128)(2,1)}, u32[]{:S(2)}, u32[]{:S(2)}) %collective-permute-start.7) | collective-permute-done | bytes 1048608 | tf_op jit(solution)/shard_map/ppermute | solution.py:242
  86.2 0.0 collective-permute-start.15
  86.2 5.0 %input_grad_rows.7 = bf16[4,256,2048]{2,1,0:T(8,128)(2,1)} custom-call(s32[1]{0:T(128)} %bitcast.me, bf16[256,2048]{1,0:T(8,128)(2,1)S(1)} %collective-permute-done.2.refs_0_, bf16[256,2048]{1,0:T(8,128)(2,1)} %collective-permute-done.7.refs_1_, bf16[2048,2048]{1,0:T(8,128)(2,1)S(1)} %copy-done.3, ...), custom_call_target="tpu_custom_call", output_to_operand_aliasing={{}: (4, {})} | custom-call | flops 524288 | bytes 524288 | tf_op jit(solution)/shard_map/input_grad_rows/pallas_call | solution.py:98
  91.3 0.0 collective-permute-done.12
  91.3 0.0 collective-permute-done.13
  91.3 0.0 collective-permute-done.14
  91.3 0.0 collective-permute-done.15
  91.3 0.6 add_add_fusion
  (7 shorter events, 0.1 us)
Async XLA Ops:
  0.6 75.3 %copy-start = (bf16[512,2048]{1,0:T(8,128)(2,1)S(1)}, bf16[512,2048]{1,0:T(8,128)(2,1)}, u32[]{:S(2)}) copy-start(bf16[512,2048]{1,0:T(8,128)(2,1)} %param.11) | copy-start | bytes 6291460
  0.6 28.6 %collective-permute-start = (bf16[256,2048]{1,0:T(8,128)(2,1)}, bf16[256,2048]{1,0:T(8,128)(2,1)}, u32[]{:S(2)}, u32[]{:S(2)}) collective-permute-start(bf16[256,2048]{1,0:T(8,128)(2,1)} %refs_1_.1), channel_id=1, source_target_pairs={{0,1},{1,0},{2,3},{3,2},{4,5},{5,4},{6,7},{7,6},{8,9},{9,8},{10,11... | collective-permute-start | bytes 3145736 | tf_op jit(solution)/shard_map/ppermute | solution.py:214
  3.7 26.2 %collective-permute-start.3 = (bf16[256,2048]{1,0:T(8,128)(2,1)}, bf16[256,2048]{1,0:T(8,128)(2,1)}, u32[]{:S(2)}, u32[]{:S(2)}) collective-permute-start(bf16[256,2048]{1,0:T(8,128)(2,1)} %refs_1_.1), channel_id=1, source_target_pairs={{1,2},{2,1},{5,6},{6,5},{9,10},{10,9},{13,14},{14,13},{17,18},{18,... | collective-permute-start | bytes 3145736 | tf_op jit(solution)/shard_map/ppermute | solution.py:213
  6.4 0.8 copy-start.6
  7.2 10.8 %copy-start.4 = (bf16[256,2048]{1,0:T(8,128)(2,1)S(1)}, bf16[256,2048]{1,0:T(8,128)(2,1)}, u32[]{:S(2)}) copy-start(bf16[256,2048]{1,0:T(8,128)(2,1)} %refs_1_.1) | copy-start | bytes 3145732
  9.0 20.2 %collective-permute-start.1 = (f32[256,128]{1,0:T(8,128)S(1)}, f32[256,128]{1,0:T(8,128)S(1)}, u32[]{:S(2)}, u32[]{:S(2)}) collective-permute-start(f32[256,128]{1,0:T(8,128)S(1)} %convolution_bitcast_fusion.1.own_low), channel_id=1, source_target_pairs={{3,1},{0,2},{7,5},{4,6},{11,9},{8,10},{15,13},{12,14},{19,17},{16,... | collective-permute-start | bytes 393224 | tf_op jit(solution)/shard_map/ppermute | solution.py:220
  18.1 3.4 %copy-start.1 = (bf16[2048,2048]{1,0:T(8,128)(2,1)S(1)}, bf16[2048,2048]{1,0:T(8,128)(2,1)}, u32[]{:S(2)}) copy-start(bf16[2048,2048]{1,0:T(8,128)(2,1)} %refs_2_.7) | copy-start | bytes 25165828
  21.5 9.8 %copy-start.5 = (f32[1024,128]{1,0:T(8,128)S(1)}, f32[1024,128]{1,0:T(8,128)}, u32[]{:S(2)}) copy-start(f32[1024,128]{1,0:T(8,128)} %fusion.13.low_in) | copy-start | bytes 1572868
  21.5 26.3 %copy-start.7 = (bf16[2048,128]{0,1:T(8,128)(2,1)S(1)}, bf16[2048,128]{0,1:T(8,128)(2,1)}, u32[]{:S(2)}) copy-start(bf16[2048,128]{0,1:T(8,128)(2,1)} %copy-done.6) | copy-start | bytes 1572868
  29.2 23.3 %collective-permute-start.2 = (bf16[256,2048]{1,0:T(8,128)(2,1)}, bf16[256,2048]{1,0:T(8,128)(2,1)S(1)}, u32[]{:S(2)}, u32[]{:S(2)}) collective-permute-start(bf16[256,2048]{1,0:T(8,128)(2,1)} %collective-permute-done.refs_0_.refs_1_), channel_id=1, source_target_pairs={{1,2},{2,1},{5,6},{6,5},{9,10},{10,9},{13,14},{14,13},{17,18},{18,... | collective-permute-start | bytes 3145736 | tf_op jit(solution)/shard_map/ppermute | solution.py:223
  30.0 28.7 %collective-permute-start.4 = (bf16[256,2048]{1,0:T(8,128)(2,1)}, bf16[256,2048]{1,0:T(8,128)(2,1)}, u32[]{:S(2)}, u32[]{:S(2)}) collective-permute-start(bf16[256,2048]{1,0:T(8,128)(2,1)} %collective-permute-done.3.refs_0_), channel_id=1, source_target_pairs={{1,0},{2,3},{5,4},{6,7},{9,8},{10,11},{13,12},{14,15},{17,16},{18,... | collective-permute-start | bytes 3145736 | tf_op jit(solution)/shard_map/ppermute | solution.py:224
  31.3 19.8 %collective-permute-start.5 = (f32[1024,128]{1,0:T(8,128)S(1)}, f32[1024,128]{1,0:T(8,128)S(1)}, u32[]{:S(2)}, u32[]{:S(2)}) collective-permute-start(f32[1024,128]{1,0:T(8,128)S(1)} %copy-done.5), channel_id=1, source_target_pairs={{0,1},{3,2},{4,5},{7,6},{8,9},{11,10},{12,13},{15,14},{16,17},{19,... | collective-permute-start | bytes 1572872 | tf_op jit(solution)/shard_map/ppermute | solution.py:225
  39.4 3.4 %copy-start.2 = (bf16[2048,2048]{1,0:T(8,128)(2,1)S(1)}, bf16[2048,2048]{1,0:T(8,128)(2,1)}, u32[]{:S(2)}) copy-start(bf16[2048,2048]{1,0:T(8,128)(2,1)} %refs_2_.7) | copy-start | bytes 25165828
  51.8 0.7 collective-permute-start.6
  58.7 6.6 %collective-permute-start.8 = (f32[1,32,64]{2,1,0:T(8,128)S(1)}, f32[1,32,64]{2,1,0:T(8,128)S(1)}, u32[]{:S(2)}, u32[]{:S(2)}) collective-permute-start(f32[1,32,64]{2,1,0:T(8,128)S(1)} %dynamic-slice_bitcast_fusion), channel_id=1, source_target_pairs={{2,0},{1,3},{6,4},{5,7},{10,8},{9,11},{14,12},{13,15},{18,16},{17,... | collective-permute-start | bytes 24584 | tf_op jit(solution)/shard_map/ppermute | solution.py:243
  59.9 26.3 %collective-permute-start.7 = (bf16[256,2048]{1,0:T(8,128)(2,1)S(1)}, bf16[256,2048]{1,0:T(8,128)(2,1)}, u32[]{:S(2)}, u32[]{:S(2)}) collective-permute-start(bf16[256,2048]{1,0:T(8,128)(2,1)S(1)} %collective-permute-done.2.refs_0_), channel_id=1, source_target_pairs={{1,0},{2,3},{5,4},{6,7},{9,8},{10,11},{13,12},{14,15},{17,16},{18,... | collective-permute-start | bytes 3145736 | tf_op jit(solution)/shard_map/ppermute | solution.py:242
  65.4 10.4 %collective-permute-start.10 = (f32[1,2048]{1,0:T(1,128)S(1)}, f32[1,2048]{1,0:T(1,128)S(1)}, u32[]{:S(2)}, u32[]{:S(2)}) collective-permute-start(f32[1,2048]{1,0:T(1,128)S(1)} %reshape.28), channel_id=1, source_target_pairs={{0,8},{4,12},{8,0},{12,4},{1,9},{5,13},{9,1},{13,5},{2,10},{6,14},... | collective-permute-start | bytes 24584 | tf_op jit(solution)/shard_map/ppermute | solution.py:269
  66.9 8.9 %collective-permute-start.11 = (f32[1,2048]{1,0:T(1,128)S(1)}, f32[1,2048]{1,0:T(1,128)S(1)}, u32[]{:S(2)}, u32[]{:S(2)}) collective-permute-start(f32[1,2048]{1,0:T(1,128)S(1)} %reshape.28), channel_id=1, source_target_pairs={{0,12},{4,0},{8,4},{12,8},{1,13},{5,1},{9,5},{13,9},{2,14},{6,2},{... | collective-permute-start | bytes 24584 | tf_op jit(solution)/shard_map/ppermute | solution.py:269
  66.9 8.9 %collective-permute-start.9 = (f32[1,2048]{1,0:T(1,128)S(1)}, f32[1,2048]{1,0:T(1,128)S(1)}, u32[]{:S(2)}, u32[]{:S(2)}) collective-permute-start(f32[1,2048]{1,0:T(1,128)S(1)} %reshape.28), channel_id=1, source_target_pairs={{0,4},{4,8},{8,12},{12,0},{1,5},{5,9},{9,13},{13,1},{2,6},{6,10},{... | collective-permute-start | bytes 24584 | tf_op jit(solution)/shard_map/ppermute | solution.py:269
  67.4 3.4 %copy-start.3 = (bf16[2048,2048]{1,0:T(8,128)(2,1)S(1)}, bf16[2048,2048]{1,0:T(8,128)(2,1)}, u32[]{:S(2)}) copy-start(bf16[2048,2048]{1,0:T(8,128)(2,1)} %refs_2_.7) | copy-start | bytes 25165828
  76.6 14.7 %collective-permute-start.12 = (f32[1,512]{1,0:T(1,128)S(1)}, f32[1,512]{1,0:T(1,128)S(1)}, u32[]{:S(2)}, u32[]{:S(2)}) collective-permute-start(f32[1,512]{1,0:T(1,128)S(1)} %get-tuple-element.33), channel_id=1, source_target_pairs={{0,0},{1,4},{2,8},{3,12},{4,1},{5,5},{6,9},{7,13},{8,2},{9,6},{10,... | collective-permute-start | bytes 6152 | tf_op jit(solution)/shard_map/ppermute | solution.py:285
  77.2 14.0 %collective-permute-start.13 = (f32[1,512]{1,0:T(1,128)S(1)}, f32[1,512]{1,0:T(1,128)S(1)}, u32[]{:S(2)}, u32[]{:S(2)}) collective-permute-start(f32[1,512]{1,0:T(1,128)S(1)} %get-tuple-element.31), channel_id=1, source_target_pairs={{0,4},{1,8},{2,12},{3,0},{4,5},{5,9},{6,13},{7,1},{8,6},{9,10},{10... | collective-permute-start | bytes 6152 | tf_op jit(solution)/shard_map/ppermute | solution.py:285
  79.2 12.0 %collective-permute-start.14 = (f32[1,512]{1,0:T(1,128)S(1)}, f32[1,512]{1,0:T(1,128)S(1)}, u32[]{:S(2)}, u32[]{:S(2)}) collective-permute-start(f32[1,512]{1,0:T(1,128)S(1)} %get-tuple-element.32), channel_id=1, source_target_pairs={{0,8},{1,12},{2,0},{3,4},{4,9},{5,13},{6,1},{7,5},{8,10},{9,14},{1... | collective-permute-start | bytes 6152 | tf_op jit(solution)/shard_map/ppermute | solution.py:285
  86.2 5.1 %collective-permute-start.15 = (f32[1,512]{1,0:T(1,128)S(1)}, f32[1,512]{1,0:T(1,128)S(1)}, u32[]{:S(2)}, u32[]{:S(2)}) collective-permute-start(f32[1,512]{1,0:T(1,128)S(1)} %dynamic-slice_bitcast_fusion.1), channel_id=1, source_target_pairs={{0,12},{1,0},{2,4},{3,8},{4,13},{5,1},{6,5},{7,9},{8,14},{9,2},{10... | collective-permute-start | bytes 6152 | tf_op jit(solution)/shard_map/ppermute | solution.py:285

commit v12 on v11

--- a/solution.py
+++ b/solution.py
@@ -16,6 +16,39 @@
     middle = lax.reduce_precision(rest, 8, 7)
     low = rest - middle
     return [term.astype(jnp.bfloat16) for term in (high, middle, low)]
+
+
+def scores_kernel(shards, first, *refs):
+    features, queries = refs[:shards], refs[shards]
+    rows, found = refs[shards + 1 : -1], refs[-1]
+    count = features[0].shape[0]
+    value = jnp.concatenate([part[...] for part in features], axis=0)
+    total = jnp.zeros(found.shape, jnp.float32)
+    for _ in range(3):
+        term = value.astype(jnp.bfloat16)
+        value = value - term.astype(jnp.float32)
+        total += lax.dot_general(
+            term, queries[...], (((1,), (1,)), ((), ())), preferred_element_type=jnp.float32
+        )
+    found[...] = total
+    for step, row in enumerate(rows):
+        row[...] = found[pl.ds((first[0] - step + shards) % shards * count, count), :]
+
+
+def scores_by_step(features, queries, first):
+    shards = len(features)
+    count = features[0].shape[0]
+    block_rows = queries.shape[0]
+    whole = pl.BlockSpec(memory_space=pltpu.VMEM)
+    return pl.pallas_call(
+        functools.partial(scores_kernel, shards),
+        in_specs=[pl.BlockSpec(memory_space=pltpu.SMEM)] + [whole] * (shards + 1),
+        out_specs=[whole] * shards,
+        out_shape=[jax.ShapeDtypeStruct((count, block_rows), jnp.float32)] * shards,
+        scratch_shapes=[pltpu.VMEM((shards * count, block_rows), jnp.float32)],
+        compiler_params=pltpu.CompilerParams(vmem_limit_bytes=GRANT),
+        name="scores",
+    )(first.reshape(1).astype(jnp.int32), *features, queries)
 
 
 def block_diagonal(proj_out):
@@ -193,7 +226,7 @@
     low_in = jnp.dot(hidden, proj_in, preferred_element_type=jnp.float32)
     sums = slabs_of(sequence_sums(low_in, jnp.dot(whole, block_diagonal(proj_out), preferred_element_type=jnp.float32), rank), n)
     features = lax.psum_scatter(sums, "mp", scatter_dimension=0, tiled=False)
-    return features, lambda scores: (scores, scores), lambda: input_grad
+    return features, lambda rows: rows, lambda: input_grad
 
 
 def line_of_four(hidden, w_kv, grad_kv, proj_in, proj_out):
@@ -244,9 +277,10 @@
     mine = jnp.where(middle, take(slabs, me), mine)
     output = put_rows(me, 2, output, [facing], [second], w_kv, local_rows)
 
-    def finish(scores):
-        scores = tied((scores, output))[0]
-        return scores, tied((scores, third))[0]
+    def finish(rows):
+        rows = list(tied((*rows, output))[:-1])
+        rows[-1] = tied((rows[-1], third))[0]
+        return rows
 
     def rest():
         done = put_rows(me, 3, output, [beside_across], [third], w_kv, local_rows)
@@ -269,21 +303,21 @@
         lax.ppermute(mine, "dp", [(source, (source + step) % shards) for source in range(shards)])
         for step in range(1, shards)
     ]
-    terms = jnp.concatenate(three_terms(jnp.concatenate(all_features, axis=0)), axis=0)
-    products = lax.dot_general(
-        terms, queries, (((1,), (1,)), ((), ())), preferred_element_type=jnp.float32
-    ).reshape(3, shards, count, block_rows)
-    partial_scores, last_scores = finish(products[0] + (products[1] + products[2]))
-
-    if shards == n:
+    if shards == n == 4:
+        rows = finish(scores_by_step(all_features, queries, (shard - me + n) % n))
         scores = jnp.zeros((count, block_rows), jnp.float32)
         for step in range(n):
             pairs = [
                 (q * n + slab, (slab + step) % n * n + q) for q in range(n) for slab in range(n)
             ]
-            row = take(partial_scores if step < n - 1 else last_scores, (shard - me - step + 2 * n) % n)
-            scores = scores + lax.ppermute(row, ("dp", "mp"), pairs)
+            scores = scores + lax.ppermute(rows[step], ("dp", "mp"), pairs)
         return (rest(), scores)
+
+    terms = jnp.concatenate(three_terms(jnp.concatenate(all_features, axis=0)), axis=0)
+    products = lax.dot_general(
+        terms, queries, (((1,), (1,)), ((), ())), preferred_element_type=jnp.float32
+    ).reshape(3, shards, count, block_rows)
+    partial_scores = products[0] + (products[1] + products[2])
 
     total = jnp.zeros((count, shards * block_rows), jnp.float32)
     for step in range(shards):

time: 92.5 us -> 94 us (1.016)
  matrix products: 10 us -> 7.38 us
  starting transfers between devices: 30 us -> 31.5 us
  local copies, waits for them, and re-layouts: 12 us -> 13.4 us
  waiting for transfers between devices: 17.9 us -> 19.1 us
    ppermute x1, waiting for transfers between devices: 4.45 us -> 0.01 us  [line_of_four(): third = lax.ppermute(beside_across, 'mp', outward)]
    ppermute x1, waiting for transfers between devices: 6.09 us -> 8.7 us  [line_of_four(): second = lax.ppermute(facing, 'mp', outward)]
    ppermute x4, starting transfers between devices: 5.17 us -> 7.52 us  [on_device(): scores = scores + lax.ppermute(rows[step], ('dp', 'mp'), pairs)]
    pallas_call x0 -> x1, Pallas kernels: none -> 1.74 us  [scores_by_step(): pl.pallas_call(functools.partial(scores_kernel, shards), in_specs=[pl.Blo...]
    pallas_call x4, Pallas kernels: 19.5 us -> 17.9 us  [put_rows(): pl.pallas_call(functools.partial(rows_kernel, block, start, count), in_sp...]
    ppermute x1, waiting for transfers between devices: 3.32 us -> 4.84 us  [line_of_four(): far_low = lax.ppermute(own_low, 'mp', [(3, 1), (0, 2)])]
    ppermute x1, waiting for transfers between devices: 4.03 us -> 5.49 us  [line_of_four(): mine = lax.ppermute(take(slabs, me ^ 2), 'mp', [(2, 0), (1, 3)])]
    unnamed x16 -> x22, local copies, waits for them, and re-layouts: 11 us -> 12.3 us
  transfers between devices with their start and end apart: 16 -> 16, of which waited for: 4 -> 3; matrix products, arithmetic and copies ran while one was open for 12% -> 9% of each run, Pallas kernels for 22% -> 22%
where the time goes in v12:
time: 94 us; the launch traced here: 93.3 us
  starting transfers between devices  31.5 us (34%)
  Pallas kernels  20.4 us (22%)
  waiting for transfers between devices  19.1 us (20%)
  local copies, waits for them, and re-layouts  13.4 us (14%)
  matrix products  7.38 us (8%)
  between operations  0.98 us (1%)
    pallas_call x4, Pallas kernels, put_rows(): pl.pallas_call(functools.partial(rows_kernel, block, start, count), in_sp...  17.9 us
    unnamed x22, local copies, waits for them, and re-layouts  12.3 us
    ppermute x1, waiting for transfers between devices, line_of_four(): second = lax.ppermute(facing, 'mp', outward)  8.7 us
    ppermute x4, starting transfers between devices, on_device(): scores = scores + lax.ppermute(rows[step], ('dp', 'mp'), pairs)  7.52 us
    ppermute x1, starting transfers between devices, line_of_four(): low_in_beside = lax.ppermute(low_in, 'mp', inward)  7.19 us
    ppermute x1, waiting for transfers between devices, line_of_four(): mine = lax.ppermute(take(slabs, me ^ 2), 'mp', [(2, 0), (1, 3)])  5.49 us
    ppermute x1, waiting for transfers between devices, line_of_four(): far_low = lax.ppermute(own_low, 'mp', [(3, 1), (0, 2)])  4.84 us
    ppermute x1, starting transfers between devices, line_of_four(): far_low = lax.ppermute(own_low, 'mp', [(3, 1), (0, 2)])  4.76 us
  transfers between devices with their start and end apart: 16, of which 3 were waited for; matrix products, arithmetic and copies ran while one was open for 9% of the time, Pallas kernels for 22%

profile of v12, /device:TPU:0, one launch (start us, length us, event | category | flops | bytes accessed | tf_op | source)
XLA Modules:
  0.0 93.3 jit_solution(11780449862247185429)
XLA Ops:
  0.6 0.0 copy-start
  0.6 3.1 %collective-permute-start = (bf16[256,2048]{1,0:T(8,128)(2,1)}, bf16[256,2048]{1,0:T(8,128)(2,1)S(1)}, u32[]{:S(2)}, u32[]{:S(2)}) collective-permute-start(bf16[256,2048]{1,0:T(8,128)(2,1)} %refs_1_.1), channel_id=1, source_target_pairs={{0,1},{1,0},{2,3},{3,2},{4,5},{5,4},{6,7},{7,6},{8,9},{9,8},{10,11... | collective-permute-start | bytes 3145736 | tf_op jit(solution)/shard_map/ppermute | solution.py:247
  3.7 1.7 %collective-permute-start.3 = (bf16[256,2048]{1,0:T(8,128)(2,1)}, bf16[256,2048]{1,0:T(8,128)(2,1)}, u32[]{:S(2)}, u32[]{:S(2)}) collective-permute-start(bf16[256,2048]{1,0:T(8,128)(2,1)} %refs_1_.1), channel_id=1, source_target_pairs={{1,2},{2,1},{5,6},{6,5},{9,10},{10,9},{13,14},{14,13},{17,18},{18,... | collective-permute-start | bytes 3145736 | tf_op jit(solution)/shard_map/ppermute | solution.py:246
  5.4 1.0 %slice_bitcast_fusion.1 = (bf16[1024,64]{0,1:T(8,128)(2,1)S(1)}, bf16[1024,64]{0,1:T(8,128)(2,1)S(1)}) fusion(bf16[2,1024,64]{1,2,0:T(8,128)(2,1)} %param.10), kind=kLoop, calls=%fused_computation.8 | loop fusion | bytes 524288 | tf_op jit(solution)/shard_map/squeeze | solution.py:59
  6.4 0.0 copy-start.9
  6.4 0.0 copy-start.5
  6.5 1.9 %convolution_bitcast_fusion.1.own_low = f32[256,128]{1,0:T(8,128)S(1)} fusion(bf16[2048,128]{0,1:T(8,128)(2,1)S(1)} %fusion.2, bf16[256,2048]{1,0:T(8,128)(2,1)} %refs_1_.1), kind=kOutput, calls=%fused_computation.1 | convolution fusion | flops 134217728 | bytes 1703936 | tf_op jit(solution)/shard_map/dot_general | solution.py:244
  8.3 0.0 copy-done.9
  8.3 4.8 %collective-permute-start.1 = (f32[256,128]{1,0:T(8,128)S(1)}, f32[256,128]{1,0:T(8,128)S(1)}, u32[]{:S(2)}, u32[]{:S(2)}) collective-permute-start(f32[256,128]{1,0:T(8,128)S(1)} %convolution_bitcast_fusion.1.own_low), channel_id=1, source_target_pairs={{3,1},{0,2},{7,5},{4,6},{11,9},{8,10},{15,13},{12,14},{19,17},{16,... | collective-permute-start | bytes 393224 | tf_op jit(solution)/shard_map/ppermute | solution.py:253
  13.1 0.0 copy-done
  13.1 3.4 %fusion.3.low_in = f32[1024,128]{1,0:T(8,128)S(1)} fusion(bf16[1024,2048]{1,0:T(8,128)(2,1)} %param.6, bf16[2048,128]{1,0:T(8,128)(2,1)S(1)} %copy-done), kind=kOutput, calls=%fused_computation.13 | convolution fusion | flops 536870912 | bytes 5242880 | tf_op jit(solution)/shard_map/dot_general | solution.py:250
  16.5 0.0 copy-done.5
  16.6 0.0 copy-start.1
  16.6 3.4 %copy-done.1 = bf16[2048,2048]{1,0:T(8,128)(2,1)S(1)} copy-done((bf16[2048,2048]{1,0:T(8,128)(2,1)S(1)}, bf16[2048,2048]{1,0:T(8,128)(2,1)}, u32[]{:S(2)}) %copy-start.1) | copy-done | bytes 8388632
  19.9 0.0 copy-start.10
  19.9 4.4 %input_grad_rows.4.refs_3_ = bf16[4,256,2048]{2,1,0:T(8,128)(2,1)} custom-call(s32[1]{0:T(128)} %bitcast.me, bf16[256,2048]{1,0:T(8,128)(2,1)S(1)} %copy-done.5, bf16[256,2048]{1,0:T(8,128)(2,1)S(1)} %copy-done.5, bf16[2048,2048]{1,0:T(8,128)(2,1)S(1)} %copy-done.1), custom_call_target="tpu_custom_call" | custom-call | flops 524288 | bytes 524288 | tf_op jit(solution)/shard_map/input_grad_rows/pallas_call | solution.py:131
  24.4 4.8 %collective-permute-done.1.far_low = f32[256,128]{1,0:T(8,128)S(1)} collective-permute-done((f32[256,128]{1,0:T(8,128)S(1)}, f32[256,128]{1,0:T(8,128)S(1)}, u32[]{:S(2)}, u32[]{:S(2)}) %collective-permute-start.1) | collective-permute-done | bytes 131104 | tf_op jit(solution)/shard_map/ppermute | solution.py:253
  29.2 0.0 collective-permute-done.refs_0_.refs_1_
  29.2 0.7 collective-permute-start.2
  29.9 0.0 collective-permute-done.3.refs_0_
  30.0 1.3 %collective-permute-start.4 = (bf16[256,2048]{1,0:T(8,128)(2,1)}, bf16[256,2048]{1,0:T(8,128)(2,1)S(1)}, u32[]{:S(2)}, u32[]{:S(2)}) collective-permute-start(bf16[256,2048]{1,0:T(8,128)(2,1)} %collective-permute-done.3.refs_0_), channel_id=1, source_target_pairs={{1,0},{2,3},{5,4},{6,7},{9,8},{10,11},{13,12},{14,15},{17,16},{18,... | collective-permute-start | bytes 3145736 | tf_op jit(solution)/shard_map/ppermute | solution.py:257
  31.3 7.2 %collective-permute-start.5 = (f32[1024,128]{1,0:T(8,128)S(1)}, f32[1024,128]{1,0:T(8,128)S(1)}, u32[]{:S(2)}, u32[]{:S(2)}) collective-permute-start(f32[1024,128]{1,0:T(8,128)S(1)} %fusion.3.low_in), channel_id=1, source_target_pairs={{0,1},{3,2},{4,5},{7,6},{8,9},{11,10},{12,13},{15,14},{16,17},{19,... | collective-permute-start | bytes 1572872 | tf_op jit(solution)/shard_map/ppermute | solution.py:258
  38.5 0.0 copy-start.2
  38.5 3.4 %copy-done.2 = bf16[2048,2048]{1,0:T(8,128)(2,1)S(1)} copy-done((bf16[2048,2048]{1,0:T(8,128)(2,1)S(1)}, bf16[2048,2048]{1,0:T(8,128)(2,1)}, u32[]{:S(2)}) %copy-start.2) | copy-done | bytes 8388632
  41.8 4.4 %input_grad_rows.5.refs_3_ = bf16[4,256,2048]{2,1,0:T(8,128)(2,1)} custom-call(s32[1]{0:T(128)} %bitcast.me, bf16[256,2048]{1,0:T(8,128)(2,1)S(1)} %collective-permute-done.refs_0_.refs_1_, bf16[256,2048]{1,0:T(8,128)(2,1)S(1)} %collective-permute-done.refs_0_.refs_1_, bf16[2048,2048]{1,0:T(8,128)(2,1)S(1)} %copy-done.2, ...), custom_call_target="tpu_custom_call", output_to_operand_aliasing={{}: (4, {})} | custom-call | flops 524288 | bytes 524288 | tf_op jit(solution)/shard_map/input_grad_rows/pallas_call | solution.py:131
  46.3 0.0 copy-done.10
  46.3 0.4 fusion.4.beside_low
  46.7 1.7 %convolution_bitcast_fusion.facing_low = f32[256,128]{1,0:T(8,128)S(1)} fusion(bf16[2048,128]{0,1:T(8,128)(2,1)S(1)} %copy-done.10, bf16[256,2048]{1,0:T(8,128)(2,1)} %collective-permute-done.3.refs_0_), kind=kOutput, calls=%fused_computation | convolution fusion | flops 134217728 | bytes 1703936 | tf_op jit(solution)/shard_map/dot_general | solution.py:244
  48.4 0.0 collective-permute-done.5.low_in_beside
  48.4 0.7 token_sums.1
  49.1 0.7 collective-permute-start.6
  49.8 0.0 collective-permute-done.6
  49.8 0.0 collective-permute-done.2.refs_0_
  49.8 8.7 %collective-permute-done.4.refs_1_ = bf16[256,2048]{1,0:T(8,128)(2,1)S(1)} collective-permute-done((bf16[256,2048]{1,0:T(8,128)(2,1)}, bf16[256,2048]{1,0:T(8,128)(2,1)S(1)}, u32[]{:S(2)}, u32[]{:S(2)}) %collective-permute-start.4) | collective-permute-done | bytes 1048608 | tf_op jit(solution)/shard_map/ppermute | solution.py:257
  58.5 0.0 copy-start.7
  58.5 1.0 %copy-done.7 = bf16[256,2048]{1,0:T(8,128)(2,1)} copy-done((bf16[256,2048]{1,0:T(8,128)(2,1)}, bf16[256,2048]{1,0:T(8,128)(2,1)S(1)}, u32[]{:S(2)}) %copy-start.7) | copy-done | bytes 1048600
  59.5 1.3 %collective-permute-start.7 = (bf16[256,2048]{1,0:T(8,128)(2,1)S(1)}, bf16[256,2048]{1,0:T(8,128)(2,1)S(1)}, u32[]{:S(2)}, u32[]{:S(2)}) collective-permute-start(bf16[256,2048]{1,0:T(8,128)(2,1)S(1)} %collective-permute-done.2.refs_0_), channel_id=1, source_target_pairs={{1,0},{2,3},{5,4},{6,7},{9,8},{10,11},{13,12},{14,15},{17,16},{18,... | collective-permute-start | bytes 3145736 | tf_op jit(solution)/shard_map/ppermute | solution.py:275
  60.8 1.3 %collective-permute-start.8 = (f32[1,32,64]{2,1,0:T(8,128)S(1)}, f32[1,32,64]{2,1,0:T(8,128)S(1)}, u32[]{:S(2)}, u32[]{:S(2)}) collective-permute-start(f32[1,32,64]{2,1,0:T(8,128)S(1)} %dynamic-slice_bitcast_fusion), channel_id=1, source_target_pairs={{2,0},{1,3},{6,4},{5,7},{10,8},{9,11},{14,12},{13,15},{18,16},{17,... | collective-permute-start | bytes 24584 | tf_op jit(solution)/shard_map/ppermute | solution.py:276
  62.1 5.5 %collective-permute-done.8 = f32[1,32,64]{2,1,0:T(8,128)S(1)} collective-permute-done((f32[1,32,64]{2,1,0:T(8,128)S(1)}, f32[1,32,64]{2,1,0:T(8,128)S(1)}, u32[]{:S(2)}, u32[]{:S(2)}) %collective-permute-start.8) | collective-permute-done | bytes 8224 | tf_op jit(solution)/shard_map/ppermute | solution.py:276
  67.6 0.1 reshape.23.refs_0_
  67.7 1.5 %collective-permute-start.10 = (f32[1,2048]{1,0:T(1,128)S(1)}, f32[1,2048]{1,0:T(1,128)S(1)}, u32[]{:S(2)}, u32[]{:S(2)}) collective-permute-start(f32[1,2048]{1,0:T(1,128)S(1)} %reshape.23.refs_0_), channel_id=1, source_target_pairs={{0,8},{4,12},{8,0},{12,4},{1,9},{5,13},{9,1},{13,5},{2,10},{6,14},... | collective-permute-start | bytes 24584 | tf_op jit(solution)/shard_map/ppermute | solution.py:303
  69.2 0.0 collective-permute-start.11
  69.2 0.5 collective-permute-start.9
  69.7 0.0 copy-start.3
  69.7 3.4 %copy-done.3 = bf16[2048,2048]{1,0:T(8,128)(2,1)S(1)} copy-done((bf16[2048,2048]{1,0:T(8,128)(2,1)S(1)}, bf16[2048,2048]{1,0:T(8,128)(2,1)}, u32[]{:S(2)}) %copy-start.3) | copy-done | bytes 8388632
  73.1 1.2 %copy-done.8 = bf16[256,2048]{1,0:T(8,128)(2,1)S(1)} copy-done((bf16[256,2048]{1,0:T(8,128)(2,1)S(1)}, bf16[256,2048]{1,0:T(8,128)(2,1)}, u32[]{:S(2)}) %copy-start.8) | copy-done | bytes 1048600
  74.3 4.6 %input_grad_rows.6.refs_3_ = bf16[4,256,2048]{2,1,0:T(8,128)(2,1)} custom-call(s32[1]{0:T(128)} %bitcast.me, bf16[256,2048]{1,0:T(8,128)(2,1)} %collective-permute-done.3.refs_0_, bf16[256,2048]{1,0:T(8,128)(2,1)S(1)} %copy-done.8, bf16[2048,2048]{1,0:T(8,128)(2,1)S(1)} %copy-done.3, ...), custom_call_target="tpu_custom_call", output_to_operand_aliasing={{}: (4, {})} | custom-call | flops 524288 | bytes 524288 | tf_op jit(solution)/shard_map/input_grad_rows/pallas_call | solution.py:131
  78.9 0.0 collective-permute-done.10.refs_2_
  79.0 0.0 collective-permute-done.11.refs_3_
  79.0 0.0 collective-permute-done.9.refs_1_
  79.0 0.0 copy-done.6
  79.0 1.7 %scores.1 = (f32[1,512]{1,0:T(1,128)S(1)}, f32[1,512]{1,0:T(1,128)S(1)}, f32[1,512]{1,0:T(1,128)S(1)}, f32[1,512]{1,0:T(1,128)S(1)}) custom-call(s32[1]{0:T(128)} %bitcast.7.first, f32[1,2048]{1,0:T(1,128)S(1)} %reshape.23.refs_0_, f32[1,2048]{1,0:T(1,128)S(1)} %collective-permute-done.9.refs_1_, f32[1,2048]{1,0:T(1,128)S(1)} %collective-permute-done.10.refs_2_, ...), custom_call_target="tpu_custom_call" | custom-call | tf_op jit(solution)/shard_map/scores/pallas_call | solution.py:43
  80.7 0.7 collective-permute-start.12
  81.4 1.5 %collective-permute-start.13 = (f32[1,512]{1,0:T(1,128)S(1)}, f32[1,512]{1,0:T(1,128)S(1)}, u32[]{:S(2)}, u32[]{:S(2)}) collective-permute-start(f32[1,512]{1,0:T(1,128)S(1)} %get-tuple-element.36), channel_id=1, source_target_pairs={{0,4},{1,8},{2,12},{3,0},{4,5},{5,9},{6,13},{7,1},{8,6},{9,10},{10... | collective-permute-start | bytes 6152 | tf_op jit(solution)/shard_map/ppermute | solution.py:313
  82.9 2.5 %collective-permute-start.14 = (f32[1,512]{1,0:T(1,128)S(1)}, f32[1,512]{1,0:T(1,128)S(1)}, u32[]{:S(2)}, u32[]{:S(2)}) collective-permute-start(f32[1,512]{1,0:T(1,128)S(1)} %get-tuple-element.37), channel_id=1, source_target_pairs={{0,8},{1,12},{2,0},{3,4},{4,9},{5,13},{6,1},{7,5},{8,10},{9,14},{1... | collective-permute-start | bytes 6152 | tf_op jit(solution)/shard_map/ppermute | solution.py:313
  85.4 0.0 collective-permute-done.7.refs_1_
  85.4 2.8 %collective-permute-start.15 = (f32[1,512]{1,0:T(1,128)S(1)}, f32[1,512]{1,0:T(1,128)S(1)}, u32[]{:S(2)}, u32[]{:S(2)}) collective-permute-start(f32[1,512]{1,0:T(1,128)S(1)} %get-tuple-element.39), channel_id=1, source_target_pairs={{0,12},{1,0},{2,4},{3,8},{4,13},{5,1},{6,5},{7,9},{8,14},{9,2},{10... | collective-permute-start | bytes 6152 | tf_op jit(solution)/shard_map/ppermute | solution.py:313
  88.3 0.0 copy-done.4
  88.3 4.4 %input_grad_rows.7 = bf16[4,256,2048]{2,1,0:T(8,128)(2,1)} custom-call(s32[1]{0:T(128)} %bitcast.me, bf16[256,2048]{1,0:T(8,128)(2,1)S(1)} %collective-permute-done.2.refs_0_, bf16[256,2048]{1,0:T(8,128)(2,1)S(1)} %collective-permute-done.7.refs_1_, bf16[2048,2048]{1,0:T(8,128)(2,1)S(1)} %copy-done.4, ...), custom_call_target="tpu_custom_call", output_to_operand_aliasing={{}: (4, {})} | custom-call | flops 524288 | bytes 524288 | tf_op jit(solution)/shard_map/input_grad_rows/pallas_call | solution.py:131
  92.7 0.0 collective-permute-done.12
  92.7 0.0 collective-permute-done.13
  92.7 0.0 collective-permute-done.14
  92.7 0.0 collective-permute-done.15
  92.7 0.6 add_add_fusion
  (7 shorter events, 0.1 us)
Async XLA Ops:
  0.6 12.5 %copy-start = (bf16[2048,128]{1,0:T(8,128)(2,1)S(1)}, bf16[2048,128]{1,0:T(8,128)(2,1)}, u32[]{:S(2)}) copy-start(bf16[2048,128]{1,0:T(8,128)(2,1)} %param.9) | copy-start | bytes 1572868
  0.6 28.6 %collective-permute-start = (bf16[256,2048]{1,0:T(8,128)(2,1)}, bf16[256,2048]{1,0:T(8,128)(2,1)S(1)}, u32[]{:S(2)}, u32[]{:S(2)}) collective-permute-start(bf16[256,2048]{1,0:T(8,128)(2,1)} %refs_1_.1), channel_id=1, source_target_pairs={{0,1},{1,0},{2,3},{3,2},{4,5},{5,4},{6,7},{7,6},{8,9},{9,8},{10,11... | collective-permute-start | bytes 3145736 | tf_op jit(solution)/shard_map/ppermute | solution.py:247
  3.7 26.2 %collective-permute-start.3 = (bf16[256,2048]{1,0:T(8,128)(2,1)}, bf16[256,2048]{1,0:T(8,128)(2,1)}, u32[]{:S(2)}, u32[]{:S(2)}) collective-permute-start(bf16[256,2048]{1,0:T(8,128)(2,1)} %refs_1_.1), channel_id=1, source_target_pairs={{1,2},{2,1},{5,6},{6,5},{9,10},{10,9},{13,14},{14,13},{17,18},{18,... | collective-permute-start | bytes 3145736 | tf_op jit(solution)/shard_map/ppermute | solution.py:246
  6.4 1.9 %copy-start.9 = (bf16[2048,128]{0,1:T(8,128)(2,1)}, bf16[2048,128]{0,1:T(8,128)(2,1)S(1)}, u32[]{:S(2)}) copy-start(bf16[2048,128]{0,1:T(8,128)(2,1)S(1)} %fusion.2) | copy-start | bytes 1572868
  6.4 10.1 %copy-start.5 = (bf16[256,2048]{1,0:T(8,128)(2,1)S(1)}, bf16[256,2048]{1,0:T(8,128)(2,1)}, u32[]{:S(2)}) copy-start(bf16[256,2048]{1,0:T(8,128)(2,1)} %refs_1_.1) | copy-start | bytes 3145732
  8.3 20.9 %collective-permute-start.1 = (f32[256,128]{1,0:T(8,128)S(1)}, f32[256,128]{1,0:T(8,128)S(1)}, u32[]{:S(2)}, u32[]{:S(2)}) collective-permute-start(f32[256,128]{1,0:T(8,128)S(1)} %convolution_bitcast_fusion.1.own_low), channel_id=1, source_target_pairs={{3,1},{0,2},{7,5},{4,6},{11,9},{8,10},{15,13},{12,14},{19,17},{16,... | collective-permute-start | bytes 393224 | tf_op jit(solution)/shard_map/ppermute | solution.py:253
  16.6 3.4 %copy-start.1 = (bf16[2048,2048]{1,0:T(8,128)(2,1)S(1)}, bf16[2048,2048]{1,0:T(8,128)(2,1)}, u32[]{:S(2)}) copy-start(bf16[2048,2048]{1,0:T(8,128)(2,1)} %refs_2_.7) | copy-start | bytes 25165828
  19.9 26.3 %copy-start.10 = (bf16[2048,128]{0,1:T(8,128)(2,1)S(1)}, bf16[2048,128]{0,1:T(8,128)(2,1)}, u32[]{:S(2)}) copy-start(bf16[2048,128]{0,1:T(8,128)(2,1)} %copy-done.9) | copy-start | bytes 1572868
  29.2 20.6 %collective-permute-start.2 = (bf16[256,2048]{1,0:T(8,128)(2,1)S(1)}, bf16[256,2048]{1,0:T(8,128)(2,1)S(1)}, u32[]{:S(2)}, u32[]{:S(2)}) collective-permute-start(bf16[256,2048]{1,0:T(8,128)(2,1)S(1)} %collective-permute-done.refs_0_.refs_1_), channel_id=1, source_target_pairs={{1,2},{2,1},{5,6},{6,5},{9,10},{10,9},{13,14},{14,13},{17,18},{18,... | collective-permute-start | bytes 3145736 | tf_op jit(solution)/shard_map/ppermute | solution.py:256
  30.0 28.6 %collective-permute-start.4 = (bf16[256,2048]{1,0:T(8,128)(2,1)}, bf16[256,2048]{1,0:T(8,128)(2,1)S(1)}, u32[]{:S(2)}, u32[]{:S(2)}) collective-permute-start(bf16[256,2048]{1,0:T(8,128)(2,1)} %collective-permute-done.3.refs_0_), channel_id=1, source_target_pairs={{1,0},{2,3},{5,4},{6,7},{9,8},{10,11},{13,12},{14,15},{17,16},{18,... | collective-permute-start | bytes 3145736 | tf_op jit(solution)/shard_map/ppermute | solution.py:257
  31.3 17.1 %collective-permute-start.5 = (f32[1024,128]{1,0:T(8,128)S(1)}, f32[1024,128]{1,0:T(8,128)S(1)}, u32[]{:S(2)}, u32[]{:S(2)}) collective-permute-start(f32[1024,128]{1,0:T(8,128)S(1)} %fusion.3.low_in), channel_id=1, source_target_pairs={{0,1},{3,2},{4,5},{7,6},{8,9},{11,10},{12,13},{15,14},{16,17},{19,... | collective-permute-start | bytes 1572872 | tf_op jit(solution)/shard_map/ppermute | solution.py:258
  38.5 3.4 %copy-start.2 = (bf16[2048,2048]{1,0:T(8,128)(2,1)S(1)}, bf16[2048,2048]{1,0:T(8,128)(2,1)}, u32[]{:S(2)}) copy-start(bf16[2048,2048]{1,0:T(8,128)(2,1)} %refs_2_.7) | copy-start | bytes 25165828
  49.1 0.7 collective-permute-start.6
  58.5 1.0 %copy-start.7 = (bf16[256,2048]{1,0:T(8,128)(2,1)}, bf16[256,2048]{1,0:T(8,128)(2,1)S(1)}, u32[]{:S(2)}) copy-start(bf16[256,2048]{1,0:T(8,128)(2,1)S(1)} %collective-permute-done.4.refs_1_) | copy-start | bytes 3145732
  59.5 25.9 %collective-permute-start.7 = (bf16[256,2048]{1,0:T(8,128)(2,1)S(1)}, bf16[256,2048]{1,0:T(8,128)(2,1)S(1)}, u32[]{:S(2)}, u32[]{:S(2)}) collective-permute-start(bf16[256,2048]{1,0:T(8,128)(2,1)S(1)} %collective-permute-done.2.refs_0_), channel_id=1, source_target_pairs={{1,0},{2,3},{5,4},{6,7},{9,8},{10,11},{13,12},{14,15},{17,16},{18,... | collective-permute-start | bytes 3145736 | tf_op jit(solution)/shard_map/ppermute | solution.py:275
  60.8 6.8 %collective-permute-start.8 = (f32[1,32,64]{2,1,0:T(8,128)S(1)}, f32[1,32,64]{2,1,0:T(8,128)S(1)}, u32[]{:S(2)}, u32[]{:S(2)}) collective-permute-start(f32[1,32,64]{2,1,0:T(8,128)S(1)} %dynamic-slice_bitcast_fusion), channel_id=1, source_target_pairs={{2,0},{1,3},{6,4},{5,7},{10,8},{9,11},{14,12},{13,15},{18,16},{17,... | collective-permute-start | bytes 24584 | tf_op jit(solution)/shard_map/ppermute | solution.py:276
  67.7 11.2 %collective-permute-start.10 = (f32[1,2048]{1,0:T(1,128)S(1)}, f32[1,2048]{1,0:T(1,128)S(1)}, u32[]{:S(2)}, u32[]{:S(2)}) collective-permute-start(f32[1,2048]{1,0:T(1,128)S(1)} %reshape.23.refs_0_), channel_id=1, source_target_pairs={{0,8},{4,12},{8,0},{12,4},{1,9},{5,13},{9,1},{13,5},{2,10},{6,14},... | collective-permute-start | bytes 24584 | tf_op jit(solution)/shard_map/ppermute | solution.py:303
  69.2 9.7 %collective-permute-start.11 = (f32[1,2048]{1,0:T(1,128)S(1)}, f32[1,2048]{1,0:T(1,128)S(1)}, u32[]{:S(2)}, u32[]{:S(2)}) collective-permute-start(f32[1,2048]{1,0:T(1,128)S(1)} %reshape.23.refs_0_), channel_id=1, source_target_pairs={{0,12},{4,0},{8,4},{12,8},{1,13},{5,1},{9,5},{13,9},{2,14},{6,2},{... | collective-permute-start | bytes 24584 | tf_op jit(solution)/shard_map/ppermute | solution.py:303
  69.2 9.8 %collective-permute-start.9 = (f32[1,2048]{1,0:T(1,128)S(1)}, f32[1,2048]{1,0:T(1,128)S(1)}, u32[]{:S(2)}, u32[]{:S(2)}) collective-permute-start(f32[1,2048]{1,0:T(1,128)S(1)} %reshape.23.refs_0_), channel_id=1, source_target_pairs={{0,4},{4,8},{8,12},{12,0},{1,5},{5,9},{9,13},{13,1},{2,6},{6,10},{... | collective-permute-start | bytes 24584 | tf_op jit(solution)/shard_map/ppermute | solution.py:303
  69.7 3.4 %copy-start.3 = (bf16[2048,2048]{1,0:T(8,128)(2,1)S(1)}, bf16[2048,2048]{1,0:T(8,128)(2,1)}, u32[]{:S(2)}) copy-start(bf16[2048,2048]{1,0:T(8,128)(2,1)} %refs_2_.7) | copy-start | bytes 25165828
  73.1 1.2 %copy-start.8 = (bf16[256,2048]{1,0:T(8,128)(2,1)S(1)}, bf16[256,2048]{1,0:T(8,128)(2,1)}, u32[]{:S(2)}) copy-start(bf16[256,2048]{1,0:T(8,128)(2,1)} %copy-done.7) | copy-start | bytes 3145732
  74.3 4.7 %copy-start.6 = (bf16[512,2048]{1,0:T(8,128)(2,1)S(1)}, bf16[512,2048]{1,0:T(8,128)(2,1)}, u32[]{:S(2)}) copy-start(bf16[512,2048]{1,0:T(8,128)(2,1)} %refs_4_.1) | copy-start | bytes 6291460
  74.3 13.9 %copy-start.4 = (bf16[2048,2048]{1,0:T(8,128)(2,1)S(1)}, bf16[2048,2048]{1,0:T(8,128)(2,1)}, u32[]{:S(2)}) copy-start(bf16[2048,2048]{1,0:T(8,128)(2,1)} %refs_2_.7) | copy-start | bytes 25165828
  80.7 12.0 %collective-permute-start.12 = (f32[1,512]{1,0:T(1,128)S(1)}, f32[1,512]{1,0:T(1,128)S(1)}, u32[]{:S(2)}, u32[]{:S(2)}) collective-permute-start(f32[1,512]{1,0:T(1,128)S(1)} %get-tuple-element.35), channel_id=1, source_target_pairs={{0,0},{1,4},{2,8},{3,12},{4,1},{5,5},{6,9},{7,13},{8,2},{9,6},{10,... | collective-permute-start | bytes 6152 | tf_op jit(solution)/shard_map/ppermute | solution.py:313
  81.4 11.3 %collective-permute-start.13 = (f32[1,512]{1,0:T(1,128)S(1)}, f32[1,512]{1,0:T(1,128)S(1)}, u32[]{:S(2)}, u32[]{:S(2)}) collective-permute-start(f32[1,512]{1,0:T(1,128)S(1)} %get-tuple-element.36), channel_id=1, source_target_pairs={{0,4},{1,8},{2,12},{3,0},{4,5},{5,9},{6,13},{7,1},{8,6},{9,10},{10... | collective-permute-start | bytes 6152 | tf_op jit(solution)/shard_map/ppermute | solution.py:313
  82.9 9.8 %collective-permute-start.14 = (f32[1,512]{1,0:T(1,128)S(1)}, f32[1,512]{1,0:T(1,128)S(1)}, u32[]{:S(2)}, u32[]{:S(2)}) collective-permute-start(f32[1,512]{1,0:T(1,128)S(1)} %get-tuple-element.37), channel_id=1, source_target_pairs={{0,8},{1,12},{2,0},{3,4},{4,9},{5,13},{6,1},{7,5},{8,10},{9,14},{1... | collective-permute-start | bytes 6152 | tf_op jit(solution)/shard_map/ppermute | solution.py:313
  85.4 7.3 %collective-permute-start.15 = (f32[1,512]{1,0:T(1,128)S(1)}, f32[1,512]{1,0:T(1,128)S(1)}, u32[]{:S(2)}, u32[]{:S(2)}) collective-permute-start(f32[1,512]{1,0:T(1,128)S(1)} %get-tuple-element.39), channel_id=1, source_target_pairs={{0,12},{1,0},{2,4},{3,8},{4,13},{5,1},{6,5},{7,9},{8,14},{9,2},{10... | collective-permute-start | bytes 6152 | tf_op jit(solution)/shard_map/ppermute | solution.py:313

commit v13 on v12

--- a/solution.py
+++ b/solution.py
@@ -71,7 +71,7 @@
 
 FETCH = 256
 TILE = 512
-GRANT = 24 * 2**20
+GRANT = 48 * 2**20
 
 
 def rows_kernel(block, start, count, me, *refs):

time: 94 us -> 92.6 us (0.985)
  local copies, waits for them, and re-layouts: 13.4 us -> 3.3 us
  waiting for transfers between devices: 19.1 us -> 25.8 us
  Pallas kernels: 20.4 us -> 24.2 us
  starting transfers between devices: 31.5 us -> 29.8 us
    unnamed x22 -> x14, local copies, waits for them, and re-layouts: 12.3 us -> 2.22 us
    pallas_call x4, Pallas kernels: 17.9 us -> 21.7 us  [put_rows(): pl.pallas_call(functools.partial(rows_kernel, block, start, count), in_sp...]
    ppermute x1, waiting for transfers between devices: 4.84 us -> 7.25 us  [line_of_four(): far_low = lax.ppermute(own_low, 'mp', [(3, 1), (0, 2)])]
    ppermute x1, waiting for transfers between devices: 0.01 us -> 2.36 us  [line_of_four(): low_in_beside = lax.ppermute(low_in, 'mp', inward)]
    ppermute x1, waiting for transfers between devices: 0.01 us -> 1.9 us  [line_of_four(): third = lax.ppermute(beside_across, 'mp', outward)]
    ppermute x4, starting transfers between devices: 7.52 us -> 5.8 us  [on_device(): scores = scores + lax.ppermute(rows[step], ('dp', 'mp'), pairs)]
  transfers between devices with their start and end apart: 16 -> 16, of which waited for: 3 -> 5; matrix products, arithmetic and copies ran while one was open for 9% -> 9% of each run, Pallas kernels for 22% -> 26%
where the time goes in v13:
time: 92.6 us; the launch traced here: 92 us
  starting transfers between devices  29.8 us (32%)
  waiting for transfers between devices  25.8 us (28%)
  Pallas kernels  24.2 us (26%)
  matrix products  7.39 us (8%)
  local copies, waits for them, and re-layouts  3.3 us (4%)
  between operations  0.96 us (1%)
    pallas_call x4, Pallas kernels, put_rows(): pl.pallas_call(functools.partial(rows_kernel, block, start, count), in_sp...  21.7 us
    ppermute x1, waiting for transfers between devices, line_of_four(): second = lax.ppermute(facing, 'mp', outward)  8.76 us
    ppermute x1, waiting for transfers between devices, line_of_four(): far_low = lax.ppermute(own_low, 'mp', [(3, 1), (0, 2)])  7.25 us
    ppermute x1, starting transfers between devices, line_of_four(): low_in_beside = lax.ppermute(low_in, 'mp', inward)  7.19 us
    ppermute x4, starting transfers between devices, on_device(): scores = scores + lax.ppermute(rows[step], ('dp', 'mp'), pairs)  5.8 us
    ppermute x1, waiting for transfers between devices, line_of_four(): mine = lax.ppermute(take(slabs, me ^ 2), 'mp', [(2, 0), (1, 3)])  5.49 us
    ppermute x1, starting transfers between devices, line_of_four(): far_low = lax.ppermute(own_low, 'mp', [(3, 1), (0, 2)])  4.77 us
    dot_general x3, matrix products, low_rank(): return jnp.dot(rows, proj_both, preferred_element_type=jnp.float32)  3.96 us
  transfers between devices with their start and end apart: 16, of which 5 were waited for; matrix products, arithmetic and copies ran while one was open for 9% of the time, Pallas kernels for 26%

profile of v13, /device:TPU:0, one launch (start us, length us, event | category | flops | bytes accessed | tf_op | source)
XLA Modules:
  0.0 92.0 jit_solution(11224554359629466422)
XLA Ops:
  0.6 0.0 copy-start
  0.6 3.1 %collective-permute-start = (bf16[256,2048]{1,0:T(8,128)(2,1)}, bf16[256,2048]{1,0:T(8,128)(2,1)S(1)}, u32[]{:S(2)}, u32[]{:S(2)}) collective-permute-start(bf16[256,2048]{1,0:T(8,128)(2,1)} %refs_1_.1), channel_id=1, source_target_pairs={{0,1},{1,0},{2,3},{3,2},{4,5},{5,4},{6,7},{7,6},{8,9},{9,8},{10,11... | collective-permute-start | bytes 3145736 | tf_op jit(solution)/shard_map/ppermute | solution.py:247
  3.7 1.6 %collective-permute-start.3 = (bf16[256,2048]{1,0:T(8,128)(2,1)}, bf16[256,2048]{1,0:T(8,128)(2,1)}, u32[]{:S(2)}, u32[]{:S(2)}) collective-permute-start(bf16[256,2048]{1,0:T(8,128)(2,1)} %refs_1_.1), channel_id=1, source_target_pairs={{1,2},{2,1},{5,6},{6,5},{9,10},{10,9},{13,14},{14,13},{17,18},{18,... | collective-permute-start | bytes 3145736 | tf_op jit(solution)/shard_map/ppermute | solution.py:246
  5.4 1.0 %slice_bitcast_fusion.1 = (bf16[1024,64]{0,1:T(8,128)(2,1)S(1)}, bf16[1024,64]{0,1:T(8,128)(2,1)S(1)}) fusion(bf16[2,1024,64]{1,2,0:T(8,128)(2,1)} %param.10), kind=kLoop, calls=%fused_computation.8 | loop fusion | bytes 524288 | tf_op jit(solution)/shard_map/squeeze | solution.py:59
  6.4 0.0 copy-start.5
  6.4 0.0 copy-start.1
  6.4 1.9 %convolution_bitcast_fusion.1.own_low = f32[256,128]{1,0:T(8,128)S(1)} fusion(bf16[2048,128]{0,1:T(8,128)(2,1)S(1)} %fusion.2, bf16[256,2048]{1,0:T(8,128)(2,1)} %refs_1_.1), kind=kOutput, calls=%fused_computation.1 | convolution fusion | flops 134217728 | bytes 1703936 | tf_op jit(solution)/shard_map/dot_general | solution.py:244
  8.3 0.0 copy-done.5
  8.3 4.8 %collective-permute-start.1 = (f32[256,128]{1,0:T(8,128)S(1)}, f32[256,128]{1,0:T(8,128)S(1)}, u32[]{:S(2)}, u32[]{:S(2)}) collective-permute-start(f32[256,128]{1,0:T(8,128)S(1)} %convolution_bitcast_fusion.1.own_low), channel_id=1, source_target_pairs={{3,1},{0,2},{7,5},{4,6},{11,9},{8,10},{15,13},{12,14},{19,17},{16,... | collective-permute-start | bytes 393224 | tf_op jit(solution)/shard_map/ppermute | solution.py:253
  13.1 0.0 copy-done
  13.1 3.4 %fusion.3.low_in = f32[1024,128]{1,0:T(8,128)S(1)} fusion(bf16[1024,2048]{1,0:T(8,128)(2,1)} %param.6, bf16[2048,128]{1,0:T(8,128)(2,1)S(1)} %copy-done), kind=kOutput, calls=%fused_computation.13 | convolution fusion | flops 536870912 | bytes 5242880 | tf_op jit(solution)/shard_map/dot_general | solution.py:250
  16.5 0.0 copy-done.1
  16.6 5.4 %input_grad_rows.4.refs_3_ = bf16[4,256,2048]{2,1,0:T(8,128)(2,1)} custom-call(s32[1]{0:T(128)} %bitcast.me, bf16[256,2048]{1,0:T(8,128)(2,1)S(1)} %copy-done.1, bf16[256,2048]{1,0:T(8,128)(2,1)S(1)} %copy-done.1, bf16[2048,2048]{1,0:T(8,128)(2,1)} %refs_2_.7), custom_call_target="tpu_custom_call" | custom-call | flops 524288 | bytes 524288 | tf_op jit(solution)/shard_map/input_grad_rows/pallas_call | solution.py:131
  22.0 0.0 copy-start.6
  22.0 7.2 %collective-permute-done.1.far_low = f32[256,128]{1,0:T(8,128)S(1)} collective-permute-done((f32[256,128]{1,0:T(8,128)S(1)}, f32[256,128]{1,0:T(8,128)S(1)}, u32[]{:S(2)}, u32[]{:S(2)}) %collective-permute-start.1) | collective-permute-done | bytes 131104 | tf_op jit(solution)/shard_map/ppermute | solution.py:253
  29.2 0.0 collective-permute-done.refs_0_.refs_1_
  29.2 0.7 collective-permute-start.2
  29.9 0.0 collective-permute-done.3.refs_0_
  30.0 1.3 %collective-permute-start.4 = (bf16[256,2048]{1,0:T(8,128)(2,1)}, bf16[256,2048]{1,0:T(8,128)(2,1)S(1)}, u32[]{:S(2)}, u32[]{:S(2)}) collective-permute-start(bf16[256,2048]{1,0:T(8,128)(2,1)} %collective-permute-done.3.refs_0_), channel_id=1, source_target_pairs={{1,0},{2,3},{5,4},{6,7},{9,8},{10,11},{13,12},{14,15},{17,16},{18,... | collective-permute-start | bytes 3145736 | tf_op jit(solution)/shard_map/ppermute | solution.py:257
  31.3 7.2 %collective-permute-start.5 = (f32[1024,128]{1,0:T(8,128)S(1)}, f32[1024,128]{1,0:T(8,128)S(1)}, u32[]{:S(2)}, u32[]{:S(2)}) collective-permute-start(f32[1024,128]{1,0:T(8,128)S(1)} %fusion.3.low_in), channel_id=1, source_target_pairs={{0,1},{3,2},{4,5},{7,6},{8,9},{11,10},{12,13},{15,14},{16,17},{19,... | collective-permute-start | bytes 1572872 | tf_op jit(solution)/shard_map/ppermute | solution.py:258
  38.5 5.4 %input_grad_rows.5.refs_3_ = bf16[4,256,2048]{2,1,0:T(8,128)(2,1)} custom-call(s32[1]{0:T(128)} %bitcast.me, bf16[256,2048]{1,0:T(8,128)(2,1)S(1)} %collective-permute-done.refs_0_.refs_1_, bf16[256,2048]{1,0:T(8,128)(2,1)S(1)} %collective-permute-done.refs_0_.refs_1_, bf16[2048,2048]{1,0:T(8,128)(2,1)} %refs_2_.7, ...), custom_call_target="tpu_custom_call", output_to_operand_aliasing={{}: (4, {})} | custom-call | flops 524288 | bytes 524288 | tf_op jit(solution)/shard_map/input_grad_rows/pallas_call | solution.py:131
  43.9 0.0 copy-done.6
  43.9 0.4 fusion.4.beside_low
  44.3 1.7 %convolution_bitcast_fusion.facing_low = f32[256,128]{1,0:T(8,128)S(1)} fusion(bf16[2048,128]{0,1:T(8,128)(2,1)S(1)} %copy-done.6, bf16[256,2048]{1,0:T(8,128)(2,1)} %collective-permute-done.3.refs_0_), kind=kOutput, calls=%fused_computation | convolution fusion | flops 134217728 | bytes 1703936 | tf_op jit(solution)/shard_map/dot_general | solution.py:244
  46.0 2.4 %collective-permute-done.5.low_in_beside = f32[1024,128]{1,0:T(8,128)S(1)} collective-permute-done((f32[1024,128]{1,0:T(8,128)S(1)}, f32[1024,128]{1,0:T(8,128)S(1)}, u32[]{:S(2)}, u32[]{:S(2)}) %collective-permute-start.5) | collective-permute-done | bytes 524320 | tf_op jit(solution)/shard_map/ppermute | solution.py:258
  48.3 0.7 token_sums.1
  49.1 0.7 collective-permute-start.6
  49.7 0.0 collective-permute-done.6
  49.8 0.0 collective-permute-done.2.refs_0_
  49.8 8.8 %collective-permute-done.4.refs_1_ = bf16[256,2048]{1,0:T(8,128)(2,1)S(1)} collective-permute-done((bf16[256,2048]{1,0:T(8,128)(2,1)}, bf16[256,2048]{1,0:T(8,128)(2,1)S(1)}, u32[]{:S(2)}, u32[]{:S(2)}) %collective-permute-start.4) | collective-permute-done | bytes 1048608 | tf_op jit(solution)/shard_map/ppermute | solution.py:257
  58.5 0.0 copy-start.3
  58.5 1.0 %copy-done.3 = bf16[256,2048]{1,0:T(8,128)(2,1)} copy-done((bf16[256,2048]{1,0:T(8,128)(2,1)}, bf16[256,2048]{1,0:T(8,128)(2,1)S(1)}, u32[]{:S(2)}) %copy-start.3) | copy-done | bytes 1048600
  59.5 1.3 %collective-permute-start.7 = (bf16[256,2048]{1,0:T(8,128)(2,1)S(1)}, bf16[256,2048]{1,0:T(8,128)(2,1)S(1)}, u32[]{:S(2)}, u32[]{:S(2)}) collective-permute-start(bf16[256,2048]{1,0:T(8,128)(2,1)S(1)} %collective-permute-done.2.refs_0_), channel_id=1, source_target_pairs={{1,0},{2,3},{5,4},{6,7},{9,8},{10,11},{13,12},{14,15},{17,16},{18,... | collective-permute-start | bytes 3145736 | tf_op jit(solution)/shard_map/ppermute | solution.py:275
  60.8 1.3 %collective-permute-start.8 = (f32[1,32,64]{2,1,0:T(8,128)S(1)}, f32[1,32,64]{2,1,0:T(8,128)S(1)}, u32[]{:S(2)}, u32[]{:S(2)}) collective-permute-start(f32[1,32,64]{2,1,0:T(8,128)S(1)} %dynamic-slice_bitcast_fusion), channel_id=1, source_target_pairs={{2,0},{1,3},{6,4},{5,7},{10,8},{9,11},{14,12},{13,15},{18,16},{17,... | collective-permute-start | bytes 24584 | tf_op jit(solution)/shard_map/ppermute | solution.py:276
  62.1 5.5 %collective-permute-done.8 = f32[1,32,64]{2,1,0:T(8,128)S(1)} collective-permute-done((f32[1,32,64]{2,1,0:T(8,128)S(1)}, f32[1,32,64]{2,1,0:T(8,128)S(1)}, u32[]{:S(2)}, u32[]{:S(2)}) %collective-permute-start.8) | collective-permute-done | bytes 8224 | tf_op jit(solution)/shard_map/ppermute | solution.py:276
  67.6 0.1 reshape.23.refs_0_
  67.7 1.5 %collective-permute-start.10 = (f32[1,2048]{1,0:T(1,128)S(1)}, f32[1,2048]{1,0:T(1,128)S(1)}, u32[]{:S(2)}, u32[]{:S(2)}) collective-permute-start(f32[1,2048]{1,0:T(1,128)S(1)} %reshape.23.refs_0_), channel_id=1, source_target_pairs={{0,8},{4,12},{8,0},{12,4},{1,9},{5,13},{9,1},{13,5},{2,10},{6,14},... | collective-permute-start | bytes 24584 | tf_op jit(solution)/shard_map/ppermute | solution.py:303
  69.2 0.0 collective-permute-start.11
  69.2 0.5 collective-permute-start.9
  69.7 0.0 copy-start.4
  69.7 1.2 %copy-done.4 = bf16[256,2048]{1,0:T(8,128)(2,1)S(1)} copy-done((bf16[256,2048]{1,0:T(8,128)(2,1)S(1)}, bf16[256,2048]{1,0:T(8,128)(2,1)}, u32[]{:S(2)}) %copy-start.4) | copy-done | bytes 1048600
  71.0 0.0 copy-start.2
  71.0 5.5 %input_grad_rows.6.refs_3_ = bf16[4,256,2048]{2,1,0:T(8,128)(2,1)} custom-call(s32[1]{0:T(128)} %bitcast.me, bf16[256,2048]{1,0:T(8,128)(2,1)} %collective-permute-done.3.refs_0_, bf16[256,2048]{1,0:T(8,128)(2,1)S(1)} %copy-done.4, bf16[2048,2048]{1,0:T(8,128)(2,1)} %refs_2_.7, ...), custom_call_target="tpu_custom_call", output_to_operand_aliasing={{}: (4, {})} | custom-call | flops 524288 | bytes 524288 | tf_op jit(solution)/shard_map/input_grad_rows/pallas_call | solution.py:131
  76.5 0.0 collective-permute-done.10.refs_2_
  76.5 0.0 collective-permute-done.11.refs_3_
  76.5 0.0 collective-permute-done.9.refs_1_
  76.5 0.0 copy-done.2
  76.5 1.7 %scores.1 = (f32[1,512]{1,0:T(1,128)S(1)}, f32[1,512]{1,0:T(1,128)S(1)}, f32[1,512]{1,0:T(1,128)S(1)}, f32[1,512]{1,0:T(1,128)S(1)}) custom-call(s32[1]{0:T(128)} %bitcast.7.first, f32[1,2048]{1,0:T(1,128)S(1)} %reshape.23.refs_0_, f32[1,2048]{1,0:T(1,128)S(1)} %collective-permute-done.9.refs_1_, f32[1,2048]{1,0:T(1,128)S(1)} %collective-permute-done.10.refs_2_, ...), custom_call_target="tpu_custom_call" | custom-call | tf_op jit(solution)/shard_map/scores/pallas_call | solution.py:43
  78.3 0.7 collective-permute-start.12
  79.0 1.6 %collective-permute-start.13 = (f32[1,512]{1,0:T(1,128)S(1)}, f32[1,512]{1,0:T(1,128)S(1)}, u32[]{:S(2)}, u32[]{:S(2)}) collective-permute-start(f32[1,512]{1,0:T(1,128)S(1)} %get-tuple-element.36), channel_id=1, source_target_pairs={{0,4},{1,8},{2,12},{3,0},{4,5},{5,9},{6,13},{7,1},{8,6},{9,10},{10... | collective-permute-start | bytes 6152 | tf_op jit(solution)/shard_map/ppermute | solution.py:313
  80.6 2.3 %collective-permute-start.14 = (f32[1,512]{1,0:T(1,128)S(1)}, f32[1,512]{1,0:T(1,128)S(1)}, u32[]{:S(2)}, u32[]{:S(2)}) collective-permute-start(f32[1,512]{1,0:T(1,128)S(1)} %get-tuple-element.37), channel_id=1, source_target_pairs={{0,8},{1,12},{2,0},{3,4},{4,9},{5,13},{6,1},{7,5},{8,10},{9,14},{1... | collective-permute-start | bytes 6152 | tf_op jit(solution)/shard_map/ppermute | solution.py:313
  82.9 1.9 %collective-permute-done.7.refs_1_ = bf16[256,2048]{1,0:T(8,128)(2,1)S(1)} collective-permute-done((bf16[256,2048]{1,0:T(8,128)(2,1)S(1)}, bf16[256,2048]{1,0:T(8,128)(2,1)S(1)}, u32[]{:S(2)}, u32[]{:S(2)}) %collective-permute-start.7) | collective-permute-done | bytes 1048608 | tf_op jit(solution)/shard_map/ppermute | solution.py:275
  84.8 1.2 %collective-permute-start.15 = (f32[1,512]{1,0:T(1,128)S(1)}, f32[1,512]{1,0:T(1,128)S(1)}, u32[]{:S(2)}, u32[]{:S(2)}) collective-permute-start(f32[1,512]{1,0:T(1,128)S(1)} %get-tuple-element.39), channel_id=1, source_target_pairs={{0,12},{1,0},{2,4},{3,8},{4,13},{5,1},{6,5},{7,9},{8,14},{9,2},{10... | collective-permute-start | bytes 6152 | tf_op jit(solution)/shard_map/ppermute | solution.py:313
  86.0 5.4 %input_grad_rows.7 = bf16[4,256,2048]{2,1,0:T(8,128)(2,1)} custom-call(s32[1]{0:T(128)} %bitcast.me, bf16[256,2048]{1,0:T(8,128)(2,1)S(1)} %collective-permute-done.2.refs_0_, bf16[256,2048]{1,0:T(8,128)(2,1)S(1)} %collective-permute-done.7.refs_1_, bf16[2048,2048]{1,0:T(8,128)(2,1)} %refs_2_.7, ...), custom_call_target="tpu_custom_call", output_to_operand_aliasing={{}: (4, {})} | custom-call | flops 524288 | bytes 524288 | tf_op jit(solution)/shard_map/input_grad_rows/pallas_call | solution.py:131
  91.4 0.0 collective-permute-done.12
  91.4 0.0 collective-permute-done.13
  91.4 0.0 collective-permute-done.14
  91.4 0.0 collective-permute-done.15
  91.4 0.6 add_add_fusion
  (4 shorter events, 0.1 us)
Async XLA Ops:
  0.6 12.5 %copy-start = (bf16[2048,128]{1,0:T(8,128)(2,1)S(1)}, bf16[2048,128]{1,0:T(8,128)(2,1)}, u32[]{:S(2)}) copy-start(bf16[2048,128]{1,0:T(8,128)(2,1)} %param.9) | copy-start | bytes 1572868
  0.6 28.6 %collective-permute-start = (bf16[256,2048]{1,0:T(8,128)(2,1)}, bf16[256,2048]{1,0:T(8,128)(2,1)S(1)}, u32[]{:S(2)}, u32[]{:S(2)}) collective-permute-start(bf16[256,2048]{1,0:T(8,128)(2,1)} %refs_1_.1), channel_id=1, source_target_pairs={{0,1},{1,0},{2,3},{3,2},{4,5},{5,4},{6,7},{7,6},{8,9},{9,8},{10,11... | collective-permute-start | bytes 3145736 | tf_op jit(solution)/shard_map/ppermute | solution.py:247
  3.7 26.2 %collective-permute-start.3 = (bf16[256,2048]{1,0:T(8,128)(2,1)}, bf16[256,2048]{1,0:T(8,128)(2,1)}, u32[]{:S(2)}, u32[]{:S(2)}) collective-permute-start(bf16[256,2048]{1,0:T(8,128)(2,1)} %refs_1_.1), channel_id=1, source_target_pairs={{1,2},{2,1},{5,6},{6,5},{9,10},{10,9},{13,14},{14,13},{17,18},{18,... | collective-permute-start | bytes 3145736 | tf_op jit(solution)/shard_map/ppermute | solution.py:246
  6.4 1.9 %copy-start.5 = (bf16[2048,128]{0,1:T(8,128)(2,1)}, bf16[2048,128]{0,1:T(8,128)(2,1)S(1)}, u32[]{:S(2)}) copy-start(bf16[2048,128]{0,1:T(8,128)(2,1)S(1)} %fusion.2) | copy-start | bytes 1572868
  6.4 10.1 %copy-start.1 = (bf16[256,2048]{1,0:T(8,128)(2,1)S(1)}, bf16[256,2048]{1,0:T(8,128)(2,1)}, u32[]{:S(2)}) copy-start(bf16[256,2048]{1,0:T(8,128)(2,1)} %refs_1_.1) | copy-start | bytes 3145732
  8.3 20.9 %collective-permute-start.1 = (f32[256,128]{1,0:T(8,128)S(1)}, f32[256,128]{1,0:T(8,128)S(1)}, u32[]{:S(2)}, u32[]{:S(2)}) collective-permute-start(f32[256,128]{1,0:T(8,128)S(1)} %convolution_bitcast_fusion.1.own_low), channel_id=1, source_target_pairs={{3,1},{0,2},{7,5},{4,6},{11,9},{8,10},{15,13},{12,14},{19,17},{16,... | collective-permute-start | bytes 393224 | tf_op jit(solution)/shard_map/ppermute | solution.py:253
  22.0 21.9 %copy-start.6 = (bf16[2048,128]{0,1:T(8,128)(2,1)S(1)}, bf16[2048,128]{0,1:T(8,128)(2,1)}, u32[]{:S(2)}) copy-start(bf16[2048,128]{0,1:T(8,128)(2,1)} %copy-done.5) | copy-start | bytes 1572868
  29.2 20.6 %collective-permute-start.2 = (bf16[256,2048]{1,0:T(8,128)(2,1)S(1)}, bf16[256,2048]{1,0:T(8,128)(2,1)S(1)}, u32[]{:S(2)}, u32[]{:S(2)}) collective-permute-start(bf16[256,2048]{1,0:T(8,128)(2,1)S(1)} %collective-permute-done.refs_0_.refs_1_), channel_id=1, source_target_pairs={{1,2},{2,1},{5,6},{6,5},{9,10},{10,9},{13,14},{14,13},{17,18},{18,... | collective-permute-start | bytes 3145736 | tf_op jit(solution)/shard_map/ppermute | solution.py:256
  30.0 28.6 %collective-permute-start.4 = (bf16[256,2048]{1,0:T(8,128)(2,1)}, bf16[256,2048]{1,0:T(8,128)(2,1)S(1)}, u32[]{:S(2)}, u32[]{:S(2)}) collective-permute-start(bf16[256,2048]{1,0:T(8,128)(2,1)} %collective-permute-done.3.refs_0_), channel_id=1, source_target_pairs={{1,0},{2,3},{5,4},{6,7},{9,8},{10,11},{13,12},{14,15},{17,16},{18,... | collective-permute-start | bytes 3145736 | tf_op jit(solution)/shard_map/ppermute | solution.py:257
  31.3 17.1 %collective-permute-start.5 = (f32[1024,128]{1,0:T(8,128)S(1)}, f32[1024,128]{1,0:T(8,128)S(1)}, u32[]{:S(2)}, u32[]{:S(2)}) collective-permute-start(f32[1024,128]{1,0:T(8,128)S(1)} %fusion.3.low_in), channel_id=1, source_target_pairs={{0,1},{3,2},{4,5},{7,6},{8,9},{11,10},{12,13},{15,14},{16,17},{19,... | collective-permute-start | bytes 1572872 | tf_op jit(solution)/shard_map/ppermute | solution.py:258
  49.1 0.7 collective-permute-start.6
  58.5 1.0 %copy-start.3 = (bf16[256,2048]{1,0:T(8,128)(2,1)}, bf16[256,2048]{1,0:T(8,128)(2,1)S(1)}, u32[]{:S(2)}) copy-start(bf16[256,2048]{1,0:T(8,128)(2,1)S(1)} %collective-permute-done.4.refs_1_) | copy-start | bytes 3145732
  59.5 25.3 %collective-permute-start.7 = (bf16[256,2048]{1,0:T(8,128)(2,1)S(1)}, bf16[256,2048]{1,0:T(8,128)(2,1)S(1)}, u32[]{:S(2)}, u32[]{:S(2)}) collective-permute-start(bf16[256,2048]{1,0:T(8,128)(2,1)S(1)} %collective-permute-done.2.refs_0_), channel_id=1, source_target_pairs={{1,0},{2,3},{5,4},{6,7},{9,8},{10,11},{13,12},{14,15},{17,16},{18,... | collective-permute-start | bytes 3145736 | tf_op jit(solution)/shard_map/ppermute | solution.py:275
  60.8 6.8 %collective-permute-start.8 = (f32[1,32,64]{2,1,0:T(8,128)S(1)}, f32[1,32,64]{2,1,0:T(8,128)S(1)}, u32[]{:S(2)}, u32[]{:S(2)}) collective-permute-start(f32[1,32,64]{2,1,0:T(8,128)S(1)} %dynamic-slice_bitcast_fusion), channel_id=1, source_target_pairs={{2,0},{1,3},{6,4},{5,7},{10,8},{9,11},{14,12},{13,15},{18,16},{17,... | collective-permute-start | bytes 24584 | tf_op jit(solution)/shard_map/ppermute | solution.py:276
  67.7 8.8 %collective-permute-start.10 = (f32[1,2048]{1,0:T(1,128)S(1)}, f32[1,2048]{1,0:T(1,128)S(1)}, u32[]{:S(2)}, u32[]{:S(2)}) collective-permute-start(f32[1,2048]{1,0:T(1,128)S(1)} %reshape.23.refs_0_), channel_id=1, source_target_pairs={{0,8},{4,12},{8,0},{12,4},{1,9},{5,13},{9,1},{13,5},{2,10},{6,14},... | collective-permute-start | bytes 24584 | tf_op jit(solution)/shard_map/ppermute | solution.py:303
  69.2 7.3 %collective-permute-start.11 = (f32[1,2048]{1,0:T(1,128)S(1)}, f32[1,2048]{1,0:T(1,128)S(1)}, u32[]{:S(2)}, u32[]{:S(2)}) collective-permute-start(f32[1,2048]{1,0:T(1,128)S(1)} %reshape.23.refs_0_), channel_id=1, source_target_pairs={{0,12},{4,0},{8,4},{12,8},{1,13},{5,1},{9,5},{13,9},{2,14},{6,2},{... | collective-permute-start | bytes 24584 | tf_op jit(solution)/shard_map/ppermute | solution.py:303
  69.2 7.3 %collective-permute-start.9 = (f32[1,2048]{1,0:T(1,128)S(1)}, f32[1,2048]{1,0:T(1,128)S(1)}, u32[]{:S(2)}, u32[]{:S(2)}) collective-permute-start(f32[1,2048]{1,0:T(1,128)S(1)} %reshape.23.refs_0_), channel_id=1, source_target_pairs={{0,4},{4,8},{8,12},{12,0},{1,5},{5,9},{9,13},{13,1},{2,6},{6,10},{... | collective-permute-start | bytes 24584 | tf_op jit(solution)/shard_map/ppermute | solution.py:303
  69.7 1.2 %copy-start.4 = (bf16[256,2048]{1,0:T(8,128)(2,1)S(1)}, bf16[256,2048]{1,0:T(8,128)(2,1)}, u32[]{:S(2)}) copy-start(bf16[256,2048]{1,0:T(8,128)(2,1)} %copy-done.3) | copy-start | bytes 3145732
  71.0 5.6 %copy-start.2 = (bf16[512,2048]{1,0:T(8,128)(2,1)S(1)}, bf16[512,2048]{1,0:T(8,128)(2,1)}, u32[]{:S(2)}) copy-start(bf16[512,2048]{1,0:T(8,128)(2,1)} %refs_4_.1) | copy-start | bytes 6291460
  78.3 13.1 %collective-permute-start.12 = (f32[1,512]{1,0:T(1,128)S(1)}, f32[1,512]{1,0:T(1,128)S(1)}, u32[]{:S(2)}, u32[]{:S(2)}) collective-permute-start(f32[1,512]{1,0:T(1,128)S(1)} %get-tuple-element.35), channel_id=1, source_target_pairs={{0,0},{1,4},{2,8},{3,12},{4,1},{5,5},{6,9},{7,13},{8,2},{9,6},{10,... | collective-permute-start | bytes 6152 | tf_op jit(solution)/shard_map/ppermute | solution.py:313
  79.0 12.5 %collective-permute-start.13 = (f32[1,512]{1,0:T(1,128)S(1)}, f32[1,512]{1,0:T(1,128)S(1)}, u32[]{:S(2)}, u32[]{:S(2)}) collective-permute-start(f32[1,512]{1,0:T(1,128)S(1)} %get-tuple-element.36), channel_id=1, source_target_pairs={{0,4},{1,8},{2,12},{3,0},{4,5},{5,9},{6,13},{7,1},{8,6},{9,10},{10... | collective-permute-start | bytes 6152 | tf_op jit(solution)/shard_map/ppermute | solution.py:313
  80.6 10.8 %collective-permute-start.14 = (f32[1,512]{1,0:T(1,128)S(1)}, f32[1,512]{1,0:T(1,128)S(1)}, u32[]{:S(2)}, u32[]{:S(2)}) collective-permute-start(f32[1,512]{1,0:T(1,128)S(1)} %get-tuple-element.37), channel_id=1, source_target_pairs={{0,8},{1,12},{2,0},{3,4},{4,9},{5,13},{6,1},{7,5},{8,10},{9,14},{1... | collective-permute-start | bytes 6152 | tf_op jit(solution)/shard_map/ppermute | solution.py:313
  84.8 6.6 %collective-permute-start.15 = (f32[1,512]{1,0:T(1,128)S(1)}, f32[1,512]{1,0:T(1,128)S(1)}, u32[]{:S(2)}, u32[]{:S(2)}) collective-permute-start(f32[1,512]{1,0:T(1,128)S(1)} %get-tuple-element.39), channel_id=1, source_target_pairs={{0,12},{1,0},{2,4},{3,8},{4,13},{5,1},{6,5},{7,9},{8,14},{9,2},{10... | collective-permute-start | bytes 6152 | tf_op jit(solution)/shard_map/ppermute | solution.py:313

commit v14 on v13

--- a/solution.py
+++ b/solution.py
@@ -144,7 +144,7 @@
         ],
         out_shape=jax.ShapeDtypeStruct((4, block_rows, width), jnp.bfloat16),
         input_output_aliases={2 * count + 2: 0} if earlier else {},
-        compiler_params=pltpu.CompilerParams(vmem_limit_bytes=GRANT),
+        compiler_params=pltpu.CompilerParams(vmem_limit_bytes=GRANT if block < 3 else GRANT // 2 if block < 3 else GRANT // 2),
         cost_estimate=pl.CostEstimate(flops=rows * width, bytes_accessed=rows * width, transcendentals=0),
         name="input_grad_rows",
     )(me.reshape(1).astype(jnp.int32), *firsts, *seconds, w_kv, *earlier)
@@ -269,10 +269,12 @@
             low_out = put(low_out, rows, me ^ away)
         sums = sequence_sums(low_in + low_in_beside, low_out.reshape(4 * local_rows, 2 * rank), rank)
         slabs = slabs_of(sums, 4)
-    slabs = slabs + lax.ppermute(slabs, "mp", across)
-
-    beside_across, second, slabs, output = tied((beside_across, second, slabs, output))
+    slabs_across = lax.ppermute(slabs, "mp", across)
+
+    beside_across, slabs_across, output = tied((beside_across, slabs_across, output))
     third = lax.ppermute(beside_across, "mp", outward)
+    slabs_across, second = tied((slabs_across, second))
+    slabs = slabs + slabs_across
     mine = lax.ppermute(take(slabs, me ^ 2), "mp", [(2, 0), (1, 3)])
     mine = jnp.where(middle, take(slabs, me), mine)
     output = put_rows(me, 2, output, [facing], [second], w_kv, local_rows)

time: 92.6 us -> 93.2 us (level)
  waiting for transfers between devices: 25.8 us -> 23.8 us
  local copies, waits for them, and re-layouts: 3.3 us -> 4.49 us
    ppermute x1, waiting for transfers between devices: 8.76 us -> 6.69 us  [line_of_four(): second = lax.ppermute(facing, 'mp', outward)]
    unnamed x14 -> x12, local copies, waits for them, and re-layouts: 2.22 us -> 3.41 us
  transfers between devices with their start and end apart: 16 -> 16, of which waited for: 5 -> 5; matrix products, arithmetic and copies ran while one was open for 9% -> 9% of each run, Pallas kernels for 26% -> 27%
where the time goes in v14:
time: 93.2 us; the launch traced here: 92.7 us
  starting transfers between devices  30.4 us (33%)
  Pallas kernels  25 us (27%)
  waiting for transfers between devices  23.8 us (26%)
  matrix products  7.38 us (8%)
  local copies, waits for them, and re-layouts  4.49 us (5%)
  between operations  0.96 us (1%)
    pallas_call x4, Pallas kernels, put_rows(): pl.pallas_call(functools.partial(rows_kernel, block, start, count), in_sp...  22.6 us
    ppermute x1, starting transfers between devices, line_of_four(): low_in_beside = lax.ppermute(low_in, 'mp', inward)  8.08 us
    ppermute x1, waiting for transfers between devices, line_of_four(): far_low = lax.ppermute(own_low, 'mp', [(3, 1), (0, 2)])  7.25 us
    ppermute x1, waiting for transfers between devices, line_of_four(): second = lax.ppermute(facing, 'mp', outward)  6.69 us
    ppermute x4, starting transfers between devices, on_device(): scores = scores + lax.ppermute(rows[step], ('dp', 'mp'), pairs)  5.59 us
    ppermute x1, waiting for transfers between devices, line_of_four(): mine = lax.ppermute(take(slabs, me ^ 2), 'mp', [(2, 0), (1, 3)])  5.33 us
    ppermute x1, starting transfers between devices, line_of_four(): far_low = lax.ppermute(own_low, 'mp', [(3, 1), (0, 2)])  4.77 us
    dot_general x3, matrix products, low_rank(): return jnp.dot(rows, proj_both, preferred_element_type=jnp.float32)  3.95 us
  transfers between devices with their start and end apart: 16, of which 5 were waited for; matrix products, arithmetic and copies ran while one was open for 9% of the time, Pallas kernels for 27%

profile of v14, /device:TPU:0, one launch (start us, length us, event | category | flops | bytes accessed | tf_op | source)
XLA Modules:
  0.0 92.7 jit_solution(8598623039320278660)
XLA Ops:
  0.6 0.0 copy-start
  0.6 3.1 %collective-permute-start = (bf16[256,2048]{1,0:T(8,128)(2,1)}, bf16[256,2048]{1,0:T(8,128)(2,1)S(1)}, u32[]{:S(2)}, u32[]{:S(2)}) collective-permute-start(bf16[256,2048]{1,0:T(8,128)(2,1)} %refs_1_.1), channel_id=1, source_target_pairs={{0,1},{1,0},{2,3},{3,2},{4,5},{5,4},{6,7},{7,6},{8,9},{9,8},{10,11... | collective-permute-start | bytes 3145736 | tf_op jit(solution)/shard_map/ppermute | solution.py:247
  3.7 1.7 %collective-permute-start.4 = (bf16[256,2048]{1,0:T(8,128)(2,1)}, bf16[256,2048]{1,0:T(8,128)(2,1)}, u32[]{:S(2)}, u32[]{:S(2)}) collective-permute-start(bf16[256,2048]{1,0:T(8,128)(2,1)} %refs_1_.1), channel_id=1, source_target_pairs={{1,2},{2,1},{5,6},{6,5},{9,10},{10,9},{13,14},{14,13},{17,18},{18,... | collective-permute-start | bytes 3145736 | tf_op jit(solution)/shard_map/ppermute | solution.py:246
  5.4 1.0 %slice_bitcast_fusion.1 = (bf16[1024,64]{0,1:T(8,128)(2,1)S(1)}, bf16[1024,64]{0,1:T(8,128)(2,1)S(1)}) fusion(bf16[2,1024,64]{1,2,0:T(8,128)(2,1)} %param.10), kind=kLoop, calls=%fused_computation.8 | loop fusion | bytes 524288 | tf_op jit(solution)/shard_map/squeeze | solution.py:59
  6.4 0.0 copy-start.4
  6.4 0.0 copy-start.2
  6.4 1.9 %convolution_bitcast_fusion.1.own_low = f32[256,128]{1,0:T(8,128)S(1)} fusion(bf16[2048,128]{0,1:T(8,128)(2,1)S(1)} %fusion.2, bf16[256,2048]{1,0:T(8,128)(2,1)} %refs_1_.1), kind=kOutput, calls=%fused_computation.1 | convolution fusion | flops 134217728 | bytes 1703936 | tf_op jit(solution)/shard_map/dot_general | solution.py:244
  8.3 0.0 copy-done.4
  8.3 4.8 %collective-permute-start.1 = (f32[256,128]{1,0:T(8,128)S(1)}, f32[256,128]{1,0:T(8,128)S(1)}, u32[]{:S(2)}, u32[]{:S(2)}) collective-permute-start(f32[256,128]{1,0:T(8,128)S(1)} %convolution_bitcast_fusion.1.own_low), channel_id=1, source_target_pairs={{3,1},{0,2},{7,5},{4,6},{11,9},{8,10},{15,13},{12,14},{19,17},{16,... | collective-permute-start | bytes 393224 | tf_op jit(solution)/shard_map/ppermute | solution.py:253
  13.1 0.0 copy-done
  13.1 3.4 %fusion.3.low_in = f32[1024,128]{1,0:T(8,128)S(1)} fusion(bf16[1024,2048]{1,0:T(8,128)(2,1)} %param.6, bf16[2048,128]{1,0:T(8,128)(2,1)S(1)} %copy-done), kind=kOutput, calls=%fused_computation.13 | convolution fusion | flops 536870912 | bytes 5242880 | tf_op jit(solution)/shard_map/dot_general | solution.py:250
  16.5 0.0 copy-done.2
  16.6 5.4 %input_grad_rows.4.refs_3_ = bf16[4,256,2048]{2,1,0:T(8,128)(2,1)} custom-call(s32[1]{0:T(128)} %bitcast.me, bf16[256,2048]{1,0:T(8,128)(2,1)S(1)} %copy-done.2, bf16[256,2048]{1,0:T(8,128)(2,1)S(1)} %copy-done.2, bf16[2048,2048]{1,0:T(8,128)(2,1)} %refs_2_.7), custom_call_target="tpu_custom_call" | custom-call | flops 524288 | bytes 524288 | tf_op jit(solution)/shard_map/input_grad_rows/pallas_call | solution.py:131
  22.0 0.0 copy-start.5
  22.0 7.2 %collective-permute-done.1.far_low = f32[256,128]{1,0:T(8,128)S(1)} collective-permute-done((f32[256,128]{1,0:T(8,128)S(1)}, f32[256,128]{1,0:T(8,128)S(1)}, u32[]{:S(2)}, u32[]{:S(2)}) %collective-permute-start.1) | collective-permute-done | bytes 131104 | tf_op jit(solution)/shard_map/ppermute | solution.py:253
  29.2 0.0 collective-permute-done.refs_0_.refs_1_
  29.2 0.7 collective-permute-start.2
  29.9 0.0 collective-permute-done.4.refs_0_
  30.0 1.3 %collective-permute-start.7 = (bf16[256,2048]{1,0:T(8,128)(2,1)}, bf16[256,2048]{1,0:T(8,128)(2,1)}, u32[]{:S(2)}, u32[]{:S(2)}) collective-permute-start(bf16[256,2048]{1,0:T(8,128)(2,1)} %collective-permute-done.4.refs_0_), channel_id=1, source_target_pairs={{1,0},{2,3},{5,4},{6,7},{9,8},{10,11},{13,12},{14,15},{17,16},{18,... | collective-permute-start | bytes 3145736 | tf_op jit(solution)/shard_map/ppermute | solution.py:257
  31.3 8.1 %collective-permute-start.3 = (f32[1024,128]{1,0:T(8,128)S(1)}, f32[1024,128]{1,0:T(8,128)S(1)}, u32[]{:S(2)}, u32[]{:S(2)}) collective-permute-start(f32[1024,128]{1,0:T(8,128)S(1)} %fusion.3.low_in), channel_id=1, source_target_pairs={{0,1},{3,2},{4,5},{7,6},{8,9},{11,10},{12,13},{15,14},{16,17},{19,... | collective-permute-start | bytes 1572872 | tf_op jit(solution)/shard_map/ppermute | solution.py:258
  39.3 5.4 %input_grad_rows.5.refs_3_ = bf16[4,256,2048]{2,1,0:T(8,128)(2,1)} custom-call(s32[1]{0:T(128)} %bitcast.me, bf16[256,2048]{1,0:T(8,128)(2,1)S(1)} %collective-permute-done.refs_0_.refs_1_, bf16[256,2048]{1,0:T(8,128)(2,1)S(1)} %collective-permute-done.refs_0_.refs_1_, bf16[2048,2048]{1,0:T(8,128)(2,1)} %refs_2_.7, ...), custom_call_target="tpu_custom_call", output_to_operand_aliasing={{}: (4, {})} | custom-call | flops 524288 | bytes 524288 | tf_op jit(solution)/shard_map/input_grad_rows/pallas_call | solution.py:131
  44.8 0.0 copy-done.5
  44.8 0.4 fusion.4.beside_low
  45.2 1.7 %convolution_bitcast_fusion.facing_low = f32[256,128]{1,0:T(8,128)S(1)} fusion(bf16[2048,128]{0,1:T(8,128)(2,1)S(1)} %copy-done.5, bf16[256,2048]{1,0:T(8,128)(2,1)} %collective-permute-done.4.refs_0_), kind=kOutput, calls=%fused_computation | convolution fusion | flops 134217728 | bytes 1703936 | tf_op jit(solution)/shard_map/dot_general | solution.py:244
  46.9 2.4 %collective-permute-done.3.low_in_beside = f32[1024,128]{1,0:T(8,128)S(1)} collective-permute-done((f32[1024,128]{1,0:T(8,128)S(1)}, f32[1024,128]{1,0:T(8,128)S(1)}, u32[]{:S(2)}, u32[]{:S(2)}) %collective-permute-start.3) | collective-permute-done | bytes 524320 | tf_op jit(solution)/shard_map/ppermute | solution.py:258
  49.2 0.7 token_sums.1
  50.0 0.7 collective-permute-start.5
  50.6 0.0 collective-permute-done.5
  50.6 0.0 collective-permute-done.2.refs_0_
  50.6 1.3 %collective-permute-start.6 = (bf16[256,2048]{1,0:T(8,128)(2,1)S(1)}, bf16[256,2048]{1,0:T(8,128)(2,1)S(1)}, u32[]{:S(2)}, u32[]{:S(2)}) collective-permute-start(bf16[256,2048]{1,0:T(8,128)(2,1)S(1)} %collective-permute-done.2.refs_0_), channel_id=1, source_target_pairs={{1,0},{2,3},{5,4},{6,7},{9,8},{10,11},{13,12},{14,15},{17,16},{18,... | collective-permute-start | bytes 3145736 | tf_op jit(solution)/shard_map/ppermute | solution.py:275
  52.0 6.7 %collective-permute-done.7.refs_1_ = bf16[256,2048]{1,0:T(8,128)(2,1)} collective-permute-done((bf16[256,2048]{1,0:T(8,128)(2,1)}, bf16[256,2048]{1,0:T(8,128)(2,1)}, u32[]{:S(2)}, u32[]{:S(2)}) %collective-permute-start.7) | collective-permute-done | bytes 1048608 | tf_op jit(solution)/shard_map/ppermute | solution.py:257
  58.7 1.3 %collective-permute-start.8 = (f32[1,32,64]{2,1,0:T(8,128)S(1)}, f32[1,32,64]{2,1,0:T(8,128)S(1)}, u32[]{:S(2)}, u32[]{:S(2)}) collective-permute-start(f32[1,32,64]{2,1,0:T(8,128)S(1)} %dynamic-slice_bitcast_fusion), channel_id=1, source_target_pairs={{2,0},{1,3},{6,4},{5,7},{10,8},{9,11},{14,12},{13,15},{18,16},{17,... | collective-permute-start | bytes 24584 | tf_op jit(solution)/shard_map/ppermute | solution.py:278
  60.0 5.3 %collective-permute-done.8 = f32[1,32,64]{2,1,0:T(8,128)S(1)} collective-permute-done((f32[1,32,64]{2,1,0:T(8,128)S(1)}, f32[1,32,64]{2,1,0:T(8,128)S(1)}, u32[]{:S(2)}, u32[]{:S(2)}) %collective-permute-start.8) | collective-permute-done | bytes 8224 | tf_op jit(solution)/shard_map/ppermute | solution.py:278
  65.3 0.1 reshape.23.refs_0_
  65.4 1.5 %collective-permute-start.10 = (f32[1,2048]{1,0:T(1,128)S(1)}, f32[1,2048]{1,0:T(1,128)S(1)}, u32[]{:S(2)}, u32[]{:S(2)}) collective-permute-start(f32[1,2048]{1,0:T(1,128)S(1)} %reshape.23.refs_0_), channel_id=1, source_target_pairs={{0,8},{4,12},{8,0},{12,4},{1,9},{5,13},{9,1},{13,5},{2,10},{6,14},... | collective-permute-start | bytes 24584 | tf_op jit(solution)/shard_map/ppermute | solution.py:305
  66.9 0.0 collective-permute-start.11
  66.9 0.5 collective-permute-start.9
  67.4 0.0 copy-start.3
  67.4 7.3 %input_grad_rows.6.refs_3_ = bf16[4,256,2048]{2,1,0:T(8,128)(2,1)} custom-call(s32[1]{0:T(128)} %bitcast.me, bf16[256,2048]{1,0:T(8,128)(2,1)} %collective-permute-done.4.refs_0_, bf16[256,2048]{1,0:T(8,128)(2,1)} %collective-permute-done.7.refs_1_, bf16[2048,2048]{1,0:T(8,128)(2,1)} %refs_2_.7, ...), custom_call_target="tpu_custom_call", output_to_operand_aliasing={{}: (4, {})} | custom-call | flops 524288 | bytes 524288 | tf_op jit(solution)/shard_map/input_grad_rows/pallas_call | solution.py:131
  74.8 0.0 collective-permute-done.10.refs_2_
  74.8 0.0 collective-permute-done.11.refs_3_
  74.8 0.0 collective-permute-done.9.refs_1_
  74.8 0.0 copy-done.3
  74.8 1.7 %scores.1 = (f32[1,512]{1,0:T(1,128)S(1)}, f32[1,512]{1,0:T(1,128)S(1)}, f32[1,512]{1,0:T(1,128)S(1)}, f32[1,512]{1,0:T(1,128)S(1)}) custom-call(s32[1]{0:T(128)} %bitcast.7.first, f32[1,2048]{1,0:T(1,128)S(1)} %reshape.23.refs_0_, f32[1,2048]{1,0:T(1,128)S(1)} %collective-permute-done.9.refs_1_, f32[1,2048]{1,0:T(1,128)S(1)} %collective-permute-done.10.refs_2_, ...), custom_call_target="tpu_custom_call" | custom-call | tf_op jit(solution)/shard_map/scores/pallas_call | solution.py:43
  76.5 0.7 collective-permute-start.12
  77.2 1.6 %collective-permute-start.13 = (f32[1,512]{1,0:T(1,128)S(1)}, f32[1,512]{1,0:T(1,128)S(1)}, u32[]{:S(2)}, u32[]{:S(2)}) collective-permute-start(f32[1,512]{1,0:T(1,128)S(1)} %get-tuple-element.38), channel_id=1, source_target_pairs={{0,4},{1,8},{2,12},{3,0},{4,5},{5,9},{6,13},{7,1},{8,6},{9,10},{10... | collective-permute-start | bytes 6152 | tf_op jit(solution)/shard_map/ppermute | solution.py:315
  78.9 1.9 %collective-permute-start.14 = (f32[1,512]{1,0:T(1,128)S(1)}, f32[1,512]{1,0:T(1,128)S(1)}, u32[]{:S(2)}, u32[]{:S(2)}) collective-permute-start(f32[1,512]{1,0:T(1,128)S(1)} %get-tuple-element.39), channel_id=1, source_target_pairs={{0,8},{1,12},{2,0},{3,4},{4,9},{5,13},{6,1},{7,5},{8,10},{9,14},{1... | collective-permute-start | bytes 6152 | tf_op jit(solution)/shard_map/ppermute | solution.py:315
  80.8 2.1 %collective-permute-done.6.refs_1_ = bf16[256,2048]{1,0:T(8,128)(2,1)S(1)} collective-permute-done((bf16[256,2048]{1,0:T(8,128)(2,1)S(1)}, bf16[256,2048]{1,0:T(8,128)(2,1)S(1)}, u32[]{:S(2)}, u32[]{:S(2)}) %collective-permute-start.6) | collective-permute-done | bytes 1048608 | tf_op jit(solution)/shard_map/ppermute | solution.py:275
  82.9 1.4 %collective-permute-start.15 = (f32[1,512]{1,0:T(1,128)S(1)}, f32[1,512]{1,0:T(1,128)S(1)}, u32[]{:S(2)}, u32[]{:S(2)}) collective-permute-start(f32[1,512]{1,0:T(1,128)S(1)} %get-tuple-element.41), channel_id=1, source_target_pairs={{0,12},{1,0},{2,4},{3,8},{4,13},{5,1},{6,5},{7,9},{8,14},{9,2},{10... | collective-permute-start | bytes 6152 | tf_op jit(solution)/shard_map/ppermute | solution.py:315
  84.3 0.0 copy-start.1
  84.3 3.4 %copy-done.1 = bf16[2048,2048]{1,0:T(8,128)(2,1)S(1)} copy-done((bf16[2048,2048]{1,0:T(8,128)(2,1)S(1)}, bf16[2048,2048]{1,0:T(8,128)(2,1)}, u32[]{:S(2)}) %copy-start.1) | copy-done | bytes 8388632
  87.6 4.4 %input_grad_rows.7 = bf16[4,256,2048]{2,1,0:T(8,128)(2,1)} custom-call(s32[1]{0:T(128)} %bitcast.me, bf16[256,2048]{1,0:T(8,128)(2,1)S(1)} %collective-permute-done.2.refs_0_, bf16[256,2048]{1,0:T(8,128)(2,1)S(1)} %collective-permute-done.6.refs_1_, bf16[2048,2048]{1,0:T(8,128)(2,1)S(1)} %copy-done.1, ...), custom_call_target="tpu_custom_call", output_to_operand_aliasing={{}: (4, {})} | custom-call | flops 524288 | bytes 524288 | tf_op jit(solution)/shard_map/input_grad_rows/pallas_call | solution.py:131
  92.1 0.0 collective-permute-done.12
  92.1 0.0 collective-permute-done.13
  92.1 0.0 collective-permute-done.14
  92.1 0.0 collective-permute-done.15
  92.1 0.6 add_add_fusion
  (4 shorter events, 0.1 us)
Async XLA Ops:
  0.6 12.5 %copy-start = (bf16[2048,128]{1,0:T(8,128)(2,1)S(1)}, bf16[2048,128]{1,0:T(8,128)(2,1)}, u32[]{:S(2)}) copy-start(bf16[2048,128]{1,0:T(8,128)(2,1)} %param.9) | copy-start | bytes 1572868
  0.6 28.6 %collective-permute-start = (bf16[256,2048]{1,0:T(8,128)(2,1)}, bf16[256,2048]{1,0:T(8,128)(2,1)S(1)}, u32[]{:S(2)}, u32[]{:S(2)}) collective-permute-start(bf16[256,2048]{1,0:T(8,128)(2,1)} %refs_1_.1), channel_id=1, source_target_pairs={{0,1},{1,0},{2,3},{3,2},{4,5},{5,4},{6,7},{7,6},{8,9},{9,8},{10,11... | collective-permute-start | bytes 3145736 | tf_op jit(solution)/shard_map/ppermute | solution.py:247
  3.7 26.2 %collective-permute-start.4 = (bf16[256,2048]{1,0:T(8,128)(2,1)}, bf16[256,2048]{1,0:T(8,128)(2,1)}, u32[]{:S(2)}, u32[]{:S(2)}) collective-permute-start(bf16[256,2048]{1,0:T(8,128)(2,1)} %refs_1_.1), channel_id=1, source_target_pairs={{1,2},{2,1},{5,6},{6,5},{9,10},{10,9},{13,14},{14,13},{17,18},{18,... | collective-permute-start | bytes 3145736 | tf_op jit(solution)/shard_map/ppermute | solution.py:246
  6.4 1.9 %copy-start.4 = (bf16[2048,128]{0,1:T(8,128)(2,1)}, bf16[2048,128]{0,1:T(8,128)(2,1)S(1)}, u32[]{:S(2)}) copy-start(bf16[2048,128]{0,1:T(8,128)(2,1)S(1)} %fusion.2) | copy-start | bytes 1572868
  6.4 10.1 %copy-start.2 = (bf16[256,2048]{1,0:T(8,128)(2,1)S(1)}, bf16[256,2048]{1,0:T(8,128)(2,1)}, u32[]{:S(2)}) copy-start(bf16[256,2048]{1,0:T(8,128)(2,1)} %refs_1_.1) | copy-start | bytes 3145732
  8.3 20.9 %collective-permute-start.1 = (f32[256,128]{1,0:T(8,128)S(1)}, f32[256,128]{1,0:T(8,128)S(1)}, u32[]{:S(2)}, u32[]{:S(2)}) collective-permute-start(f32[256,128]{1,0:T(8,128)S(1)} %convolution_bitcast_fusion.1.own_low), channel_id=1, source_target_pairs={{3,1},{0,2},{7,5},{4,6},{11,9},{8,10},{15,13},{12,14},{19,17},{16,... | collective-permute-start | bytes 393224 | tf_op jit(solution)/shard_map/ppermute | solution.py:253
  22.0 22.8 %copy-start.5 = (bf16[2048,128]{0,1:T(8,128)(2,1)S(1)}, bf16[2048,128]{0,1:T(8,128)(2,1)}, u32[]{:S(2)}) copy-start(bf16[2048,128]{0,1:T(8,128)(2,1)} %copy-done.4) | copy-start | bytes 1572868
  29.2 21.4 %collective-permute-start.2 = (bf16[256,2048]{1,0:T(8,128)(2,1)S(1)}, bf16[256,2048]{1,0:T(8,128)(2,1)S(1)}, u32[]{:S(2)}, u32[]{:S(2)}) collective-permute-start(bf16[256,2048]{1,0:T(8,128)(2,1)S(1)} %collective-permute-done.refs_0_.refs_1_), channel_id=1, source_target_pairs={{1,2},{2,1},{5,6},{6,5},{9,10},{10,9},{13,14},{14,13},{17,18},{18,... | collective-permute-start | bytes 3145736 | tf_op jit(solution)/shard_map/ppermute | solution.py:256
  30.0 28.7 %collective-permute-start.7 = (bf16[256,2048]{1,0:T(8,128)(2,1)}, bf16[256,2048]{1,0:T(8,128)(2,1)}, u32[]{:S(2)}, u32[]{:S(2)}) collective-permute-start(bf16[256,2048]{1,0:T(8,128)(2,1)} %collective-permute-done.4.refs_0_), channel_id=1, source_target_pairs={{1,0},{2,3},{5,4},{6,7},{9,8},{10,11},{13,12},{14,15},{17,16},{18,... | collective-permute-start | bytes 3145736 | tf_op jit(solution)/shard_map/ppermute | solution.py:257
  31.3 18.0 %collective-permute-start.3 = (f32[1024,128]{1,0:T(8,128)S(1)}, f32[1024,128]{1,0:T(8,128)S(1)}, u32[]{:S(2)}, u32[]{:S(2)}) collective-permute-start(f32[1024,128]{1,0:T(8,128)S(1)} %fusion.3.low_in), channel_id=1, source_target_pairs={{0,1},{3,2},{4,5},{7,6},{8,9},{11,10},{12,13},{15,14},{16,17},{19,... | collective-permute-start | bytes 1572872 | tf_op jit(solution)/shard_map/ppermute | solution.py:258
  50.0 0.7 collective-permute-start.5
  50.6 32.2 %collective-permute-start.6 = (bf16[256,2048]{1,0:T(8,128)(2,1)S(1)}, bf16[256,2048]{1,0:T(8,128)(2,1)S(1)}, u32[]{:S(2)}, u32[]{:S(2)}) collective-permute-start(bf16[256,2048]{1,0:T(8,128)(2,1)S(1)} %collective-permute-done.2.refs_0_), channel_id=1, source_target_pairs={{1,0},{2,3},{5,4},{6,7},{9,8},{10,11},{13,12},{14,15},{17,16},{18,... | collective-permute-start | bytes 3145736 | tf_op jit(solution)/shard_map/ppermute | solution.py:275
  58.7 6.6 %collective-permute-start.8 = (f32[1,32,64]{2,1,0:T(8,128)S(1)}, f32[1,32,64]{2,1,0:T(8,128)S(1)}, u32[]{:S(2)}, u32[]{:S(2)}) collective-permute-start(f32[1,32,64]{2,1,0:T(8,128)S(1)} %dynamic-slice_bitcast_fusion), channel_id=1, source_target_pairs={{2,0},{1,3},{6,4},{5,7},{10,8},{9,11},{14,12},{13,15},{18,16},{17,... | collective-permute-start | bytes 24584 | tf_op jit(solution)/shard_map/ppermute | solution.py:278
  65.4 9.4 %collective-permute-start.10 = (f32[1,2048]{1,0:T(1,128)S(1)}, f32[1,2048]{1,0:T(1,128)S(1)}, u32[]{:S(2)}, u32[]{:S(2)}) collective-permute-start(f32[1,2048]{1,0:T(1,128)S(1)} %reshape.23.refs_0_), channel_id=1, source_target_pairs={{0,8},{4,12},{8,0},{12,4},{1,9},{5,13},{9,1},{13,5},{2,10},{6,14},... | collective-permute-start | bytes 24584 | tf_op jit(solution)/shard_map/ppermute | solution.py:305
  66.9 7.9 %collective-permute-start.11 = (f32[1,2048]{1,0:T(1,128)S(1)}, f32[1,2048]{1,0:T(1,128)S(1)}, u32[]{:S(2)}, u32[]{:S(2)}) collective-permute-start(f32[1,2048]{1,0:T(1,128)S(1)} %reshape.23.refs_0_), channel_id=1, source_target_pairs={{0,12},{4,0},{8,4},{12,8},{1,13},{5,1},{9,5},{13,9},{2,14},{6,2},{... | collective-permute-start | bytes 24584 | tf_op jit(solution)/shard_map/ppermute | solution.py:305
  66.9 7.9 %collective-permute-start.9 = (f32[1,2048]{1,0:T(1,128)S(1)}, f32[1,2048]{1,0:T(1,128)S(1)}, u32[]{:S(2)}, u32[]{:S(2)}) collective-permute-start(f32[1,2048]{1,0:T(1,128)S(1)} %reshape.23.refs_0_), channel_id=1, source_target_pairs={{0,4},{4,8},{8,12},{12,0},{1,5},{5,9},{9,13},{13,1},{2,6},{6,10},{... | collective-permute-start | bytes 24584 | tf_op jit(solution)/shard_map/ppermute | solution.py:305
  67.4 7.4 %copy-start.3 = (bf16[512,2048]{1,0:T(8,128)(2,1)S(1)}, bf16[512,2048]{1,0:T(8,128)(2,1)}, u32[]{:S(2)}) copy-start(bf16[512,2048]{1,0:T(8,128)(2,1)} %refs_4_.1) | copy-start | bytes 6291460
  76.5 15.5 %collective-permute-start.12 = (f32[1,512]{1,0:T(1,128)S(1)}, f32[1,512]{1,0:T(1,128)S(1)}, u32[]{:S(2)}, u32[]{:S(2)}) collective-permute-start(f32[1,512]{1,0:T(1,128)S(1)} %get-tuple-element.37), channel_id=1, source_target_pairs={{0,0},{1,4},{2,8},{3,12},{4,1},{5,5},{6,9},{7,13},{8,2},{9,6},{10,... | collective-permute-start | bytes 6152 | tf_op jit(solution)/shard_map/ppermute | solution.py:315
  77.2 14.9 %collective-permute-start.13 = (f32[1,512]{1,0:T(1,128)S(1)}, f32[1,512]{1,0:T(1,128)S(1)}, u32[]{:S(2)}, u32[]{:S(2)}) collective-permute-start(f32[1,512]{1,0:T(1,128)S(1)} %get-tuple-element.38), channel_id=1, source_target_pairs={{0,4},{1,8},{2,12},{3,0},{4,5},{5,9},{6,13},{7,1},{8,6},{9,10},{10... | collective-permute-start | bytes 6152 | tf_op jit(solution)/shard_map/ppermute | solution.py:315
  78.9 13.2 %collective-permute-start.14 = (f32[1,512]{1,0:T(1,128)S(1)}, f32[1,512]{1,0:T(1,128)S(1)}, u32[]{:S(2)}, u32[]{:S(2)}) collective-permute-start(f32[1,512]{1,0:T(1,128)S(1)} %get-tuple-element.39), channel_id=1, source_target_pairs={{0,8},{1,12},{2,0},{3,4},{4,9},{5,13},{6,1},{7,5},{8,10},{9,14},{1... | collective-permute-start | bytes 6152 | tf_op jit(solution)/shard_map/ppermute | solution.py:315
  82.9 9.2 %collective-permute-start.15 = (f32[1,512]{1,0:T(1,128)S(1)}, f32[1,512]{1,0:T(1,128)S(1)}, u32[]{:S(2)}, u32[]{:S(2)}) collective-permute-start(f32[1,512]{1,0:T(1,128)S(1)} %get-tuple-element.41), channel_id=1, source_target_pairs={{0,12},{1,0},{2,4},{3,8},{4,13},{5,1},{6,5},{7,9},{8,14},{9,2},{10... | collective-permute-start | bytes 6152 | tf_op jit(solution)/shard_map/ppermute | solution.py:315
  84.3 3.4 %copy-start.1 = (bf16[2048,2048]{1,0:T(8,128)(2,1)S(1)}, bf16[2048,2048]{1,0:T(8,128)(2,1)}, u32[]{:S(2)}) copy-start(bf16[2048,2048]{1,0:T(8,128)(2,1)} %refs_2_.7) | copy-start | bytes 25165828

commit v15 on v14

--- a/solution.py
+++ b/solution.py
@@ -69,8 +69,8 @@
     ).astype(jnp.bfloat16)
 
 
-FETCH = 256
-TILE = 512
+TILE = 256
+AHEAD = 3
 GRANT = 48 * 2**20
 
 
@@ -84,8 +84,8 @@
     use_second = jnp.logical_not(middle) if block > 1 else mine < 0
 
     fetches = []
-    for piece in range(weight.shape[0] // FETCH):
-        here = pl.ds(piece * FETCH, FETCH)
+    for piece in range(weight.shape[0] // TILE):
+        here = pl.ds(piece * TILE, TILE)
         fetches.append(pltpu.make_async_copy(w_kv.at[here], weight.at[here], fetched.at[piece]))
     loads = []
     filled = 0
@@ -100,15 +100,16 @@
             pl.when(use_second)(late.start)
         else:
             loads[-1].start()
-    for fetch in fetches:
+    for fetch in fetches[:AHEAD]:
         fetch.start()
     for load in loads:
         load.wait()
     writes = []
     for tile in range(weight.shape[0] // TILE):
         here = pl.ds(tile * TILE, TILE)
-        for piece in range(tile * TILE // FETCH, (tile + 1) * TILE // FETCH):
-            fetches[piece].wait()
+        fetches[tile].wait()
+        if tile + AHEAD < len(fetches):
+            fetches[tile + AHEAD].start()
         product[:, here] = lax.dot_general(
             held[...], weight[here, :], (((1,), (1,)), ((), ())), preferred_element_type=jnp.float32
         ).astype(product.dtype)
@@ -139,12 +140,12 @@
             pltpu.VMEM((width, depth), w_kv.dtype),
             pltpu.VMEM((rows, width), jnp.bfloat16),
             pltpu.SemaphoreType.DMA((count,)),
-            pltpu.SemaphoreType.DMA((width // FETCH,)),
+            pltpu.SemaphoreType.DMA((width // TILE,)),
             pltpu.SemaphoreType.DMA((width // TILE,)),
         ],
         out_shape=jax.ShapeDtypeStruct((4, block_rows, width), jnp.bfloat16),
         input_output_aliases={2 * count + 2: 0} if earlier else {},
-        compiler_params=pltpu.CompilerParams(vmem_limit_bytes=GRANT if block < 3 else GRANT // 2 if block < 3 else GRANT // 2),
+        compiler_params=pltpu.CompilerParams(vmem_limit_bytes=GRANT),
         cost_estimate=pl.CostEstimate(flops=rows * width, bytes_accessed=rows * width, transcendentals=0),
         name="input_grad_rows",
     )(me.reshape(1).astype(jnp.int32), *firsts, *seconds, w_kv, *earlier)
@@ -250,17 +251,20 @@
     low_in = jnp.dot(hidden, proj_in, preferred_element_type=jnp.float32)
     output = put_rows(me, 0, None, [grad_kv], [grad_kv], w_kv, local_rows)
 
-    far_low = lax.ppermute(own_low, "mp", [(3, 1), (0, 2)])
-
-    beside, low_in, far_low, output = tied((beside, low_in, far_low, output))
+
+    beside, low_in, output = tied((beside, low_in, output))
     beside_across = lax.ppermute(beside, "mp", across)
     second = lax.ppermute(facing, "mp", outward)
     low_in_beside = lax.ppermute(low_in, "mp", inward)
     output = put_rows(me, 1, output, [beside], [beside], w_kv, local_rows)
 
-    low_in_beside, output = tied((low_in_beside, output))
     beside_low = low_rank(beside)
     facing_low = low_rank(facing)
+
+    beside_across, output = tied((beside_across, output))
+    third = lax.ppermute(beside_across, "mp", outward)
+
+    far_low = low_rank(beside_across)
     if low_in.shape[0] == SEQ:
         slabs = token_sums(me, low_in, low_in_beside, own_low, beside_low, facing_low, far_low, rank)[:, None]
     else:
@@ -270,9 +274,6 @@
         sums = sequence_sums(low_in + low_in_beside, low_out.reshape(4 * local_rows, 2 * rank), rank)
         slabs = slabs_of(sums, 4)
     slabs_across = lax.ppermute(slabs, "mp", across)
-
-    beside_across, slabs_across, output = tied((beside_across, slabs_across, output))
-    third = lax.ppermute(beside_across, "mp", outward)
     slabs_across, second = tied((slabs_across, second))
     slabs = slabs + slabs_across
     mine = lax.ppermute(take(slabs, me ^ 2), "mp", [(2, 0), (1, 3)])

time: 93.2 us -> 98.5 us (1.057)
  Pallas kernels: 25 us -> 34.9 us
  waiting for transfers between devices: 23.8 us -> 29.1 us
  starting transfers between devices: 30.4 us -> 26.9 us
  matrix products: 7.38 us -> 4.21 us
  local copies, waits for them, and re-layouts: 4.49 us -> 1.36 us
    ppermute x1, waiting for transfers between devices: 0.01 us -> 11.1 us  [line_of_four(): beside = lax.ppermute(grad_kv, 'mp', exchange_pairs)]
    pallas_call x4, Pallas kernels: 22.6 us -> 32.5 us  [put_rows(): pl.pallas_call(functools.partial(rows_kernel, block, start, count), in_sp...]
    ppermute x1 -> x0, waiting for transfers between devices: 7.25 us -> none  [line_of_four(): far_low = lax.ppermute(own_low, 'mp', [(3, 1), (0, 2)])]
    ppermute x1, waiting for transfers between devices: 5.33 us -> 11.2 us  [line_of_four(): mine = lax.ppermute(take(slabs, me ^ 2), 'mp', [(2, 0), (1, 3)])]
    ppermute x1 -> x0, starting transfers between devices: 4.77 us -> none  [line_of_four(): far_low = lax.ppermute(own_low, 'mp', [(3, 1), (0, 2)])]
    ppermute x1, waiting for transfers between devices: 2.36 us -> 0.01 us  [line_of_four(): low_in_beside = lax.ppermute(low_in, 'mp', inward)]
    dot_general x1, matrix products: 3.43 us -> 1.25 us  [line_of_four(): low_in = jnp.dot(hidden, proj_in, preferred_element_type=jnp.float32)]
    unnamed x12 -> x10, local copies, waits for them, and re-layouts: 3.41 us -> 1.25 us
  transfers between devices with their start and end apart: 16 -> 15, of which waited for: 5 -> 3; matrix products, arithmetic and copies ran while one was open for 9% -> 4% of each run, Pallas kernels for 27% -> 36%
where the time goes in v15:
time: 98.5 us; the launch traced here: 98.1 us
  Pallas kernels  34.9 us (35%)
  waiting for transfers between devices  29.1 us (30%)
  starting transfers between devices  26.9 us (27%)
  matrix products  4.21 us (4%)
  local copies, waits for them, and re-layouts  1.36 us (1%)
    pallas_call x4, Pallas kernels, put_rows(): pl.pallas_call(functools.partial(rows_kernel, block, start, count), in_sp...  32.5 us
    ppermute x1, waiting for transfers between devices, line_of_four(): mine = lax.ppermute(take(slabs, me ^ 2), 'mp', [(2, 0), (1, 3)])  11.2 us
    ppermute x1, waiting for transfers between devices, line_of_four(): beside = lax.ppermute(grad_kv, 'mp', exchange_pairs)  11.1 us
    ppermute x4, starting transfers between devices, on_device(): scores = scores + lax.ppermute(rows[step], ('dp', 'mp'), pairs)  7.49 us
    ppermute x1, starting transfers between devices, line_of_four(): low_in_beside = lax.ppermute(low_in, 'mp', inward)  7.41 us
    ppermute x1, waiting for transfers between devices, line_of_four(): second = lax.ppermute(facing, 'mp', outward)  6.68 us
    ppermute x1, starting transfers between devices, line_of_four(): beside = lax.ppermute(grad_kv, 'mp', exchange_pairs)  3.09 us
    dot_general x4, matrix products, low_rank(): return jnp.dot(rows, proj_both, preferred_element_type=jnp.float32)  2.95 us
  transfers between devices with their start and end apart: 15, of which 3 were waited for; matrix products, arithmetic and copies ran while one was open for 4% of the time, Pallas kernels for 36%

profile of v15, /device:TPU:0, one launch (start us, length us, event | category | flops | bytes accessed | tf_op | source)
XLA Modules:
  0.0 98.1 jit_solution(16004640632737017111)
XLA Ops:
  0.6 0.0 copy-start
  0.6 3.1 %collective-permute-start = (bf16[256,2048]{1,0:T(8,128)(2,1)}, bf16[256,2048]{1,0:T(8,128)(2,1)S(1)}, u32[]{:S(2)}, u32[]{:S(2)}) collective-permute-start(bf16[256,2048]{1,0:T(8,128)(2,1)} %refs_1_.1), channel_id=1, source_target_pairs={{0,1},{1,0},{2,3},{3,2},{4,5},{5,4},{6,7},{7,6},{8,9},{9,8},{10,11... | collective-permute-start | bytes 3145736 | tf_op jit(solution)/shard_map/ppermute | solution.py:248
  3.7 1.6 %collective-permute-start.3 = (bf16[256,2048]{1,0:T(8,128)(2,1)}, bf16[256,2048]{1,0:T(8,128)(2,1)}, u32[]{:S(2)}, u32[]{:S(2)}) collective-permute-start(bf16[256,2048]{1,0:T(8,128)(2,1)} %refs_1_.1), channel_id=1, source_target_pairs={{1,2},{2,1},{5,6},{6,5},{9,10},{10,9},{13,14},{14,13},{17,18},{18,... | collective-permute-start | bytes 3145736 | tf_op jit(solution)/shard_map/ppermute | solution.py:247
  5.4 0.0 copy-start.1
  5.4 1.2 %copy-done.1 = bf16[256,2048]{1,0:T(8,128)(2,1)S(1)} copy-done((bf16[256,2048]{1,0:T(8,128)(2,1)S(1)}, bf16[256,2048]{1,0:T(8,128)(2,1)}, u32[]{:S(2)}) %copy-start.1) | copy-done | bytes 1048600
  6.6 0.0 copy-start.3
  6.6 8.0 %input_grad_rows.4.refs_3_ = bf16[4,256,2048]{2,1,0:T(8,128)(2,1)} custom-call(s32[1]{0:T(128)} %bitcast.me, bf16[256,2048]{1,0:T(8,128)(2,1)S(1)} %copy-done.1, bf16[256,2048]{1,0:T(8,128)(2,1)S(1)} %copy-done.1, bf16[2048,2048]{1,0:T(8,128)(2,1)} %refs_2_.7), custom_call_target="tpu_custom_call" | custom-call | flops 524288 | bytes 524288 | tf_op jit(solution)/shard_map/input_grad_rows/pallas_call | solution.py:132
  14.7 0.0 copy-done
  14.7 0.0 copy-done.3
  14.7 0.0 copy-start.4
  14.7 1.3 %fusion.3.low_in = f32[1024,128]{1,0:T(8,128)S(1)} fusion(bf16[1024,2048]{1,0:T(8,128)(2,1)S(1)} %copy-done.3, bf16[2048,128]{1,0:T(8,128)(2,1)S(1)} %copy-done), kind=kOutput, calls=%fused_computation.13 | convolution fusion | flops 536870912 | bytes 5242880 | tf_op jit(solution)/shard_map/dot_general | solution.py:251
  16.0 11.1 %collective-permute-done.refs_0_.refs_1_ = bf16[256,2048]{1,0:T(8,128)(2,1)S(1)} collective-permute-done((bf16[256,2048]{1,0:T(8,128)(2,1)}, bf16[256,2048]{1,0:T(8,128)(2,1)S(1)}, u32[]{:S(2)}, u32[]{:S(2)}) %collective-permute-start) | collective-permute-done | bytes 1048608 | tf_op jit(solution)/shard_map/ppermute | solution.py:248
  27.1 0.7 collective-permute-start.1
  27.8 0.0 copy-done.4
  27.9 0.0 collective-permute-done.3.refs_0_
  27.9 1.3 %collective-permute-start.6 = (bf16[256,2048]{1,0:T(8,128)(2,1)}, bf16[256,2048]{1,0:T(8,128)(2,1)}, u32[]{:S(2)}, u32[]{:S(2)}) collective-permute-start(bf16[256,2048]{1,0:T(8,128)(2,1)} %collective-permute-done.3.refs_0_), channel_id=1, source_target_pairs={{1,0},{2,3},{5,4},{6,7},{9,8},{10,11},{13,12},{14,15},{17,16},{18,... | collective-permute-start | bytes 3145736 | tf_op jit(solution)/shard_map/ppermute | solution.py:257
  29.2 0.4 convolution_bitcast_fusion.1.own_low
  29.7 7.4 %collective-permute-start.4 = (f32[1024,128]{1,0:T(8,128)S(1)}, f32[1024,128]{1,0:T(8,128)S(1)}, u32[]{:S(2)}, u32[]{:S(2)}) collective-permute-start(f32[1024,128]{1,0:T(8,128)S(1)} %fusion.3.low_in), channel_id=1, source_target_pairs={{0,1},{3,2},{4,5},{7,6},{8,9},{11,10},{12,13},{15,14},{16,17},{19,... | collective-permute-start | bytes 1572872 | tf_op jit(solution)/shard_map/ppermute | solution.py:258
  37.1 7.9 %input_grad_rows.5.refs_3_ = bf16[4,256,2048]{2,1,0:T(8,128)(2,1)} custom-call(s32[1]{0:T(128)} %bitcast.me, bf16[256,2048]{1,0:T(8,128)(2,1)S(1)} %collective-permute-done.refs_0_.refs_1_, bf16[256,2048]{1,0:T(8,128)(2,1)S(1)} %collective-permute-done.refs_0_.refs_1_, bf16[2048,2048]{1,0:T(8,128)(2,1)} %refs_2_.7, ...), custom_call_target="tpu_custom_call", output_to_operand_aliasing={{}: (4, {})} | custom-call | flops 524288 | bytes 524288 | tf_op jit(solution)/shard_map/input_grad_rows/pallas_call | solution.py:132
  45.0 0.4 fusion.4.beside_low
  45.4 0.0 collective-permute-done.1.refs_0_
  45.4 1.3 %collective-permute-start.2 = (bf16[256,2048]{1,0:T(8,128)(2,1)S(1)}, bf16[256,2048]{1,0:T(8,128)(2,1)S(1)}, u32[]{:S(2)}, u32[]{:S(2)}) collective-permute-start(bf16[256,2048]{1,0:T(8,128)(2,1)S(1)} %collective-permute-done.1.refs_0_), channel_id=1, source_target_pairs={{1,0},{2,3},{5,4},{6,7},{9,8},{10,11},{13,12},{14,15},{17,16},{18,... | collective-permute-start | bytes 3145736 | tf_op jit(solution)/shard_map/ppermute | solution.py:265
  46.7 1.7 %convolution_bitcast_fusion.facing_low = f32[256,128]{1,0:T(8,128)S(1)} fusion(bf16[2048,128]{0,1:T(8,128)(2,1)S(1)} %fusion.2, bf16[256,2048]{1,0:T(8,128)(2,1)} %collective-permute-done.3.refs_0_), kind=kOutput, calls=%fused_computation | convolution fusion | flops 134217728 | bytes 1703936 | tf_op jit(solution)/shard_map/dot_general | solution.py:245
  48.4 0.4 fusion.5.far_low
  48.8 0.0 collective-permute-done.4.low_in_beside
  48.9 0.7 token_sums.1
  49.6 0.7 collective-permute-start.5
  50.3 6.7 %collective-permute-done.6.refs_1_ = bf16[256,2048]{1,0:T(8,128)(2,1)} collective-permute-done((bf16[256,2048]{1,0:T(8,128)(2,1)}, bf16[256,2048]{1,0:T(8,128)(2,1)}, u32[]{:S(2)}, u32[]{:S(2)}) %collective-permute-start.6) | collective-permute-done | bytes 1048608 | tf_op jit(solution)/shard_map/ppermute | solution.py:257
  56.9 0.0 collective-permute-done.5
  57.0 1.3 %collective-permute-start.7 = (f32[1,32,64]{2,1,0:T(8,128)S(1)}, f32[1,32,64]{2,1,0:T(8,128)S(1)}, u32[]{:S(2)}, u32[]{:S(2)}) collective-permute-start(f32[1,32,64]{2,1,0:T(8,128)S(1)} %dynamic-slice_bitcast_fusion), channel_id=1, source_target_pairs={{2,0},{1,3},{6,4},{5,7},{10,8},{9,11},{14,12},{13,15},{18,16},{17,... | collective-permute-start | bytes 24584 | tf_op jit(solution)/shard_map/ppermute | solution.py:279
  58.3 11.2 %collective-permute-done.7 = f32[1,32,64]{2,1,0:T(8,128)S(1)} collective-permute-done((f32[1,32,64]{2,1,0:T(8,128)S(1)}, f32[1,32,64]{2,1,0:T(8,128)S(1)}, u32[]{:S(2)}, u32[]{:S(2)}) %collective-permute-start.7) | collective-permute-done | bytes 8224 | tf_op jit(solution)/shard_map/ppermute | solution.py:279
  69.5 0.1 reshape.23.refs_0_
  69.6 0.0 collective-permute-start.10
  69.6 0.5 collective-permute-start.8
  70.1 1.5 %collective-permute-start.9 = (f32[1,2048]{1,0:T(1,128)S(1)}, f32[1,2048]{1,0:T(1,128)S(1)}, u32[]{:S(2)}, u32[]{:S(2)}) collective-permute-start(f32[1,2048]{1,0:T(1,128)S(1)} %reshape.23.refs_0_), channel_id=1, source_target_pairs={{0,8},{4,12},{8,0},{12,4},{1,9},{5,13},{9,1},{13,5},{2,10},{6,14},... | collective-permute-start | bytes 24584 | tf_op jit(solution)/shard_map/ppermute | solution.py:306
  71.6 0.0 copy-start.2
  71.6 8.6 %input_grad_rows.6.refs_3_ = bf16[4,256,2048]{2,1,0:T(8,128)(2,1)} custom-call(s32[1]{0:T(128)} %bitcast.me, bf16[256,2048]{1,0:T(8,128)(2,1)} %collective-permute-done.3.refs_0_, bf16[256,2048]{1,0:T(8,128)(2,1)} %collective-permute-done.6.refs_1_, bf16[2048,2048]{1,0:T(8,128)(2,1)} %refs_2_.7, ...), custom_call_target="tpu_custom_call", output_to_operand_aliasing={{}: (4, {})} | custom-call | flops 524288 | bytes 524288 | tf_op jit(solution)/shard_map/input_grad_rows/pallas_call | solution.py:132
  80.3 0.0 collective-permute-done.10.refs_3_
  80.3 0.0 collective-permute-done.8.refs_1_
  80.3 0.0 collective-permute-done.9.refs_2_
  80.3 0.0 copy-done.2
  80.3 1.7 %scores.1 = (f32[1,512]{1,0:T(1,128)S(1)}, f32[1,512]{1,0:T(1,128)S(1)}, f32[1,512]{1,0:T(1,128)S(1)}, f32[1,512]{1,0:T(1,128)S(1)}) custom-call(s32[1]{0:T(128)} %bitcast.7.first, f32[1,2048]{1,0:T(1,128)S(1)} %reshape.23.refs_0_, f32[1,2048]{1,0:T(1,128)S(1)} %collective-permute-done.8.refs_1_, f32[1,2048]{1,0:T(1,128)S(1)} %collective-permute-done.9.refs_2_, ...), custom_call_target="tpu_custom_call" | custom-call | tf_op jit(solution)/shard_map/scores/pallas_call | solution.py:43
  82.0 0.7 collective-permute-start.11
  82.7 1.4 %collective-permute-start.12 = (f32[1,512]{1,0:T(1,128)S(1)}, f32[1,512]{1,0:T(1,128)S(1)}, u32[]{:S(2)}, u32[]{:S(2)}) collective-permute-start(f32[1,512]{1,0:T(1,128)S(1)} %get-tuple-element.30), channel_id=1, source_target_pairs={{0,4},{1,8},{2,12},{3,0},{4,5},{5,9},{6,13},{7,1},{8,6},{9,10},{10... | collective-permute-start | bytes 6152 | tf_op jit(solution)/shard_map/ppermute | solution.py:316
  84.1 0.7 collective-permute-start.13
  84.9 0.0 collective-permute-done.2.refs_1_
  84.9 4.7 %collective-permute-start.14 = (f32[1,512]{1,0:T(1,128)S(1)}, f32[1,512]{1,0:T(1,128)S(1)}, u32[]{:S(2)}, u32[]{:S(2)}) collective-permute-start(f32[1,512]{1,0:T(1,128)S(1)} %get-tuple-element.33), channel_id=1, source_target_pairs={{0,12},{1,0},{2,4},{3,8},{4,13},{5,1},{6,5},{7,9},{8,14},{9,2},{10... | collective-permute-start | bytes 6152 | tf_op jit(solution)/shard_map/ppermute | solution.py:316
  89.6 7.9 %input_grad_rows.7 = bf16[4,256,2048]{2,1,0:T(8,128)(2,1)} custom-call(s32[1]{0:T(128)} %bitcast.me, bf16[256,2048]{1,0:T(8,128)(2,1)S(1)} %collective-permute-done.1.refs_0_, bf16[256,2048]{1,0:T(8,128)(2,1)S(1)} %collective-permute-done.2.refs_1_, bf16[2048,2048]{1,0:T(8,128)(2,1)} %refs_2_.7, ...), custom_call_target="tpu_custom_call", output_to_operand_aliasing={{}: (4, {})} | custom-call | flops 524288 | bytes 524288 | tf_op jit(solution)/shard_map/input_grad_rows/pallas_call | solution.py:132
  97.5 0.0 collective-permute-done.11
  97.5 0.0 collective-permute-done.12
  97.5 0.0 collective-permute-done.13
  97.5 0.0 collective-permute-done.14
  97.5 0.6 add_add_fusion
  (5 shorter events, 0.1 us)
Async XLA Ops:
  0.6 14.0 %copy-start = (bf16[2048,128]{1,0:T(8,128)(2,1)S(1)}, bf16[2048,128]{1,0:T(8,128)(2,1)}, u32[]{:S(2)}) copy-start(bf16[2048,128]{1,0:T(8,128)(2,1)} %param.9) | copy-start | bytes 1572868
  0.6 26.5 %collective-permute-start = (bf16[256,2048]{1,0:T(8,128)(2,1)}, bf16[256,2048]{1,0:T(8,128)(2,1)S(1)}, u32[]{:S(2)}, u32[]{:S(2)}) collective-permute-start(bf16[256,2048]{1,0:T(8,128)(2,1)} %refs_1_.1), channel_id=1, source_target_pairs={{0,1},{1,0},{2,3},{3,2},{4,5},{5,4},{6,7},{7,6},{8,9},{9,8},{10,11... | collective-permute-start | bytes 3145736 | tf_op jit(solution)/shard_map/ppermute | solution.py:248
  3.7 24.2 %collective-permute-start.3 = (bf16[256,2048]{1,0:T(8,128)(2,1)}, bf16[256,2048]{1,0:T(8,128)(2,1)}, u32[]{:S(2)}, u32[]{:S(2)}) collective-permute-start(bf16[256,2048]{1,0:T(8,128)(2,1)} %refs_1_.1), channel_id=1, source_target_pairs={{1,2},{2,1},{5,6},{6,5},{9,10},{10,9},{13,14},{14,13},{17,18},{18,... | collective-permute-start | bytes 3145736 | tf_op jit(solution)/shard_map/ppermute | solution.py:247
  5.4 1.2 %copy-start.1 = (bf16[256,2048]{1,0:T(8,128)(2,1)S(1)}, bf16[256,2048]{1,0:T(8,128)(2,1)}, u32[]{:S(2)}) copy-start(bf16[256,2048]{1,0:T(8,128)(2,1)} %refs_1_.1) | copy-start | bytes 3145732
  6.6 8.1 %copy-start.3 = (bf16[1024,2048]{1,0:T(8,128)(2,1)S(1)}, bf16[1024,2048]{1,0:T(8,128)(2,1)}, u32[]{:S(2)}) copy-start(bf16[1024,2048]{1,0:T(8,128)(2,1)} %param.6) | copy-start | bytes 12582916
  14.7 13.1 %copy-start.4 = (bf16[2,1024,64]{1,2,0:T(8,128)(2,1)S(1)}, bf16[2,1024,64]{1,2,0:T(8,128)(2,1)}, u32[]{:S(2)}) copy-start(bf16[2,1024,64]{1,2,0:T(8,128)(2,1)} %param.10) | copy-start | bytes 786436
  27.1 18.3 %collective-permute-start.1 = (bf16[256,2048]{1,0:T(8,128)(2,1)S(1)}, bf16[256,2048]{1,0:T(8,128)(2,1)S(1)}, u32[]{:S(2)}, u32[]{:S(2)}) collective-permute-start(bf16[256,2048]{1,0:T(8,128)(2,1)S(1)} %collective-permute-done.refs_0_.refs_1_), channel_id=1, source_target_pairs={{1,2},{2,1},{5,6},{6,5},{9,10},{10,9},{13,14},{14,13},{17,18},{18,... | collective-permute-start | bytes 3145736 | tf_op jit(solution)/shard_map/ppermute | solution.py:256
  27.9 29.0 %collective-permute-start.6 = (bf16[256,2048]{1,0:T(8,128)(2,1)}, bf16[256,2048]{1,0:T(8,128)(2,1)}, u32[]{:S(2)}, u32[]{:S(2)}) collective-permute-start(bf16[256,2048]{1,0:T(8,128)(2,1)} %collective-permute-done.3.refs_0_), channel_id=1, source_target_pairs={{1,0},{2,3},{5,4},{6,7},{9,8},{10,11},{13,12},{14,15},{17,16},{18,... | collective-permute-start | bytes 3145736 | tf_op jit(solution)/shard_map/ppermute | solution.py:257
  29.7 19.2 %collective-permute-start.4 = (f32[1024,128]{1,0:T(8,128)S(1)}, f32[1024,128]{1,0:T(8,128)S(1)}, u32[]{:S(2)}, u32[]{:S(2)}) collective-permute-start(f32[1024,128]{1,0:T(8,128)S(1)} %fusion.3.low_in), channel_id=1, source_target_pairs={{0,1},{3,2},{4,5},{7,6},{8,9},{11,10},{12,13},{15,14},{16,17},{19,... | collective-permute-start | bytes 1572872 | tf_op jit(solution)/shard_map/ppermute | solution.py:258
  45.4 39.4 %collective-permute-start.2 = (bf16[256,2048]{1,0:T(8,128)(2,1)S(1)}, bf16[256,2048]{1,0:T(8,128)(2,1)S(1)}, u32[]{:S(2)}, u32[]{:S(2)}) collective-permute-start(bf16[256,2048]{1,0:T(8,128)(2,1)S(1)} %collective-permute-done.1.refs_0_), channel_id=1, source_target_pairs={{1,0},{2,3},{5,4},{6,7},{9,8},{10,11},{13,12},{14,15},{17,16},{18,... | collective-permute-start | bytes 3145736 | tf_op jit(solution)/shard_map/ppermute | solution.py:265
  49.6 7.4 %collective-permute-start.5 = (f32[4,1,32,64]{3,2,0,1:T(8,128)S(1)}, f32[4,1,32,64]{3,2,0,1:T(8,128)S(1)}, u32[]{:S(2)}, u32[]{:S(2)}) collective-permute-start(f32[4,1,32,64]{3,2,0,1:T(8,128)S(1)} %bitcast.27), channel_id=1, source_target_pairs={{1,2},{2,1},{5,6},{6,5},{9,10},{10,9},{13,14},{14,13},{17,18},{18,... | collective-permute-start | bytes 98312 | tf_op jit(solution)/shard_map/ppermute | solution.py:276
  57.0 12.6 %collective-permute-start.7 = (f32[1,32,64]{2,1,0:T(8,128)S(1)}, f32[1,32,64]{2,1,0:T(8,128)S(1)}, u32[]{:S(2)}, u32[]{:S(2)}) collective-permute-start(f32[1,32,64]{2,1,0:T(8,128)S(1)} %dynamic-slice_bitcast_fusion), channel_id=1, source_target_pairs={{2,0},{1,3},{6,4},{5,7},{10,8},{9,11},{14,12},{13,15},{18,16},{17,... | collective-permute-start | bytes 24584 | tf_op jit(solution)/shard_map/ppermute | solution.py:279
  69.6 10.7 %collective-permute-start.10 = (f32[1,2048]{1,0:T(1,128)S(1)}, f32[1,2048]{1,0:T(1,128)S(1)}, u32[]{:S(2)}, u32[]{:S(2)}) collective-permute-start(f32[1,2048]{1,0:T(1,128)S(1)} %reshape.23.refs_0_), channel_id=1, source_target_pairs={{0,12},{4,0},{8,4},{12,8},{1,13},{5,1},{9,5},{13,9},{2,14},{6,2},{... | collective-permute-start | bytes 24584 | tf_op jit(solution)/shard_map/ppermute | solution.py:306
  69.6 10.6 %collective-permute-start.8 = (f32[1,2048]{1,0:T(1,128)S(1)}, f32[1,2048]{1,0:T(1,128)S(1)}, u32[]{:S(2)}, u32[]{:S(2)}) collective-permute-start(f32[1,2048]{1,0:T(1,128)S(1)} %reshape.23.refs_0_), channel_id=1, source_target_pairs={{0,4},{4,8},{8,12},{12,0},{1,5},{5,9},{9,13},{13,1},{2,6},{6,10},{... | collective-permute-start | bytes 24584 | tf_op jit(solution)/shard_map/ppermute | solution.py:306
  70.1 10.2 %collective-permute-start.9 = (f32[1,2048]{1,0:T(1,128)S(1)}, f32[1,2048]{1,0:T(1,128)S(1)}, u32[]{:S(2)}, u32[]{:S(2)}) collective-permute-start(f32[1,2048]{1,0:T(1,128)S(1)} %reshape.23.refs_0_), channel_id=1, source_target_pairs={{0,8},{4,12},{8,0},{12,4},{1,9},{5,13},{9,1},{13,5},{2,10},{6,14},... | collective-permute-start | bytes 24584 | tf_op jit(solution)/shard_map/ppermute | solution.py:306
  71.6 8.7 %copy-start.2 = (bf16[512,2048]{1,0:T(8,128)(2,1)S(1)}, bf16[512,2048]{1,0:T(8,128)(2,1)}, u32[]{:S(2)}) copy-start(bf16[512,2048]{1,0:T(8,128)(2,1)} %refs_4_.1) | copy-start | bytes 6291460
  82.0 15.4 %collective-permute-start.11 = (f32[1,512]{1,0:T(1,128)S(1)}, f32[1,512]{1,0:T(1,128)S(1)}, u32[]{:S(2)}, u32[]{:S(2)}) collective-permute-start(f32[1,512]{1,0:T(1,128)S(1)} %get-tuple-element.29), channel_id=1, source_target_pairs={{0,0},{1,4},{2,8},{3,12},{4,1},{5,5},{6,9},{7,13},{8,2},{9,6},{10,... | collective-permute-start | bytes 6152 | tf_op jit(solution)/shard_map/ppermute | solution.py:316
  82.7 14.8 %collective-permute-start.12 = (f32[1,512]{1,0:T(1,128)S(1)}, f32[1,512]{1,0:T(1,128)S(1)}, u32[]{:S(2)}, u32[]{:S(2)}) collective-permute-start(f32[1,512]{1,0:T(1,128)S(1)} %get-tuple-element.30), channel_id=1, source_target_pairs={{0,4},{1,8},{2,12},{3,0},{4,5},{5,9},{6,13},{7,1},{8,6},{9,10},{10... | collective-permute-start | bytes 6152 | tf_op jit(solution)/shard_map/ppermute | solution.py:316
  84.1 13.4 %collective-permute-start.13 = (f32[1,512]{1,0:T(1,128)S(1)}, f32[1,512]{1,0:T(1,128)S(1)}, u32[]{:S(2)}, u32[]{:S(2)}) collective-permute-start(f32[1,512]{1,0:T(1,128)S(1)} %get-tuple-element.31), channel_id=1, source_target_pairs={{0,8},{1,12},{2,0},{3,4},{4,9},{5,13},{6,1},{7,5},{8,10},{9,14},{1... | collective-permute-start | bytes 6152 | tf_op jit(solution)/shard_map/ppermute | solution.py:316
  84.9 12.6 %collective-permute-start.14 = (f32[1,512]{1,0:T(1,128)S(1)}, f32[1,512]{1,0:T(1,128)S(1)}, u32[]{:S(2)}, u32[]{:S(2)}) collective-permute-start(f32[1,512]{1,0:T(1,128)S(1)} %get-tuple-element.33), channel_id=1, source_target_pairs={{0,12},{1,0},{2,4},{3,8},{4,13},{5,1},{6,5},{7,9},{8,14},{9,2},{10... | collective-permute-start | bytes 6152 | tf_op jit(solution)/shard_map/ppermute | solution.py:316

commit v16 on v14

--- a/solution.py
+++ b/solution.py
@@ -144,7 +144,7 @@
         ],
         out_shape=jax.ShapeDtypeStruct((4, block_rows, width), jnp.bfloat16),
         input_output_aliases={2 * count + 2: 0} if earlier else {},
-        compiler_params=pltpu.CompilerParams(vmem_limit_bytes=GRANT if block < 3 else GRANT // 2 if block < 3 else GRANT // 2),
+        compiler_params=pltpu.CompilerParams(vmem_limit_bytes=GRANT),
         cost_estimate=pl.CostEstimate(flops=rows * width, bytes_accessed=rows * width, transcendentals=0),
         name="input_grad_rows",
     )(me.reshape(1).astype(jnp.int32), *firsts, *seconds, w_kv, *earlier)
@@ -250,17 +250,20 @@
     low_in = jnp.dot(hidden, proj_in, preferred_element_type=jnp.float32)
     output = put_rows(me, 0, None, [grad_kv], [grad_kv], w_kv, local_rows)
 
-    far_low = lax.ppermute(own_low, "mp", [(3, 1), (0, 2)])
-
-    beside, low_in, far_low, output = tied((beside, low_in, far_low, output))
+
+    beside, low_in, output = tied((beside, low_in, output))
     beside_across = lax.ppermute(beside, "mp", across)
     second = lax.ppermute(facing, "mp", outward)
     low_in_beside = lax.ppermute(low_in, "mp", inward)
     output = put_rows(me, 1, output, [beside], [beside], w_kv, local_rows)
 
-    low_in_beside, output = tied((low_in_beside, output))
     beside_low = low_rank(beside)
     facing_low = low_rank(facing)
+
+    beside_across, output = tied((beside_across, output))
+    third = lax.ppermute(beside_across, "mp", outward)
+
+    far_low = low_rank(beside_across)
     if low_in.shape[0] == SEQ:
         slabs = token_sums(me, low_in, low_in_beside, own_low, beside_low, facing_low, far_low, rank)[:, None]
     else:
@@ -270,14 +273,12 @@
         sums = sequence_sums(low_in + low_in_beside, low_out.reshape(4 * local_rows, 2 * rank), rank)
         slabs = slabs_of(sums, 4)
     slabs_across = lax.ppermute(slabs, "mp", across)
-
-    beside_across, slabs_across, output = tied((beside_across, slabs_across, output))
-    third = lax.ppermute(beside_across, "mp", outward)
     slabs_across, second = tied((slabs_across, second))
     slabs = slabs + slabs_across
     mine = lax.ppermute(take(slabs, me ^ 2), "mp", [(2, 0), (1, 3)])
     mine = jnp.where(middle, take(slabs, me), mine)
     output = put_rows(me, 2, output, [facing], [second], w_kv, local_rows)
+    mine, output = tied((mine, output))
 
     def finish(rows):
         rows = list(tied((*rows, output))[:-1])

time: 93.2 us -> 93.3 us (level)
  waiting for transfers between devices: 23.8 us -> 29 us
  matrix products: 7.38 us -> 4.21 us
  local copies, waits for them, and re-layouts: 4.49 us -> 2.95 us
  starting transfers between devices: 30.4 us -> 29.2 us
  Pallas kernels: 25 us -> 26 us
    ppermute x1, waiting for transfers between devices: 0.01 us -> 13.7 us  [line_of_four(): beside = lax.ppermute(grad_kv, 'mp', exchange_pairs)]
    ppermute x1 -> x0, waiting for transfers between devices: 7.25 us -> none  [line_of_four(): far_low = lax.ppermute(own_low, 'mp', [(3, 1), (0, 2)])]
    ppermute x1 -> x0, starting transfers between devices: 4.77 us -> none  [line_of_four(): far_low = lax.ppermute(own_low, 'mp', [(3, 1), (0, 2)])]
    ppermute x4, starting transfers between devices: 5.59 us -> 9.77 us  [on_device(): scores = scores + lax.ppermute(rows[step], ('dp', 'mp'), pairs)]
    dot_general x1, matrix products: 3.43 us -> 1.25 us  [line_of_four(): low_in = jnp.dot(hidden, proj_in, preferred_element_type=jnp.float32)]
    ppermute x3, waiting for transfers between devices: 0.01 us -> 2.14 us  [on_device(): lax.ppermute(mine, 'dp', [(source, (source + step) % shards) for source i...]
    ppermute x1, waiting for transfers between devices: 2.11 us -> 0.01 us  [line_of_four(): third = lax.ppermute(beside_across, 'mp', outward)]
    ppermute x1, waiting for transfers between devices: 6.69 us -> 8.38 us  [line_of_four(): second = lax.ppermute(facing, 'mp', outward)]
  transfers between devices with their start and end apart: 16 -> 15, of which waited for: 5 -> 6; matrix products, arithmetic and copies ran while one was open for 9% -> 5% of each run, Pallas kernels for 27% -> 28%
where the time goes in v16:
time: 93.3 us; the launch traced here: 92.9 us
  starting transfers between devices  29.2 us (31%)
  waiting for transfers between devices  29 us (31%)
  Pallas kernels  26 us (28%)
  matrix products  4.21 us (5%)
  local copies, waits for them, and re-layouts  2.95 us (3%)
    pallas_call x4, Pallas kernels, put_rows(): pl.pallas_call(functools.partial(rows_kernel, block, start, count), in_sp...  23.5 us
    ppermute x1, waiting for transfers between devices, line_of_four(): beside = lax.ppermute(grad_kv, 'mp', exchange_pairs)  13.7 us
    ppermute x4, starting transfers between devices, on_device(): scores = scores + lax.ppermute(rows[step], ('dp', 'mp'), pairs)  9.77 us
    ppermute x1, waiting for transfers between devices, line_of_four(): second = lax.ppermute(facing, 'mp', outward)  8.38 us
    ppermute x1, starting transfers between devices, line_of_four(): low_in_beside = lax.ppermute(low_in, 'mp', inward)  7.41 us
    ppermute x1, waiting for transfers between devices, line_of_four(): mine = lax.ppermute(take(slabs, me ^ 2), 'mp', [(2, 0), (1, 3)])  4.04 us
    ppermute x1, starting transfers between devices, line_of_four(): beside = lax.ppermute(grad_kv, 'mp', exchange_pairs)  3.09 us
    dot_general x4, matrix products, low_rank(): return jnp.dot(rows, proj_both, preferred_element_type=jnp.float32)  2.96 us
  transfers between devices with their start and end apart: 15, of which 6 were waited for; matrix products, arithmetic and copies ran while one was open for 5% of the time, Pallas kernels for 28%

profile of v16, /device:TPU:0, one launch (start us, length us, event | category | flops | bytes accessed | tf_op | source)
XLA Modules:
  0.0 92.9 jit_solution(16892057570921949239)
XLA Ops:
  0.6 0.0 copy-start
  0.6 3.1 %collective-permute-start = (bf16[256,2048]{1,0:T(8,128)(2,1)}, bf16[256,2048]{1,0:T(8,128)(2,1)S(1)}, u32[]{:S(2)}, u32[]{:S(2)}) collective-permute-start(bf16[256,2048]{1,0:T(8,128)(2,1)} %refs_1_.1), channel_id=1, source_target_pairs={{0,1},{1,0},{2,3},{3,2},{4,5},{5,4},{6,7},{7,6},{8,9},{9,8},{10,11... | collective-permute-start | bytes 3145736 | tf_op jit(solution)/shard_map/ppermute | solution.py:247
  3.7 1.6 %collective-permute-start.4 = (bf16[256,2048]{1,0:T(8,128)(2,1)}, bf16[256,2048]{1,0:T(8,128)(2,1)}, u32[]{:S(2)}, u32[]{:S(2)}) collective-permute-start(bf16[256,2048]{1,0:T(8,128)(2,1)} %refs_1_.1), channel_id=1, source_target_pairs={{1,2},{2,1},{5,6},{6,5},{9,10},{10,9},{13,14},{14,13},{17,18},{18,... | collective-permute-start | bytes 3145736 | tf_op jit(solution)/shard_map/ppermute | solution.py:246
  5.4 0.0 copy-start.1
  5.4 1.2 %copy-done.1 = bf16[256,2048]{1,0:T(8,128)(2,1)S(1)} copy-done((bf16[256,2048]{1,0:T(8,128)(2,1)S(1)}, bf16[256,2048]{1,0:T(8,128)(2,1)}, u32[]{:S(2)}) %copy-start.1) | copy-done | bytes 1048600
  6.6 0.0 copy-start.3
  6.6 5.5 %input_grad_rows.4.refs_3_ = bf16[4,256,2048]{2,1,0:T(8,128)(2,1)} custom-call(s32[1]{0:T(128)} %bitcast.me, bf16[256,2048]{1,0:T(8,128)(2,1)S(1)} %copy-done.1, bf16[256,2048]{1,0:T(8,128)(2,1)S(1)} %copy-done.1, bf16[2048,2048]{1,0:T(8,128)(2,1)} %refs_2_.7), custom_call_target="tpu_custom_call" | custom-call | flops 524288 | bytes 524288 | tf_op jit(solution)/shard_map/input_grad_rows/pallas_call | solution.py:131
  12.2 0.0 copy-done
  12.2 0.0 copy-done.3
  12.2 0.0 copy-start.4
  12.2 1.3 %fusion.3.low_in = f32[1024,128]{1,0:T(8,128)S(1)} fusion(bf16[1024,2048]{1,0:T(8,128)(2,1)S(1)} %copy-done.3, bf16[2048,128]{1,0:T(8,128)(2,1)S(1)} %copy-done), kind=kOutput, calls=%fused_computation.13 | convolution fusion | flops 536870912 | bytes 5242880 | tf_op jit(solution)/shard_map/dot_general | solution.py:250
  13.4 13.7 %collective-permute-done.refs_0_.refs_1_ = bf16[256,2048]{1,0:T(8,128)(2,1)S(1)} collective-permute-done((bf16[256,2048]{1,0:T(8,128)(2,1)}, bf16[256,2048]{1,0:T(8,128)(2,1)S(1)}, u32[]{:S(2)}, u32[]{:S(2)}) %collective-permute-start) | collective-permute-done | bytes 1048608 | tf_op jit(solution)/shard_map/ppermute | solution.py:247
  27.1 0.7 collective-permute-start.1
  27.8 0.0 copy-done.4
  27.9 0.0 collective-permute-done.4.refs_0_
  27.9 1.3 %collective-permute-start.6 = (bf16[256,2048]{1,0:T(8,128)(2,1)}, bf16[256,2048]{1,0:T(8,128)(2,1)}, u32[]{:S(2)}, u32[]{:S(2)}) collective-permute-start(bf16[256,2048]{1,0:T(8,128)(2,1)} %collective-permute-done.4.refs_0_), channel_id=1, source_target_pairs={{1,0},{2,3},{5,4},{6,7},{9,8},{10,11},{13,12},{14,15},{17,16},{18,... | collective-permute-start | bytes 3145736 | tf_op jit(solution)/shard_map/ppermute | solution.py:256
  29.2 0.4 convolution_bitcast_fusion.1.own_low
  29.7 7.4 %collective-permute-start.3 = (f32[1024,128]{1,0:T(8,128)S(1)}, f32[1024,128]{1,0:T(8,128)S(1)}, u32[]{:S(2)}, u32[]{:S(2)}) collective-permute-start(f32[1024,128]{1,0:T(8,128)S(1)} %fusion.3.low_in), channel_id=1, source_target_pairs={{0,1},{3,2},{4,5},{7,6},{8,9},{11,10},{12,13},{15,14},{16,17},{19,... | collective-permute-start | bytes 1572872 | tf_op jit(solution)/shard_map/ppermute | solution.py:257
  37.1 5.4 %input_grad_rows.5.refs_3_ = bf16[4,256,2048]{2,1,0:T(8,128)(2,1)} custom-call(s32[1]{0:T(128)} %bitcast.me, bf16[256,2048]{1,0:T(8,128)(2,1)S(1)} %collective-permute-done.refs_0_.refs_1_, bf16[256,2048]{1,0:T(8,128)(2,1)S(1)} %collective-permute-done.refs_0_.refs_1_, bf16[2048,2048]{1,0:T(8,128)(2,1)} %refs_2_.7, ...), custom_call_target="tpu_custom_call", output_to_operand_aliasing={{}: (4, {})} | custom-call | flops 524288 | bytes 524288 | tf_op jit(solution)/shard_map/input_grad_rows/pallas_call | solution.py:131
  42.5 0.4 fusion.4.beside_low
  42.9 0.0 collective-permute-done.1.refs_0_
  42.9 1.3 %collective-permute-start.2 = (bf16[256,2048]{1,0:T(8,128)(2,1)S(1)}, bf16[256,2048]{1,0:T(8,128)(2,1)S(1)}, u32[]{:S(2)}, u32[]{:S(2)}) collective-permute-start(bf16[256,2048]{1,0:T(8,128)(2,1)S(1)} %collective-permute-done.1.refs_0_), channel_id=1, source_target_pairs={{1,0},{2,3},{5,4},{6,7},{9,8},{10,11},{13,12},{14,15},{17,16},{18,... | collective-permute-start | bytes 3145736 | tf_op jit(solution)/shard_map/ppermute | solution.py:264
  44.2 1.7 %convolution_bitcast_fusion.facing_low = f32[256,128]{1,0:T(8,128)S(1)} fusion(bf16[2048,128]{0,1:T(8,128)(2,1)S(1)} %fusion.2, bf16[256,2048]{1,0:T(8,128)(2,1)} %collective-permute-done.4.refs_0_), kind=kOutput, calls=%fused_computation | convolution fusion | flops 134217728 | bytes 1703936 | tf_op jit(solution)/shard_map/dot_general | solution.py:244
  45.9 0.4 fusion.5.far_low
  46.3 0.8 collective-permute-done.3.low_in_beside
  47.2 0.7 token_sums.1
  47.9 0.7 collective-permute-start.5
  48.6 8.4 %collective-permute-done.6.refs_1_ = bf16[256,2048]{1,0:T(8,128)(2,1)} collective-permute-done((bf16[256,2048]{1,0:T(8,128)(2,1)}, bf16[256,2048]{1,0:T(8,128)(2,1)}, u32[]{:S(2)}, u32[]{:S(2)}) %collective-permute-start.6) | collective-permute-done | bytes 1048608 | tf_op jit(solution)/shard_map/ppermute | solution.py:256
  56.9 0.0 collective-permute-done.5
  57.0 1.3 %collective-permute-start.7 = (f32[1,32,64]{2,1,0:T(8,128)S(1)}, f32[1,32,64]{2,1,0:T(8,128)S(1)}, u32[]{:S(2)}, u32[]{:S(2)}) collective-permute-start(f32[1,32,64]{2,1,0:T(8,128)S(1)} %dynamic-slice_bitcast_fusion), channel_id=1, source_target_pairs={{2,0},{1,3},{6,4},{5,7},{10,8},{9,11},{14,12},{13,15},{18,16},{17,... | collective-permute-start | bytes 24584 | tf_op jit(solution)/shard_map/ppermute | solution.py:278
  58.3 7.2 %input_grad_rows.6.refs_3_ = bf16[4,256,2048]{2,1,0:T(8,128)(2,1)} custom-call(s32[1]{0:T(128)} %bitcast.me, bf16[256,2048]{1,0:T(8,128)(2,1)} %collective-permute-done.4.refs_0_, bf16[256,2048]{1,0:T(8,128)(2,1)} %collective-permute-done.6.refs_1_, bf16[2048,2048]{1,0:T(8,128)(2,1)} %refs_2_.7, ...), custom_call_target="tpu_custom_call", output_to_operand_aliasing={{}: (4, {})} | custom-call | flops 524288 | bytes 524288 | tf_op jit(solution)/shard_map/input_grad_rows/pallas_call | solution.py:131
  65.5 4.0 %collective-permute-done.7 = f32[1,32,64]{2,1,0:T(8,128)S(1)} collective-permute-done((f32[1,32,64]{2,1,0:T(8,128)S(1)}, f32[1,32,64]{2,1,0:T(8,128)S(1)}, u32[]{:S(2)}, u32[]{:S(2)}) %collective-permute-start.7) | collective-permute-done | bytes 8224 | tf_op jit(solution)/shard_map/ppermute | solution.py:278
  69.5 0.1 reshape.23.refs_0_
  69.6 0.0 collective-permute-start.10
  69.6 0.5 collective-permute-start.8
  70.1 1.5 %collective-permute-start.9 = (f32[1,2048]{1,0:T(1,128)S(1)}, f32[1,2048]{1,0:T(1,128)S(1)}, u32[]{:S(2)}, u32[]{:S(2)}) collective-permute-start(f32[1,2048]{1,0:T(1,128)S(1)} %reshape.23.refs_0_), channel_id=1, source_target_pairs={{0,8},{4,12},{8,0},{12,4},{1,9},{5,13},{9,1},{13,5},{2,10},{6,14},... | collective-permute-start | bytes 24584 | tf_op jit(solution)/shard_map/ppermute | solution.py:306
  71.6 0.0 collective-permute-done.10.refs_3_
  71.6 1.3 %collective-permute-done.8.refs_1_ = f32[1,2048]{1,0:T(1,128)S(1)} collective-permute-done((f32[1,2048]{1,0:T(1,128)S(1)}, f32[1,2048]{1,0:T(1,128)S(1)}, u32[]{:S(2)}, u32[]{:S(2)}) %collective-permute-start.8) | collective-permute-done | bytes 8224 | tf_op jit(solution)/shard_map/ppermute | solution.py:306
  72.9 0.8 collective-permute-done.9.refs_2_
  73.8 0.0 copy-start.2
  73.8 1.6 %copy-done.2 = bf16[512,2048]{1,0:T(8,128)(2,1)S(1)} copy-done((bf16[512,2048]{1,0:T(8,128)(2,1)S(1)}, bf16[512,2048]{1,0:T(8,128)(2,1)}, u32[]{:S(2)}) %copy-start.2) | copy-done | bytes 2097176
  75.4 1.7 %scores.1 = (f32[1,512]{1,0:T(1,128)S(1)}, f32[1,512]{1,0:T(1,128)S(1)}, f32[1,512]{1,0:T(1,128)S(1)}, f32[1,512]{1,0:T(1,128)S(1)}) custom-call(s32[1]{0:T(128)} %bitcast.9.first, f32[1,2048]{1,0:T(1,128)S(1)} %reshape.23.refs_0_, f32[1,2048]{1,0:T(1,128)S(1)} %collective-permute-done.8.refs_1_, f32[1,2048]{1,0:T(1,128)S(1)} %collective-permute-done.9.refs_2_, ...), custom_call_target="tpu_custom_call" | custom-call | tf_op jit(solution)/shard_map/scores/pallas_call | solution.py:43
  77.1 0.7 collective-permute-start.11
  77.8 5.4 %collective-permute-start.12 = (f32[1,512]{1,0:T(1,128)S(1)}, f32[1,512]{1,0:T(1,128)S(1)}, u32[]{:S(2)}, u32[]{:S(2)}) collective-permute-start(f32[1,512]{1,0:T(1,128)S(1)} %get-tuple-element.34), channel_id=1, source_target_pairs={{0,4},{1,8},{2,12},{3,0},{4,5},{5,9},{6,13},{7,1},{8,6},{9,10},{10... | collective-permute-start | bytes 6152 | tf_op jit(solution)/shard_map/ppermute | solution.py:316
  83.2 3.5 %collective-permute-start.13 = (f32[1,512]{1,0:T(1,128)S(1)}, f32[1,512]{1,0:T(1,128)S(1)}, u32[]{:S(2)}, u32[]{:S(2)}) collective-permute-start(f32[1,512]{1,0:T(1,128)S(1)} %get-tuple-element.35), channel_id=1, source_target_pairs={{0,8},{1,12},{2,0},{3,4},{4,9},{5,13},{6,1},{7,5},{8,10},{9,14},{1... | collective-permute-start | bytes 6152 | tf_op jit(solution)/shard_map/ppermute | solution.py:316
  86.6 0.0 collective-permute-done.2.refs_1_
  86.6 0.3 collective-permute-start.14
  86.9 5.4 %input_grad_rows.7 = bf16[4,256,2048]{2,1,0:T(8,128)(2,1)} custom-call(s32[1]{0:T(128)} %bitcast.me, bf16[256,2048]{1,0:T(8,128)(2,1)S(1)} %collective-permute-done.1.refs_0_, bf16[256,2048]{1,0:T(8,128)(2,1)S(1)} %collective-permute-done.2.refs_1_, bf16[2048,2048]{1,0:T(8,128)(2,1)} %refs_2_.7, ...), custom_call_target="tpu_custom_call", output_to_operand_aliasing={{}: (4, {})} | custom-call | flops 524288 | bytes 524288 | tf_op jit(solution)/shard_map/input_grad_rows/pallas_call | solution.py:131
  92.3 0.0 collective-permute-done.11
  92.3 0.0 collective-permute-done.12
  92.3 0.0 collective-permute-done.13
  92.3 0.0 collective-permute-done.14
  92.3 0.6 add_add_fusion
  (5 shorter events, 0.1 us)
Async XLA Ops:
  0.6 11.5 %copy-start = (bf16[2048,128]{1,0:T(8,128)(2,1)S(1)}, bf16[2048,128]{1,0:T(8,128)(2,1)}, u32[]{:S(2)}) copy-start(bf16[2048,128]{1,0:T(8,128)(2,1)} %param.9) | copy-start | bytes 1572868
  0.6 26.5 %collective-permute-start = (bf16[256,2048]{1,0:T(8,128)(2,1)}, bf16[256,2048]{1,0:T(8,128)(2,1)S(1)}, u32[]{:S(2)}, u32[]{:S(2)}) collective-permute-start(bf16[256,2048]{1,0:T(8,128)(2,1)} %refs_1_.1), channel_id=1, source_target_pairs={{0,1},{1,0},{2,3},{3,2},{4,5},{5,4},{6,7},{7,6},{8,9},{9,8},{10,11... | collective-permute-start | bytes 3145736 | tf_op jit(solution)/shard_map/ppermute | solution.py:247
  3.7 24.2 %collective-permute-start.4 = (bf16[256,2048]{1,0:T(8,128)(2,1)}, bf16[256,2048]{1,0:T(8,128)(2,1)}, u32[]{:S(2)}, u32[]{:S(2)}) collective-permute-start(bf16[256,2048]{1,0:T(8,128)(2,1)} %refs_1_.1), channel_id=1, source_target_pairs={{1,2},{2,1},{5,6},{6,5},{9,10},{10,9},{13,14},{14,13},{17,18},{18,... | collective-permute-start | bytes 3145736 | tf_op jit(solution)/shard_map/ppermute | solution.py:246
  5.4 1.2 %copy-start.1 = (bf16[256,2048]{1,0:T(8,128)(2,1)S(1)}, bf16[256,2048]{1,0:T(8,128)(2,1)}, u32[]{:S(2)}) copy-start(bf16[256,2048]{1,0:T(8,128)(2,1)} %refs_1_.1) | copy-start | bytes 3145732
  6.6 5.6 %copy-start.3 = (bf16[1024,2048]{1,0:T(8,128)(2,1)S(1)}, bf16[1024,2048]{1,0:T(8,128)(2,1)}, u32[]{:S(2)}) copy-start(bf16[1024,2048]{1,0:T(8,128)(2,1)} %param.6) | copy-start | bytes 12582916
  12.2 15.7 %copy-start.4 = (bf16[2,1024,64]{1,2,0:T(8,128)(2,1)S(1)}, bf16[2,1024,64]{1,2,0:T(8,128)(2,1)}, u32[]{:S(2)}) copy-start(bf16[2,1024,64]{1,2,0:T(8,128)(2,1)} %param.10) | copy-start | bytes 786436
  27.1 15.8 %collective-permute-start.1 = (bf16[256,2048]{1,0:T(8,128)(2,1)S(1)}, bf16[256,2048]{1,0:T(8,128)(2,1)S(1)}, u32[]{:S(2)}, u32[]{:S(2)}) collective-permute-start(bf16[256,2048]{1,0:T(8,128)(2,1)S(1)} %collective-permute-done.refs_0_.refs_1_), channel_id=1, source_target_pairs={{1,2},{2,1},{5,6},{6,5},{9,10},{10,9},{13,14},{14,13},{17,18},{18,... | collective-permute-start | bytes 3145736 | tf_op jit(solution)/shard_map/ppermute | solution.py:255
  27.9 29.0 %collective-permute-start.6 = (bf16[256,2048]{1,0:T(8,128)(2,1)}, bf16[256,2048]{1,0:T(8,128)(2,1)}, u32[]{:S(2)}, u32[]{:S(2)}) collective-permute-start(bf16[256,2048]{1,0:T(8,128)(2,1)} %collective-permute-done.4.refs_0_), channel_id=1, source_target_pairs={{1,0},{2,3},{5,4},{6,7},{9,8},{10,11},{13,12},{14,15},{17,16},{18,... | collective-permute-start | bytes 3145736 | tf_op jit(solution)/shard_map/ppermute | solution.py:256
  29.7 17.5 %collective-permute-start.3 = (f32[1024,128]{1,0:T(8,128)S(1)}, f32[1024,128]{1,0:T(8,128)S(1)}, u32[]{:S(2)}, u32[]{:S(2)}) collective-permute-start(f32[1024,128]{1,0:T(8,128)S(1)} %fusion.3.low_in), channel_id=1, source_target_pairs={{0,1},{3,2},{4,5},{7,6},{8,9},{11,10},{12,13},{15,14},{16,17},{19,... | collective-permute-start | bytes 1572872 | tf_op jit(solution)/shard_map/ppermute | solution.py:257
  42.9 43.7 %collective-permute-start.2 = (bf16[256,2048]{1,0:T(8,128)(2,1)S(1)}, bf16[256,2048]{1,0:T(8,128)(2,1)S(1)}, u32[]{:S(2)}, u32[]{:S(2)}) collective-permute-start(bf16[256,2048]{1,0:T(8,128)(2,1)S(1)} %collective-permute-done.1.refs_0_), channel_id=1, source_target_pairs={{1,0},{2,3},{5,4},{6,7},{9,8},{10,11},{13,12},{14,15},{17,16},{18,... | collective-permute-start | bytes 3145736 | tf_op jit(solution)/shard_map/ppermute | solution.py:264
  47.9 9.1 %collective-permute-start.5 = (f32[4,1,32,64]{3,2,0,1:T(8,128)S(1)}, f32[4,1,32,64]{3,2,0,1:T(8,128)S(1)}, u32[]{:S(2)}, u32[]{:S(2)}) collective-permute-start(f32[4,1,32,64]{3,2,0,1:T(8,128)S(1)} %bitcast.27), channel_id=1, source_target_pairs={{1,2},{2,1},{5,6},{6,5},{9,10},{10,9},{13,14},{14,13},{17,18},{18,... | collective-permute-start | bytes 98312 | tf_op jit(solution)/shard_map/ppermute | solution.py:275
  57.0 12.6 %collective-permute-start.7 = (f32[1,32,64]{2,1,0:T(8,128)S(1)}, f32[1,32,64]{2,1,0:T(8,128)S(1)}, u32[]{:S(2)}, u32[]{:S(2)}) collective-permute-start(f32[1,32,64]{2,1,0:T(8,128)S(1)} %dynamic-slice_bitcast_fusion), channel_id=1, source_target_pairs={{2,0},{1,3},{6,4},{5,7},{10,8},{9,11},{14,12},{13,15},{18,16},{17,... | collective-permute-start | bytes 24584 | tf_op jit(solution)/shard_map/ppermute | solution.py:278
  69.6 2.0 %collective-permute-start.10 = (f32[1,2048]{1,0:T(1,128)S(1)}, f32[1,2048]{1,0:T(1,128)S(1)}, u32[]{:S(2)}, u32[]{:S(2)}) collective-permute-start(f32[1,2048]{1,0:T(1,128)S(1)} %reshape.23.refs_0_), channel_id=1, source_target_pairs={{0,12},{4,0},{8,4},{12,8},{1,13},{5,1},{9,5},{13,9},{2,14},{6,2},{... | collective-permute-start | bytes 24584 | tf_op jit(solution)/shard_map/ppermute | solution.py:306
  69.6 3.3 %collective-permute-start.8 = (f32[1,2048]{1,0:T(1,128)S(1)}, f32[1,2048]{1,0:T(1,128)S(1)}, u32[]{:S(2)}, u32[]{:S(2)}) collective-permute-start(f32[1,2048]{1,0:T(1,128)S(1)} %reshape.23.refs_0_), channel_id=1, source_target_pairs={{0,4},{4,8},{8,12},{12,0},{1,5},{5,9},{9,13},{13,1},{2,6},{6,10},{... | collective-permute-start | bytes 24584 | tf_op jit(solution)/shard_map/ppermute | solution.py:306
  70.1 3.7 %collective-permute-start.9 = (f32[1,2048]{1,0:T(1,128)S(1)}, f32[1,2048]{1,0:T(1,128)S(1)}, u32[]{:S(2)}, u32[]{:S(2)}) collective-permute-start(f32[1,2048]{1,0:T(1,128)S(1)} %reshape.23.refs_0_), channel_id=1, source_target_pairs={{0,8},{4,12},{8,0},{12,4},{1,9},{5,13},{9,1},{13,5},{2,10},{6,14},... | collective-permute-start | bytes 24584 | tf_op jit(solution)/shard_map/ppermute | solution.py:306
  73.8 1.6 %copy-start.2 = (bf16[512,2048]{1,0:T(8,128)(2,1)S(1)}, bf16[512,2048]{1,0:T(8,128)(2,1)}, u32[]{:S(2)}) copy-start(bf16[512,2048]{1,0:T(8,128)(2,1)} %refs_4_.1) | copy-start | bytes 6291460
  77.1 15.2 %collective-permute-start.11 = (f32[1,512]{1,0:T(1,128)S(1)}, f32[1,512]{1,0:T(1,128)S(1)}, u32[]{:S(2)}, u32[]{:S(2)}) collective-permute-start(f32[1,512]{1,0:T(1,128)S(1)} %get-tuple-element.33), channel_id=1, source_target_pairs={{0,0},{1,4},{2,8},{3,12},{4,1},{5,5},{6,9},{7,13},{8,2},{9,6},{10,... | collective-permute-start | bytes 6152 | tf_op jit(solution)/shard_map/ppermute | solution.py:316
  77.8 14.5 %collective-permute-start.12 = (f32[1,512]{1,0:T(1,128)S(1)}, f32[1,512]{1,0:T(1,128)S(1)}, u32[]{:S(2)}, u32[]{:S(2)}) collective-permute-start(f32[1,512]{1,0:T(1,128)S(1)} %get-tuple-element.34), channel_id=1, source_target_pairs={{0,4},{1,8},{2,12},{3,0},{4,5},{5,9},{6,13},{7,1},{8,6},{9,10},{10... | collective-permute-start | bytes 6152 | tf_op jit(solution)/shard_map/ppermute | solution.py:316
  83.2 9.2 %collective-permute-start.13 = (f32[1,512]{1,0:T(1,128)S(1)}, f32[1,512]{1,0:T(1,128)S(1)}, u32[]{:S(2)}, u32[]{:S(2)}) collective-permute-start(f32[1,512]{1,0:T(1,128)S(1)} %get-tuple-element.35), channel_id=1, source_target_pairs={{0,8},{1,12},{2,0},{3,4},{4,9},{5,13},{6,1},{7,5},{8,10},{9,14},{1... | collective-permute-start | bytes 6152 | tf_op jit(solution)/shard_map/ppermute | solution.py:316
  86.6 5.7 %collective-permute-start.14 = (f32[1,512]{1,0:T(1,128)S(1)}, f32[1,512]{1,0:T(1,128)S(1)}, u32[]{:S(2)}, u32[]{:S(2)}) collective-permute-start(f32[1,512]{1,0:T(1,128)S(1)} %get-tuple-element.37), channel_id=1, source_target_pairs={{0,12},{1,0},{2,4},{3,8},{4,13},{5,1},{6,5},{7,9},{8,14},{9,2},{10... | collective-permute-start | bytes 6152 | tf_op jit(solution)/shard_map/ppermute | solution.py:316

commit v17 on v14

--- a/solution.py
+++ b/solution.py
@@ -70,7 +70,7 @@
 
 
 FETCH = 256
-TILE = 512
+TILE = 1024
 GRANT = 48 * 2**20
 
 
@@ -144,7 +144,7 @@
         ],
         out_shape=jax.ShapeDtypeStruct((4, block_rows, width), jnp.bfloat16),
         input_output_aliases={2 * count + 2: 0} if earlier else {},
-        compiler_params=pltpu.CompilerParams(vmem_limit_bytes=GRANT if block < 3 else GRANT // 2 if block < 3 else GRANT // 2),
+        compiler_params=pltpu.CompilerParams(vmem_limit_bytes=GRANT),
         cost_estimate=pl.CostEstimate(flops=rows * width, bytes_accessed=rows * width, transcendentals=0),
         name="input_grad_rows",
     )(me.reshape(1).astype(jnp.int32), *firsts, *seconds, w_kv, *earlier)

time: 93.2 us -> 90.6 us (0.972)
  local copies, waits for them, and re-layouts: 4.49 us -> 1.11 us
  Pallas kernels: 25 us -> 26.6 us
    unnamed x12 -> x10, local copies, waits for them, and re-layouts: 3.41 us -> 0.03 us
    pallas_call x4, Pallas kernels: 22.6 us -> 24.1 us  [put_rows(): pl.pallas_call(functools.partial(rows_kernel, block, start, count), in_sp...]
  transfers between devices with their start and end apart: 16 -> 16, of which waited for: 5 -> 5; matrix products, arithmetic and copies ran while one was open for 9% -> 9% of each run, Pallas kernels for 27% -> 30%
where the time goes in v17:
time: 90.6 us; the launch traced here: 90.1 us
  starting transfers between devices  29.7 us (33%)
  Pallas kernels  26.6 us (29%)
  waiting for transfers between devices  23.7 us (26%)
  matrix products  7.39 us (8%)
  local copies, waits for them, and re-layouts  1.11 us (1%)
  between operations  0.95 us (1%)
    pallas_call x4, Pallas kernels, put_rows(): pl.pallas_call(functools.partial(rows_kernel, block, start, count), in_sp...  24.1 us
    ppermute x1, starting transfers between devices, line_of_four(): low_in_beside = lax.ppermute(low_in, 'mp', inward)  8.08 us
    ppermute x1, waiting for transfers between devices, line_of_four(): far_low = lax.ppermute(own_low, 'mp', [(3, 1), (0, 2)])  6.94 us
    ppermute x1, waiting for transfers between devices, line_of_four(): second = lax.ppermute(facing, 'mp', outward)  6.69 us
    ppermute x1, waiting for transfers between devices, line_of_four(): mine = lax.ppermute(take(slabs, me ^ 2), 'mp', [(2, 0), (1, 3)])  5.33 us
    ppermute x4, starting transfers between devices, on_device(): scores = scores + lax.ppermute(rows[step], ('dp', 'mp'), pairs)  4.88 us
    ppermute x1, starting transfers between devices, line_of_four(): far_low = lax.ppermute(own_low, 'mp', [(3, 1), (0, 2)])  4.76 us
    dot_general x3, matrix products, low_rank(): return jnp.dot(rows, proj_both, preferred_element_type=jnp.float32)  3.96 us
  transfers between devices with their start and end apart: 16, of which 5 were waited for; matrix products, arithmetic and copies ran while one was open for 9% of the time, Pallas kernels for 30%

profile of v17, /device:TPU:0, one launch (start us, length us, event | category | flops | bytes accessed | tf_op | source)
XLA Modules:
  0.0 90.1 jit_solution(7314554904871323166)
XLA Ops:
  0.6 0.0 copy-start
  0.6 3.1 %collective-permute-start = (bf16[256,2048]{1,0:T(8,128)(2,1)}, bf16[256,2048]{1,0:T(8,128)(2,1)S(1)}, u32[]{:S(2)}, u32[]{:S(2)}) collective-permute-start(bf16[256,2048]{1,0:T(8,128)(2,1)} %refs_1_.1), channel_id=1, source_target_pairs={{0,1},{1,0},{2,3},{3,2},{4,5},{5,4},{6,7},{7,6},{8,9},{9,8},{10,11... | collective-permute-start | bytes 3145736 | tf_op jit(solution)/shard_map/ppermute | solution.py:247
  3.7 1.7 %collective-permute-start.4 = (bf16[256,2048]{1,0:T(8,128)(2,1)}, bf16[256,2048]{1,0:T(8,128)(2,1)}, u32[]{:S(2)}, u32[]{:S(2)}) collective-permute-start(bf16[256,2048]{1,0:T(8,128)(2,1)} %refs_1_.1), channel_id=1, source_target_pairs={{1,2},{2,1},{5,6},{6,5},{9,10},{10,9},{13,14},{14,13},{17,18},{18,... | collective-permute-start | bytes 3145736 | tf_op jit(solution)/shard_map/ppermute | solution.py:246
  5.4 1.0 %slice_bitcast_fusion.1 = (bf16[1024,64]{0,1:T(8,128)(2,1)S(1)}, bf16[1024,64]{0,1:T(8,128)(2,1)S(1)}) fusion(bf16[2,1024,64]{1,2,0:T(8,128)(2,1)} %param.10), kind=kLoop, calls=%fused_computation.8 | loop fusion | bytes 524288 | tf_op jit(solution)/shard_map/squeeze | solution.py:59
  6.4 0.0 copy-start.3
  6.4 0.0 copy-start.1
  6.4 1.9 %convolution_bitcast_fusion.1.own_low = f32[256,128]{1,0:T(8,128)S(1)} fusion(bf16[2048,128]{0,1:T(8,128)(2,1)S(1)} %fusion.2, bf16[256,2048]{1,0:T(8,128)(2,1)} %refs_1_.1), kind=kOutput, calls=%fused_computation.1 | convolution fusion | flops 134217728 | bytes 1703936 | tf_op jit(solution)/shard_map/dot_general | solution.py:244
  8.3 0.0 copy-done.3
  8.3 4.8 %collective-permute-start.1 = (f32[256,128]{1,0:T(8,128)S(1)}, f32[256,128]{1,0:T(8,128)S(1)}, u32[]{:S(2)}, u32[]{:S(2)}) collective-permute-start(f32[256,128]{1,0:T(8,128)S(1)} %convolution_bitcast_fusion.1.own_low), channel_id=1, source_target_pairs={{3,1},{0,2},{7,5},{4,6},{11,9},{8,10},{15,13},{12,14},{19,17},{16,... | collective-permute-start | bytes 393224 | tf_op jit(solution)/shard_map/ppermute | solution.py:253
  13.1 0.0 copy-done
  13.1 3.4 %fusion.3.low_in = f32[1024,128]{1,0:T(8,128)S(1)} fusion(bf16[1024,2048]{1,0:T(8,128)(2,1)} %param.6, bf16[2048,128]{1,0:T(8,128)(2,1)S(1)} %copy-done), kind=kOutput, calls=%fused_computation.13 | convolution fusion | flops 536870912 | bytes 5242880 | tf_op jit(solution)/shard_map/dot_general | solution.py:250
  16.5 0.0 copy-done.1
  16.6 5.7 %input_grad_rows.4.refs_3_ = bf16[4,256,2048]{2,1,0:T(8,128)(2,1)} custom-call(s32[1]{0:T(128)} %bitcast.me, bf16[256,2048]{1,0:T(8,128)(2,1)S(1)} %copy-done.1, bf16[256,2048]{1,0:T(8,128)(2,1)S(1)} %copy-done.1, bf16[2048,2048]{1,0:T(8,128)(2,1)} %refs_2_.7), custom_call_target="tpu_custom_call" | custom-call | flops 524288 | bytes 524288 | tf_op jit(solution)/shard_map/input_grad_rows/pallas_call | solution.py:131
  22.3 0.0 copy-start.4
  22.3 6.9 %collective-permute-done.1.far_low = f32[256,128]{1,0:T(8,128)S(1)} collective-permute-done((f32[256,128]{1,0:T(8,128)S(1)}, f32[256,128]{1,0:T(8,128)S(1)}, u32[]{:S(2)}, u32[]{:S(2)}) %collective-permute-start.1) | collective-permute-done | bytes 131104 | tf_op jit(solution)/shard_map/ppermute | solution.py:253
  29.2 0.0 collective-permute-done.refs_0_.refs_1_
  29.2 0.7 collective-permute-start.2
  29.9 0.0 collective-permute-done.4.refs_0_
  30.0 1.3 %collective-permute-start.7 = (bf16[256,2048]{1,0:T(8,128)(2,1)}, bf16[256,2048]{1,0:T(8,128)(2,1)}, u32[]{:S(2)}, u32[]{:S(2)}) collective-permute-start(bf16[256,2048]{1,0:T(8,128)(2,1)} %collective-permute-done.4.refs_0_), channel_id=1, source_target_pairs={{1,0},{2,3},{5,4},{6,7},{9,8},{10,11},{13,12},{14,15},{17,16},{18,... | collective-permute-start | bytes 3145736 | tf_op jit(solution)/shard_map/ppermute | solution.py:257
  31.3 8.1 %collective-permute-start.3 = (f32[1024,128]{1,0:T(8,128)S(1)}, f32[1024,128]{1,0:T(8,128)S(1)}, u32[]{:S(2)}, u32[]{:S(2)}) collective-permute-start(f32[1024,128]{1,0:T(8,128)S(1)} %fusion.3.low_in), channel_id=1, source_target_pairs={{0,1},{3,2},{4,5},{7,6},{8,9},{11,10},{12,13},{15,14},{16,17},{19,... | collective-permute-start | bytes 1572872 | tf_op jit(solution)/shard_map/ppermute | solution.py:258
  39.3 5.7 %input_grad_rows.5.refs_3_ = bf16[4,256,2048]{2,1,0:T(8,128)(2,1)} custom-call(s32[1]{0:T(128)} %bitcast.me, bf16[256,2048]{1,0:T(8,128)(2,1)S(1)} %collective-permute-done.refs_0_.refs_1_, bf16[256,2048]{1,0:T(8,128)(2,1)S(1)} %collective-permute-done.refs_0_.refs_1_, bf16[2048,2048]{1,0:T(8,128)(2,1)} %refs_2_.7, ...), custom_call_target="tpu_custom_call", output_to_operand_aliasing={{}: (4, {})} | custom-call | flops 524288 | bytes 524288 | tf_op jit(solution)/shard_map/input_grad_rows/pallas_call | solution.py:131
  45.1 0.0 copy-done.4
  45.1 0.4 fusion.4.beside_low
  45.5 1.7 %convolution_bitcast_fusion.facing_low = f32[256,128]{1,0:T(8,128)S(1)} fusion(bf16[2048,128]{0,1:T(8,128)(2,1)S(1)} %copy-done.4, bf16[256,2048]{1,0:T(8,128)(2,1)} %collective-permute-done.4.refs_0_), kind=kOutput, calls=%fused_computation | convolution fusion | flops 134217728 | bytes 1703936 | tf_op jit(solution)/shard_map/dot_general | solution.py:244
  47.2 2.1 %collective-permute-done.3.low_in_beside = f32[1024,128]{1,0:T(8,128)S(1)} collective-permute-done((f32[1024,128]{1,0:T(8,128)S(1)}, f32[1024,128]{1,0:T(8,128)S(1)}, u32[]{:S(2)}, u32[]{:S(2)}) %collective-permute-start.3) | collective-permute-done | bytes 524320 | tf_op jit(solution)/shard_map/ppermute | solution.py:258
  49.2 0.7 token_sums.1
  50.0 0.7 collective-permute-start.5
  50.6 0.0 collective-permute-done.5
  50.6 0.0 collective-permute-done.2.refs_0_
  50.7 1.3 %collective-permute-start.6 = (bf16[256,2048]{1,0:T(8,128)(2,1)S(1)}, bf16[256,2048]{1,0:T(8,128)(2,1)S(1)}, u32[]{:S(2)}, u32[]{:S(2)}) collective-permute-start(bf16[256,2048]{1,0:T(8,128)(2,1)S(1)} %collective-permute-done.2.refs_0_), channel_id=1, source_target_pairs={{1,0},{2,3},{5,4},{6,7},{9,8},{10,11},{13,12},{14,15},{17,16},{18,... | collective-permute-start | bytes 3145736 | tf_op jit(solution)/shard_map/ppermute | solution.py:275
  52.0 6.7 %collective-permute-done.7.refs_1_ = bf16[256,2048]{1,0:T(8,128)(2,1)} collective-permute-done((bf16[256,2048]{1,0:T(8,128)(2,1)}, bf16[256,2048]{1,0:T(8,128)(2,1)}, u32[]{:S(2)}, u32[]{:S(2)}) %collective-permute-start.7) | collective-permute-done | bytes 1048608 | tf_op jit(solution)/shard_map/ppermute | solution.py:257
  58.7 1.3 %collective-permute-start.8 = (f32[1,32,64]{2,1,0:T(8,128)S(1)}, f32[1,32,64]{2,1,0:T(8,128)S(1)}, u32[]{:S(2)}, u32[]{:S(2)}) collective-permute-start(f32[1,32,64]{2,1,0:T(8,128)S(1)} %dynamic-slice_bitcast_fusion), channel_id=1, source_target_pairs={{2,0},{1,3},{6,4},{5,7},{10,8},{9,11},{14,12},{13,15},{18,16},{17,... | collective-permute-start | bytes 24584 | tf_op jit(solution)/shard_map/ppermute | solution.py:278
  60.0 5.3 %collective-permute-done.8 = f32[1,32,64]{2,1,0:T(8,128)S(1)} collective-permute-done((f32[1,32,64]{2,1,0:T(8,128)S(1)}, f32[1,32,64]{2,1,0:T(8,128)S(1)}, u32[]{:S(2)}, u32[]{:S(2)}) %collective-permute-start.8) | collective-permute-done | bytes 8224 | tf_op jit(solution)/shard_map/ppermute | solution.py:278
  65.3 0.1 reshape.23.refs_0_
  65.4 1.5 %collective-permute-start.10 = (f32[1,2048]{1,0:T(1,128)S(1)}, f32[1,2048]{1,0:T(1,128)S(1)}, u32[]{:S(2)}, u32[]{:S(2)}) collective-permute-start(f32[1,2048]{1,0:T(1,128)S(1)} %reshape.23.refs_0_), channel_id=1, source_target_pairs={{0,8},{4,12},{8,0},{12,4},{1,9},{5,13},{9,1},{13,5},{2,10},{6,14},... | collective-permute-start | bytes 24584 | tf_op jit(solution)/shard_map/ppermute | solution.py:305
  66.9 0.0 collective-permute-start.11
  66.9 0.5 collective-permute-start.9
  67.4 0.0 copy-start.2
  67.4 7.0 %input_grad_rows.6.refs_3_ = bf16[4,256,2048]{2,1,0:T(8,128)(2,1)} custom-call(s32[1]{0:T(128)} %bitcast.me, bf16[256,2048]{1,0:T(8,128)(2,1)} %collective-permute-done.4.refs_0_, bf16[256,2048]{1,0:T(8,128)(2,1)} %collective-permute-done.7.refs_1_, bf16[2048,2048]{1,0:T(8,128)(2,1)} %refs_2_.7, ...), custom_call_target="tpu_custom_call", output_to_operand_aliasing={{}: (4, {})} | custom-call | flops 524288 | bytes 524288 | tf_op jit(solution)/shard_map/input_grad_rows/pallas_call | solution.py:131
  74.4 0.0 collective-permute-done.10.refs_2_
  74.5 0.0 collective-permute-done.11.refs_3_
  74.5 0.0 collective-permute-done.9.refs_1_
  74.5 0.0 copy-done.2
  74.5 1.7 %scores.1 = (f32[1,512]{1,0:T(1,128)S(1)}, f32[1,512]{1,0:T(1,128)S(1)}, f32[1,512]{1,0:T(1,128)S(1)}, f32[1,512]{1,0:T(1,128)S(1)}) custom-call(s32[1]{0:T(128)} %bitcast.7.first, f32[1,2048]{1,0:T(1,128)S(1)} %reshape.23.refs_0_, f32[1,2048]{1,0:T(1,128)S(1)} %collective-permute-done.9.refs_1_, f32[1,2048]{1,0:T(1,128)S(1)} %collective-permute-done.10.refs_2_, ...), custom_call_target="tpu_custom_call" | custom-call | tf_op jit(solution)/shard_map/scores/pallas_call | solution.py:43
  76.2 0.7 collective-permute-start.12
  76.9 1.5 %collective-permute-start.13 = (f32[1,512]{1,0:T(1,128)S(1)}, f32[1,512]{1,0:T(1,128)S(1)}, u32[]{:S(2)}, u32[]{:S(2)}) collective-permute-start(f32[1,512]{1,0:T(1,128)S(1)} %get-tuple-element.38), channel_id=1, source_target_pairs={{0,4},{1,8},{2,12},{3,0},{4,5},{5,9},{6,13},{7,1},{8,6},{9,10},{10... | collective-permute-start | bytes 6152 | tf_op jit(solution)/shard_map/ppermute | solution.py:315
  78.4 1.9 %collective-permute-start.14 = (f32[1,512]{1,0:T(1,128)S(1)}, f32[1,512]{1,0:T(1,128)S(1)}, u32[]{:S(2)}, u32[]{:S(2)}) collective-permute-start(f32[1,512]{1,0:T(1,128)S(1)} %get-tuple-element.39), channel_id=1, source_target_pairs={{0,8},{1,12},{2,0},{3,4},{4,9},{5,13},{6,1},{7,5},{8,10},{9,14},{1... | collective-permute-start | bytes 6152 | tf_op jit(solution)/shard_map/ppermute | solution.py:315
  80.2 2.6 %collective-permute-done.6.refs_1_ = bf16[256,2048]{1,0:T(8,128)(2,1)S(1)} collective-permute-done((bf16[256,2048]{1,0:T(8,128)(2,1)S(1)}, bf16[256,2048]{1,0:T(8,128)(2,1)S(1)}, u32[]{:S(2)}, u32[]{:S(2)}) %collective-permute-start.6) | collective-permute-done | bytes 1048608 | tf_op jit(solution)/shard_map/ppermute | solution.py:275
  82.9 0.9 collective-permute-start.15
  83.8 5.7 %input_grad_rows.7 = bf16[4,256,2048]{2,1,0:T(8,128)(2,1)} custom-call(s32[1]{0:T(128)} %bitcast.me, bf16[256,2048]{1,0:T(8,128)(2,1)S(1)} %collective-permute-done.2.refs_0_, bf16[256,2048]{1,0:T(8,128)(2,1)S(1)} %collective-permute-done.6.refs_1_, bf16[2048,2048]{1,0:T(8,128)(2,1)} %refs_2_.7, ...), custom_call_target="tpu_custom_call", output_to_operand_aliasing={{}: (4, {})} | custom-call | flops 524288 | bytes 524288 | tf_op jit(solution)/shard_map/input_grad_rows/pallas_call | solution.py:131
  89.5 0.0 collective-permute-done.12
  89.5 0.0 collective-permute-done.13
  89.5 0.0 collective-permute-done.14
  89.5 0.0 collective-permute-done.15
  89.5 0.6 add_add_fusion
  (4 shorter events, 0.1 us)
Async XLA Ops:
  0.6 12.5 %copy-start = (bf16[2048,128]{1,0:T(8,128)(2,1)S(1)}, bf16[2048,128]{1,0:T(8,128)(2,1)}, u32[]{:S(2)}) copy-start(bf16[2048,128]{1,0:T(8,128)(2,1)} %param.9) | copy-start | bytes 1572868
  0.6 28.6 %collective-permute-start = (bf16[256,2048]{1,0:T(8,128)(2,1)}, bf16[256,2048]{1,0:T(8,128)(2,1)S(1)}, u32[]{:S(2)}, u32[]{:S(2)}) collective-permute-start(bf16[256,2048]{1,0:T(8,128)(2,1)} %refs_1_.1), channel_id=1, source_target_pairs={{0,1},{1,0},{2,3},{3,2},{4,5},{5,4},{6,7},{7,6},{8,9},{9,8},{10,11... | collective-permute-start | bytes 3145736 | tf_op jit(solution)/shard_map/ppermute | solution.py:247
  3.7 26.2 %collective-permute-start.4 = (bf16[256,2048]{1,0:T(8,128)(2,1)}, bf16[256,2048]{1,0:T(8,128)(2,1)}, u32[]{:S(2)}, u32[]{:S(2)}) collective-permute-start(bf16[256,2048]{1,0:T(8,128)(2,1)} %refs_1_.1), channel_id=1, source_target_pairs={{1,2},{2,1},{5,6},{6,5},{9,10},{10,9},{13,14},{14,13},{17,18},{18,... | collective-permute-start | bytes 3145736 | tf_op jit(solution)/shard_map/ppermute | solution.py:246
  6.4 1.9 %copy-start.3 = (bf16[2048,128]{0,1:T(8,128)(2,1)}, bf16[2048,128]{0,1:T(8,128)(2,1)S(1)}, u32[]{:S(2)}) copy-start(bf16[2048,128]{0,1:T(8,128)(2,1)S(1)} %fusion.2) | copy-start | bytes 1572868
  6.4 10.1 %copy-start.1 = (bf16[256,2048]{1,0:T(8,128)(2,1)S(1)}, bf16[256,2048]{1,0:T(8,128)(2,1)}, u32[]{:S(2)}) copy-start(bf16[256,2048]{1,0:T(8,128)(2,1)} %refs_1_.1) | copy-start | bytes 3145732
  8.3 20.9 %collective-permute-start.1 = (f32[256,128]{1,0:T(8,128)S(1)}, f32[256,128]{1,0:T(8,128)S(1)}, u32[]{:S(2)}, u32[]{:S(2)}) collective-permute-start(f32[256,128]{1,0:T(8,128)S(1)} %convolution_bitcast_fusion.1.own_low), channel_id=1, source_target_pairs={{3,1},{0,2},{7,5},{4,6},{11,9},{8,10},{15,13},{12,14},{19,17},{16,... | collective-permute-start | bytes 393224 | tf_op jit(solution)/shard_map/ppermute | solution.py:253
  22.3 22.8 %copy-start.4 = (bf16[2048,128]{0,1:T(8,128)(2,1)S(1)}, bf16[2048,128]{0,1:T(8,128)(2,1)}, u32[]{:S(2)}) copy-start(bf16[2048,128]{0,1:T(8,128)(2,1)} %copy-done.3) | copy-start | bytes 1572868
  29.2 21.4 %collective-permute-start.2 = (bf16[256,2048]{1,0:T(8,128)(2,1)S(1)}, bf16[256,2048]{1,0:T(8,128)(2,1)S(1)}, u32[]{:S(2)}, u32[]{:S(2)}) collective-permute-start(bf16[256,2048]{1,0:T(8,128)(2,1)S(1)} %collective-permute-done.refs_0_.refs_1_), channel_id=1, source_target_pairs={{1,2},{2,1},{5,6},{6,5},{9,10},{10,9},{13,14},{14,13},{17,18},{18,... | collective-permute-start | bytes 3145736 | tf_op jit(solution)/shard_map/ppermute | solution.py:256
  30.0 28.7 %collective-permute-start.7 = (bf16[256,2048]{1,0:T(8,128)(2,1)}, bf16[256,2048]{1,0:T(8,128)(2,1)}, u32[]{:S(2)}, u32[]{:S(2)}) collective-permute-start(bf16[256,2048]{1,0:T(8,128)(2,1)} %collective-permute-done.4.refs_0_), channel_id=1, source_target_pairs={{1,0},{2,3},{5,4},{6,7},{9,8},{10,11},{13,12},{14,15},{17,16},{18,... | collective-permute-start | bytes 3145736 | tf_op jit(solution)/shard_map/ppermute | solution.py:257
  31.3 18.0 %collective-permute-start.3 = (f32[1024,128]{1,0:T(8,128)S(1)}, f32[1024,128]{1,0:T(8,128)S(1)}, u32[]{:S(2)}, u32[]{:S(2)}) collective-permute-start(f32[1024,128]{1,0:T(8,128)S(1)} %fusion.3.low_in), channel_id=1, source_target_pairs={{0,1},{3,2},{4,5},{7,6},{8,9},{11,10},{12,13},{15,14},{16,17},{19,... | collective-permute-start | bytes 1572872 | tf_op jit(solution)/shard_map/ppermute | solution.py:258
  50.0 0.7 collective-permute-start.5
  50.7 32.2 %collective-permute-start.6 = (bf16[256,2048]{1,0:T(8,128)(2,1)S(1)}, bf16[256,2048]{1,0:T(8,128)(2,1)S(1)}, u32[]{:S(2)}, u32[]{:S(2)}) collective-permute-start(bf16[256,2048]{1,0:T(8,128)(2,1)S(1)} %collective-permute-done.2.refs_0_), channel_id=1, source_target_pairs={{1,0},{2,3},{5,4},{6,7},{9,8},{10,11},{13,12},{14,15},{17,16},{18,... | collective-permute-start | bytes 3145736 | tf_op jit(solution)/shard_map/ppermute | solution.py:275
  58.7 6.6 %collective-permute-start.8 = (f32[1,32,64]{2,1,0:T(8,128)S(1)}, f32[1,32,64]{2,1,0:T(8,128)S(1)}, u32[]{:S(2)}, u32[]{:S(2)}) collective-permute-start(f32[1,32,64]{2,1,0:T(8,128)S(1)} %dynamic-slice_bitcast_fusion), channel_id=1, source_target_pairs={{2,0},{1,3},{6,4},{5,7},{10,8},{9,11},{14,12},{13,15},{18,16},{17,... | collective-permute-start | bytes 24584 | tf_op jit(solution)/shard_map/ppermute | solution.py:278
  65.4 9.0 %collective-permute-start.10 = (f32[1,2048]{1,0:T(1,128)S(1)}, f32[1,2048]{1,0:T(1,128)S(1)}, u32[]{:S(2)}, u32[]{:S(2)}) collective-permute-start(f32[1,2048]{1,0:T(1,128)S(1)} %reshape.23.refs_0_), channel_id=1, source_target_pairs={{0,8},{4,12},{8,0},{12,4},{1,9},{5,13},{9,1},{13,5},{2,10},{6,14},... | collective-permute-start | bytes 24584 | tf_op jit(solution)/shard_map/ppermute | solution.py:305
  66.9 7.5 %collective-permute-start.11 = (f32[1,2048]{1,0:T(1,128)S(1)}, f32[1,2048]{1,0:T(1,128)S(1)}, u32[]{:S(2)}, u32[]{:S(2)}) collective-permute-start(f32[1,2048]{1,0:T(1,128)S(1)} %reshape.23.refs_0_), channel_id=1, source_target_pairs={{0,12},{4,0},{8,4},{12,8},{1,13},{5,1},{9,5},{13,9},{2,14},{6,2},{... | collective-permute-start | bytes 24584 | tf_op jit(solution)/shard_map/ppermute | solution.py:305
  66.9 7.5 %collective-permute-start.9 = (f32[1,2048]{1,0:T(1,128)S(1)}, f32[1,2048]{1,0:T(1,128)S(1)}, u32[]{:S(2)}, u32[]{:S(2)}) collective-permute-start(f32[1,2048]{1,0:T(1,128)S(1)} %reshape.23.refs_0_), channel_id=1, source_target_pairs={{0,4},{4,8},{8,12},{12,0},{1,5},{5,9},{9,13},{13,1},{2,6},{6,10},{... | collective-permute-start | bytes 24584 | tf_op jit(solution)/shard_map/ppermute | solution.py:305
  67.4 7.0 %copy-start.2 = (bf16[512,2048]{1,0:T(8,128)(2,1)S(1)}, bf16[512,2048]{1,0:T(8,128)(2,1)}, u32[]{:S(2)}) copy-start(bf16[512,2048]{1,0:T(8,128)(2,1)} %refs_4_.1) | copy-start | bytes 6291460
  76.2 13.2 %collective-permute-start.12 = (f32[1,512]{1,0:T(1,128)S(1)}, f32[1,512]{1,0:T(1,128)S(1)}, u32[]{:S(2)}, u32[]{:S(2)}) collective-permute-start(f32[1,512]{1,0:T(1,128)S(1)} %get-tuple-element.37), channel_id=1, source_target_pairs={{0,0},{1,4},{2,8},{3,12},{4,1},{5,5},{6,9},{7,13},{8,2},{9,6},{10,... | collective-permute-start | bytes 6152 | tf_op jit(solution)/shard_map/ppermute | solution.py:315
  76.9 12.6 %collective-permute-start.13 = (f32[1,512]{1,0:T(1,128)S(1)}, f32[1,512]{1,0:T(1,128)S(1)}, u32[]{:S(2)}, u32[]{:S(2)}) collective-permute-start(f32[1,512]{1,0:T(1,128)S(1)} %get-tuple-element.38), channel_id=1, source_target_pairs={{0,4},{1,8},{2,12},{3,0},{4,5},{5,9},{6,13},{7,1},{8,6},{9,10},{10... | collective-permute-start | bytes 6152 | tf_op jit(solution)/shard_map/ppermute | solution.py:315
  78.4 11.1 %collective-permute-start.14 = (f32[1,512]{1,0:T(1,128)S(1)}, f32[1,512]{1,0:T(1,128)S(1)}, u32[]{:S(2)}, u32[]{:S(2)}) collective-permute-start(f32[1,512]{1,0:T(1,128)S(1)} %get-tuple-element.39), channel_id=1, source_target_pairs={{0,8},{1,12},{2,0},{3,4},{4,9},{5,13},{6,1},{7,5},{8,10},{9,14},{1... | collective-permute-start | bytes 6152 | tf_op jit(solution)/shard_map/ppermute | solution.py:315
  82.9 6.6 %collective-permute-start.15 = (f32[1,512]{1,0:T(1,128)S(1)}, f32[1,512]{1,0:T(1,128)S(1)}, u32[]{:S(2)}, u32[]{:S(2)}) collective-permute-start(f32[1,512]{1,0:T(1,128)S(1)} %get-tuple-element.41), channel_id=1, source_target_pairs={{0,12},{1,0},{2,4},{3,8},{4,13},{5,1},{6,5},{7,9},{8,14},{9,2},{10... | collective-permute-start | bytes 6152 | tf_op jit(solution)/shard_map/ppermute | solution.py:315

commit v18 on v16

--- a/solution.py
+++ b/solution.py
@@ -260,7 +260,7 @@
     beside_low = low_rank(beside)
     facing_low = low_rank(facing)
 
-    beside_across, output = tied((beside_across, output))
+    beside_across, facing_low, output = tied((beside_across, facing_low, output))
     third = lax.ppermute(beside_across, "mp", outward)
 
     far_low = low_rank(beside_across)

time: 93.3 us -> 94.8 us (1.016)
  Pallas kernels: 26 us -> 27.8 us
    pallas_call x4, Pallas kernels: 23.5 us -> 25.3 us  [put_rows(): pl.pallas_call(functools.partial(rows_kernel, block, start, count), in_sp...]
  transfers between devices with their start and end apart: 15 -> 15, of which waited for: 6 -> 6; matrix products, arithmetic and copies ran while one was open for 5% -> 5% of each run, Pallas kernels for 28% -> 29%
where the time goes in v18:
time: 94.8 us; the launch traced here: 94.4 us
  starting transfers between devices  29.2 us (31%)
  waiting for transfers between devices  28.8 us (30%)
  Pallas kernels  27.8 us (29%)
  matrix products  4.21 us (4%)
  local copies, waits for them, and re-layouts  2.95 us (3%)
    pallas_call x4, Pallas kernels, put_rows(): pl.pallas_call(functools.partial(rows_kernel, block, start, count), in_sp...  25.3 us
    ppermute x1, waiting for transfers between devices, line_of_four(): beside = lax.ppermute(grad_kv, 'mp', exchange_pairs)  13.7 us
    ppermute x4, starting transfers between devices, on_device(): scores = scores + lax.ppermute(rows[step], ('dp', 'mp'), pairs)  9.77 us
    ppermute x1, waiting for transfers between devices, line_of_four(): second = lax.ppermute(facing, 'mp', outward)  8.38 us
    ppermute x1, starting transfers between devices, line_of_four(): low_in_beside = lax.ppermute(low_in, 'mp', inward)  7.41 us
    ppermute x1, waiting for transfers between devices, line_of_four(): mine = lax.ppermute(take(slabs, me ^ 2), 'mp', [(2, 0), (1, 3)])  3.74 us
    ppermute x1, starting transfers between devices, line_of_four(): beside = lax.ppermute(grad_kv, 'mp', exchange_pairs)  3.09 us
    dot_general x4, matrix products, low_rank(): return jnp.dot(rows, proj_both, preferred_element_type=jnp.float32)  2.96 us
  transfers between devices with their start and end apart: 15, of which 6 were waited for; matrix products, arithmetic and copies ran while one was open for 5% of the time, Pallas kernels for 29%

profile of v18, /device:TPU:0, one launch (start us, length us, event | category | flops | bytes accessed | tf_op | source)
XLA Modules:
  0.0 94.4 jit_solution(16966056597005059085)
XLA Ops:
  0.6 0.0 copy-start
  0.6 3.1 %collective-permute-start = (bf16[256,2048]{1,0:T(8,128)(2,1)}, bf16[256,2048]{1,0:T(8,128)(2,1)S(1)}, u32[]{:S(2)}, u32[]{:S(2)}) collective-permute-start(bf16[256,2048]{1,0:T(8,128)(2,1)} %refs_1_.1), channel_id=1, source_target_pairs={{0,1},{1,0},{2,3},{3,2},{4,5},{5,4},{6,7},{7,6},{8,9},{9,8},{10,11... | collective-permute-start | bytes 3145736 | tf_op jit(solution)/shard_map/ppermute | solution.py:247
  3.7 1.6 %collective-permute-start.2 = (bf16[256,2048]{1,0:T(8,128)(2,1)}, bf16[256,2048]{1,0:T(8,128)(2,1)}, u32[]{:S(2)}, u32[]{:S(2)}) collective-permute-start(bf16[256,2048]{1,0:T(8,128)(2,1)} %refs_1_.1), channel_id=1, source_target_pairs={{1,2},{2,1},{5,6},{6,5},{9,10},{10,9},{13,14},{14,13},{17,18},{18,... | collective-permute-start | bytes 3145736 | tf_op jit(solution)/shard_map/ppermute | solution.py:246
  5.4 0.0 copy-start.1
  5.4 1.2 %copy-done.1 = bf16[256,2048]{1,0:T(8,128)(2,1)S(1)} copy-done((bf16[256,2048]{1,0:T(8,128)(2,1)S(1)}, bf16[256,2048]{1,0:T(8,128)(2,1)}, u32[]{:S(2)}) %copy-start.1) | copy-done | bytes 1048600
  6.6 0.0 copy-start.3
  6.6 5.5 %input_grad_rows.4.refs_3_ = bf16[4,256,2048]{2,1,0:T(8,128)(2,1)} custom-call(s32[1]{0:T(128)} %bitcast.me, bf16[256,2048]{1,0:T(8,128)(2,1)S(1)} %copy-done.1, bf16[256,2048]{1,0:T(8,128)(2,1)S(1)} %copy-done.1, bf16[2048,2048]{1,0:T(8,128)(2,1)} %refs_2_.7), custom_call_target="tpu_custom_call" | custom-call | flops 524288 | bytes 524288 | tf_op jit(solution)/shard_map/input_grad_rows/pallas_call | solution.py:131
  12.1 0.0 copy-done
  12.2 0.0 copy-done.3
  12.2 0.0 copy-start.4
  12.2 1.3 %fusion.3.low_in = f32[1024,128]{1,0:T(8,128)S(1)} fusion(bf16[1024,2048]{1,0:T(8,128)(2,1)S(1)} %copy-done.3, bf16[2048,128]{1,0:T(8,128)(2,1)S(1)} %copy-done), kind=kOutput, calls=%fused_computation.13 | convolution fusion | flops 536870912 | bytes 5242880 | tf_op jit(solution)/shard_map/dot_general | solution.py:250
  13.4 13.7 %collective-permute-done.refs_0_.refs_1_ = bf16[256,2048]{1,0:T(8,128)(2,1)S(1)} collective-permute-done((bf16[256,2048]{1,0:T(8,128)(2,1)}, bf16[256,2048]{1,0:T(8,128)(2,1)S(1)}, u32[]{:S(2)}, u32[]{:S(2)}) %collective-permute-start) | collective-permute-done | bytes 1048608 | tf_op jit(solution)/shard_map/ppermute | solution.py:247
  27.1 0.7 collective-permute-start.1
  27.8 0.0 copy-done.4
  27.9 0.0 collective-permute-done.2.refs_0_
  27.9 1.3 %collective-permute-start.6 = (bf16[256,2048]{1,0:T(8,128)(2,1)}, bf16[256,2048]{1,0:T(8,128)(2,1)}, u32[]{:S(2)}, u32[]{:S(2)}) collective-permute-start(bf16[256,2048]{1,0:T(8,128)(2,1)} %collective-permute-done.2.refs_0_), channel_id=1, source_target_pairs={{1,0},{2,3},{5,4},{6,7},{9,8},{10,11},{13,12},{14,15},{17,16},{18,... | collective-permute-start | bytes 3145736 | tf_op jit(solution)/shard_map/ppermute | solution.py:256
  29.2 0.4 convolution_bitcast_fusion.own_low
  29.7 7.4 %collective-permute-start.4 = (f32[1024,128]{1,0:T(8,128)S(1)}, f32[1024,128]{1,0:T(8,128)S(1)}, u32[]{:S(2)}, u32[]{:S(2)}) collective-permute-start(f32[1024,128]{1,0:T(8,128)S(1)} %fusion.3.low_in), channel_id=1, source_target_pairs={{0,1},{3,2},{4,5},{7,6},{8,9},{11,10},{12,13},{15,14},{16,17},{19,... | collective-permute-start | bytes 1572872 | tf_op jit(solution)/shard_map/ppermute | solution.py:257
  37.1 5.4 %input_grad_rows.5.refs_3_ = bf16[4,256,2048]{2,1,0:T(8,128)(2,1)} custom-call(s32[1]{0:T(128)} %bitcast.me, bf16[256,2048]{1,0:T(8,128)(2,1)S(1)} %collective-permute-done.refs_0_.refs_1_, bf16[256,2048]{1,0:T(8,128)(2,1)S(1)} %collective-permute-done.refs_0_.refs_1_, bf16[2048,2048]{1,0:T(8,128)(2,1)} %refs_2_.7, ...), custom_call_target="tpu_custom_call", output_to_operand_aliasing={{}: (4, {})} | custom-call | flops 524288 | bytes 524288 | tf_op jit(solution)/shard_map/input_grad_rows/pallas_call | solution.py:131
  42.5 1.7 %convolution_bitcast_fusion.1.facing_low = f32[256,128]{1,0:T(8,128)S(1)} fusion(bf16[2048,128]{0,1:T(8,128)(2,1)S(1)} %fusion.2, bf16[256,2048]{1,0:T(8,128)(2,1)} %collective-permute-done.2.refs_0_), kind=kOutput, calls=%fused_computation.1 | convolution fusion | flops 134217728 | bytes 1703936 | tf_op jit(solution)/shard_map/dot_general | solution.py:244
  44.1 0.0 collective-permute-done.1.refs_0_
  44.2 1.3 %collective-permute-start.3 = (bf16[256,2048]{1,0:T(8,128)(2,1)S(1)}, bf16[256,2048]{1,0:T(8,128)(2,1)}, u32[]{:S(2)}, u32[]{:S(2)}) collective-permute-start(bf16[256,2048]{1,0:T(8,128)(2,1)S(1)} %collective-permute-done.1.refs_0_), channel_id=1, source_target_pairs={{1,0},{2,3},{5,4},{6,7},{9,8},{10,11},{13,12},{14,15},{17,16},{18,... | collective-permute-start | bytes 3145736 | tf_op jit(solution)/shard_map/ppermute | solution.py:264
  45.5 0.4 fusion.4.beside_low
  45.9 0.4 fusion.5.far_low
  46.3 0.8 collective-permute-done.4.low_in_beside
  47.2 0.7 token_sums.1
  47.9 0.7 collective-permute-start.5
  48.6 8.4 %collective-permute-done.6.refs_1_ = bf16[256,2048]{1,0:T(8,128)(2,1)} collective-permute-done((bf16[256,2048]{1,0:T(8,128)(2,1)}, bf16[256,2048]{1,0:T(8,128)(2,1)}, u32[]{:S(2)}, u32[]{:S(2)}) %collective-permute-start.6) | collective-permute-done | bytes 1048608 | tf_op jit(solution)/shard_map/ppermute | solution.py:256
  56.9 0.0 collective-permute-done.5
  57.0 1.3 %collective-permute-start.7 = (f32[1,32,64]{2,1,0:T(8,128)S(1)}, f32[1,32,64]{2,1,0:T(8,128)S(1)}, u32[]{:S(2)}, u32[]{:S(2)}) collective-permute-start(f32[1,32,64]{2,1,0:T(8,128)S(1)} %dynamic-slice_bitcast_fusion), channel_id=1, source_target_pairs={{2,0},{1,3},{6,4},{5,7},{10,8},{9,11},{14,12},{13,15},{18,16},{17,... | collective-permute-start | bytes 24584 | tf_op jit(solution)/shard_map/ppermute | solution.py:278
  58.3 7.2 %input_grad_rows.6.refs_3_ = bf16[4,256,2048]{2,1,0:T(8,128)(2,1)} custom-call(s32[1]{0:T(128)} %bitcast.me, bf16[256,2048]{1,0:T(8,128)(2,1)} %collective-permute-done.2.refs_0_, bf16[256,2048]{1,0:T(8,128)(2,1)} %collective-permute-done.6.refs_1_, bf16[2048,2048]{1,0:T(8,128)(2,1)} %refs_2_.7, ...), custom_call_target="tpu_custom_call", output_to_operand_aliasing={{}: (4, {})} | custom-call | flops 524288 | bytes 524288 | tf_op jit(solution)/shard_map/input_grad_rows/pallas_call | solution.py:131
  65.5 3.7 %collective-permute-done.7 = f32[1,32,64]{2,1,0:T(8,128)S(1)} collective-permute-done((f32[1,32,64]{2,1,0:T(8,128)S(1)}, f32[1,32,64]{2,1,0:T(8,128)S(1)}, u32[]{:S(2)}, u32[]{:S(2)}) %collective-permute-start.7) | collective-permute-done | bytes 8224 | tf_op jit(solution)/shard_map/ppermute | solution.py:278
  69.2 0.1 reshape.23.refs_0_
  69.3 0.0 collective-permute-start.10
  69.3 0.5 collective-permute-start.8
  69.8 1.5 %collective-permute-start.9 = (f32[1,2048]{1,0:T(1,128)S(1)}, f32[1,2048]{1,0:T(1,128)S(1)}, u32[]{:S(2)}, u32[]{:S(2)}) collective-permute-start(f32[1,2048]{1,0:T(1,128)S(1)} %reshape.23.refs_0_), channel_id=1, source_target_pairs={{0,8},{4,12},{8,0},{12,4},{1,9},{5,13},{9,1},{13,5},{2,10},{6,14},... | collective-permute-start | bytes 24584 | tf_op jit(solution)/shard_map/ppermute | solution.py:306
  71.3 0.0 collective-permute-done.10.refs_3_
  71.3 1.3 %collective-permute-done.8.refs_1_ = f32[1,2048]{1,0:T(1,128)S(1)} collective-permute-done((f32[1,2048]{1,0:T(1,128)S(1)}, f32[1,2048]{1,0:T(1,128)S(1)}, u32[]{:S(2)}, u32[]{:S(2)}) %collective-permute-start.8) | collective-permute-done | bytes 8224 | tf_op jit(solution)/shard_map/ppermute | solution.py:306
  72.6 0.8 collective-permute-done.9.refs_2_
  73.5 0.0 copy-start.2
  73.5 1.6 %copy-done.2 = bf16[512,2048]{1,0:T(8,128)(2,1)S(1)} copy-done((bf16[512,2048]{1,0:T(8,128)(2,1)S(1)}, bf16[512,2048]{1,0:T(8,128)(2,1)}, u32[]{:S(2)}) %copy-start.2) | copy-done | bytes 2097176
  75.1 1.7 %scores.1 = (f32[1,512]{1,0:T(1,128)S(1)}, f32[1,512]{1,0:T(1,128)S(1)}, f32[1,512]{1,0:T(1,128)S(1)}, f32[1,512]{1,0:T(1,128)S(1)}) custom-call(s32[1]{0:T(128)} %bitcast.9.first, f32[1,2048]{1,0:T(1,128)S(1)} %reshape.23.refs_0_, f32[1,2048]{1,0:T(1,128)S(1)} %collective-permute-done.8.refs_1_, f32[1,2048]{1,0:T(1,128)S(1)} %collective-permute-done.9.refs_2_, ...), custom_call_target="tpu_custom_call" | custom-call | tf_op jit(solution)/shard_map/scores/pallas_call | solution.py:43
  76.8 0.7 collective-permute-start.11
  77.5 5.4 %collective-permute-start.12 = (f32[1,512]{1,0:T(1,128)S(1)}, f32[1,512]{1,0:T(1,128)S(1)}, u32[]{:S(2)}, u32[]{:S(2)}) collective-permute-start(f32[1,512]{1,0:T(1,128)S(1)} %get-tuple-element.36), channel_id=1, source_target_pairs={{0,4},{1,8},{2,12},{3,0},{4,5},{5,9},{6,13},{7,1},{8,6},{9,10},{10... | collective-permute-start | bytes 6152 | tf_op jit(solution)/shard_map/ppermute | solution.py:316
  82.9 3.5 %collective-permute-start.13 = (f32[1,512]{1,0:T(1,128)S(1)}, f32[1,512]{1,0:T(1,128)S(1)}, u32[]{:S(2)}, u32[]{:S(2)}) collective-permute-start(f32[1,512]{1,0:T(1,128)S(1)} %get-tuple-element.37), channel_id=1, source_target_pairs={{0,8},{1,12},{2,0},{3,4},{4,9},{5,13},{6,1},{7,5},{8,10},{9,14},{1... | collective-permute-start | bytes 6152 | tf_op jit(solution)/shard_map/ppermute | solution.py:316
  86.3 0.0 collective-permute-done.3.refs_1_
  86.3 0.3 collective-permute-start.14
  86.6 7.2 %input_grad_rows.7 = bf16[4,256,2048]{2,1,0:T(8,128)(2,1)} custom-call(s32[1]{0:T(128)} %bitcast.me, bf16[256,2048]{1,0:T(8,128)(2,1)S(1)} %collective-permute-done.1.refs_0_, bf16[256,2048]{1,0:T(8,128)(2,1)} %collective-permute-done.3.refs_1_, bf16[2048,2048]{1,0:T(8,128)(2,1)} %refs_2_.7, ...), custom_call_target="tpu_custom_call", output_to_operand_aliasing={{}: (4, {})} | custom-call | flops 524288 | bytes 524288 | tf_op jit(solution)/shard_map/input_grad_rows/pallas_call | solution.py:131
  93.8 0.0 collective-permute-done.11
  93.8 0.0 collective-permute-done.12
  93.8 0.0 collective-permute-done.13
  93.8 0.0 collective-permute-done.14
  93.8 0.6 add_add_fusion
  (5 shorter events, 0.1 us)
Async XLA Ops:
  0.6 11.5 %copy-start = (bf16[2048,128]{1,0:T(8,128)(2,1)S(1)}, bf16[2048,128]{1,0:T(8,128)(2,1)}, u32[]{:S(2)}) copy-start(bf16[2048,128]{1,0:T(8,128)(2,1)} %param.9) | copy-start | bytes 1572868
  0.6 26.5 %collective-permute-start = (bf16[256,2048]{1,0:T(8,128)(2,1)}, bf16[256,2048]{1,0:T(8,128)(2,1)S(1)}, u32[]{:S(2)}, u32[]{:S(2)}) collective-permute-start(bf16[256,2048]{1,0:T(8,128)(2,1)} %refs_1_.1), channel_id=1, source_target_pairs={{0,1},{1,0},{2,3},{3,2},{4,5},{5,4},{6,7},{7,6},{8,9},{9,8},{10,11... | collective-permute-start | bytes 3145736 | tf_op jit(solution)/shard_map/ppermute | solution.py:247
  3.7 24.2 %collective-permute-start.2 = (bf16[256,2048]{1,0:T(8,128)(2,1)}, bf16[256,2048]{1,0:T(8,128)(2,1)}, u32[]{:S(2)}, u32[]{:S(2)}) collective-permute-start(bf16[256,2048]{1,0:T(8,128)(2,1)} %refs_1_.1), channel_id=1, source_target_pairs={{1,2},{2,1},{5,6},{6,5},{9,10},{10,9},{13,14},{14,13},{17,18},{18,... | collective-permute-start | bytes 3145736 | tf_op jit(solution)/shard_map/ppermute | solution.py:246
  5.4 1.2 %copy-start.1 = (bf16[256,2048]{1,0:T(8,128)(2,1)S(1)}, bf16[256,2048]{1,0:T(8,128)(2,1)}, u32[]{:S(2)}) copy-start(bf16[256,2048]{1,0:T(8,128)(2,1)} %refs_1_.1) | copy-start | bytes 3145732
  6.6 5.6 %copy-start.3 = (bf16[1024,2048]{1,0:T(8,128)(2,1)S(1)}, bf16[1024,2048]{1,0:T(8,128)(2,1)}, u32[]{:S(2)}) copy-start(bf16[1024,2048]{1,0:T(8,128)(2,1)} %param.6) | copy-start | bytes 12582916
  12.2 15.7 %copy-start.4 = (bf16[2,1024,64]{1,2,0:T(8,128)(2,1)S(1)}, bf16[2,1024,64]{1,2,0:T(8,128)(2,1)}, u32[]{:S(2)}) copy-start(bf16[2,1024,64]{1,2,0:T(8,128)(2,1)} %param.10) | copy-start | bytes 786436
  27.1 17.0 %collective-permute-start.1 = (bf16[256,2048]{1,0:T(8,128)(2,1)S(1)}, bf16[256,2048]{1,0:T(8,128)(2,1)S(1)}, u32[]{:S(2)}, u32[]{:S(2)}) collective-permute-start(bf16[256,2048]{1,0:T(8,128)(2,1)S(1)} %collective-permute-done.refs_0_.refs_1_), channel_id=1, source_target_pairs={{1,2},{2,1},{5,6},{6,5},{9,10},{10,9},{13,14},{14,13},{17,18},{18,... | collective-permute-start | bytes 3145736 | tf_op jit(solution)/shard_map/ppermute | solution.py:255
  27.9 29.0 %collective-permute-start.6 = (bf16[256,2048]{1,0:T(8,128)(2,1)}, bf16[256,2048]{1,0:T(8,128)(2,1)}, u32[]{:S(2)}, u32[]{:S(2)}) collective-permute-start(bf16[256,2048]{1,0:T(8,128)(2,1)} %collective-permute-done.2.refs_0_), channel_id=1, source_target_pairs={{1,0},{2,3},{5,4},{6,7},{9,8},{10,11},{13,12},{14,15},{17,16},{18,... | collective-permute-start | bytes 3145736 | tf_op jit(solution)/shard_map/ppermute | solution.py:256
  29.7 17.5 %collective-permute-start.4 = (f32[1024,128]{1,0:T(8,128)S(1)}, f32[1024,128]{1,0:T(8,128)S(1)}, u32[]{:S(2)}, u32[]{:S(2)}) collective-permute-start(f32[1024,128]{1,0:T(8,128)S(1)} %fusion.3.low_in), channel_id=1, source_target_pairs={{0,1},{3,2},{4,5},{7,6},{8,9},{11,10},{12,13},{15,14},{16,17},{19,... | collective-permute-start | bytes 1572872 | tf_op jit(solution)/shard_map/ppermute | solution.py:257
  44.2 42.2 %collective-permute-start.3 = (bf16[256,2048]{1,0:T(8,128)(2,1)S(1)}, bf16[256,2048]{1,0:T(8,128)(2,1)}, u32[]{:S(2)}, u32[]{:S(2)}) collective-permute-start(bf16[256,2048]{1,0:T(8,128)(2,1)S(1)} %collective-permute-done.1.refs_0_), channel_id=1, source_target_pairs={{1,0},{2,3},{5,4},{6,7},{9,8},{10,11},{13,12},{14,15},{17,16},{18,... | collective-permute-start | bytes 3145736 | tf_op jit(solution)/shard_map/ppermute | solution.py:264
  47.9 9.1 %collective-permute-start.5 = (f32[4,1,32,64]{3,2,0,1:T(8,128)S(1)}, f32[4,1,32,64]{3,2,0,1:T(8,128)S(1)}, u32[]{:S(2)}, u32[]{:S(2)}) collective-permute-start(f32[4,1,32,64]{3,2,0,1:T(8,128)S(1)} %bitcast.27), channel_id=1, source_target_pairs={{1,2},{2,1},{5,6},{6,5},{9,10},{10,9},{13,14},{14,13},{17,18},{18,... | collective-permute-start | bytes 98312 | tf_op jit(solution)/shard_map/ppermute | solution.py:275
  57.0 12.3 %collective-permute-start.7 = (f32[1,32,64]{2,1,0:T(8,128)S(1)}, f32[1,32,64]{2,1,0:T(8,128)S(1)}, u32[]{:S(2)}, u32[]{:S(2)}) collective-permute-start(f32[1,32,64]{2,1,0:T(8,128)S(1)} %dynamic-slice_bitcast_fusion), channel_id=1, source_target_pairs={{2,0},{1,3},{6,4},{5,7},{10,8},{9,11},{14,12},{13,15},{18,16},{17,... | collective-permute-start | bytes 24584 | tf_op jit(solution)/shard_map/ppermute | solution.py:278
  69.3 2.0 %collective-permute-start.10 = (f32[1,2048]{1,0:T(1,128)S(1)}, f32[1,2048]{1,0:T(1,128)S(1)}, u32[]{:S(2)}, u32[]{:S(2)}) collective-permute-start(f32[1,2048]{1,0:T(1,128)S(1)} %reshape.23.refs_0_), channel_id=1, source_target_pairs={{0,12},{4,0},{8,4},{12,8},{1,13},{5,1},{9,5},{13,9},{2,14},{6,2},{... | collective-permute-start | bytes 24584 | tf_op jit(solution)/shard_map/ppermute | solution.py:306
  69.3 3.3 %collective-permute-start.8 = (f32[1,2048]{1,0:T(1,128)S(1)}, f32[1,2048]{1,0:T(1,128)S(1)}, u32[]{:S(2)}, u32[]{:S(2)}) collective-permute-start(f32[1,2048]{1,0:T(1,128)S(1)} %reshape.23.refs_0_), channel_id=1, source_target_pairs={{0,4},{4,8},{8,12},{12,0},{1,5},{5,9},{9,13},{13,1},{2,6},{6,10},{... | collective-permute-start | bytes 24584 | tf_op jit(solution)/shard_map/ppermute | solution.py:306
  69.8 3.7 %collective-permute-start.9 = (f32[1,2048]{1,0:T(1,128)S(1)}, f32[1,2048]{1,0:T(1,128)S(1)}, u32[]{:S(2)}, u32[]{:S(2)}) collective-permute-start(f32[1,2048]{1,0:T(1,128)S(1)} %reshape.23.refs_0_), channel_id=1, source_target_pairs={{0,8},{4,12},{8,0},{12,4},{1,9},{5,13},{9,1},{13,5},{2,10},{6,14},... | collective-permute-start | bytes 24584 | tf_op jit(solution)/shard_map/ppermute | solution.py:306
  73.5 1.6 %copy-start.2 = (bf16[512,2048]{1,0:T(8,128)(2,1)S(1)}, bf16[512,2048]{1,0:T(8,128)(2,1)}, u32[]{:S(2)}) copy-start(bf16[512,2048]{1,0:T(8,128)(2,1)} %refs_4_.1) | copy-start | bytes 6291460
  76.8 17.0 %collective-permute-start.11 = (f32[1,512]{1,0:T(1,128)S(1)}, f32[1,512]{1,0:T(1,128)S(1)}, u32[]{:S(2)}, u32[]{:S(2)}) collective-permute-start(f32[1,512]{1,0:T(1,128)S(1)} %get-tuple-element.35), channel_id=1, source_target_pairs={{0,0},{1,4},{2,8},{3,12},{4,1},{5,5},{6,9},{7,13},{8,2},{9,6},{10,... | collective-permute-start | bytes 6152 | tf_op jit(solution)/shard_map/ppermute | solution.py:316
  77.5 16.3 %collective-permute-start.12 = (f32[1,512]{1,0:T(1,128)S(1)}, f32[1,512]{1,0:T(1,128)S(1)}, u32[]{:S(2)}, u32[]{:S(2)}) collective-permute-start(f32[1,512]{1,0:T(1,128)S(1)} %get-tuple-element.36), channel_id=1, source_target_pairs={{0,4},{1,8},{2,12},{3,0},{4,5},{5,9},{6,13},{7,1},{8,6},{9,10},{10... | collective-permute-start | bytes 6152 | tf_op jit(solution)/shard_map/ppermute | solution.py:316
  82.9 11.0 %collective-permute-start.13 = (f32[1,512]{1,0:T(1,128)S(1)}, f32[1,512]{1,0:T(1,128)S(1)}, u32[]{:S(2)}, u32[]{:S(2)}) collective-permute-start(f32[1,512]{1,0:T(1,128)S(1)} %get-tuple-element.37), channel_id=1, source_target_pairs={{0,8},{1,12},{2,0},{3,4},{4,9},{5,13},{6,1},{7,5},{8,10},{9,14},{1... | collective-permute-start | bytes 6152 | tf_op jit(solution)/shard_map/ppermute | solution.py:316
  86.3 7.5 %collective-permute-start.14 = (f32[1,512]{1,0:T(1,128)S(1)}, f32[1,512]{1,0:T(1,128)S(1)}, u32[]{:S(2)}, u32[]{:S(2)}) collective-permute-start(f32[1,512]{1,0:T(1,128)S(1)} %get-tuple-element.39), channel_id=1, source_target_pairs={{0,12},{1,0},{2,4},{3,8},{4,13},{5,1},{6,5},{7,9},{8,14},{9,2},{10... | collective-permute-start | bytes 6152 | tf_op jit(solution)/shard_map/ppermute | solution.py:316

commit v19 on v17

--- a/solution.py
+++ b/solution.py
@@ -70,7 +70,7 @@
 
 
 FETCH = 256
-TILE = 1024
+TILE = 512
 GRANT = 48 * 2**20
 
 

time: 90.6 us -> 90.8 us (level)
  transfers between devices with their start and end apart: 16 -> 16, of which waited for: 5 -> 5; matrix products, arithmetic and copies ran while one was open for 9% -> 9% of each run, Pallas kernels for 30% -> 29%
where the time goes in v19:
time: 90.8 us; the launch traced here: 90.3 us
  starting transfers between devices  30.5 us (34%)
  Pallas kernels  26 us (29%)
  waiting for transfers between devices  23.8 us (26%)
  matrix products  7.38 us (8%)
  local copies, waits for them, and re-layouts  1.11 us (1%)
  between operations  0.96 us (1%)
    pallas_call x4, Pallas kernels, put_rows(): pl.pallas_call(functools.partial(rows_kernel, block, start, count), in_sp...  23.5 us
    ppermute x1, starting transfers between devices, line_of_four(): low_in_beside = lax.ppermute(low_in, 'mp', inward)  8.08 us
    ppermute x1, waiting for transfers between devices, line_of_four(): far_low = lax.ppermute(own_low, 'mp', [(3, 1), (0, 2)])  7.25 us
    ppermute x1, waiting for transfers between devices, line_of_four(): second = lax.ppermute(facing, 'mp', outward)  6.68 us
    ppermute x4, starting transfers between devices, on_device(): scores = scores + lax.ppermute(rows[step], ('dp', 'mp'), pairs)  5.59 us
    ppermute x1, waiting for transfers between devices, line_of_four(): mine = lax.ppermute(take(slabs, me ^ 2), 'mp', [(2, 0), (1, 3)])  5.33 us
    ppermute x1, starting transfers between devices, line_of_four(): far_low = lax.ppermute(own_low, 'mp', [(3, 1), (0, 2)])  4.76 us
    dot_general x3, matrix products, low_rank(): return jnp.dot(rows, proj_both, preferred_element_type=jnp.float32)  3.95 us
  transfers between devices with their start and end apart: 16, of which 5 were waited for; matrix products, arithmetic and copies ran while one was open for 9% of the time, Pallas kernels for 29%

profile of v19, /device:TPU:0, one launch (start us, length us, event | category | flops | bytes accessed | tf_op | source)
XLA Modules:
  0.0 90.3 jit_solution(10949798074256497858)
XLA Ops:
  0.6 0.0 copy-start
  0.6 3.1 %collective-permute-start = (bf16[256,2048]{1,0:T(8,128)(2,1)}, bf16[256,2048]{1,0:T(8,128)(2,1)S(1)}, u32[]{:S(2)}, u32[]{:S(2)}) collective-permute-start(bf16[256,2048]{1,0:T(8,128)(2,1)} %refs_1_.1), channel_id=1, source_target_pairs={{0,1},{1,0},{2,3},{3,2},{4,5},{5,4},{6,7},{7,6},{8,9},{9,8},{10,11... | collective-permute-start | bytes 3145736 | tf_op jit(solution)/shard_map/ppermute | solution.py:247
  3.7 1.7 %collective-permute-start.4 = (bf16[256,2048]{1,0:T(8,128)(2,1)}, bf16[256,2048]{1,0:T(8,128)(2,1)}, u32[]{:S(2)}, u32[]{:S(2)}) collective-permute-start(bf16[256,2048]{1,0:T(8,128)(2,1)} %refs_1_.1), channel_id=1, source_target_pairs={{1,2},{2,1},{5,6},{6,5},{9,10},{10,9},{13,14},{14,13},{17,18},{18,... | collective-permute-start | bytes 3145736 | tf_op jit(solution)/shard_map/ppermute | solution.py:246
  5.4 1.0 %slice_bitcast_fusion.1 = (bf16[1024,64]{0,1:T(8,128)(2,1)S(1)}, bf16[1024,64]{0,1:T(8,128)(2,1)S(1)}) fusion(bf16[2,1024,64]{1,2,0:T(8,128)(2,1)} %param.10), kind=kLoop, calls=%fused_computation.8 | loop fusion | bytes 524288 | tf_op jit(solution)/shard_map/squeeze | solution.py:59
  6.4 0.0 copy-start.3
  6.4 0.0 copy-start.1
  6.4 1.9 %convolution_bitcast_fusion.1.own_low = f32[256,128]{1,0:T(8,128)S(1)} fusion(bf16[2048,128]{0,1:T(8,128)(2,1)S(1)} %fusion.2, bf16[256,2048]{1,0:T(8,128)(2,1)} %refs_1_.1), kind=kOutput, calls=%fused_computation.1 | convolution fusion | flops 134217728 | bytes 1703936 | tf_op jit(solution)/shard_map/dot_general | solution.py:244
  8.3 0.0 copy-done.3
  8.3 4.8 %collective-permute-start.1 = (f32[256,128]{1,0:T(8,128)S(1)}, f32[256,128]{1,0:T(8,128)S(1)}, u32[]{:S(2)}, u32[]{:S(2)}) collective-permute-start(f32[256,128]{1,0:T(8,128)S(1)} %convolution_bitcast_fusion.1.own_low), channel_id=1, source_target_pairs={{3,1},{0,2},{7,5},{4,6},{11,9},{8,10},{15,13},{12,14},{19,17},{16,... | collective-permute-start | bytes 393224 | tf_op jit(solution)/shard_map/ppermute | solution.py:253
  13.1 0.0 copy-done
  13.1 3.4 %fusion.3.low_in = f32[1024,128]{1,0:T(8,128)S(1)} fusion(bf16[1024,2048]{1,0:T(8,128)(2,1)} %param.6, bf16[2048,128]{1,0:T(8,128)(2,1)S(1)} %copy-done), kind=kOutput, calls=%fused_computation.13 | convolution fusion | flops 536870912 | bytes 5242880 | tf_op jit(solution)/shard_map/dot_general | solution.py:250
  16.5 0.0 copy-done.1
  16.6 5.4 %input_grad_rows.4.refs_3_ = bf16[4,256,2048]{2,1,0:T(8,128)(2,1)} custom-call(s32[1]{0:T(128)} %bitcast.me, bf16[256,2048]{1,0:T(8,128)(2,1)S(1)} %copy-done.1, bf16[256,2048]{1,0:T(8,128)(2,1)S(1)} %copy-done.1, bf16[2048,2048]{1,0:T(8,128)(2,1)} %refs_2_.7), custom_call_target="tpu_custom_call" | custom-call | flops 524288 | bytes 524288 | tf_op jit(solution)/shard_map/input_grad_rows/pallas_call | solution.py:131
  22.0 0.0 copy-start.4
  22.0 7.2 %collective-permute-done.1.far_low = f32[256,128]{1,0:T(8,128)S(1)} collective-permute-done((f32[256,128]{1,0:T(8,128)S(1)}, f32[256,128]{1,0:T(8,128)S(1)}, u32[]{:S(2)}, u32[]{:S(2)}) %collective-permute-start.1) | collective-permute-done | bytes 131104 | tf_op jit(solution)/shard_map/ppermute | solution.py:253
  29.2 0.0 collective-permute-done.refs_0_.refs_1_
  29.2 0.7 collective-permute-start.2
  29.9 0.0 collective-permute-done.4.refs_0_
  30.0 1.3 %collective-permute-start.7 = (bf16[256,2048]{1,0:T(8,128)(2,1)}, bf16[256,2048]{1,0:T(8,128)(2,1)}, u32[]{:S(2)}, u32[]{:S(2)}) collective-permute-start(bf16[256,2048]{1,0:T(8,128)(2,1)} %collective-permute-done.4.refs_0_), channel_id=1, source_target_pairs={{1,0},{2,3},{5,4},{6,7},{9,8},{10,11},{13,12},{14,15},{17,16},{18,... | collective-permute-start | bytes 3145736 | tf_op jit(solution)/shard_map/ppermute | solution.py:257
  31.3 8.1 %collective-permute-start.3 = (f32[1024,128]{1,0:T(8,128)S(1)}, f32[1024,128]{1,0:T(8,128)S(1)}, u32[]{:S(2)}, u32[]{:S(2)}) collective-permute-start(f32[1024,128]{1,0:T(8,128)S(1)} %fusion.3.low_in), channel_id=1, source_target_pairs={{0,1},{3,2},{4,5},{7,6},{8,9},{11,10},{12,13},{15,14},{16,17},{19,... | collective-permute-start | bytes 1572872 | tf_op jit(solution)/shard_map/ppermute | solution.py:258
  39.3 5.4 %input_grad_rows.5.refs_3_ = bf16[4,256,2048]{2,1,0:T(8,128)(2,1)} custom-call(s32[1]{0:T(128)} %bitcast.me, bf16[256,2048]{1,0:T(8,128)(2,1)S(1)} %collective-permute-done.refs_0_.refs_1_, bf16[256,2048]{1,0:T(8,128)(2,1)S(1)} %collective-permute-done.refs_0_.refs_1_, bf16[2048,2048]{1,0:T(8,128)(2,1)} %refs_2_.7, ...), custom_call_target="tpu_custom_call", output_to_operand_aliasing={{}: (4, {})} | custom-call | flops 524288 | bytes 524288 | tf_op jit(solution)/shard_map/input_grad_rows/pallas_call | solution.py:131
  44.8 0.0 copy-done.4
  44.8 0.4 fusion.4.beside_low
  45.2 1.7 %convolution_bitcast_fusion.facing_low = f32[256,128]{1,0:T(8,128)S(1)} fusion(bf16[2048,128]{0,1:T(8,128)(2,1)S(1)} %copy-done.4, bf16[256,2048]{1,0:T(8,128)(2,1)} %collective-permute-done.4.refs_0_), kind=kOutput, calls=%fused_computation | convolution fusion | flops 134217728 | bytes 1703936 | tf_op jit(solution)/shard_map/dot_general | solution.py:244
  46.9 2.4 %collective-permute-done.3.low_in_beside = f32[1024,128]{1,0:T(8,128)S(1)} collective-permute-done((f32[1024,128]{1,0:T(8,128)S(1)}, f32[1024,128]{1,0:T(8,128)S(1)}, u32[]{:S(2)}, u32[]{:S(2)}) %collective-permute-start.3) | collective-permute-done | bytes 524320 | tf_op jit(solution)/shard_map/ppermute | solution.py:258
  49.2 0.7 token_sums.1
  50.0 0.7 collective-permute-start.5
  50.6 0.0 collective-permute-done.5
  50.6 0.0 collective-permute-done.2.refs_0_
  50.7 1.3 %collective-permute-start.6 = (bf16[256,2048]{1,0:T(8,128)(2,1)S(1)}, bf16[256,2048]{1,0:T(8,128)(2,1)S(1)}, u32[]{:S(2)}, u32[]{:S(2)}) collective-permute-start(bf16[256,2048]{1,0:T(8,128)(2,1)S(1)} %collective-permute-done.2.refs_0_), channel_id=1, source_target_pairs={{1,0},{2,3},{5,4},{6,7},{9,8},{10,11},{13,12},{14,15},{17,16},{18,... | collective-permute-start | bytes 3145736 | tf_op jit(solution)/shard_map/ppermute | solution.py:275
  52.0 6.7 %collective-permute-done.7.refs_1_ = bf16[256,2048]{1,0:T(8,128)(2,1)} collective-permute-done((bf16[256,2048]{1,0:T(8,128)(2,1)}, bf16[256,2048]{1,0:T(8,128)(2,1)}, u32[]{:S(2)}, u32[]{:S(2)}) %collective-permute-start.7) | collective-permute-done | bytes 1048608 | tf_op jit(solution)/shard_map/ppermute | solution.py:257
  58.7 1.3 %collective-permute-start.8 = (f32[1,32,64]{2,1,0:T(8,128)S(1)}, f32[1,32,64]{2,1,0:T(8,128)S(1)}, u32[]{:S(2)}, u32[]{:S(2)}) collective-permute-start(f32[1,32,64]{2,1,0:T(8,128)S(1)} %dynamic-slice_bitcast_fusion), channel_id=1, source_target_pairs={{2,0},{1,3},{6,4},{5,7},{10,8},{9,11},{14,12},{13,15},{18,16},{17,... | collective-permute-start | bytes 24584 | tf_op jit(solution)/shard_map/ppermute | solution.py:278
  60.0 5.3 %collective-permute-done.8 = f32[1,32,64]{2,1,0:T(8,128)S(1)} collective-permute-done((f32[1,32,64]{2,1,0:T(8,128)S(1)}, f32[1,32,64]{2,1,0:T(8,128)S(1)}, u32[]{:S(2)}, u32[]{:S(2)}) %collective-permute-start.8) | collective-permute-done | bytes 8224 | tf_op jit(solution)/shard_map/ppermute | solution.py:278
  65.3 0.1 reshape.23.refs_0_
  65.4 1.5 %collective-permute-start.10 = (f32[1,2048]{1,0:T(1,128)S(1)}, f32[1,2048]{1,0:T(1,128)S(1)}, u32[]{:S(2)}, u32[]{:S(2)}) collective-permute-start(f32[1,2048]{1,0:T(1,128)S(1)} %reshape.23.refs_0_), channel_id=1, source_target_pairs={{0,8},{4,12},{8,0},{12,4},{1,9},{5,13},{9,1},{13,5},{2,10},{6,14},... | collective-permute-start | bytes 24584 | tf_op jit(solution)/shard_map/ppermute | solution.py:305
  66.9 0.0 collective-permute-start.11
  66.9 0.5 collective-permute-start.9
  67.4 0.0 copy-start.2
  67.4 7.3 %input_grad_rows.6.refs_3_ = bf16[4,256,2048]{2,1,0:T(8,128)(2,1)} custom-call(s32[1]{0:T(128)} %bitcast.me, bf16[256,2048]{1,0:T(8,128)(2,1)} %collective-permute-done.4.refs_0_, bf16[256,2048]{1,0:T(8,128)(2,1)} %collective-permute-done.7.refs_1_, bf16[2048,2048]{1,0:T(8,128)(2,1)} %refs_2_.7, ...), custom_call_target="tpu_custom_call", output_to_operand_aliasing={{}: (4, {})} | custom-call | flops 524288 | bytes 524288 | tf_op jit(solution)/shard_map/input_grad_rows/pallas_call | solution.py:131
  74.8 0.0 collective-permute-done.10.refs_2_
  74.8 0.0 collective-permute-done.11.refs_3_
  74.8 0.0 collective-permute-done.9.refs_1_
  74.8 0.0 copy-done.2
  74.8 1.7 %scores.1 = (f32[1,512]{1,0:T(1,128)S(1)}, f32[1,512]{1,0:T(1,128)S(1)}, f32[1,512]{1,0:T(1,128)S(1)}, f32[1,512]{1,0:T(1,128)S(1)}) custom-call(s32[1]{0:T(128)} %bitcast.7.first, f32[1,2048]{1,0:T(1,128)S(1)} %reshape.23.refs_0_, f32[1,2048]{1,0:T(1,128)S(1)} %collective-permute-done.9.refs_1_, f32[1,2048]{1,0:T(1,128)S(1)} %collective-permute-done.10.refs_2_, ...), custom_call_target="tpu_custom_call" | custom-call | tf_op jit(solution)/shard_map/scores/pallas_call | solution.py:43
  76.5 0.7 collective-permute-start.12
  77.2 1.6 %collective-permute-start.13 = (f32[1,512]{1,0:T(1,128)S(1)}, f32[1,512]{1,0:T(1,128)S(1)}, u32[]{:S(2)}, u32[]{:S(2)}) collective-permute-start(f32[1,512]{1,0:T(1,128)S(1)} %get-tuple-element.38), channel_id=1, source_target_pairs={{0,4},{1,8},{2,12},{3,0},{4,5},{5,9},{6,13},{7,1},{8,6},{9,10},{10... | collective-permute-start | bytes 6152 | tf_op jit(solution)/shard_map/ppermute | solution.py:315
  78.9 1.9 %collective-permute-start.14 = (f32[1,512]{1,0:T(1,128)S(1)}, f32[1,512]{1,0:T(1,128)S(1)}, u32[]{:S(2)}, u32[]{:S(2)}) collective-permute-start(f32[1,512]{1,0:T(1,128)S(1)} %get-tuple-element.39), channel_id=1, source_target_pairs={{0,8},{1,12},{2,0},{3,4},{4,9},{5,13},{6,1},{7,5},{8,10},{9,14},{1... | collective-permute-start | bytes 6152 | tf_op jit(solution)/shard_map/ppermute | solution.py:315
  80.8 2.1 %collective-permute-done.6.refs_1_ = bf16[256,2048]{1,0:T(8,128)(2,1)S(1)} collective-permute-done((bf16[256,2048]{1,0:T(8,128)(2,1)S(1)}, bf16[256,2048]{1,0:T(8,128)(2,1)S(1)}, u32[]{:S(2)}, u32[]{:S(2)}) %collective-permute-start.6) | collective-permute-done | bytes 1048608 | tf_op jit(solution)/shard_map/ppermute | solution.py:275
  82.9 1.4 %collective-permute-start.15 = (f32[1,512]{1,0:T(1,128)S(1)}, f32[1,512]{1,0:T(1,128)S(1)}, u32[]{:S(2)}, u32[]{:S(2)}) collective-permute-start(f32[1,512]{1,0:T(1,128)S(1)} %get-tuple-element.41), channel_id=1, source_target_pairs={{0,12},{1,0},{2,4},{3,8},{4,13},{5,1},{6,5},{7,9},{8,14},{9,2},{10... | collective-permute-start | bytes 6152 | tf_op jit(solution)/shard_map/ppermute | solution.py:315
  84.3 5.4 %input_grad_rows.7 = bf16[4,256,2048]{2,1,0:T(8,128)(2,1)} custom-call(s32[1]{0:T(128)} %bitcast.me, bf16[256,2048]{1,0:T(8,128)(2,1)S(1)} %collective-permute-done.2.refs_0_, bf16[256,2048]{1,0:T(8,128)(2,1)S(1)} %collective-permute-done.6.refs_1_, bf16[2048,2048]{1,0:T(8,128)(2,1)} %refs_2_.7, ...), custom_call_target="tpu_custom_call", output_to_operand_aliasing={{}: (4, {})} | custom-call | flops 524288 | bytes 524288 | tf_op jit(solution)/shard_map/input_grad_rows/pallas_call | solution.py:131
  89.7 0.0 collective-permute-done.12
  89.7 0.0 collective-permute-done.13
  89.7 0.0 collective-permute-done.14
  89.7 0.0 collective-permute-done.15
  89.7 0.6 add_add_fusion
  (4 shorter events, 0.1 us)
Async XLA Ops:
  0.6 12.5 %copy-start = (bf16[2048,128]{1,0:T(8,128)(2,1)S(1)}, bf16[2048,128]{1,0:T(8,128)(2,1)}, u32[]{:S(2)}) copy-start(bf16[2048,128]{1,0:T(8,128)(2,1)} %param.9) | copy-start | bytes 1572868
  0.6 28.6 %collective-permute-start = (bf16[256,2048]{1,0:T(8,128)(2,1)}, bf16[256,2048]{1,0:T(8,128)(2,1)S(1)}, u32[]{:S(2)}, u32[]{:S(2)}) collective-permute-start(bf16[256,2048]{1,0:T(8,128)(2,1)} %refs_1_.1), channel_id=1, source_target_pairs={{0,1},{1,0},{2,3},{3,2},{4,5},{5,4},{6,7},{7,6},{8,9},{9,8},{10,11... | collective-permute-start | bytes 3145736 | tf_op jit(solution)/shard_map/ppermute | solution.py:247
  3.7 26.2 %collective-permute-start.4 = (bf16[256,2048]{1,0:T(8,128)(2,1)}, bf16[256,2048]{1,0:T(8,128)(2,1)}, u32[]{:S(2)}, u32[]{:S(2)}) collective-permute-start(bf16[256,2048]{1,0:T(8,128)(2,1)} %refs_1_.1), channel_id=1, source_target_pairs={{1,2},{2,1},{5,6},{6,5},{9,10},{10,9},{13,14},{14,13},{17,18},{18,... | collective-permute-start | bytes 3145736 | tf_op jit(solution)/shard_map/ppermute | solution.py:246
  6.4 1.9 %copy-start.3 = (bf16[2048,128]{0,1:T(8,128)(2,1)}, bf16[2048,128]{0,1:T(8,128)(2,1)S(1)}, u32[]{:S(2)}) copy-start(bf16[2048,128]{0,1:T(8,128)(2,1)S(1)} %fusion.2) | copy-start | bytes 1572868
  6.4 10.1 %copy-start.1 = (bf16[256,2048]{1,0:T(8,128)(2,1)S(1)}, bf16[256,2048]{1,0:T(8,128)(2,1)}, u32[]{:S(2)}) copy-start(bf16[256,2048]{1,0:T(8,128)(2,1)} %refs_1_.1) | copy-start | bytes 3145732
  8.3 20.9 %collective-permute-start.1 = (f32[256,128]{1,0:T(8,128)S(1)}, f32[256,128]{1,0:T(8,128)S(1)}, u32[]{:S(2)}, u32[]{:S(2)}) collective-permute-start(f32[256,128]{1,0:T(8,128)S(1)} %convolution_bitcast_fusion.1.own_low), channel_id=1, source_target_pairs={{3,1},{0,2},{7,5},{4,6},{11,9},{8,10},{15,13},{12,14},{19,17},{16,... | collective-permute-start | bytes 393224 | tf_op jit(solution)/shard_map/ppermute | solution.py:253
  22.0 22.8 %copy-start.4 = (bf16[2048,128]{0,1:T(8,128)(2,1)S(1)}, bf16[2048,128]{0,1:T(8,128)(2,1)}, u32[]{:S(2)}) copy-start(bf16[2048,128]{0,1:T(8,128)(2,1)} %copy-done.3) | copy-start | bytes 1572868
  29.2 21.4 %collective-permute-start.2 = (bf16[256,2048]{1,0:T(8,128)(2,1)S(1)}, bf16[256,2048]{1,0:T(8,128)(2,1)S(1)}, u32[]{:S(2)}, u32[]{:S(2)}) collective-permute-start(bf16[256,2048]{1,0:T(8,128)(2,1)S(1)} %collective-permute-done.refs_0_.refs_1_), channel_id=1, source_target_pairs={{1,2},{2,1},{5,6},{6,5},{9,10},{10,9},{13,14},{14,13},{17,18},{18,... | collective-permute-start | bytes 3145736 | tf_op jit(solution)/shard_map/ppermute | solution.py:256
  30.0 28.7 %collective-permute-start.7 = (bf16[256,2048]{1,0:T(8,128)(2,1)}, bf16[256,2048]{1,0:T(8,128)(2,1)}, u32[]{:S(2)}, u32[]{:S(2)}) collective-permute-start(bf16[256,2048]{1,0:T(8,128)(2,1)} %collective-permute-done.4.refs_0_), channel_id=1, source_target_pairs={{1,0},{2,3},{5,4},{6,7},{9,8},{10,11},{13,12},{14,15},{17,16},{18,... | collective-permute-start | bytes 3145736 | tf_op jit(solution)/shard_map/ppermute | solution.py:257
  31.3 18.0 %collective-permute-start.3 = (f32[1024,128]{1,0:T(8,128)S(1)}, f32[1024,128]{1,0:T(8,128)S(1)}, u32[]{:S(2)}, u32[]{:S(2)}) collective-permute-start(f32[1024,128]{1,0:T(8,128)S(1)} %fusion.3.low_in), channel_id=1, source_target_pairs={{0,1},{3,2},{4,5},{7,6},{8,9},{11,10},{12,13},{15,14},{16,17},{19,... | collective-permute-start | bytes 1572872 | tf_op jit(solution)/shard_map/ppermute | solution.py:258
  50.0 0.7 collective-permute-start.5
  50.7 32.2 %collective-permute-start.6 = (bf16[256,2048]{1,0:T(8,128)(2,1)S(1)}, bf16[256,2048]{1,0:T(8,128)(2,1)S(1)}, u32[]{:S(2)}, u32[]{:S(2)}) collective-permute-start(bf16[256,2048]{1,0:T(8,128)(2,1)S(1)} %collective-permute-done.2.refs_0_), channel_id=1, source_target_pairs={{1,0},{2,3},{5,4},{6,7},{9,8},{10,11},{13,12},{14,15},{17,16},{18,... | collective-permute-start | bytes 3145736 | tf_op jit(solution)/shard_map/ppermute | solution.py:275
  58.7 6.6 %collective-permute-start.8 = (f32[1,32,64]{2,1,0:T(8,128)S(1)}, f32[1,32,64]{2,1,0:T(8,128)S(1)}, u32[]{:S(2)}, u32[]{:S(2)}) collective-permute-start(f32[1,32,64]{2,1,0:T(8,128)S(1)} %dynamic-slice_bitcast_fusion), channel_id=1, source_target_pairs={{2,0},{1,3},{6,4},{5,7},{10,8},{9,11},{14,12},{13,15},{18,16},{17,... | collective-permute-start | bytes 24584 | tf_op jit(solution)/shard_map/ppermute | solution.py:278
  65.4 9.4 %collective-permute-start.10 = (f32[1,2048]{1,0:T(1,128)S(1)}, f32[1,2048]{1,0:T(1,128)S(1)}, u32[]{:S(2)}, u32[]{:S(2)}) collective-permute-start(f32[1,2048]{1,0:T(1,128)S(1)} %reshape.23.refs_0_), channel_id=1, source_target_pairs={{0,8},{4,12},{8,0},{12,4},{1,9},{5,13},{9,1},{13,5},{2,10},{6,14},... | collective-permute-start | bytes 24584 | tf_op jit(solution)/shard_map/ppermute | solution.py:305
  66.9 7.9 %collective-permute-start.11 = (f32[1,2048]{1,0:T(1,128)S(1)}, f32[1,2048]{1,0:T(1,128)S(1)}, u32[]{:S(2)}, u32[]{:S(2)}) collective-permute-start(f32[1,2048]{1,0:T(1,128)S(1)} %reshape.23.refs_0_), channel_id=1, source_target_pairs={{0,12},{4,0},{8,4},{12,8},{1,13},{5,1},{9,5},{13,9},{2,14},{6,2},{... | collective-permute-start | bytes 24584 | tf_op jit(solution)/shard_map/ppermute | solution.py:305
  66.9 7.9 %collective-permute-start.9 = (f32[1,2048]{1,0:T(1,128)S(1)}, f32[1,2048]{1,0:T(1,128)S(1)}, u32[]{:S(2)}, u32[]{:S(2)}) collective-permute-start(f32[1,2048]{1,0:T(1,128)S(1)} %reshape.23.refs_0_), channel_id=1, source_target_pairs={{0,4},{4,8},{8,12},{12,0},{1,5},{5,9},{9,13},{13,1},{2,6},{6,10},{... | collective-permute-start | bytes 24584 | tf_op jit(solution)/shard_map/ppermute | solution.py:305
  67.4 7.4 %copy-start.2 = (bf16[512,2048]{1,0:T(8,128)(2,1)S(1)}, bf16[512,2048]{1,0:T(8,128)(2,1)}, u32[]{:S(2)}) copy-start(bf16[512,2048]{1,0:T(8,128)(2,1)} %refs_4_.1) | copy-start | bytes 6291460
  76.5 13.1 %collective-permute-start.12 = (f32[1,512]{1,0:T(1,128)S(1)}, f32[1,512]{1,0:T(1,128)S(1)}, u32[]{:S(2)}, u32[]{:S(2)}) collective-permute-start(f32[1,512]{1,0:T(1,128)S(1)} %get-tuple-element.37), channel_id=1, source_target_pairs={{0,0},{1,4},{2,8},{3,12},{4,1},{5,5},{6,9},{7,13},{8,2},{9,6},{10,... | collective-permute-start | bytes 6152 | tf_op jit(solution)/shard_map/ppermute | solution.py:315
  77.2 12.4 %collective-permute-start.13 = (f32[1,512]{1,0:T(1,128)S(1)}, f32[1,512]{1,0:T(1,128)S(1)}, u32[]{:S(2)}, u32[]{:S(2)}) collective-permute-start(f32[1,512]{1,0:T(1,128)S(1)} %get-tuple-element.38), channel_id=1, source_target_pairs={{0,4},{1,8},{2,12},{3,0},{4,5},{5,9},{6,13},{7,1},{8,6},{9,10},{10... | collective-permute-start | bytes 6152 | tf_op jit(solution)/shard_map/ppermute | solution.py:315
  78.9 10.8 %collective-permute-start.14 = (f32[1,512]{1,0:T(1,128)S(1)}, f32[1,512]{1,0:T(1,128)S(1)}, u32[]{:S(2)}, u32[]{:S(2)}) collective-permute-start(f32[1,512]{1,0:T(1,128)S(1)} %get-tuple-element.39), channel_id=1, source_target_pairs={{0,8},{1,12},{2,0},{3,4},{4,9},{5,13},{6,1},{7,5},{8,10},{9,14},{1... | collective-permute-start | bytes 6152 | tf_op jit(solution)/shard_map/ppermute | solution.py:315
  82.9 6.8 %collective-permute-start.15 = (f32[1,512]{1,0:T(1,128)S(1)}, f32[1,512]{1,0:T(1,128)S(1)}, u32[]{:S(2)}, u32[]{:S(2)}) collective-permute-start(f32[1,512]{1,0:T(1,128)S(1)} %get-tuple-element.41), channel_id=1, source_target_pairs={{0,12},{1,0},{2,4},{3,8},{4,13},{5,1},{6,5},{7,9},{8,14},{9,2},{10... | collective-permute-start | bytes 6152 | tf_op jit(solution)/shard_map/ppermute | solution.py:315
